TPU v7x, 128 devices: a whole 4x4x4 slice. The times are simulated.
128 devices in a mesh: fsdp: 8 (over z, x_lo), seq: 16 (over x_hi, y, core).
Axes of the slice: x: 4 (x_hi: 2, x_lo: 2; x = x_hi * 2 + x_lo), y: 4, z: 4, core: 2. Of those that a mesh axis runs over, the one named last changes fastest.
Arguments:
- layer_input: bfloat16 [8, 2560, 1152], P('fsdp', 'seq'), may hold values from -6 to 6
- segment: int32 [8, 2560], P('fsdp'), may hold values from 0 to 12, as said below
- position: int32 [8, 2560], P('fsdp'), may hold values from 0 to 1759, as said below
- loss_token_mask: int32 [8, 2560], P('fsdp', 'seq'), may hold values from 0 to 1
- teacher: bfloat16 [8, 2560, 1152], P('fsdp', 'seq'), may hold values from -6 to 6
- attention_norm_gain: bfloat16 [1152], P(('fsdp', 'seq')), may hold values from -0.5 to 0.5
- query_weight: bfloat16 [1152, 1024], P(('fsdp', 'seq')), may hold values from -0.1875 to 0.1875
- key_weight: bfloat16 [1152, 256], P(('fsdp', 'seq')), may hold values from -0.1875 to 0.1875
- value_weight: bfloat16 [1152, 256], P(('fsdp', 'seq')), may hold values from -0.1875 to 0.1875
- output_weight: bfloat16 [1024, 1152], P(('fsdp', 'seq')), may hold values from -1.5 to 1.5
- adapter_query_first: bfloat16 [1152, 256], P(('fsdp', 'seq')), may hold values from -0.1875 to 0.1875
- adapter_query_second: bfloat16 [256, 1024], P(('fsdp', 'seq')), may hold values from -0.1875 to 0.1875
- adapter_key_first: bfloat16 [1152, 256], P(('fsdp', 'seq')), may hold values from -0.1875 to 0.1875
- adapter_key_second: bfloat16 [256, 256], P(('fsdp', 'seq')), may hold values from -0.1875 to 0.1875
- adapter_value_first: bfloat16 [1152, 256], P(('fsdp', 'seq')), may hold values from -0.1875 to 0.1875
- adapter_value_second: bfloat16 [256, 256], P(('fsdp', 'seq')), may hold values from -0.1875 to 0.1875
- adapter_output_first: bfloat16 [1024, 256], P(('fsdp', 'seq')), may hold values from -0.1875 to 0.1875
- adapter_output_second: bfloat16 [256, 1152], P(('fsdp', 'seq')), may hold values from -1.5 to 1.5
- feedforward_norm_gain: bfloat16 [1152], P(('fsdp', 'seq')), may hold values from -0.5 to 0.5
- gate_weight: bfloat16 [1152, 6912], P(('fsdp', 'seq')), may hold values from -0.1875 to 0.1875
- up_weight: bfloat16 [1152, 6912], P(('fsdp', 'seq')), may hold values from -0.1875 to 0.1875
- down_weight: bfloat16 [6912, 1152], P(('fsdp', 'seq')), may hold values from -0.078125 to 0.078125
- adapter_gate_first: bfloat16 [1152, 256], P(('fsdp', 'seq')), may hold values from -0.1875 to 0.1875
- adapter_gate_second: bfloat16 [256, 6912], P(('fsdp', 'seq')), may hold values from -0.1875 to 0.1875
- adapter_up_first: bfloat16 [1152, 256], P(('fsdp', 'seq')), may hold values from -0.1875 to 0.1875
- adapter_up_second: bfloat16 [256, 6912], P(('fsdp', 'seq')), may hold values from -0.1875 to 0.1875
- adapter_down_first: bfloat16 [6912, 256], P(('fsdp', 'seq')), may hold values from -0.078125 to 0.078125
- adapter_down_second: bfloat16 [256, 1152], P(('fsdp', 'seq')), may hold values from -0.1875 to 0.1875
Outputs:
- hidden_out: bfloat16 [8, 2560, 1152], P('fsdp', 'seq')
- loss_value: float32 [], replicated
- grad_hidden: bfloat16 [8, 2560, 1152], P('fsdp', 'seq')
- grad_gain_attention: float32 [1152], P(('fsdp', 'seq'))
- grad_w_query: float32 [1152, 1024], P(('fsdp', 'seq'))
- grad_w_key: float32 [1152, 256], P(('fsdp', 'seq'))
- grad_w_value: float32 [1152, 256], P(('fsdp', 'seq'))
- grad_w_output: float32 [1024, 1152], P(('fsdp', 'seq'))
- grad_lora_query_in: float32 [1152, 256], P(('fsdp', 'seq'))
- grad_lora_query_out: float32 [256, 1024], P(('fsdp', 'seq'))
- grad_lora_key_in: float32 [1152, 256], P(('fsdp', 'seq'))
- grad_lora_key_out: float32 [256, 256], P(('fsdp', 'seq'))
- grad_lora_value_in: float32 [1152, 256], P(('fsdp', 'seq'))
- grad_lora_value_out: float32 [256, 256], P(('fsdp', 'seq'))
- grad_lora_output_in: float32 [1024, 256], P(('fsdp', 'seq'))
- grad_lora_output_out: float32 [256, 1152], P(('fsdp', 'seq'))
- grad_gain_feedforward: float32 [1152], P(('fsdp', 'seq'))
- grad_w_gate: float32 [1152, 6912], P(('fsdp', 'seq'))
- grad_w_up: float32 [1152, 6912], P(('fsdp', 'seq'))
- grad_w_down: float32 [6912, 1152], P(('fsdp', 'seq'))
- grad_lora_gate_in: float32 [1152, 256], P(('fsdp', 'seq'))
- grad_lora_gate_out: float32 [256, 6912], P(('fsdp', 'seq'))
- grad_lora_up_in: float32 [1152, 256], P(('fsdp', 'seq'))
- grad_lora_up_out: float32 [256, 6912], P(('fsdp', 'seq'))
- grad_lora_down_in: float32 [6912, 256], P(('fsdp', 'seq'))
- grad_lora_down_out: float32 [256, 1152], P(('fsdp', 'seq'))
Inputs may be any that keep to these rules, and one draw needn't show every extreme that they name: Within each tree the tokens run, in order: the trunk (segment 0), then for each branch b from 1 to 4 the branch b followed by its two leaves 3 + 2 b and 4 + 2 b. Every segment is a whole number of blocks of 80 tokens; the trunk has 16 to 20 of them. A token's position is its distance from the tree's root along its root-to-leaf path; the longest path of every tree has 1760 tokens.
All inputs are finite; a program needn't handle non-finite values.
Results may differ from a plain program's by a relative error of at most 0.015.
Values may be sent and summed in bfloat16 or wider, within the bound.
No kernel may reach another device: no remote copies, remote signals or barrier semaphores. Data moves between devices by JAX's collectives and lax.ppermute only.
A program may use at most 512 MiB of HBM per device.

v0:
```python
import jax
import jax.numpy as jnp
from jax import lax
from jax.sharding import PartitionSpec as P

EPSILON = 1e-06
ROPE_BASE = 10000.0
MASKED_SCORE = -1e30


def plain_product(left_side, right_side):
    return jnp.dot(left_side, right_side, preferred_element_type=jnp.float32)


def product_left_transposed(left_side, right_side):
    return lax.dot_general(
        left_side, right_side, (((0,), (0,)), ((), ())), preferred_element_type=jnp.float32
    )


def product_right_transposed(left_side, right_side):
    return lax.dot_general(
        left_side, right_side, (((1,), (1,)), ((), ())), preferred_element_type=jnp.float32
    )


def ancestor_mask(query_seg, key_seg, query_pos, key_pos):
    q_column = query_seg[:, None]
    k_row = key_seg[None, :]
    parent_branch = (
        (k_row >= 1) & (k_row <= 4) & (q_column >= 5) & ((q_column - 5) // 2 + 1 == k_row)
    )
    related = (k_row == q_column) | (k_row == 0) | parent_branch
    return related & (key_pos[None, :] <= query_pos[:, None])


def rope_tables(own_pos, head_size):
    half_size = head_size // 2
    frequency = ROPE_BASE ** (-(jnp.arange(half_size, dtype=jnp.float32) * 2.0 / head_size))
    angles = own_pos.astype(jnp.float32)[:, None] * frequency[None, :]
    return (jnp.cos(angles), jnp.sin(angles))


def rotate(values, cos_table, sin_table):
    half_size = values.shape[-1] // 2
    first_half = values[..., :half_size]
    second_half = values[..., half_size:]
    cos_part = cos_table[:, None, :]
    sin_part = sin_table[:, None, :]
    return jnp.concatenate(
        [
            first_half * cos_part - second_half * sin_part,
            second_half * cos_part + first_half * sin_part,
        ],
        axis=-1,
    )


def rotate_back(gradient, cos_table, sin_table):
    half_size = gradient.shape[-1] // 2
    first_half = gradient[..., :half_size]
    second_half = gradient[..., half_size:]
    cos_part = cos_table[:, None, :]
    sin_part = sin_table[:, None, :]
    return jnp.concatenate(
        [
            first_half * cos_part + second_half * sin_part,
            second_half * cos_part - first_half * sin_part,
        ],
        axis=-1,
    )


def norm_scale(values, gain_vector):
    return (
        values
        * lax.rsqrt(jnp.mean(values * values, axis=-1, keepdims=True) + EPSILON)
        * (1.0 + gain_vector)
    )


def gated_gelu(gate_logits, up_logits):
    return jax.nn.gelu(gate_logits, approximate=True) * up_logits


def adapter_projection(input_rows, frozen_weight, adapter_first_factor, adapter_second_factor):
    rank_row_block = plain_product(input_rows, adapter_first_factor).astype(jnp.bfloat16)
    return (
        plain_product(input_rows, frozen_weight)
        + plain_product(rank_row_block, adapter_second_factor),
        rank_row_block,
    )


def adapter_backward(
    input_rows,
    rank_row_block,
    frozen_weight,
    adapter_first_factor,
    adapter_second_factor,
    gradient_row_block,
):
    gradient_adapter_second = product_left_transposed(rank_row_block, gradient_row_block)
    gradient_rank_rows = product_right_transposed(gradient_row_block, adapter_second_factor).astype(
        jnp.bfloat16
    )
    gradient_adapter_first = product_left_transposed(input_rows, gradient_rank_rows)
    gradient_frozen = product_left_transposed(input_rows, gradient_row_block)
    gradient_input_rows = product_right_transposed(
        gradient_row_block, frozen_weight
    ) + product_right_transposed(gradient_rank_rows, adapter_first_factor)
    return (gradient_input_rows, gradient_frozen, gradient_adapter_first, gradient_adapter_second)


def on_device(
    layer_input,
    segment,
    position,
    loss_token_mask,
    teacher,
    attention_norm_gain,
    query_weight,
    key_weight,
    value_weight,
    output_weight,
    adapter_query_first,
    adapter_query_second,
    adapter_key_first,
    adapter_key_second,
    adapter_value_first,
    adapter_value_second,
    adapter_output_first,
    adapter_output_second,
    feedforward_norm_gain,
    gate_weight,
    up_weight,
    down_weight,
    adapter_gate_first,
    adapter_gate_second,
    adapter_up_first,
    adapter_up_second,
    adapter_down_first,
    adapter_down_second,
):
    tokens_here = layer_input.shape[1]
    model_width = layer_input.shape[2]
    head_size = key_weight.shape[1]
    head_count = query_weight.shape[1] // head_size
    score_scale = head_size ** (-0.5)
    first_token = lax.axis_index("seq") * tokens_here
    tree_seg = segment[0]
    tree_pos = position[0]
    own_seg = lax.dynamic_slice_in_dim(tree_seg, first_token, tokens_here)
    own_pos = lax.dynamic_slice_in_dim(tree_pos, first_token, tokens_here)
    cos_table, sin_table = rope_tables(own_pos, head_size)
    allowed = ancestor_mask(
        jnp.repeat(own_seg, head_count), tree_seg, jnp.repeat(own_pos, head_count), tree_pos
    )
    hidden = layer_input[0].astype(jnp.float32)
    (
        full_gain,
        complete_query,
        complete_key,
        complete_value,
        full_output,
        complete_query_first,
        complete_query_second,
        complete_key_first,
        complete_key_second,
        complete_value_first,
        complete_value_second,
        full_output_in,
        full_output_out,
    ) = (
        lax.all_gather(attention_norm_gain, ("fsdp", "seq"), axis=0, tiled=True),
        lax.all_gather(query_weight, ("fsdp", "seq"), axis=0, tiled=True),
        lax.all_gather(key_weight, ("fsdp", "seq"), axis=0, tiled=True),
        lax.all_gather(value_weight, ("fsdp", "seq"), axis=0, tiled=True),
        lax.all_gather(output_weight, ("fsdp", "seq"), axis=0, tiled=True),
        lax.all_gather(adapter_query_first, ("fsdp", "seq"), axis=0, tiled=True),
        lax.all_gather(adapter_query_second, ("fsdp", "seq"), axis=0, tiled=True),
        lax.all_gather(adapter_key_first, ("fsdp", "seq"), axis=0, tiled=True),
        lax.all_gather(adapter_key_second, ("fsdp", "seq"), axis=0, tiled=True),
        lax.all_gather(adapter_value_first, ("fsdp", "seq"), axis=0, tiled=True),
        lax.all_gather(adapter_value_second, ("fsdp", "seq"), axis=0, tiled=True),
        lax.all_gather(adapter_output_first, ("fsdp", "seq"), axis=0, tiled=True),
        lax.all_gather(adapter_output_second, ("fsdp", "seq"), axis=0, tiled=True),
    )
    attention_normed, norm_one_pull = jax.vjp(norm_scale, hidden, full_gain.astype(jnp.float32))
    attention_normed_copy = attention_normed.astype(jnp.bfloat16)
    unrotated_queries, query_rank_rows = adapter_projection(
        attention_normed_copy, complete_query, complete_query_first, complete_query_second
    )
    unrotated_keys, key_rank_rows = adapter_projection(
        attention_normed_copy, complete_key, complete_key_first, complete_key_second
    )
    value_projection_rows, value_rank_rows = adapter_projection(
        attention_normed_copy, complete_value, complete_value_first, complete_value_second
    )
    values_own = value_projection_rows.astype(jnp.bfloat16)
    queries_rot = rotate(
        unrotated_queries.reshape(tokens_here, head_count, head_size), cos_table, sin_table
    ).astype(jnp.bfloat16)
    keys_rot = rotate(unrotated_keys[:, None, :], cos_table, sin_table)[:, 0, :].astype(
        jnp.bfloat16
    )
    query_rows = queries_rot.reshape(tokens_here * head_count, head_size)
    keys_tree, values_tree = (
        lax.all_gather(keys_rot, "seq", axis=0, tiled=True),
        lax.all_gather(values_own, "seq", axis=0, tiled=True),
    )
    scores = jnp.where(
        allowed, product_right_transposed(query_rows, keys_tree) * score_scale, MASKED_SCORE
    )
    row_max = jnp.max(scores, axis=-1, keepdims=True)
    exponent = jnp.exp(scores - row_max)
    row_total = jnp.sum(exponent, axis=-1, keepdims=True)
    log_total = row_max + jnp.log(row_total)
    attention_mix = plain_product((exponent / row_total).astype(jnp.bfloat16), values_tree)
    attention_mix = attention_mix.reshape(tokens_here, head_count * head_size).astype(jnp.bfloat16)
    attention_result, output_rank_rows = adapter_projection(
        attention_mix, full_output, full_output_in, full_output_out
    )
    after_attention = hidden + attention_result
    (
        ff_gain,
        feedforward_gate,
        feedforward_up,
        feedforward_down,
        feedforward_gate_first,
        feedforward_gate_second,
        feedforward_up_first,
        feedforward_up_second,
        feedforward_down_first,
        feedforward_down_second,
    ) = (
        lax.all_gather(feedforward_norm_gain, ("fsdp", "seq"), axis=0, tiled=True),
        lax.all_gather(gate_weight, ("fsdp", "seq"), axis=0, tiled=True),
        lax.all_gather(up_weight, ("fsdp", "seq"), axis=0, tiled=True),
        lax.all_gather(down_weight, ("fsdp", "seq"), axis=0, tiled=True),
        lax.all_gather(adapter_gate_first, ("fsdp", "seq"), axis=0, tiled=True),
        lax.all_gather(adapter_gate_second, ("fsdp", "seq"), axis=0, tiled=True),
        lax.all_gather(adapter_up_first, ("fsdp", "seq"), axis=0, tiled=True),
        lax.all_gather(adapter_up_second, ("fsdp", "seq"), axis=0, tiled=True),
        lax.all_gather(adapter_down_first, ("fsdp", "seq"), axis=0, tiled=True),
        lax.all_gather(adapter_down_second, ("fsdp", "seq"), axis=0, tiled=True),
    )
    feedforward_normed, norm_two_pull = jax.vjp(
        norm_scale, after_attention, ff_gain.astype(jnp.float32)
    )
    feedforward_normed_copy = feedforward_normed.astype(jnp.bfloat16)
    gate_logits, gate_rank_rows = adapter_projection(
        feedforward_normed_copy, feedforward_gate, feedforward_gate_first, feedforward_gate_second
    )
    up_logits, up_rank_rows = adapter_projection(
        feedforward_normed_copy, feedforward_up, feedforward_up_first, feedforward_up_second
    )
    gated_hidden, activation_pull = jax.vjp(gated_gelu, gate_logits, up_logits)
    gated_hidden_copy = gated_hidden.astype(jnp.bfloat16)
    feedforward_result, down_rank_rows = adapter_projection(
        gated_hidden_copy, feedforward_down, feedforward_down_first, feedforward_down_second
    )
    result = after_attention + feedforward_result
    valid_rows = loss_token_mask[0].astype(jnp.float32)[:, None]
    error_rows = result - teacher[0].astype(jnp.float32)
    loss_sum, valid_count = lax.psum(
        (jnp.sum(valid_rows * error_rows * error_rows), jnp.sum(valid_rows)), ("fsdp", "seq")
    )
    loss_value = loss_sum / (model_width * valid_count)
    total_tokens = segment.shape[1] * lax.axis_size("fsdp")
    grad_result = 2.0 * total_tokens / valid_count * valid_rows * error_rows
    gradient_gated_hidden, gradient_feedforward_down, gradient_down_first, gradient_down_second = (
        adapter_backward(
            gated_hidden_copy,
            down_rank_rows,
            feedforward_down,
            feedforward_down_first,
            feedforward_down_second,
            grad_result.astype(jnp.bfloat16),
        )
    )
    grad_gate, grad_up = activation_pull(
        gradient_gated_hidden.astype(jnp.bfloat16).astype(jnp.float32)
    )
    gradient_via_gate, gradient_feedforward_gate, gradient_gate_first, gradient_gate_second = (
        adapter_backward(
            feedforward_normed_copy,
            gate_rank_rows,
            feedforward_gate,
            feedforward_gate_first,
            feedforward_gate_second,
            grad_gate.astype(jnp.bfloat16),
        )
    )
    gradient_via_up, gradient_feedforward_up, gradient_up_first, gradient_up_second = (
        adapter_backward(
            feedforward_normed_copy,
            up_rank_rows,
            feedforward_up,
            feedforward_up_first,
            feedforward_up_second,
            grad_up.astype(jnp.bfloat16),
        )
    )
    grad_after_norm, grad_gain_ff = norm_two_pull(gradient_via_gate + gradient_via_up)
    grad_after = grad_result + grad_after_norm
    ff_shards = (
        lax.psum_scatter(grad_gain_ff, ("fsdp", "seq"), scatter_dimension=0, tiled=True),
        lax.psum_scatter(
            gradient_feedforward_gate, ("fsdp", "seq"), scatter_dimension=0, tiled=True
        ),
        lax.psum_scatter(gradient_feedforward_up, ("fsdp", "seq"), scatter_dimension=0, tiled=True),
        lax.psum_scatter(
            gradient_feedforward_down, ("fsdp", "seq"), scatter_dimension=0, tiled=True
        ),
        lax.psum_scatter(gradient_gate_first, ("fsdp", "seq"), scatter_dimension=0, tiled=True),
        lax.psum_scatter(gradient_gate_second, ("fsdp", "seq"), scatter_dimension=0, tiled=True),
        lax.psum_scatter(gradient_up_first, ("fsdp", "seq"), scatter_dimension=0, tiled=True),
        lax.psum_scatter(gradient_up_second, ("fsdp", "seq"), scatter_dimension=0, tiled=True),
        lax.psum_scatter(gradient_down_first, ("fsdp", "seq"), scatter_dimension=0, tiled=True),
        lax.psum_scatter(gradient_down_second, ("fsdp", "seq"), scatter_dimension=0, tiled=True),
    )
    (
        full_gain,
        complete_query,
        complete_key,
        complete_value,
        full_output,
        complete_query_first,
        complete_query_second,
        complete_key_first,
        complete_key_second,
        complete_value_first,
        complete_value_second,
        full_output_in,
        full_output_out,
    ) = (
        lax.all_gather(attention_norm_gain, ("fsdp", "seq"), axis=0, tiled=True),
        lax.all_gather(query_weight, ("fsdp", "seq"), axis=0, tiled=True),
        lax.all_gather(key_weight, ("fsdp", "seq"), axis=0, tiled=True),
        lax.all_gather(value_weight, ("fsdp", "seq"), axis=0, tiled=True),
        lax.all_gather(output_weight, ("fsdp", "seq"), axis=0, tiled=True),
        lax.all_gather(adapter_query_first, ("fsdp", "seq"), axis=0, tiled=True),
        lax.all_gather(adapter_query_second, ("fsdp", "seq"), axis=0, tiled=True),
        lax.all_gather(adapter_key_first, ("fsdp", "seq"), axis=0, tiled=True),
        lax.all_gather(adapter_key_second, ("fsdp", "seq"), axis=0, tiled=True),
        lax.all_gather(adapter_value_first, ("fsdp", "seq"), axis=0, tiled=True),
        lax.all_gather(adapter_value_second, ("fsdp", "seq"), axis=0, tiled=True),
        lax.all_gather(adapter_output_first, ("fsdp", "seq"), axis=0, tiled=True),
        lax.all_gather(adapter_output_second, ("fsdp", "seq"), axis=0, tiled=True),
    )
    (
        gradient_attention_mix,
        gradient_attention_output,
        gradient_output_first,
        gradient_output_second,
    ) = adapter_backward(
        attention_mix,
        output_rank_rows,
        full_output,
        full_output_in,
        full_output_out,
        grad_after.astype(jnp.bfloat16),
    )
    gradient_row_block = gradient_attention_mix.astype(jnp.bfloat16).reshape(
        tokens_here * head_count, head_size
    )
    scores_again = jnp.where(
        allowed, product_right_transposed(query_rows, keys_tree) * score_scale, MASKED_SCORE
    )
    attn_probs = jnp.where(allowed, jnp.exp(scores_again - log_total), 0.0)
    grad_probs = product_right_transposed(gradient_row_block, values_tree)
    grad_scores = (
        attn_probs * (grad_probs - jnp.sum(attn_probs * grad_probs, axis=-1, keepdims=True))
    ).astype(jnp.bfloat16)
    grad_query_rows = plain_product(grad_scores, keys_tree) * score_scale
    key_terms = product_left_transposed(grad_scores, query_rows) * score_scale
    value_terms = product_left_transposed(attn_probs.astype(jnp.bfloat16), gradient_row_block)
    grad_keys_rot, grad_values = (
        lax.psum_scatter(
            key_terms.astype(jnp.bfloat16), "seq", scatter_dimension=0, tiled=True
        ).astype(jnp.float32),
        lax.psum_scatter(
            value_terms.astype(jnp.bfloat16), "seq", scatter_dimension=0, tiled=True
        ).astype(jnp.float32),
    )
    grad_queries_pre = rotate_back(
        grad_query_rows.reshape(tokens_here, head_count, head_size), cos_table, sin_table
    ).reshape(tokens_here, head_count * head_size)
    grad_keys_pre = rotate_back(grad_keys_rot[:, None, :], cos_table, sin_table)[:, 0, :]
    gradient_via_query, gradient_attention_query, gradient_query_first, gradient_query_second = (
        adapter_backward(
            attention_normed_copy,
            query_rank_rows,
            complete_query,
            complete_query_first,
            complete_query_second,
            grad_queries_pre.astype(jnp.bfloat16),
        )
    )
    gradient_via_key, gradient_attention_key, gradient_key_first, gradient_key_second = (
        adapter_backward(
            attention_normed_copy,
            key_rank_rows,
            complete_key,
            complete_key_first,
            complete_key_second,
            grad_keys_pre.astype(jnp.bfloat16),
        )
    )
    gradient_via_value, gradient_attention_value, gradient_value_first, gradient_value_second = (
        adapter_backward(
            attention_normed_copy,
            value_rank_rows,
            complete_value,
            complete_value_first,
            complete_value_second,
            grad_values.astype(jnp.bfloat16),
        )
    )
    grad_hidden_norm, grad_gain_att = norm_one_pull(
        gradient_via_query + gradient_via_key + gradient_via_value
    )
    grad_input = grad_after + grad_hidden_norm
    att_shards = (
        lax.psum_scatter(grad_gain_att, ("fsdp", "seq"), scatter_dimension=0, tiled=True),
        lax.psum_scatter(
            gradient_attention_query, ("fsdp", "seq"), scatter_dimension=0, tiled=True
        ),
        lax.psum_scatter(gradient_attention_key, ("fsdp", "seq"), scatter_dimension=0, tiled=True),
        lax.psum_scatter(
            gradient_attention_value, ("fsdp", "seq"), scatter_dimension=0, tiled=True
        ),
        lax.psum_scatter(
            gradient_attention_output, ("fsdp", "seq"), scatter_dimension=0, tiled=True
        ),
        lax.psum_scatter(gradient_query_first, ("fsdp", "seq"), scatter_dimension=0, tiled=True),
        lax.psum_scatter(gradient_query_second, ("fsdp", "seq"), scatter_dimension=0, tiled=True),
        lax.psum_scatter(gradient_key_first, ("fsdp", "seq"), scatter_dimension=0, tiled=True),
        lax.psum_scatter(gradient_key_second, ("fsdp", "seq"), scatter_dimension=0, tiled=True),
        lax.psum_scatter(gradient_value_first, ("fsdp", "seq"), scatter_dimension=0, tiled=True),
        lax.psum_scatter(gradient_value_second, ("fsdp", "seq"), scatter_dimension=0, tiled=True),
        lax.psum_scatter(gradient_output_first, ("fsdp", "seq"), scatter_dimension=0, tiled=True),
        lax.psum_scatter(gradient_output_second, ("fsdp", "seq"), scatter_dimension=0, tiled=True),
    )
    return (
        result.astype(jnp.bfloat16)[None],
        loss_value,
        grad_input.astype(jnp.bfloat16)[None],
        att_shards[0],
        att_shards[1],
        att_shards[2],
        att_shards[3],
        att_shards[4],
        att_shards[5],
        att_shards[6],
        att_shards[7],
        att_shards[8],
        att_shards[9],
        att_shards[10],
        att_shards[11],
        att_shards[12],
        ff_shards[0],
        ff_shards[1],
        ff_shards[2],
        ff_shards[3],
        ff_shards[4],
        ff_shards[5],
        ff_shards[6],
        ff_shards[7],
        ff_shards[8],
        ff_shards[9],
    )


def solution(mesh):
    return jax.shard_map(
        on_device,
        mesh=mesh,
        in_specs=(
            P("fsdp", "seq", None),
            P("fsdp", None),
            P("fsdp", None),
            P("fsdp", "seq"),
            P("fsdp", "seq", None),
            P(("fsdp", "seq")),
            P(("fsdp", "seq"), None),
            P(("fsdp", "seq"), None),
            P(("fsdp", "seq"), None),
            P(("fsdp", "seq"), None),
            P(("fsdp", "seq"), None),
            P(("fsdp", "seq"), None),
            P(("fsdp", "seq"), None),
            P(("fsdp", "seq"), None),
            P(("fsdp", "seq"), None),
            P(("fsdp", "seq"), None),
            P(("fsdp", "seq"), None),
            P(("fsdp", "seq"), None),
            P(("fsdp", "seq")),
            P(("fsdp", "seq"), None),
            P(("fsdp", "seq"), None),
            P(("fsdp", "seq"), None),
            P(("fsdp", "seq"), None),
            P(("fsdp", "seq"), None),
            P(("fsdp", "seq"), None),
            P(("fsdp", "seq"), None),
            P(("fsdp", "seq"), None),
            P(("fsdp", "seq"), None),
        ),
        out_specs=(
            P("fsdp", "seq", None),
            P(),
            P("fsdp", "seq", None),
            P(("fsdp", "seq")),
            P(("fsdp", "seq"), None),
            P(("fsdp", "seq"), None),
            P(("fsdp", "seq"), None),
            P(("fsdp", "seq"), None),
            P(("fsdp", "seq"), None),
            P(("fsdp", "seq"), None),
            P(("fsdp", "seq"), None),
            P(("fsdp", "seq"), None),
            P(("fsdp", "seq"), None),
            P(("fsdp", "seq"), None),
            P(("fsdp", "seq"), None),
            P(("fsdp", "seq"), None),
            P(("fsdp", "seq")),
            P(("fsdp", "seq"), None),
            P(("fsdp", "seq"), None),
            P(("fsdp", "seq"), None),
            P(("fsdp", "seq"), None),
            P(("fsdp", "seq"), None),
            P(("fsdp", "seq"), None),
            P(("fsdp", "seq"), None),
            P(("fsdp", "seq"), None),
            P(("fsdp", "seq"), None),
        ),
        check_vma=False,
    )
```

profile of v0, /device:TPU:1, one launch (start us, length us, event | category | flops | bytes accessed | tf_op | source)
XLA Modules:
  0.0 4685.1 jit_solution(10944861432234891934)
XLA Ops:
  8.8 180.5 %all-gather.6 = bf16[128,2,256]{2,1,0:T(2,128)(2,1)S(1)} all-gather(bf16[1,2,256]{2,1,0:T(2,128)(2,1)} %bitcast.258), channel_id=1, replica_groups=mesh['fsdp'=8,'seq'=16] {'fsdp','seq'}, dimensions={0}, use_global_device_ids=true | all-gather | bytes 132096 | tf_op jit(solution)/shard_map/all_gather | solution.py:183
  189.3 173.5 %all-gather.4 = bf16[128,9,256]{2,1,0:T(8,128)(2,1)S(1)} all-gather(bf16[1,9,256]{2,1,0:T(8,128)(2,1)} %bitcast.247), channel_id=1, replica_groups=mesh['fsdp'=8,'seq'=16] {'fsdp','seq'}, dimensions={0}, use_global_device_ids=true | all-gather | bytes 594432 | tf_op jit(solution)/shard_map/all_gather | solution.py:177
  363.2 175.0 %all-gather.5 = bf16[128,9,256]{2,1,0:T(8,128)(2,1)S(1)} all-gather(bf16[1,9,256]{2,1,0:T(8,128)(2,1)} %bitcast.248), channel_id=1, replica_groups=mesh['fsdp'=8,'seq'=16] {'fsdp','seq'}, dimensions={0}, use_global_device_ids=true | all-gather | bytes 594432 | tf_op jit(solution)/shard_map/all_gather | solution.py:182
  539.0 62.0 %all-reduce.28 = (bf16[1152]{0:T(1024)(128)(2,1)S(1)}, bf16[1152]{0:T(1024)(128)(2,1)S(1)}) all-reduce(bf16[1152]{0:T(1024)(128)(2,1)S(1)} %dynamic-update-slice, bf16[1152]{0:T(1024)(128)(2,1)S(1)} %dynamic-update-slice.1), channel_id=1, replica_groups=mesh['fsdp'=8,'seq'=16] {'fsdp','seq'}, use_global_device_ids=true, to_apply=%add | all-reduce | flops 2304 | bytes 9216
  603.2 174.1 %all-gather.9 = bf16[128,2,256]{2,1,0:T(2,128)(2,1)S(1)} all-gather(bf16[1,2,256]{2,1,0:T(2,128)(2,1)S(1)} %bitcast.259), channel_id=1, replica_groups=mesh['fsdp'=8,'seq'=16] {'fsdp','seq'}, dimensions={0}, use_global_device_ids=true | all-gather | bytes 132096 | tf_op jit(solution)/shard_map/all_gather | solution.py:185
  777.4 173.3 %all-gather.7 = bf16[128,9,256]{2,1,0:T(8,128)(2,1)S(1)} all-gather(bf16[1,9,256]{2,1,0:T(8,128)(2,1)S(1)} %bitcast.249), channel_id=1, replica_groups=mesh['fsdp'=8,'seq'=16] {'fsdp','seq'}, dimensions={0}, use_global_device_ids=true | all-gather | bytes 594432 | tf_op jit(solution)/shard_map/all_gather | solution.py:178
  951.8 174.9 %all-gather.8 = bf16[128,9,256]{2,1,0:T(8,128)(2,1)S(1)} all-gather(bf16[1,9,256]{2,1,0:T(8,128)(2,1)S(1)} %bitcast.250), channel_id=1, replica_groups=mesh['fsdp'=8,'seq'=16] {'fsdp','seq'}, dimensions={0}, use_global_device_ids=true | all-gather | bytes 594432 | tf_op jit(solution)/shard_map/all_gather | solution.py:184
  1135.7 62.6 %psum.15 = f32[]{:T(128)} all-reduce(f32[]{:T(128)} %convert_reduce_fusion), channel_id=1, replica_groups=mesh['fsdp'=8,'seq'=16] {'fsdp','seq'}, use_global_device_ids=true, to_apply=%region_7.8 | all-reduce | flops 1 | bytes 8 | tf_op jit(solution)/shard_map/psum | solution.py:266
  1198.7 175.1 %all-gather.3 = bf16[128,2,1024]{2,1,0:T(2,128)(2,1)S(1)} all-gather(bf16[1,2,1024]{2,1,0:T(2,128)(2,1)S(1)} %bitcast.256), channel_id=1, replica_groups=mesh['fsdp'=8,'seq'=16] {'fsdp','seq'}, dimensions={0}, use_global_device_ids=true | all-gather | bytes 528384 | tf_op jit(solution)/shard_map/all_gather | solution.py:181
  1374.1 172.0 %all-gather.10 = bf16[128,2,1152]{2,1,0:T(2,128)(2,1)S(1)} all-gather(bf16[1,2,1152]{2,1,0:T(2,128)(2,1)S(1)} %bitcast.254), channel_id=1, replica_groups=mesh['fsdp'=8,'seq'=16] {'fsdp','seq'}, dimensions={0}, use_global_device_ids=true | all-gather | bytes 594432 | tf_op jit(solution)/shard_map/all_gather | solution.py:187
  1546.4 173.4 %all-gather.19 = bf16[128,2,1152]{2,1,0:T(2,128)(2,1)S(1)} all-gather(bf16[1,2,1152]{2,1,0:T(2,128)(2,1)S(1)} %bitcast.255), channel_id=1, replica_groups=mesh['fsdp'=8,'seq'=16] {'fsdp','seq'}, dimensions={0}, use_global_device_ids=true | all-gather | bytes 594432 | tf_op jit(solution)/shard_map/all_gather | solution.py:246
  1720.8 183.4 %all-gather.2 = bf16[128,9,256]{2,1,0:T(8,128)(2,1)} all-gather(bf16[1,9,256]{2,1,0:T(8,128)(2,1)S(1)} %bitcast.251), channel_id=1, replica_groups=mesh['fsdp'=8,'seq'=16] {'fsdp','seq'}, dimensions={0}, use_global_device_ids=true | all-gather | bytes 594432 | tf_op jit(solution)/shard_map/all_gather | solution.py:180
  1906.4 184.7 %all-gather.12 = bf16[128,9,256]{2,1,0:T(8,128)(2,1)} all-gather(bf16[1,9,256]{2,1,0:T(8,128)(2,1)S(1)} %bitcast.252), channel_id=1, replica_groups=mesh['fsdp'=8,'seq'=16] {'fsdp','seq'}, dimensions={0}, use_global_device_ids=true | all-gather | bytes 594432 | tf_op jit(solution)/shard_map/all_gather | solution.py:241
  2092.6 183.5 %all-gather.15 = bf16[128,9,256]{2,1,0:T(8,128)(2,1)} all-gather(bf16[1,9,256]{2,1,0:T(8,128)(2,1)S(1)} %bitcast.253), channel_id=1, replica_groups=mesh['fsdp'=8,'seq'=16] {'fsdp','seq'}, dimensions={0}, use_global_device_ids=true | all-gather | bytes 594432 | tf_op jit(solution)/shard_map/all_gather | solution.py:243
  2281.4 173.1 %all_gather.100 = bf16[1024,256]{1,0:T(8,128)(2,1)S(1)} all-gather(bf16[8,256]{1,0:T(8,128)(2,1)S(1)} %copy-done.100), channel_id=1, replica_groups=mesh['fsdp'=8,'seq'=16] {'fsdp','seq'}, dimensions={0}, use_global_device_ids=true | all-gather | bytes 528384 | tf_op jit(solution)/shard_map/all_gather | solution.py:186
  2508.6 22.7 reshape.381
  2531.3 22.5 reshape.387
  2574.1 63.0 %all-gather.47.cloned.1.call-done = bf16[128,54,1152]{2,1,0:T(8,128)(2,1)} async-done(((bf16[1,54,1152]{2,1,0:T(8,128)(2,1)}), bf16[128,54,1152]{2,1,0:T(8,128)(2,1)}) %all-gather.47.cloned.1.call-update) | async-done | bytes 15925264 | tf_op jit(solution)/shard_map/all_gather | solution.py:240
  2637.1 18.3 reshape.393
  2664.1 12.1 fusion.109
  2688.1 11.4 fusion.111
  2789.5 13.0 fusion.121
  2802.6 13.8 fusion.120
  2816.4 29.3 reduce-scatter.8.cloned.1.call-done
  2849.7 67.2 %reduce-scatter.10.cloned.1.call-done = bf16[160,256]{1,0:T(8,128)(2,1)} async-done(((bf16[2560,256]{1,0:T(8,128)(2,1)}), bf16[160,256]{1,0:T(8,128)(2,1)}) %reduce-scatter.10.cloned.1.call-update) | async-done | bytes 81936 | tf_op jit(solution)/shard_map/reduce_scatter | solution.py:383
  2929.8 14.6 fusion.122
  2944.4 514.8 %fusion.98 = (f32[64,1152]{1,0:T(8,128)S(1)}, f32[56,256]{1,0:T(8,128)S(1)}) fusion(f32[6912,1152]{1,0:T(8,128)} %fusion.122, f32[6912,256]{1,0:T(8,128)} %fusion.127), kind=kCustom, calls=%all-reduce-scatter.2 | all-reduce-scatter fusion | flops 11272194 | bytes 39280640
  3489.2 14.3 collective-permute-done.19
  3603.2 36.5 concatenate.39
  3644.5 95.8 %all-reduce.26 = (f32[]{:T(128)}, f32[1152]{0:T(1024)S(1)}, f32[1152]{0:T(1024)S(1)}) all-reduce(f32[]{:T(128)} %get-tuple-element.63, f32[1152]{0:T(1024)S(1)} %get-tuple-element.28, f32[1152]{0:T(1024)S(1)} %get-tuple-element.26), channel_id=1, replica_groups=mesh['fsdp'=8,'seq'=16] {'fsdp','seq'}, use_global_device_ids=true, to_apply=%region_5.6 | all-reduce | flops 2305 | bytes 18440 | tf_op jit(solution)/shard_map/psum | solution.py:266
  3743.1 300.1 %all-reduce.32.cloned.1.call-done = (f32[1152,1024]{1,0:T(8,128)}, f32[1152,256]{1,0:T(8,128)}, f32[1152,256]{1,0:T(8,128)}, f32[1024,1152]{1,0:T(8,128)}, f32[1...) async-done(((f32[1152,1024]{1,0:T(8,128)}, ...) | async-done | bytes 99483664
  4069.1 608.1 %reduce-scatter.12.cloned.1.call-done = f32[8,256]{1,0:T(8,128)} async-done(((f32[1024,256]{1,0:T(8,128)}), f32[8,256]{1,0:T(8,128)}) %reduce-scatter.12.cloned.1.call-update) | async-done | bytes 8208 | tf_op jit(solution)/shard_map/reduce_scatter | solution.py:443
  (459 shorter events, 387.3 us)
Async XLA Ops:
  7.2 2447.3 %all-gather.37.cloned.1.call-start = ((), (), s32[]{:S(2)}) async-start(), calls=%async_computation.9 | async-start | bytes 4227072 | tf_op jit(solution)/shard_map/all_gather | solution.py:176
  8.0 2459.5 %all-gather.35.cloned.1.call-start = ((), (), s32[]{:S(2)}) async-start(), calls=%async_computation.8 | async-start | bytes 1392640 | tf_op jit(solution)/shard_map/all_gather | solution.py:209
  603.2 1873.2 %all-gather.31.cloned.1.call-start = ((), (), s32[]{:S(2)}) async-start(), calls=%async_computation.3 | async-start | bytes 1392640 | tf_op jit(solution)/shard_map/all_gather | solution.py:210
  1130.4 1350.9 %all-gather.33.cloned.1.call-start = ((), (), s32[]{:S(2)}) async-start(), calls=%async_computation.4 | async-start | bytes 2377728 | tf_op jit(solution)/shard_map/all_gather | solution.py:179
  1131.0 1354.8 %all-gather.41.cloned.1.call-start = ((), (), s32[]{:S(2)}) async-start(), calls=%async_computation.11 | async-start | bytes 3566592 | tf_op jit(solution)/shard_map/all_gather | solution.py:242
  1131.6 1362.5 %all-gather.45.cloned.1.call-start = ((), (), s32[]{:S(2)}) async-start(), calls=%async_computation.13 | async-start | bytes 3566592 | tf_op jit(solution)/shard_map/all_gather | solution.py:244
  1132.2 1370.1 %all-gather.49.cloned.1.call-start = ((), (), s32[]{:S(2)}) async-start(), calls=%async_computation.15 | async-start | bytes 3698688 | tf_op jit(solution)/shard_map/all_gather | solution.py:245
  1132.9 1375.6 %all-gather.39.cloned.1.call-start = ((), (), s32[]{:S(2)}) async-start(), calls=%async_computation.10 | async-start | bytes 28532736 | tf_op jit(solution)/shard_map/all_gather | solution.py:238
  1133.7 1397.6 %all-gather.43.cloned.1.call-start = ((), (), s32[]{:S(2)}) async-start(), calls=%async_computation.12 | async-start | bytes 28532736 | tf_op jit(solution)/shard_map/all_gather | solution.py:239
  1134.4 1502.7 %all-gather.47.cloned.1.call-start = ((), (), s32[]{:S(2)}) async-start(), calls=%async_computation.14 | async-start | bytes 16644096 | tf_op jit(solution)/shard_map/all_gather | solution.py:240
  1135.0 1710.6 %reduce-scatter.8.cloned.1.call-start = ((), (), s32[]{:S(2)}) async-start(), calls=%async_computation.5 | async-start | bytes 1392640 | tf_op jit(solution)/shard_map/reduce_scatter | solution.py:380
  2780.6 136.2 %reduce-scatter.10.cloned.1.call-start = ((), (), s32[]{:S(2)}) async-start(), calls=%async_computation.6 | async-start | bytes 1392640 | tf_op jit(solution)/shard_map/reduce_scatter | solution.py:383
  2802.6 1240.6 %all-reduce.32.cloned.1.call-start = ((), (), s32[]{:S(2)}) async-start(), calls=%async_computation.16 | async-start | bytes 198967296
  2925.0 1752.2 %reduce-scatter.12.cloned.1.call-start = ((), (), s32[]{:S(2)}) async-start(), calls=%async_computation.7 | async-start | bytes 1056768 | tf_op jit(solution)/shard_map/reduce_scatter | solution.py:443
  3467.6 41.3 collective-permute-start.18
  3471.7 46.5 collective-permute-start.17
  3473.3 47.0 %collective-permute-start.16 = (f32[64,1152]{1,0:T(8,128)S(1)}, f32[64,1152]{1,0:T(8,128)S(1)}, u32[]{:S(2)}, u32[]{:S(2)}) collective-permute-start(f32[64,1152]{1,0:T(8,128)S(1)} %get-tuple-element.57), channel_id=1, source_target_pairs={{0,17},{1,18},{2,19},{3,20},{4,21},{5,22},{6,23},{7,24},{8,25},{9,... | collective-permute-start | bytes 884744
  3481.1 44.1 collective-permute-start.15
  3482.5 21.0 collective-permute-start.19
  3503.5 28.3 collective-permute-start.14
  3508.9 28.1 collective-permute-start.13
  3518.1 23.1 collective-permute-start.12
  3520.3 29.6 collective-permute-start.11
  3525.3 31.2 collective-permute-start.10
  3531.8 33.9 collective-permute-start.9
  3537.0 35.1 collective-permute-start.8
  3541.3 37.1 collective-permute-start.7
  3549.9 32.8 collective-permute-start.6
  3556.5 33.2 collective-permute-start.5
  3565.7 37.4 collective-permute-start.4
  3572.0 31.1 collective-permute-start.3
  3578.3 24.8 collective-permute-start.2
  (118 other events, 25117.3 us)
Sparse Core Ops, SparseCore 0:
  9.8 200.8 all-gather.36
  603.3 42.8 all-gather.34
  1130.6 38.9 all-gather.30
  1171.2 194.1 all-gather.32
  1366.9 196.1 all-gather.40
  1564.7 196.1 all-gather.44
  1762.6 195.9 all-gather.48
  1960.3 230.7 all-gather.38
  2192.8 230.3 all-gather.42
  2424.8 212.2 all-gather.46
  2780.8 64.8 reduce-scatter.7
  2849.9 66.9 reduce-scatter.9
  2925.1 1118.0 all-reduce.31
  4047.5 629.7 reduce-scatter.11
where the time goes:
time: 4710 us; the launch traced here: 4690 us
  blocking collectives  3030 us (64%)
  waiting for transfers between devices  1100 us (23%)
  matrix products  217 us (5%)
  local copies, waits for them, and re-layouts  189 us (4%)
  starting transfers between devices  114 us (2%)
    reduce_scatter x1, waiting for transfers between devices, on_device(): lax.psum_scatter(gradient_output_first, ('fsdp', 'seq'), scatter_dimensio...  608 us
    unnamed x2, blocking collectives  577 us
    unnamed x40, waiting for transfers between devices  328 us
    all_gather x1, blocking collectives, on_device(): lax.all_gather(adapter_gate_first, ('fsdp', 'seq'), axis=0, tiled=True)  185 us
    all_gather x1, blocking collectives, on_device(): lax.all_gather(adapter_up_first, ('fsdp', 'seq'), axis=0, tiled=True)  183 us
    all_gather x1, blocking collectives, on_device(): lax.all_gather(adapter_query_first, ('fsdp', 'seq'), axis=0, tiled=True)  183 us
    unnamed x272, local copies, waits for them, and re-layouts  181 us
    all_gather x1, blocking collectives, on_device(): lax.all_gather(adapter_key_second, ('fsdp', 'seq'), axis=0, tiled=True)  180 us
  transfers between devices with their start and end apart: 39, of which 11 were waited for; matrix products, arithmetic and copies ran while one was open for 17% of the time, Pallas kernels for 0%

commit v1 on v0

v1 whole, which is shorter than its diff:
```python
import jax
import jax.numpy as jnp
import numpy as np
from jax import lax
from jax.sharding import Mesh, PartitionSpec as P

EPSILON = 1e-06
ROPE_BASE = 10000.0
MASKED_SCORE = -1e30
BF = jnp.bfloat16
F32 = jnp.float32

OUTER = ("z", "xl", "xh")
CHIPS = ("z", "xl", "xh", "y")
EVERY = ("z", "xl", "xh", "y", "c")
SIZES = dict(z=4, xl=2, xh=2, y=4, c=2)


def dot(a, b):
    return jnp.dot(a, b, preferred_element_type=F32)


def dot_tl(a, b):
    return lax.dot_general(a, b, (((0,), (0,)), ((), ())), preferred_element_type=F32)


def dot_tr(a, b):
    return lax.dot_general(a, b, (((1,), (1,)), ((), ())), preferred_element_type=F32)


def count_of(axes):
    return int(np.prod([SIZES[a] for a in axes]))


def exchange(x, axes):
    return lax.all_to_all(x, axes, split_axis=0, concat_axis=0, tiled=True)


def gather(x, axes):
    return exchange(jnp.broadcast_to(x[None], (count_of(axes),) + x.shape), axes)


def scatter_sum(x, axes):
    return jnp.sum(exchange(x, axes).astype(F32), axis=0)


def other_core(x):
    return lax.ppermute(x, "c", [(0, 1), (1, 0)])


def ordered(core, mine, other):
    return jnp.where(core == 0, jnp.stack([mine, other]), jnp.stack([other, mine]))


def swap_halves(core, pieces):
    keep = jnp.where(core == 0, pieces[0], pieces[1])
    send = jnp.where(core == 0, pieces[1], pieces[0])
    return ordered(core, keep, other_core(send))


def down_route():
    pairs = []
    for o in range(16):
        for t in range(8):
            pairs.append((8 * o + t, 8 * (8 * (o % 2) + t) + o // 2))
    return pairs


def norm_parts(values, gain):
    scale = lax.rsqrt(jnp.mean(values * values, axis=-1, keepdims=True) + EPSILON)
    n = values * scale
    return scale, n, (n * (1.0 + gain)).astype(BF)


def norm_back(scale, n, gain, grad):
    m = grad * (1.0 + gain)
    back = scale * (m - n * jnp.mean(m * n, axis=-1, keepdims=True))
    return back, jnp.sum(grad * n, axis=0)


def turn(x, cos, sin):
    h = cos.shape[-1]
    a, b = x[:, :h], x[:, h:]
    return jnp.concatenate([a * cos - b * sin, b * cos + a * sin], axis=-1)


def turn_back(x, cos, sin):
    return turn(x, cos, -sin)


def gather_tokens(x):
    mine = gather(x, ("y",)).reshape(-1, x.shape[1])
    return jnp.concatenate([mine, other_core(mine)], axis=0)


def scatter_tokens(mine_part, other_part):
    summed = mine_part + other_core(other_part.astype(BF)).astype(F32)
    rows = summed.shape[0] // 4
    return scatter_sum(summed.astype(BF).reshape(4, rows, -1), ("y",))


def on_device(
    layer_input,
    segment,
    position,
    loss_token_mask,
    teacher,
    gain_one,
    wq,
    wk,
    wv,
    wo,
    aq,
    bq,
    ak,
    bk,
    av,
    bv,
    ao,
    bo,
    gain_two,
    wg,
    wu,
    wd,
    ag,
    bg,
    au,
    bu,
    ad,
    bd,
):
    core = lax.axis_index("c")
    tokens = 160
    heads = 4
    width = 256
    score_scale = width**-0.5
    hidden = layer_input[0].astype(F32)
    count_here = jnp.sum(loss_token_mask[0]).astype(BF)

    p9 = jnp.concatenate([wq, wk, wv, aq, ak, av], axis=1)
    p2 = jnp.concatenate([bq, bk, bv, bo], axis=1)

    def att_piece(k):
        rest = p2[:, 1344 * k + 1152 : 1344 * k + 1344].reshape(1, 384)
        last = jnp.concatenate(
            [rest, gain_one[None], gain_two[None], count_here.reshape(1, 1), jnp.zeros((1, 749), BF)],
            axis=1,
        )
        return jnp.concatenate(
            [p9[:, 1152 * k : 1152 * (k + 1)], p2[:, 1344 * k : 1344 * k + 1152], last], axis=0
        )

    att_own = swap_halves(core, [att_piece(0), att_piece(1)]).reshape(24, 1152)
    att_mine = gather(att_own, CHIPS)
    att_both = ordered(core, att_mine, other_core(att_mine)).reshape(2, 128, 12, 1152)
    w9 = att_both[:, :, :9].reshape(2, 1152, 1152)
    w2 = att_both[:, :, 9:11].reshape(2, 256, 1152)
    w2_rest = att_both[:, :, 11, :384].reshape(2, 256, 192)
    gain_one_full = att_both[0, :, 11, 384:393].reshape(1, 1152).astype(F32)
    gain_two_full = att_both[0, :, 11, 393:402].reshape(1, 1152).astype(F32)
    valid_count = jnp.sum(att_both[0, :, 11, 402].astype(F32))
    full9 = jnp.concatenate([w9[0], w9[1]], axis=1)
    full2 = jnp.concatenate([w2[0], w2_rest[0], w2[1], w2_rest[1]], axis=1)
    bq_full, bk_full, bv_full, bo_full = (
        full2[:, :1024],
        full2[:, 1024:1280],
        full2[:, 1280:1536],
        full2[:, 1536:],
    )
    aq_full, ak_full, av_full = full9[:, 1536:1792], full9[:, 1792:2048], full9[:, 2048:]
    w_qkv = jnp.concatenate(
        [
            full9[:, :1024].astype(F32) + dot(aq_full, bq_full),
            full9[:, 1024:1280].astype(F32) + dot(ak_full, bk_full),
            full9[:, 1280:1536].astype(F32) + dot(av_full, bv_full),
        ],
        axis=1,
    ).astype(BF)

    p8 = jnp.concatenate([wo, ao], axis=1)
    out_own = swap_halves(core, [p8[:, :768], p8[:, 640:]]).reshape(16, 768)
    out_mine = gather(out_own, CHIPS)
    out_both = ordered(core, out_mine, other_core(out_mine)).reshape(2, 1024, 768)
    full8 = jnp.concatenate([out_both[0], out_both[1][:, 128:]], axis=1)
    ao_full = full8[:, 1152:]
    w_out = (full8[:, :1152].astype(F32) + dot(ao_full, bo_full)).astype(BF)

    ff_piece = [
        jnp.concatenate([m, bd[:, 512 * k : 512 * k + 640].reshape(5, 256)], axis=0)
        for k, m in enumerate((ag, au))
    ]
    ff_own = swap_halves(core, ff_piece).reshape(28, 256)
    ff_mine = gather(ff_own, CHIPS)
    ff_both = ordered(core, ff_mine, other_core(ff_mine)).reshape(2, 128, 14, 256)
    ag_full, au_full = ff_both[0, :, :9].reshape(1152, 256), ff_both[1, :, :9].reshape(1152, 256)
    bd_halves = ff_both[:, :, 9:].reshape(2, 256, 640)
    bd_full = jnp.concatenate([bd_halves[0], bd_halves[1][:, 128:]], axis=1)

    rows22 = jnp.concatenate([wg, wu, bg, bu], axis=0)
    rows22 = exchange(rows22.reshape(22, 8, 864).transpose(1, 0, 2), ("y", "c"))
    gu_own = jnp.concatenate(
        [
            rows22[:, :9].reshape(72, 864),
            rows22[:, 9:18].reshape(72, 864),
            rows22[:, 18:20].reshape(16, 864),
            rows22[:, 20:].reshape(16, 864),
        ],
        axis=0,
    )
    gu = gather(gu_own, OUTER)
    bg_cols, bu_cols = gu[:, 144:160].reshape(256, 864), gu[:, 160:].reshape(256, 864)
    w_gate = (gu[:, :72].reshape(1152, 864).astype(F32) + dot(ag_full, bg_cols)).astype(BF)
    w_up = (gu[:, 72:144].reshape(1152, 864).astype(F32) + dot(au_full, bu_cols)).astype(BF)
    down_own = lax.ppermute(jnp.concatenate([wd, ad], axis=1), EVERY, down_route())
    down = gather(down_own, OUTER).reshape(864, 1408)
    ad_rows = down[:, 1152:]
    w_down = (down[:, :1152].astype(F32) + dot(ad_rows, bd_full)).astype(BF)

    seq = (lax.axis_index("xh") * 4 + lax.axis_index("y")) * 2 + core
    tree_seg = segment[0]
    tree_pos = position[0]
    own_seg = lax.dynamic_slice_in_dim(tree_seg, seq * tokens, tokens)
    own_pos = lax.dynamic_slice_in_dim(tree_pos, seq * tokens, tokens)
    freq = ROPE_BASE ** (-(jnp.arange(128, dtype=F32) * 2.0 / width))
    angles = own_pos.astype(F32)[:, None] * freq[None, :]
    cos, sin = jnp.cos(angles), jnp.sin(angles)

    def by_core(v):
        v = v.reshape(8, 2, tokens)
        first = jnp.where(core == 0, v[:, 0], v[:, 1]).reshape(-1)
        second = jnp.where(core == 0, v[:, 1], v[:, 0]).reshape(-1)
        return jnp.concatenate([first, second])

    key_seg, key_pos = by_core(tree_seg)[None, :], by_core(tree_pos)[None, :]
    q_seg, q_pos = own_seg[:, None], own_pos[:, None]
    parent = (key_seg >= 1) & (key_seg <= 4) & (q_seg >= 5) & ((q_seg - 5) // 2 + 1 == key_seg)
    allowed = ((key_seg == q_seg) | (key_seg == 0) | parent) & (key_pos <= q_pos)
    allowed = jnp.concatenate([allowed] * heads, axis=0)

    scale_one, n_one, u_one = norm_parts(hidden, gain_one_full)
    qkv = dot(u_one, w_qkv)
    kv_own = jnp.concatenate([turn(qkv[:, 1024:1280], cos, sin), qkv[:, 1280:]], axis=1).astype(BF)
    kv_mine = gather(kv_own, ("xh", "y")).reshape(8 * tokens, 512)
    kv = jnp.concatenate([kv_mine, other_core(kv_mine)], axis=0)
    keys, values = kv[:, :256], kv[:, 256:]
    q_rows = jnp.concatenate(
        [turn(qkv[:, width * h : width * (h + 1)], cos, sin) for h in range(heads)], axis=0
    ).astype(BF)
    scores = jnp.where(allowed, dot_tr(q_rows, keys) * score_scale, MASKED_SCORE)
    top = jnp.max(scores, axis=-1, keepdims=True)
    ex = jnp.exp(scores - top)
    total = jnp.sum(ex, axis=-1, keepdims=True)
    lse = top + jnp.log(total)
    mix_rows = dot((ex / total).astype(BF), values).astype(BF)
    mix = jnp.concatenate([mix_rows[tokens * h : tokens * (h + 1)] for h in range(heads)], axis=1)
    after = hidden + dot(mix, w_out)

    scale_two, n_two, u_two = norm_parts(after, gain_two_full)
    u_all = gather_tokens(u_two)
    gate = dot(u_all, w_gate)
    up = dot(u_all, w_up)
    act, act_pull = jax.vjp(lambda g, u: jax.nn.gelu(g, approximate=True) * u, gate, up)
    act = act.astype(BF)
    out_part = dot(act, w_down)
    half = 4 * tokens
    result = after + scatter_tokens(out_part[:half], out_part[half:])

    valid = loss_token_mask[0].astype(F32)[:, None]
    error = result - teacher[0].astype(F32)
    loss_here = jnp.sum(valid * error * error)
    loss_all = exchange(jnp.broadcast_to(loss_here, (128, 128)), EVERY)
    loss_value = jnp.sum(loss_all[:, 0]) / (1152.0 * valid_count)
    grad_result = 2.0 * 20480.0 / valid_count * valid * error

    g_all = gather_tokens(grad_result.astype(BF))
    gw_down = dot_tl(act, g_all).astype(BF)
    g_act = dot_tr(g_all, w_down).astype(BF)
    g_gate, g_up = act_pull(g_act.astype(F32))
    g_gate, g_up = g_gate.astype(BF), g_up.astype(BF)
    g_u_part = dot_tr(g_gate, w_gate) + dot_tr(g_up, w_up)
    g_u_two = scatter_tokens(g_u_part[:half], g_u_part[half:])
    gw_gate = dot_tl(u_all, g_gate).astype(BF)
    gw_up = dot_tl(u_all, g_up).astype(BF)
    gb_gate = dot_tl(ag_full, gw_gate).astype(BF)
    gb_up = dot_tl(au_full, gw_up).astype(BF)
    gb_down = dot_tl(ad_rows, gw_down).astype(BF)
    gu_sum = scatter_sum(
        jnp.concatenate(
            [
                gw_gate.reshape(16, 72, 864),
                gw_up.reshape(16, 72, 864),
                gb_gate.reshape(16, 16, 864),
                gb_up.reshape(16, 16, 864),
            ],
            axis=1,
        ),
        OUTER,
    ).astype(BF)
    down_sum = scatter_sum(gw_down.reshape(16, 54, 1152), OUTER)
    ga_part = jnp.concatenate(
        [dot_tr(gu_sum[:72], bg_cols), dot_tr(gu_sum[72:144], bu_cols), jnp.zeros((72, 352), F32)],
        axis=1,
    ).astype(BF)
    back_t = exchange(
        jnp.concatenate(
            [
                gu_sum[:72].reshape(8, 9, 864),
                gu_sum[72:144].reshape(8, 9, 864),
                gu_sum[144:160].reshape(8, 2, 864),
                gu_sum[160:].reshape(8, 2, 864),
                ga_part.reshape(8, 9, 864),
            ],
            axis=1,
        ),
        ("y", "c"),
    )
    wide = back_t[:, :22].transpose(1, 0, 2).reshape(22, 6912).astype(F32)
    ga = jnp.sum(back_t[:, 22:, :512].astype(F32), axis=0)
    gw_down_own = lax.ppermute(down_sum.astype(BF), EVERY, [(b, a) for a, b in down_route()])
    ga_down_own = dot_tr(gw_down_own, bd_full)

    norm_two_back, g_gain_two = norm_back(scale_two, n_two, gain_two_full, g_u_two)
    g_after = grad_result + norm_two_back
    g_after_b = g_after.astype(BF)
    gw_out = dot_tl(mix, g_after_b).astype(BF)
    gb_out = dot_tl(ao_full, gw_out).astype(BF)

    def to_owners(parts, columns, starts):
        stacked = jnp.concatenate([p.reshape(64, p.shape[0] // 64, p.shape[1]) for p in parts], axis=1)
        first = stacked[:, :, starts[0] : starts[0] + columns]
        second = stacked[:, :, starts[1] : starts[1] + columns]
        keep = jnp.where(core == 0, first, second)
        send = jnp.where(core == 0, second, first)
        summed = (keep.astype(F32) + other_core(send).astype(F32)).astype(BF)
        total_rows = scatter_sum(summed, CHIPS).astype(BF)
        mine, away, at = [], [], 0
        for p in parts:
            r = p.shape[0] // 128
            block = total_rows[at : at + 2 * r]
            mine.append(jnp.where(core == 0, block[:r], block[r:]))
            away.append(jnp.where(core == 0, block[r:], block[:r]))
            at += 2 * r
        mine, away = jnp.concatenate(mine, axis=0), jnp.concatenate(away, axis=0)
        both = ordered(core, mine, other_core(away))
        skip = starts[0] + columns - starts[1]
        joined = jnp.concatenate([both[0], both[1][:, skip:]], axis=1)
        outs, at = [], 0
        for p in parts:
            r = p.shape[0] // 128
            outs.append(joined[at : at + r])
            at += r
        return outs

    gw_out_own, gb_out_own, gb_down_own = to_owners([gw_out, gb_out, gb_down], 640, (0, 512))
    ga_out_own = dot_tr(gw_out_own, bo_full)

    g_mix = dot_tr(g_after_b, w_out).astype(BF)
    g_rows = jnp.concatenate([g_mix[:, width * h : width * (h + 1)] for h in range(heads)], axis=0)
    scores_again = jnp.where(allowed, dot_tr(q_rows, keys) * score_scale, MASKED_SCORE)
    probs = jnp.where(allowed, jnp.exp(scores_again - lse), 0.0)
    g_probs = dot_tr(g_rows, values)
    g_scores = (probs * (g_probs - jnp.sum(probs * g_probs, axis=-1, keepdims=True))).astype(BF)
    g_q_rows = dot(g_scores, keys) * score_scale
    g_keys = dot_tl(g_scores, q_rows) * score_scale
    g_values = dot_tl(probs.astype(BF), g_rows)
    g_kv = jnp.concatenate([g_keys, g_values], axis=1)
    n_mine = 8 * tokens
    g_kv_sum = g_kv[:n_mine] + other_core(g_kv[n_mine:].astype(BF)).astype(F32)
    g_kv_own = scatter_sum(g_kv_sum.astype(BF).reshape(8, tokens, 512), ("xh", "y"))
    g_qkv = jnp.concatenate(
        [turn_back(g_q_rows[tokens * h : tokens * (h + 1)], cos, sin) for h in range(heads)]
        + [turn_back(g_kv_own[:, :256], cos, sin), g_kv_own[:, 256:]],
        axis=1,
    ).astype(BF)
    g_u_one = dot_tr(g_qkv, w_qkv)
    norm_one_back, g_gain_one = norm_back(scale_one, n_one, gain_one_full, g_u_one)
    grad_hidden = (g_after + norm_one_back).astype(BF)

    gw_qkv = dot_tl(u_one, g_qkv).astype(BF)
    gb_qkv = jnp.concatenate(
        [
            dot_tl(aq_full, gw_qkv[:, :1024]),
            dot_tl(ak_full, gw_qkv[:, 1024:1280]),
            dot_tl(av_full, gw_qkv[:, 1280:]),
        ],
        axis=1,
    ).astype(BF)
    gains = jnp.concatenate([g_gain_one.reshape(128, 1, 9), g_gain_two.reshape(128, 1, 9)], axis=2)
    gains = gains.reshape(64, 1, 36).astype(BF)
    gains_row = jnp.concatenate([gains, jnp.zeros((64, 1, 768 - 36), BF)], axis=2)
    gains_rows = jnp.concatenate([gains_row, gains_row], axis=2)

    stacked = jnp.concatenate(
        [gw_qkv.reshape(64, 18, 1536), gb_qkv.reshape(64, 4, 1536), gains_rows], axis=1
    )
    keep = jnp.where(core == 0, stacked[:, :, :768], stacked[:, :, 768:])
    send = jnp.where(core == 0, stacked[:, :, 768:], stacked[:, :, :768])
    summed = (keep.astype(F32) + other_core(send).astype(F32)).astype(BF)
    owned = scatter_sum(summed, CHIPS)
    mine = jnp.where(
        core == 0,
        jnp.concatenate([owned[:9], owned[18:20]], axis=0),
        jnp.concatenate([owned[9:18], owned[20:22]], axis=0),
    )
    away = jnp.where(
        core == 0,
        jnp.concatenate([owned[9:18], owned[20:22]], axis=0),
        jnp.concatenate([owned[:9], owned[18:20]], axis=0),
    )
    both = ordered(core, mine, other_core(away))
    gw_own = jnp.concatenate([both[0], both[1]], axis=1)
    gain_pair = jnp.where(core == 0, owned[22, :18], owned[22, 18:36])
    gw_own_b = gw_own[:9].astype(BF)

    return (
        result.astype(BF)[None],
        loss_value,
        grad_hidden[None],
        gain_pair[:9],
        gw_own[:9, :1024],
        gw_own[:9, 1024:1280],
        gw_own[:9, 1280:],
        gw_out_own.astype(F32),
        dot_tr(gw_own_b[:, :1024], bq_full),
        gw_own[9:, :1024],
        dot_tr(gw_own_b[:, 1024:1280], bk_full),
        gw_own[9:, 1024:1280],
        dot_tr(gw_own_b[:, 1280:], bv_full),
        gw_own[9:, 1280:],
        ga_out_own,
        gb_out_own.astype(F32),
        gain_pair[9:],
        wide[:9],
        wide[9:18],
        gw_down_own.astype(F32),
        ga[:, :256],
        wide[18:20],
        ga[:, 256:],
        wide[20:],
        ga_down_own,
        gb_down_own.astype(F32),
    )


def solution(mesh):
    mesh = Mesh(mesh.devices.reshape([SIZES[a] for a in EVERY]), EVERY)
    tree, seq = ("z", "xl"), ("xh", "y", "c")
    rows = P(EVERY, None)
    vector = P(EVERY)
    return jax.shard_map(
        on_device,
        mesh=mesh,
        in_specs=(
            P(tree, seq, None),
            P(tree, None),
            P(tree, None),
            P(tree, seq),
            P(tree, seq, None),
            vector,
        )
        + (rows,) * 12
        + (vector,)
        + (rows,) * 9,
        out_specs=(P(tree, seq, None), P(), P(tree, seq, None), vector)
        + (rows,) * 12
        + (vector,)
        + (rows,) * 9,
        check_vma=False,
    )
```

time: 4710 us -> 851 us (0.18)
  blocking collectives: 3030 us -> 75.9 us
  waiting for transfers between devices: 1100 us -> 160 us
  other arithmetic: 19.4 us -> 119 us
  matrix products: 217 us -> 126 us
    all_gather x13 -> x0, blocking collectives: 2300 us -> none  [the longest x1 185 us: on_device(): lax.all_gather(adapter_gate_first, ('fsdp', 'seq'), axis=0, tiled=True)]
    reduce_scatter x3 -> x0, waiting for transfers between devices: 705 us -> none  [the longest x1 608 us: on_device(): lax.psum_scatter(gradient_output_first, ('fsdp', 'seq'), scatter_dimensio...]
    unnamed x2 -> x0, blocking collectives: 577 us -> none
    unnamed x40 -> x0, waiting for transfers between devices: 328 us -> none
    unnamed x272 -> x235, local copies, waits for them, and re-layouts: 181 us -> 17.3 us
    psum x2 -> x0, blocking collectives: 158 us -> none  [on_device(): lax.psum((jnp.sum(valid_rows * error_rows * error_rows), jnp.sum(valid_ro...]
    all_to_all x0 -> x16, waiting for transfers between devices: none -> 142 us  [exchange(): return lax.all_to_all(x, axes, split_axis=0, concat_axis=0, tiled=True)]
    all_to_all x0 -> x16, starting transfers between devices: none -> 119 us  [exchange(): return lax.all_to_all(x, axes, split_axis=0, concat_axis=0, tiled=True)]
  transfers between devices with their start and end apart: 39 -> 34, of which waited for: 11 -> 14; matrix products, arithmetic and copies ran while one was open for 17% -> 45% of each run, Pallas kernels for 0% -> 0%
where the time goes in v1:
time: 851 us; the launch traced here: 837 us
  local copies, waits for them, and re-layouts  200 us (24%)
  waiting for transfers between devices  160 us (19%)
  starting transfers between devices  149 us (18%)
  matrix products  126 us (15%)
  other arithmetic  119 us (14%)
  blocking collectives  75.9 us (9%)
    all_to_all x16, waiting for transfers between devices, exchange(): return lax.all_to_all(x, axes, split_axis=0, concat_axis=0, tiled=True)  142 us
    all_to_all x16, starting transfers between devices, exchange(): return lax.all_to_all(x, axes, split_axis=0, concat_axis=0, tiled=True)  119 us
    all_to_all x2, blocking collectives, exchange(): return lax.all_to_all(x, axes, split_axis=0, concat_axis=0, tiled=True)  75.9 us
    dot_general x14, matrix products, dot_tr(): lax.dot_general(a, b, (((1,), (1,)), ((), ())), preferred_element_type=F32)  44.3 us
    dot_general x14, matrix products, dot_tl(): lax.dot_general(a, b, (((0,), (0,)), ((), ())), preferred_element_type=F32)  42.4 us
    dot_general x14, matrix products, dot(): return jnp.dot(a, b, preferred_element_type=F32)  39 us
    ppermute x16, starting transfers between devices, other_core(): return lax.ppermute(x, 'c', [(0, 1), (1, 0)])  20.4 us
    select_n x8, other arithmetic, ordered(): jnp.where(core == 0, jnp.stack([mine, other]), jnp.stack([other, mine]))  19.6 us
  transfers between devices with their start and end apart: 34, of which 14 were waited for; matrix products, arithmetic and copies ran while one was open for 45% of the time, Pallas kernels for 0%

profile of v1, /device:TPU:1, one launch (start us, length us, event | category | flops | bytes accessed | tf_op | source)
XLA Modules:
  0.0 836.8 jit_solution(13529111507344636398)
XLA Ops:
  14.3 54.8 %all_to_all.94 = bf16[64,24,1152]{2,1,0:T(8,128)(2,1)S(1)} all-to-all(bf16[64,24,1152]{2,1,0:T(8,128)(2,1)S(1)} %broadcast_in_dim.40), channel_id=1, replica_groups=mesh['z'=4,'xl'=2,'xh'=2,'y'=4,'c'=2] {'z','xl','xh','y'}, dimensions={0} | all-to-all | bytes 7077888 | tf_op jit(solution)/shard_map/all_to_all | solution.py:36
  100.9 6.5 stack.110
  107.3 10.7 %maximum_select_fusion = bf16[2,128,12,1152]{3,2,1,0:T(8,128)(2,1)S(1)} fusion(bf16[1,128,12,1152]{3,2,1,0:T(8,128)(2,1)} %stack.110, bf16[1,128,12,1152]{3,2,1,0:T(8,128)(2,1)} %stack.109, pred[]{:T(512)S(6)} %eq.23), kind=kLoop, calls=%fused_computation.1 | loop fusion | flops 10616832 | bytes 14155777 | tf_op jit(solution)/shard_map/jit(_where)/select_n | solution.py:52
  128.3 7.9 all-to-all-start.6
  136.2 8.1 fusion.208
  164.8 10.1 %all-to-all-start.2 = ((bf16[64,16,768]{2,1,0:T(8,128)(2,1)}), bf16[64,16,768]{2,1,0:T(8,128)(2,1)}, u32[]{:S(2)}, u32[]{:S(2)}) async-start(bf16[64,16,768]{2,1,0:T(8,128)(2,1)} %broadcast_in_dim.43), calls=%async_computation.2 | async-start | bytes 3145728 | tf_op jit(solution)/shard_map/all_to_all | solution.py:36
  183.0 14.2 %all-to-all-done.2 = bf16[64,16,768]{2,1,0:T(8,128)(2,1)} async-done(((bf16[64,16,768]{2,1,0:T(8,128)(2,1)}), bf16[64,16,768]{2,1,0:T(8,128)(2,1)}, u32[]{:S(2)}, u32[]{:S(2)}) %all-to-all-start.2) | async-done | bytes 1572896 | tf_op jit(solution)/shard_map/all_to_all | solution.py:36
  202.7 6.9 collective-permute-start.8
  210.3 10.2 %collective-permute-done.8 = bf16[54,1408]{1,0:T(8,128)(2,1)S(1)} collective-permute-done((bf16[54,1408]{1,0:T(8,128)(2,1)S(1)}, bf16[54,1408]{1,0:T(8,128)(2,1)S(1)}, u32[]{:S(2)}, u32[]{:S(2)}) %collective-permute-start.8) | collective-permute-done | bytes 152096 | tf_op jit(solution)/shard_map/ppermute | solution.py:214
  222.5 13.1 %all-to-all-start.7 = ((bf16[16,54,1408]{2,1,0:T(8,128)(2,1)}), bf16[16,54,1408]{2,1,0:T(8,128)(2,1)S(1)}, u32[]{:S(2)}, u32[]{:S(2)}) async-start(bf16[16,54,1408]{2,1,0:T(8,128)(2,1)} %broadcast_in_dim.47), calls=%async_computation.7 | async-start | bytes 5046272 | tf_op jit(solution)/shard_map/all_to_all | solution.py:36
  253.8 13.5 %all-to-all-done.7 = bf16[16,54,1408]{2,1,0:T(8,128)(2,1)S(1)} async-done(((bf16[16,54,1408]{2,1,0:T(8,128)(2,1)}), bf16[16,54,1408]{2,1,0:T(8,128)(2,1)S(1)}, u32[]{:S(2)}, u32[]{:S(2)}) %all-to-all-start.7) | async-done | bytes 2433056 | tf_op jit(solution)/shard_map/all_to_all | solution.py:36
  300.1 38.3 %all-to-all-done.5 = bf16[16,176,864]{2,1,0:T(8,128)(2,1)} async-done(((bf16[16,176,864]{2,1,0:T(8,128)(2,1)}), bf16[16,176,864]{2,1,0:T(8,128)(2,1)}, u32[]{:S(2)}, u32[]{:S(2)}) %all-to-all-start.5) | async-done | bytes 4866080 | tf_op jit(solution)/shard_map/all_to_all | solution.py:36
  339.6 8.0 all-to-all-start.3
  398.4 9.1 %multiply_convert_fusion.1 = (bf16[1280,864]{0,1:T(8,128)(2,1)S(1)}, f32[1280,864]{0,1:T(8,128)}) fusion(f32[1280,864]{0,1:T(8,128)S(1)} %fusion.203, bf16[1152,864]{0,1:T(8,128)(2,1)S(1)} %fusion.12, bf16[640,1152]{1,0:T(8,128)(2,1)} %collective-permute-done.5, bf16[640,1152]{1,0:T(8,128)(2,1)} %bitcast.22), kind=kOutput, calls=%fused_computation.31 | convolution fusion | flops 2564997120 | bytes 15998976 | tf_op jit(solution)/shard_map/dot_general | solution.py:20
  423.7 17.2 %all-to-all-done.8 = bf16[4,160,1152]{2,1,0:T(8,128)(2,1)} async-done(((bf16[4,160,1152]{2,1,0:T(8,128)(2,1)}), bf16[4,160,1152]{2,1,0:T(8,128)(2,1)}, u32[]{:S(2)}, u32[]{:S(2)}) %all-to-all-start.8) | async-done | bytes 1474592 | tf_op jit(solution)/shard_map/all_to_all | solution.py:36
  442.8 21.1 %all_to_all.95 = bf16[4,160,1152]{2,1,0:T(8,128)(2,1)S(1)} all-to-all(bf16[4,160,1152]{2,1,0:T(8,128)(2,1)S(1)} %broadcast_in_dim.50), channel_id=1, replica_groups=mesh['z'=4,'xl'=2,'xh'=2,'y'=4,'c'=2] {'y'}, dimensions={0} | all-to-all | bytes 2949120 | tf_op jit(solution)/shard_map/all_to_all | solution.py:36
  477.0 8.6 %all-to-all-start.17 = ((bf16[16,54,1152]{2,1,0:T(8,128)(2,1)}), bf16[16,54,1152]{2,1,0:T(8,128)(2,1)}, u32[]{:S(2)}, u32[]{:S(2)}) async-start(bf16[16,54,1152]{2,1,0:T(8,128)(2,1)} %reshape.744), calls=%async_computation.17 | async-start | bytes 4128768 | tf_op jit(solution)/shard_map/all_to_all | solution.py:36
  485.6 9.5 %fusion.8 = (bf16[1280,864]{0,1:T(8,128)(2,1)S(1)}, bf16[1280,864]{0,1:T(8,128)(2,1)S(1)}) fusion(f32[1280,864]{0,1:T(8,128)} %copy-done.108, f32[1280,864]{0,1:T(8,128)} %get-tuple-element.130, bf16[864,1152]{1,0:T(8,128)(2,1)} %add_convert_fusion.1, bf16[640,1152]{1,0:T(8,128)(2,1)} %copy-done.105, bf16[640,1152]{1,0:T(8,128)(2,1)} %bitcast.158), kind=kOutput, calls=%fused_computation.30 | convolution fusion | flops 2579374080 | bytes 18210816 | tf_op jit(solution)/shard_map/dot_general | solution.py:28
  498.7 6.8 convolution_add_fusion
  506.6 6.3 convolution_convert_fusion.3
  512.9 7.3 convolution_convert_fusion.2
  558.5 8.4 %all-to-all-start.15 = ((bf16[16,176,864]{2,1,0:T(8,128)(2,1)}), bf16[16,176,864]{2,1,0:T(8,128)(2,1)}, u32[]{:S(2)}, u32[]{:S(2)}) async-start(bf16[16,176,864]{2,1,0:T(8,128)(2,1)} %pad_maximum_fusion), calls=%async_computation.15 | async-start | bytes 10092544 | tf_op jit(solution)/shard_map/all_to_all | solution.py:36
  606.8 27.1 %all-to-all-done.15 = bf16[16,176,864]{2,1,0:T(8,128)(2,1)} async-done(((bf16[16,176,864]{2,1,0:T(8,128)(2,1)}), bf16[16,176,864]{2,1,0:T(8,128)(2,1)}, u32[]{:S(2)}, u32[]{:S(2)}) %all-to-all-start.15) | async-done | bytes 4866080 | tf_op jit(solution)/shard_map/all_to_all | solution.py:36
  633.9 8.5 %all-to-all-start.12 = ((bf16[8,160,512]{2,1,0:T(8,128)(2,1)}), bf16[8,160,512]{2,1,0:T(8,128)(2,1)}, u32[]{:S(2)}, u32[]{:S(2)}) async-start(bf16[8,160,512]{2,1,0:T(8,128)(2,1)} %bitcast.148), calls=%async_computation.12 | async-start | bytes 2621440 | tf_op jit(solution)/shard_map/all_to_all | solution.py:36
  660.8 11.0 %all-to-all-start.9 = ((f32[128,1,128]{2,1,0:T(1,128)}), f32[128,1,128]{2,1,0:T(1,128)}, u32[]{:S(2)}, u32[]{:S(2)}) async-start(f32[128,1,128]{2,1,0:T(1,128)} %broadcast_in_dim.49), calls=%async_computation.9 | async-start | bytes 131072 | tf_op jit(solution)/shard_map/all_to_all | solution.py:36
  711.0 7.9 pad_maximum_fusion.1
  729.0 10.8 %concatenate.357 = bf16[8,31,864]{2,1,0:T(8,128)(2,1)} concatenate(bf16[8,9,864]{2,1,0:T(8,128)(2,1)} %reshape.740, bf16[8,9,864]{2,1,0:T(8,128)(2,1)} %reshape.741, bf16[8,2,864]{2,1,0:T(2,128)(2,1)} %reshape.742, bf16[8,2,864]{2,1,0:T(2,128)(2,1)} %reshape.743, bf16[8,9,864]{2,1,0:T(8,128)(2,1)} %maximum_maximum_fusion.1), dimensions={1} | concatenate | bytes 857088 | tf_op jit(solution)/shard_map/concatenate | solution.py:305
  752.9 8.4 %all-to-all-start.14 = ((bf16[64,24,640]{2,1,0:T(8,128)(2,1)}), bf16[64,24,640]{2,1,0:T(8,128)(2,1)S(1)}, u32[]{:S(2)}, u32[]{:S(2)}) async-start(bf16[64,24,640]{2,1,0:T(8,128)(2,1)} %add_convert_fusion.2), calls=%async_computation.14 | async-start | bytes 3932160 | tf_op jit(solution)/shard_map/all_to_all | solution.py:36
  773.8 6.3 add_convert_fusion
  780.1 7.2 all-to-all-done.14
  788.5 6.5 all-to-all-start.13
  805.4 19.1 %all-to-all-done.13 = bf16[64,23,768]{2,1,0:T(8,128)(2,1)S(1)} async-done(((bf16[64,23,768]{2,1,0:T(8,128)(2,1)}), bf16[64,23,768]{2,1,0:T(8,128)(2,1)S(1)}, u32[]{:S(2)}, u32[]{:S(2)}) %all-to-all-start.13) | async-done | bytes 2261024 | tf_op jit(solution)/shard_map/all_to_all | solution.py:36
  (539 shorter events, 420.8 us)
Async XLA Ops:
  69.2 31.7 %collective-permute-start.1 = (bf16[64,24,1152]{2,1,0:T(8,128)(2,1)S(1)}, bf16[64,24,1152]{2,1,0:T(8,128)(2,1)}, u32[]{:S(2)}, u32[]{:S(2)}) collective-permute-start(bf16[64,24,1152]{2,1,0:T(8,128)(2,1)S(1)} %all_to_all.94), channel_id=1, source_target_pairs={{0,1},{1,0},{2,3},{3,2},{4,5},{5,4},{6,7},{7,6},{8,9},{9,8},{10,11... | collective-permute-start | bytes 10616840 | tf_op jit(solution)/shard_map/ppermute | solution.py:48
  76.1 17.8 %collective-permute-start.6 = (bf16[14,256]{1,0:T(8,128)(2,1)}, bf16[14,256]{1,0:T(8,128)(2,1)}, u32[]{:S(2)}, u32[]{:S(2)}) collective-permute-start(bf16[14,256]{1,0:T(8,128)(2,1)} %maximum_select_fusion.13), channel_id=1, source_target_pairs={{0,1},{1,0},{2,3},{3,2},{4,5},{5,4},{6,7},{7,6},{8,9},{9,8},{10,11... | collective-permute-start | bytes 21512 | tf_op jit(solution)/shard_map/ppermute | solution.py:48
  77.5 19.1 %collective-permute-start.3 = (bf16[8,768]{1,0:T(8,128)(2,1)}, bf16[8,768]{1,0:T(8,128)(2,1)}, u32[]{:S(2)}, u32[]{:S(2)}) collective-permute-start(bf16[8,768]{1,0:T(8,128)(2,1)} %get-tuple-element.116), channel_id=1, source_target_pairs={{0,1},{1,0},{2,3},{3,2},{4,5},{5,4},{6,7},{7,6},{8,9},{9,8},{10,11... | collective-permute-start | bytes 36872 | tf_op jit(solution)/shard_map/ppermute | solution.py:48
  84.0 43.2 %all-to-all-start.4 = ((bf16[8,22,864]{2,1,0:T(8,128)(2,1)}), bf16[8,22,864]{2,1,0:T(8,128)(2,1)}, u32[]{:S(2)}, u32[]{:S(2)}) async-start(bf16[8,22,864]{2,1,0:T(8,128)(2,1)} %bitcast.159), calls=%async_computation.4 | async-start | bytes 688128 | tf_op jit(solution)/shard_map/all_to_all | solution.py:36
  128.3 35.3 %all-to-all-start.6 = ((bf16[64,28,256]{2,1,0:T(8,128)(2,1)}), bf16[64,28,256]{2,1,0:T(8,128)(2,1)}, u32[]{:S(2)}, u32[]{:S(2)}) async-start(bf16[64,28,256]{2,1,0:T(8,128)(2,1)} %broadcast_in_dim.46), calls=%async_computation.6 | async-start | bytes 2097152 | tf_op jit(solution)/shard_map/all_to_all | solution.py:36
  164.8 32.3 %all-to-all-start.2 = ((bf16[64,16,768]{2,1,0:T(8,128)(2,1)}), bf16[64,16,768]{2,1,0:T(8,128)(2,1)}, u32[]{:S(2)}, u32[]{:S(2)}) async-start(bf16[64,16,768]{2,1,0:T(8,128)(2,1)} %broadcast_in_dim.43), calls=%async_computation.2 | async-start | bytes 3145728 | tf_op jit(solution)/shard_map/all_to_all | solution.py:36
  198.4 22.2 %all-to-all-start.1 = ((bf16[8,160,512]{2,1,0:T(8,128)(2,1)}), bf16[8,160,512]{2,1,0:T(8,128)(2,1)S(1)}, u32[]{:S(2)}, u32[]{:S(2)}) async-start(bf16[8,160,512]{2,1,0:T(8,128)(2,1)} %broadcast_in_dim.41), calls=%async_computation.1 | async-start | bytes 2621440 | tf_op jit(solution)/shard_map/all_to_all | solution.py:36
  202.7 17.8 %collective-permute-start.8 = (bf16[54,1408]{1,0:T(8,128)(2,1)S(1)}, bf16[54,1408]{1,0:T(8,128)(2,1)S(1)}, u32[]{:S(2)}, u32[]{:S(2)}) collective-permute-start(bf16[54,1408]{1,0:T(8,128)(2,1)S(1)} %pad_maximum_fusion.27), channel_id=1, source_target_pairs={{0,0},{1,8},{2,16},{3,24},{4,32},{5,40},{6,48},{7,56},{8,64},{9,72... | collective-permute-start | bytes 456200 | tf_op jit(solution)/shard_map/ppermute | solution.py:214
  222.5 44.8 %all-to-all-start.7 = ((bf16[16,54,1408]{2,1,0:T(8,128)(2,1)}), bf16[16,54,1408]{2,1,0:T(8,128)(2,1)S(1)}, u32[]{:S(2)}, u32[]{:S(2)}) async-start(bf16[16,54,1408]{2,1,0:T(8,128)(2,1)} %broadcast_in_dim.47), calls=%async_computation.7 | async-start | bytes 5046272 | tf_op jit(solution)/shard_map/all_to_all | solution.py:36
  235.6 43.4 %collective-permute-start.4 = (bf16[64,16,768]{2,1,0:T(8,128)(2,1)}, bf16[64,16,768]{2,1,0:T(8,128)(2,1)}, u32[]{:S(2)}, u32[]{:S(2)}) collective-permute-start(bf16[64,16,768]{2,1,0:T(8,128)(2,1)} %all-to-all-done.2), channel_id=1, source_target_pairs={{0,1},{1,0},{2,3},{3,2},{4,5},{5,4},{6,7},{7,6},{8,9},{9,8},{10,11... | collective-permute-start | bytes 4718600 | tf_op jit(solution)/shard_map/ppermute | solution.py:48
  239.4 9.1 %collective-permute-start.7 = (bf16[64,28,256]{2,0,1:T(8,128)(2,1)}, bf16[64,28,256]{2,0,1:T(8,128)(2,1)}, u32[]{:S(2)}, u32[]{:S(2)}) collective-permute-start(bf16[64,28,256]{2,0,1:T(8,128)(2,1)} %copy.158), channel_id=1, source_target_pairs={{0,1},{1,0},{2,3},{3,2},{4,5},{5,4},{6,7},{7,6},{8,9},{9,8},{10,11... | collective-permute-start | bytes 2752520 | tf_op jit(solution)/shard_map/ppermute | solution.py:48
  253.3 37.6 %collective-permute-start.2 = (bf16[1280,512]{1,0:T(8,128)(2,1)}, bf16[1280,512]{1,0:T(8,128)(2,1)}, u32[]{:S(2)}, u32[]{:S(2)}) collective-permute-start(bf16[1280,512]{1,0:T(8,128)(2,1)} %bitcast.160), channel_id=1, source_target_pairs={{0,1},{1,0},{2,3},{3,2},{4,5},{5,4},{6,7},{7,6},{8,9},{9,8},{10,11... | collective-permute-start | bytes 3932168 | tf_op jit(solution)/shard_map/ppermute | solution.py:48
  270.3 68.1 %all-to-all-start.5 = ((bf16[16,176,864]{2,1,0:T(8,128)(2,1)}), bf16[16,176,864]{2,1,0:T(8,128)(2,1)}, u32[]{:S(2)}, u32[]{:S(2)}) async-start(bf16[16,176,864]{2,1,0:T(8,128)(2,1)} %broadcast_in_dim.45), calls=%async_computation.5 | async-start | bytes 10092544 | tf_op jit(solution)/shard_map/all_to_all | solution.py:36
  339.6 27.5 %all-to-all-start.3 = ((bf16[4,160,1152]{2,1,0:T(8,128)(2,1)}), bf16[4,160,1152]{2,1,0:T(8,128)(2,1)}, u32[]{:S(2)}, u32[]{:S(2)}) async-start(bf16[4,160,1152]{2,1,0:T(8,128)(2,1)} %broadcast_in_dim.44), calls=%async_computation.3 | async-start | bytes 2949120 | tf_op jit(solution)/shard_map/all_to_all | solution.py:36
  367.1 25.1 %collective-permute-start.5 = (bf16[640,1152]{1,0:T(8,128)(2,1)}, bf16[640,1152]{1,0:T(8,128)(2,1)}, u32[]{:S(2)}, u32[]{:S(2)}) collective-permute-start(bf16[640,1152]{1,0:T(8,128)(2,1)} %bitcast.22), channel_id=1, source_target_pairs={{0,1},{1,0},{2,3},{3,2},{4,5},{5,4},{6,7},{7,6},{8,9},{9,8},{10,11... | collective-permute-start | bytes 4423688 | tf_op jit(solution)/shard_map/ppermute | solution.py:48
  411.4 3.3 collective-permute-start.9
  416.1 24.7 %all-to-all-start.8 = ((bf16[4,160,1152]{2,1,0:T(8,128)(2,1)}), bf16[4,160,1152]{2,1,0:T(8,128)(2,1)}, u32[]{:S(2)}, u32[]{:S(2)}) async-start(bf16[4,160,1152]{2,1,0:T(8,128)(2,1)} %bitcast.31), calls=%async_computation.8 | async-start | bytes 2949120 | tf_op jit(solution)/shard_map/all_to_all | solution.py:36
  463.9 5.0 collective-permute-start.10
  477.0 44.7 %all-to-all-start.17 = ((bf16[16,54,1152]{2,1,0:T(8,128)(2,1)}), bf16[16,54,1152]{2,1,0:T(8,128)(2,1)}, u32[]{:S(2)}, u32[]{:S(2)}) async-start(bf16[16,54,1152]{2,1,0:T(8,128)(2,1)} %reshape.744), calls=%async_computation.17 | async-start | bytes 4128768 | tf_op jit(solution)/shard_map/all_to_all | solution.py:36
  505.7 14.5 %collective-permute-start.11 = (bf16[640,1152]{1,0:T(8,128)(2,1)S(1)}, bf16[640,1152]{1,0:T(8,128)(2,1)S(1)}, u32[]{:S(2)}, u32[]{:S(2)}) collective-permute-start(bf16[640,1152]{1,0:T(8,128)(2,1)S(1)} %slice.1069), channel_id=1, source_target_pairs={{0,1},{1,0},{2,3},{3,2},{4,5},{5,4},{6,7},{7,6},{8,9},{9,8},{10,11... | collective-permute-start | bytes 4423688 | tf_op jit(solution)/shard_map/ppermute | solution.py:48
  521.7 36.8 %all-to-all-start.11 = ((bf16[4,160,1152]{2,1,0:T(8,128)(2,1)}), bf16[4,160,1152]{2,1,0:T(8,128)(2,1)}, u32[]{:S(2)}, u32[]{:S(2)}) async-start(bf16[4,160,1152]{2,1,0:T(8,128)(2,1)} %bitcast.147), calls=%async_computation.11 | async-start | bytes 2949120 | tf_op jit(solution)/shard_map/all_to_all | solution.py:36
  555.1 206.8 %collective-permute-start.17 = (bf16[54,1152]{1,0:T(8,128)(2,1)}, bf16[54,1152]{1,0:T(8,128)(2,1)}, u32[]{:S(2)}, u32[]{:S(2)}) collective-permute-start(bf16[54,1152]{1,0:T(8,128)(2,1)} %reduce_sum.207), channel_id=1, source_target_pairs={{0,0},{8,1},{16,2},{24,3},{32,4},{40,5},{48,6},{56,7},{64,8},{72,9... | collective-permute-start | bytes 373256 | tf_op jit(solution)/shard_map/ppermute | solution.py:319
  558.5 75.4 %all-to-all-start.15 = ((bf16[16,176,864]{2,1,0:T(8,128)(2,1)}), bf16[16,176,864]{2,1,0:T(8,128)(2,1)}, u32[]{:S(2)}, u32[]{:S(2)}) async-start(bf16[16,176,864]{2,1,0:T(8,128)(2,1)} %pad_maximum_fusion), calls=%async_computation.15 | async-start | bytes 10092544 | tf_op jit(solution)/shard_map/all_to_all | solution.py:36
  581.3 162.8 %collective-permute-start.15 = (bf16[64,24,640]{2,1,0:T(8,128)(2,1)}, bf16[64,24,640]{2,1,0:T(8,128)(2,1)}, u32[]{:S(2)}, u32[]{:S(2)}) collective-permute-start(bf16[64,24,640]{2,1,0:T(8,128)(2,1)} %broadcast_select_fusion.1), channel_id=1, source_target_pairs={{0,1},{1,0},{2,3},{3,2},{4,5},{5,4},{6,7},{7,6},{8,9},{9,8},{10,11... | collective-permute-start | bytes 5898248 | tf_op jit(solution)/shard_map/ppermute | solution.py:48
  597.1 4.8 collective-permute-start.12
  633.9 25.6 %all-to-all-start.12 = ((bf16[8,160,512]{2,1,0:T(8,128)(2,1)}), bf16[8,160,512]{2,1,0:T(8,128)(2,1)}, u32[]{:S(2)}, u32[]{:S(2)}) async-start(bf16[8,160,512]{2,1,0:T(8,128)(2,1)} %bitcast.148), calls=%async_computation.12 | async-start | bytes 2621440 | tf_op jit(solution)/shard_map/all_to_all | solution.py:36
  660.8 79.1 %all-to-all-start.9 = ((f32[128,1,128]{2,1,0:T(1,128)}), f32[128,1,128]{2,1,0:T(1,128)}, u32[]{:S(2)}, u32[]{:S(2)}) async-start(f32[128,1,128]{2,1,0:T(1,128)} %broadcast_in_dim.49), calls=%async_computation.9 | async-start | bytes 131072 | tf_op jit(solution)/shard_map/all_to_all | solution.py:36
  723.0 50.8 %collective-permute-start.13 = (bf16[64,23,768]{2,0,1:T(8,128)(2,1)}, bf16[64,23,768]{2,0,1:T(8,128)(2,1)}, u32[]{:S(2)}, u32[]{:S(2)}) collective-permute-start(bf16[64,23,768]{2,0,1:T(8,128)(2,1)} %copy.166), channel_id=1, source_target_pairs={{0,1},{1,0},{2,3},{3,2},{4,5},{5,4},{6,7},{7,6},{8,9},{9,8},{10,11... | collective-permute-start | bytes 6782984 | tf_op jit(solution)/shard_map/ppermute | solution.py:48
  739.8 13.1 %all-to-all-start.16 = ((bf16[8,31,864]{2,1,0:T(8,128)(2,1)}), bf16[8,31,864]{2,1,0:T(8,128)(2,1)}, u32[]{:S(2)}, u32[]{:S(2)}) async-start(bf16[8,31,864]{2,1,0:T(8,128)(2,1)} %concatenate.357), calls=%async_computation.16 | async-start | bytes 917504 | tf_op jit(solution)/shard_map/all_to_all | solution.py:36
  752.9 34.3 %all-to-all-start.14 = ((bf16[64,24,640]{2,1,0:T(8,128)(2,1)}), bf16[64,24,640]{2,1,0:T(8,128)(2,1)S(1)}, u32[]{:S(2)}, u32[]{:S(2)}) async-start(bf16[64,24,640]{2,1,0:T(8,128)(2,1)} %add_convert_fusion.2), calls=%async_computation.14 | async-start | bytes 3932160 | tf_op jit(solution)/shard_map/all_to_all | solution.py:36
  788.5 36.0 %all-to-all-start.13 = ((bf16[64,23,768]{2,1,0:T(8,128)(2,1)}), bf16[64,23,768]{2,1,0:T(8,128)(2,1)S(1)}, u32[]{:S(2)}, u32[]{:S(2)}) async-start(bf16[64,23,768]{2,1,0:T(8,128)(2,1)} %add_convert_fusion), calls=%async_computation.13 | async-start | bytes 4718592 | tf_op jit(solution)/shard_map/all_to_all | solution.py:36
  825.6 4.9 collective-permute-start.14
  (117 other events, 1494.1 us)

commit v2 on v1

v2 whole, which is shorter than its diff:
```python
import jax
import jax.numpy as jnp
from jax import lax
from jax.sharding import Mesh, PartitionSpec as P

EPSILON = 1e-06
ROPE_BASE = 10000.0
MASKED_SCORE = -1e30
BF = jnp.bfloat16
F32 = jnp.float32

CHIPS = ("z", "xl", "xh", "y")
EVERY = ("z", "xl", "xh", "y", "c")
SIZES = dict(z=4, xl=2, xh=2, y=4, c=2)
RING = dict(z="z", x=("xl", "xh"), y="y")
TOKENS = 160
HEADS = 4
WIDTH = 256


def dot(a, b):
    return jnp.dot(a, b, preferred_element_type=F32)


def dot_tl(a, b):
    return lax.dot_general(a, b, (((0,), (0,)), ((), ())), preferred_element_type=F32)


def dot_tr(a, b):
    return lax.dot_general(a, b, (((1,), (1,)), ((), ())), preferred_element_type=F32)


def exchange(x, axes):
    return lax.all_to_all(x, axes, split_axis=0, concat_axis=0, tiled=True)


def gather_chips(x):
    return exchange(jnp.broadcast_to(x[None], (64,) + x.shape), CHIPS)


def other_core(x):
    return lax.ppermute(x, "c", [(0, 1), (1, 0)])


def shift(x, axis, k):
    number = [0, 2, 1, 3] if axis == "x" else [0, 1, 2, 3]
    return lax.ppermute(x, RING[axis], [(number[i], number[(i + k) % 4]) for i in range(4)])


def pick(cond, a, b):
    return jnp.where(cond, a, b), jnp.where(cond, b, a)


def split_in_two(x):
    high = x.astype(BF)
    return high, (x - high.astype(F32)).astype(BF)


def select_back(x, table):
    high, low = split_in_two(x)
    return dot_tr(high, table) + dot_tr(low, table)


def down_route():
    pairs = []
    for o in range(16):
        for t in range(8):
            pairs.append((8 * o + t, 8 * (8 * (o % 2) + t) + o // 2))
    return pairs


def gather_zx(x, first):
    second = "z" if first == "x" else "x"
    line = jnp.stack([x] + [shift(x, first, k) for k in (1, 2, 3)])
    lines = [line] + [shift(line, second, k) for k in (1, 2, 3)]
    return jnp.stack(lines, axis=0 if first == "x" else 1)


def scatter_zx(x, first):
    second = "z" if first == "x" else "x"
    x = [x[k] if first == "z" else x[:, k] for k in range(4)]
    line = x[0].astype(F32)
    for k in (1, 2, 3):
        line = line + shift(x[k], first, 4 - k).astype(F32)
    line = line.astype(BF)
    out = line[0].astype(F32)
    for k in (1, 2, 3):
        out = out + shift(line[k], second, 4 - k).astype(F32)
    return out


def norm_parts(values, gain):
    scale = lax.rsqrt(jnp.mean(values * values, axis=-1, keepdims=True) + EPSILON)
    n = values * scale
    return scale, n, (n * (1.0 + gain)).astype(BF)


def norm_back(scale, n, gain, grad):
    m = grad * (1.0 + gain)
    back = scale * (m - n * jnp.mean(m * n, axis=-1, keepdims=True))
    return back, jnp.sum(grad * n, axis=0, keepdims=True)


def turn(x, cos, sin):
    h = cos.shape[-1]
    a, b = x[:, :h], x[:, h:]
    return jnp.concatenate([a * cos - b * sin, b * cos + a * sin], axis=-1)


def turn_back(x, cos, sin):
    return turn(x, cos, -sin)


def gather_tokens(x):
    mine = [x] + [shift(x, "y", k) for k in (1, 2, 3)]
    return jnp.concatenate(mine + [other_core(p) for p in mine], axis=0)


def scatter_tokens(part):
    blocks = part.reshape(2, 4, TOKENS, -1)
    total = None
    for k in (2, 1, 3, 0):
        piece = blocks[0, k] + other_core(blocks[1, k].astype(BF)).astype(F32)
        if k:
            piece = shift(piece.astype(BF), "y", 4 - k).astype(F32)
        total = piece if total is None else total + piece
    return total


def table(rows, columns):
    return (rows[:, None] == columns[None, :]).astype(BF)


def on_device(
    layer_input,
    segment,
    position,
    loss_token_mask,
    teacher,
    gain_one,
    wq,
    wk,
    wv,
    wo,
    aq,
    bq,
    ak,
    bk,
    av,
    bv,
    ao,
    bo,
    gain_two,
    wg,
    wu,
    wd,
    ag,
    bg,
    au,
    bu,
    ad,
    bd,
):
    core = lax.axis_index("c")
    at_z, at_y = lax.axis_index("z"), lax.axis_index("y")
    at_xl, at_xh = lax.axis_index("xl"), lax.axis_index("xh")
    at_x = 2 * at_xh + at_xl
    is_first = core == 0
    score_scale = WIDTH**-0.5
    hidden = layer_input[0].astype(F32)
    count_here = jnp.sum(loss_token_mask[0]).astype(BF)

    extra = jnp.concatenate([gain_one[None], gain_two[None], count_here.reshape(1, 1)], axis=1)
    extra = jnp.pad(extra, ((0, 1), (0, 384 - 19)))

    def attention_half(k):
        top = jnp.concatenate(
            [m[:, m.shape[1] // 2 * k : m.shape[1] // 2 * (k + 1)] for m in (wq, wk, wv, aq, ak, av)],
            axis=1,
        )
        low = jnp.concatenate(
            [m[:, m.shape[1] // 2 * k : m.shape[1] // 2 * (k + 1)] for m in (bq, bk, bv)] + [extra],
            axis=1,
        )
        return jnp.concatenate([top, low, jnp.zeros((1, 1152), BF)], axis=0)

    keep, send = pick(is_first, attention_half(0), attention_half(1))
    lower, upper = pick(is_first, keep, other_core(send))
    raw_one = gather_chips(jnp.concatenate([lower, upper], axis=0))
    raw_two = other_core(raw_one)
    marks = raw_one.reshape(128, 12, 1152)[:, 9, 768:896]
    gain_one_full = marks[:, :9].reshape(1, 1152).astype(F32)
    gain_two_full = marks[:, 9:18].reshape(1, 1152).astype(F32)
    valid_count = jnp.sum(marks[:, 18].astype(F32))
    raw = [raw_one.reshape(1536, 1152), raw_two.reshape(1536, 1152)]

    def output_half(k):
        zero = jnp.zeros((2, 128), BF)
        return jnp.concatenate(
            [
                jnp.concatenate([wo[:, 512 * k : 512 * k + 640], ao[:, 128 * k : 128 * k + 128]], axis=1),
                jnp.concatenate([bo[:, 512 * k : 512 * k + 640], zero], axis=1),
                jnp.concatenate([bd[:, 512 * k : 512 * k + 640], zero], axis=1),
            ],
            axis=0,
        )

    keep, send = pick(is_first, output_half(0), output_half(1))
    lower, upper = pick(is_first, keep, other_core(send))
    out_own = lax.optimization_barrier((jnp.concatenate([lower, upper], axis=0), raw_one))[0]
    out_one = gather_chips(out_own)
    out_two = other_core(out_one)
    raw_out = [out_one.reshape(1536, 768), out_two.reshape(1536, 768)]

    rows31 = jnp.concatenate(
        [
            wg,
            wu,
            bg,
            bu,
        ],
        axis=0,
    )
    rows31 = rows31.reshape(22, 8, 864).transpose(1, 0, 2)
    inner_rows = jnp.concatenate([ag, au, jnp.zeros((9, 352), BF)], axis=1)
    rows31 = jnp.concatenate([rows31, jnp.broadcast_to(inner_rows[None], (8, 9, 864))], axis=1)
    slab = jnp.zeros((8, 31, 864), BF)
    for ky in range(4):
        for kc in range(2):
            to = 2 * ((at_y + ky) % 4) + (core + kc) % 2
            source = 2 * ((at_y - ky) % 4) + (core - kc) % 2
            piece = lax.dynamic_index_in_dim(rows31, to, 0, keepdims=False)
            if ky or kc:
                route = []
                for y in range(4):
                    for c in range(2):
                        route.append((2 * y + c, 2 * ((y + ky) % 4) + (c + kc) % 2))
                piece = lax.ppermute(piece, ("y", "c"), route)
            slab = lax.dynamic_update_index_in_dim(slab, piece, source, 0)
    gate_own = jnp.concatenate([slab[:, :9].reshape(72, 864), slab[:, 18:20].reshape(16, 864)], axis=0)
    up_own = jnp.concatenate([slab[:, 9:18].reshape(72, 864), slab[:, 20:22].reshape(16, 864)], axis=0)
    inner_own = slab[:, 22:, :512].reshape(72, 512)
    down_own = lax.ppermute(
        jnp.pad(jnp.concatenate([wd, ad], axis=1), ((0, 2), (0, 0))), EVERY, down_route()
    )
    gate_own, up_own, inner_own, down_own, _ = lax.optimization_barrier(
        (gate_own, up_own, inner_own, down_own, raw_one)
    )
    gate_raw = gather_zx(gate_own, "x")
    up_raw = gather_zx(up_own, "z")
    inner_raw = gather_zx(inner_own, "x").reshape(1152, 512)
    down_raw = gather_zx(down_own, "z").reshape(896, 1408)

    ids = jnp.arange(1536, dtype=jnp.int32)
    dev, j = 2 * (ids // 24) + (ids % 24) // 12, ids % 12
    halves = jnp.arange(256, dtype=jnp.int32)
    inner_ids = jnp.where(halves < 128, 128 * core + halves, 128 * (1 - core) + halves - 128)
    heads_at = jnp.arange(1024, dtype=jnp.int32)
    head_ids = jnp.where(heads_at < 512, 512 * core + heads_at, 512 * (1 - core) + heads_at - 512)
    features = jnp.arange(1152, dtype=jnp.int32)
    put_rows = table(features, jnp.where(j < 9, 9 * dev + j, -1))
    put_inner = table(inner_ids, jnp.where((j >= 9) & (j < 11), 2 * dev + j - 9, -1))
    put_marks = table(features // 9, jnp.where(j == 11, dev, -1))
    put_mix = table(head_ids, jnp.where(j < 8, 8 * dev + j, -1))
    put_inner_out = table(inner_ids, jnp.where((j >= 8) & (j < 10), 2 * dev + j - 8, -1))
    put_inner_down = table(halves, jnp.where(j >= 10, 2 * dev + j - 10, -1))

    def plane(block):
        kz, kx = block // 4, block % 4
        x = (at_x - kx) % 4
        return (((at_z - kz) % 4) * 2 + x % 2) * 2 + x // 2

    put_feature = table(features, 72 * plane(features // 72) + features % 72)
    put_b = table(halves, 16 * plane(halves // 16) + halves % 16)
    hidden_ids = jnp.arange(864, dtype=jnp.int32)
    down_ids = jnp.arange(896, dtype=jnp.int32)
    put_down = table(
        hidden_ids, jnp.where(down_ids % 56 < 54, 54 * plane(down_ids // 56) + down_ids % 56, -1)
    )

    seq = (at_xh * 4 + at_y) * 2 + core
    tree_seg = segment[0]
    tree_pos = position[0]
    own_seg = lax.dynamic_slice_in_dim(tree_seg, seq * TOKENS, TOKENS)
    own_pos = lax.dynamic_slice_in_dim(tree_pos, seq * TOKENS, TOKENS)
    freq = ROPE_BASE ** (-(jnp.arange(128, dtype=F32) * 2.0 / WIDTH))
    angles = own_pos.astype(F32)[:, None] * freq[None, :]
    cos, sin = jnp.cos(angles), jnp.sin(angles)
    back = jnp.arange(16, dtype=jnp.int32)
    block_at = (((at_xh - (back % 8) // 4) % 2) * 4 + (at_y - back % 4) % 4) * 2 + jnp.where(
        back < 8, core, 1 - core
    )
    chosen = (block_at[:, None] == back[None, :]).astype(jnp.int32)[:, :, None]
    key_seg = jnp.sum(chosen * tree_seg.reshape(1, 16, TOKENS), axis=1).reshape(1, 2560)
    key_pos = jnp.sum(chosen * tree_pos.reshape(1, 16, TOKENS), axis=1).reshape(1, 2560)
    q_seg, q_pos = own_seg[:, None], own_pos[:, None]
    parent = (key_seg >= 1) & (key_seg <= 4) & (q_seg >= 5) & ((q_seg - 5) // 2 + 1 == key_seg)
    allowed = ((key_seg == q_seg) | (key_seg == 0) | parent) & (key_pos <= q_pos)
    allowed = jnp.concatenate([allowed] * HEADS, axis=0)

    scale_one, n_one, u_one = norm_parts(hidden, gain_one_full)
    u_rows = dot(u_one, put_rows).astype(BF)
    inner = [dot(u_rows, raw[i][:, 768:]).astype(BF) for i in (0, 1)]
    sides = []
    for i in range(3):
        part = jnp.concatenate([inner[0][:, 128 * i : 128 * i + 128], inner[1][:, 128 * i : 128 * i + 128]], axis=1)
        sides.append(u_rows + dot(part, put_inner).astype(BF))
    kk = pick(is_first, *[dot(sides[1], raw[i][:, 512:640]) for i in (0, 1)])
    vv = pick(is_first, *[dot(sides[2], raw[i][:, 640:768]) for i in (0, 1)])
    kv_own = jnp.concatenate([turn(jnp.concatenate(kk, axis=1), cos, sin), vv[0], vv[1]], axis=1).astype(BF)

    def tree_shift(x, kh, ky):
        route = []
        for h in range(2):
            for y in range(4):
                route.append((4 * h + y, 4 * ((h + kh) % 2) + (y + ky) % 4))
        return lax.ppermute(x, ("xh", "y"), route)

    kv_mine = [kv_own] + [tree_shift(kv_own, k // 4, k % 4) for k in range(1, 8)]
    kv_mine = jnp.concatenate(kv_mine, axis=0)
    kv = jnp.concatenate([kv_mine, other_core(kv_mine)], axis=0)
    keys, values = kv[:, :256], kv[:, 256:]
    queries = [dot(sides[0], raw[i][:, :512]) for i in (0, 1)]
    q_rows = jnp.concatenate(
        [turn(queries[h // 2][:, WIDTH * (h % 2) : WIDTH * (h % 2 + 1)], cos, sin) for h in range(HEADS)],
        axis=0,
    ).astype(BF)
    scores = jnp.where(allowed, dot_tr(q_rows, keys) * score_scale, MASKED_SCORE)
    top = jnp.max(scores, axis=-1, keepdims=True)
    ex = jnp.exp(scores - top)
    total = jnp.sum(ex, axis=-1, keepdims=True)
    lse = top + jnp.log(total)
    mix_rows = dot((ex / total).astype(BF), values).astype(BF)
    mix = jnp.concatenate([mix_rows[TOKENS * h : TOKENS * (h + 1)] for h in range(HEADS)], axis=1)
    mix_placed = dot(mix, put_mix).astype(BF)
    inner_out = jnp.concatenate([dot(mix_placed, raw_out[i][:, 640:]) for i in (0, 1)], axis=1).astype(BF)
    side_out = mix_placed + dot(inner_out, put_inner_out).astype(BF)
    left, right = pick(is_first, *[dot(side_out, raw_out[i][:, :640]) for i in (0, 1)])
    after = hidden + jnp.concatenate([left, right[:, 128:]], axis=1)

    a_gate = dot(inner_raw[:, :256], put_b).astype(BF)
    a_up = dot(inner_raw[:, 256:], put_b).astype(BF)
    b_gate = gate_raw[:, :, 72:].reshape(256, 864)
    b_up = up_raw[:, :, 72:].reshape(256, 864)
    w_gate = (gate_raw[:, :, :72].reshape(1152, 864).astype(F32) + dot(a_gate, b_gate)).astype(BF)
    w_up = (up_raw[:, :, :72].reshape(1152, 864).astype(F32) + dot(a_up, b_up)).astype(BF)
    left, right = pick(is_first, *[dot(put_inner_down, raw_out[i][:, :640]).astype(BF) for i in (0, 1)])
    b_down = jnp.concatenate([left, right[:, 128:]], axis=1)
    a_down = dot(put_down, down_raw[:, 1152:]).astype(BF)
    w_down = (dot(put_down, down_raw[:, :1152]) + dot(a_down, b_down)).astype(BF)

    scale_two, n_two, u_two = norm_parts(after, gain_two_full)
    u_all = gather_tokens(dot(u_two, put_feature).astype(BF))
    gate = dot(u_all, w_gate)
    up = dot(u_all, w_up)
    act, act_pull = jax.vjp(lambda g, u: jax.nn.gelu(g, approximate=True) * u, gate, up)
    act = act.astype(BF)
    result = after + scatter_tokens(dot(act, w_down))

    valid = loss_token_mask[0].astype(F32)[:, None]
    error = result - teacher[0].astype(F32)
    loss_here = jnp.sum(valid * error * error)
    grad_result = 2.0 * 20480.0 / valid_count * valid * error

    g_all = gather_tokens(grad_result.astype(BF))
    g_act = dot_tr(g_all, w_down).astype(BF)
    g_gate, g_up = act_pull(g_act.astype(F32))
    g_gate, g_up = g_gate.astype(BF), g_up.astype(BF)
    g_u_two = select_back(scatter_tokens(dot_tr(g_gate, w_gate) + dot_tr(g_up, w_up)), put_feature)
    gw_gate = dot_tl(u_all, g_gate).astype(BF)
    gw_up = dot_tl(u_all, g_up).astype(BF)
    gw_down = dot_tl(act, g_all).astype(BF)
    gb_gate = dot_tl(a_gate, gw_gate).astype(BF)
    gb_up = dot_tl(a_up, gw_up).astype(BF)
    gb_down = dot_tl(a_down, gw_down).astype(BF)
    gw_down = dot_tl(put_down, gw_down).astype(BF)
    gate_sum = scatter_zx(
        jnp.concatenate([gw_gate.reshape(4, 4, 72, 864), gb_gate.reshape(4, 4, 16, 864)], axis=2), "z"
    ).astype(BF)
    up_sum = scatter_zx(
        jnp.concatenate([gw_up.reshape(4, 4, 72, 864), gb_up.reshape(4, 4, 16, 864)], axis=2), "x"
    ).astype(BF)
    down_sum = scatter_zx(gw_down.reshape(4, 4, 56, 1152), "x").astype(BF)
    ga_gate = dot_tr(dot_tr(gate_sum[:72], b_gate).astype(BF), put_b)
    ga_up = dot_tr(dot_tr(up_sum[:72], b_up).astype(BF), put_b)
    ga_part = jnp.concatenate([ga_gate, ga_up, jnp.zeros((72, 352), F32)], axis=1).astype(BF)
    leaving = jnp.concatenate(
        [
            gate_sum[:72].reshape(8, 9, 864),
            up_sum[:72].reshape(8, 9, 864),
            gate_sum[72:].reshape(8, 2, 864),
            up_sum[72:].reshape(8, 2, 864),
            ga_part.reshape(8, 9, 864),
        ],
        axis=1,
    )
    slab = jnp.zeros((8, 31, 864), BF)
    for ky in range(4):
        for kc in range(2):
            to = 2 * ((at_y + ky) % 4) + (core + kc) % 2
            source = 2 * ((at_y - ky) % 4) + (core - kc) % 2
            piece = lax.dynamic_index_in_dim(leaving, to, 0, keepdims=False)
            if ky or kc:
                route = []
                for y in range(4):
                    for c in range(2):
                        route.append((2 * y + c, 2 * ((y + ky) % 4) + (c + kc) % 2))
                piece = lax.ppermute(piece, ("y", "c"), route)
            slab = lax.dynamic_update_index_in_dim(slab, piece, source, 0)
    wide = slab[:, :22].transpose(1, 0, 2).reshape(22, 6912).astype(F32)
    ga = jnp.sum(slab[:, 22:, :512].astype(F32), axis=0)
    gw_down_own = lax.ppermute(down_sum, EVERY, [(b, a) for a, b in down_route()])[:54]
    ga_down_own = dot_tr(gw_down_own, b_down)

    norm_two_back, g_gain_two = norm_back(scale_two, n_two, gain_two_full, g_u_two)
    g_after = grad_result + norm_two_back
    g_after_b = g_after.astype(BF)
    once = jnp.where(jnp.arange(640) < 128, 0, 1).astype(BF)[None]
    g_half = pick(is_first, g_after_b[:, :640], g_after_b[:, 512:])
    g_once = pick(is_first, g_after_b[:, :640], g_after_b[:, 512:] * once)
    d_out = dot_tr(g_once[0], raw_out[0][:, :640]) + dot_tr(g_once[1], raw_out[1][:, :640])
    gi_out = dot_tr(d_out.astype(BF), put_inner_out).astype(BF)
    d_out = (
        d_out
        + dot_tr(gi_out[:, :128], raw_out[0][:, 640:])
        + dot_tr(gi_out[:, 128:], raw_out[1][:, 640:])
    )
    g_mix = dot_tr(d_out.astype(BF), put_mix).astype(BF)
    g_rows = jnp.concatenate([g_mix[:, WIDTH * h : WIDTH * (h + 1)] for h in range(HEADS)], axis=0)
    scores_again = jnp.where(allowed, dot_tr(q_rows, keys) * score_scale, MASKED_SCORE)
    probs = jnp.where(allowed, jnp.exp(scores_again - lse), 0.0)
    g_probs = dot_tr(g_rows, values)
    g_scores = (probs * (g_probs - jnp.sum(probs * g_probs, axis=-1, keepdims=True))).astype(BF)
    g_keys = dot_tl(g_scores, q_rows) * score_scale
    g_values = dot_tl(probs.astype(BF), g_rows)
    g_kv = jnp.concatenate([g_keys, g_values], axis=1)
    n_mine = 8 * TOKENS
    g_kv_sum = g_kv[:n_mine] + other_core(g_kv[n_mine:].astype(BF)).astype(F32)
    g_kv_b = g_kv_sum.astype(BF)
    g_kv_own = g_kv_sum[:TOKENS]
    for k in range(1, 8):
        away = g_kv_b[TOKENS * k : TOKENS * (k + 1)]
        g_kv_own = g_kv_own + tree_shift(away, k // 4, (4 - k % 4) % 4).astype(F32)
    g_q_rows = dot(g_scores, keys) * score_scale
    g_q = [
        jnp.concatenate(
            [turn_back(g_q_rows[TOKENS * h : TOKENS * (h + 1)], cos, sin) for h in (2 * i, 2 * i + 1)],
            axis=1,
        ).astype(BF)
        for i in (0, 1)
    ]
    g_k = turn_back(g_kv_own[:, :256], cos, sin).astype(BF)
    g_v = g_kv_own[:, 256:].astype(BF)
    g_k = pick(is_first, g_k[:, :128], g_k[:, 128:])
    g_v = pick(is_first, g_v[:, :128], g_v[:, 128:])
    d_one = None
    for i, (g, first, last) in enumerate(((g_q, 0, 512), (g_k, 512, 640), (g_v, 640, 768))):
        d = dot_tr(g[0], raw[0][:, first:last]) + dot_tr(g[1], raw[1][:, first:last])
        gi = dot_tr(d.astype(BF), put_inner).astype(BF)
        inner_at = 768 + 128 * i
        d = d + dot_tr(gi[:, :128], raw[0][:, inner_at : inner_at + 128])
        d = d + dot_tr(gi[:, 128:], raw[1][:, inner_at : inner_at + 128])
        d_one = d if d_one is None else d_one + d
    g_u_one = select_back(d_one, put_rows)
    norm_one_back, g_gain_one = norm_back(scale_one, n_one, gain_one_full, g_u_one)
    grad_hidden = (g_after + norm_one_back).astype(BF)

    def to_owners(own, away):
        summed = (own + other_core(away.astype(BF)).astype(F32)).astype(BF)
        return jnp.sum(exchange(summed.reshape(64, 24, -1), CHIPS).astype(F32), axis=0)

    def both_halves(owned):
        mine, away = pick(is_first, owned[:12], owned[12:])
        return pick(is_first, mine, other_core(away.astype(BF)).astype(F32))

    left, right = pick(is_first, gb_down[:, :640], gb_down[:, 512:])
    owned_out = to_owners(
        dot_tl(side_out, g_half[0]) + dot_tl(put_inner_down, left),
        dot_tl(side_out, g_half[1]) + dot_tl(put_inner_down, right),
    )
    left, right = both_halves(owned_out)
    own_out = jnp.concatenate([left, right[:, 128:]], axis=1)
    d = dot_tr(own_out[:8, :640].astype(BF), pick(is_first, *raw_out)[0][:, :640]) + dot_tr(
        own_out[:8, 640:].astype(BF), pick(is_first, *raw_out)[1][:, 128:640]
    )
    ga_out_own = dot_tr(d.astype(BF), put_inner_out)
    ga_out_own = jnp.concatenate(pick(is_first, ga_out_own[:, :128], ga_out_own[:, 128:]), axis=1)

    nines = jnp.arange(9, dtype=jnp.int32)[:, None] == features[None, :] % 9
    loss_high, loss_rest = split_in_two(loss_here)
    loss_mid, loss_low = split_in_two(loss_here - loss_high.astype(F32))
    at_marks = (j == 11).astype(BF)[None, :]
    more_side = jnp.concatenate(
        [
            dot(jnp.where(nines, g_gain_one, 0.0).astype(BF), put_marks).astype(BF),
            dot(jnp.where(nines, g_gain_two, 0.0).astype(BF), put_marks).astype(BF),
            loss_high * at_marks,
            loss_mid * at_marks,
            loss_low * at_marks,
            jnp.zeros((11, 1536), BF),
        ],
        axis=0,
    )
    lines = jnp.arange(32, dtype=jnp.int32)
    line_at = jnp.where(lines < 18, lines, jnp.where(lines < 21, lines + 3 * core, -1))
    more_grad = table(line_at, jnp.arange(512, dtype=jnp.int32))
    side_q = jnp.concatenate([sides[0], more_side], axis=0)
    sums = [
        jnp.concatenate(
            [
                dot_tl(side_q, jnp.concatenate([g_q[i], more_grad], axis=0)),
                dot_tl(sides[1], g_k[i]),
                dot_tl(sides[2], g_v[i]),
            ],
            axis=1,
        )
        for i in (0, 1)
    ]
    owned = to_owners(sums[0], sums[1])
    loss_value = jnp.sum(owned[11, 18:24]) / (1152.0 * valid_count)
    left, right = both_halves(owned)
    gains = left[11]
    left_b, right_b = left.astype(BF), right.astype(BF)
    mine_b, other_b = pick(is_first, left_b, right_b)
    ga_own = []
    for first, last in ((0, 512), (512, 640), (640, 768)):
        d = dot_tr(mine_b[:, first:last], raw[0][:, first:last]) + dot_tr(
            other_b[:, first:last], raw[1][:, first:last]
        )
        g = dot_tr(d.astype(BF), put_inner)[:9]
        ga_own.append(jnp.concatenate(pick(is_first, g[:, :128], g[:, 128:]), axis=1))

    def columns(first, last, rows):
        return jnp.concatenate([left[rows, first:last], right[rows, first:last]], axis=1)

    top_rows, low_rows = slice(0, 9), slice(9, 11)

    return (
        result.astype(BF)[None],
        loss_value,
        grad_hidden[None],
        gains[:9],
        columns(0, 512, top_rows),
        columns(512, 640, top_rows),
        columns(640, 768, top_rows),
        own_out[:8],
        ga_own[0],
        columns(0, 512, low_rows),
        ga_own[1],
        columns(512, 640, low_rows),
        ga_own[2],
        columns(640, 768, low_rows),
        ga_out_own,
        own_out[8:10],
        gains[9:18],
        wide[:9],
        wide[9:18],
        gw_down_own.astype(F32),
        ga[:, :256],
        wide[18:20],
        ga[:, 256:],
        wide[20:],
        ga_down_own,
        own_out[10:],
    )


def solution(mesh):
    mesh = Mesh(mesh.devices.reshape([SIZES[a] for a in EVERY]), EVERY)
    tree, seq = ("z", "xl"), ("xh", "y", "c")
    rows = P(EVERY, None)
    vector = P(EVERY)
    return jax.shard_map(
        on_device,
        mesh=mesh,
        in_specs=(
            P(tree, seq, None),
            P(tree, None),
            P(tree, None),
            P(tree, seq),
            P(tree, seq, None),
            vector,
        )
        + (rows,) * 12
        + (vector,)
        + (rows,) * 9,
        out_specs=(P(tree, seq, None), P(), P(tree, seq, None), vector)
        + (rows,) * 12
        + (vector,)
        + (rows,) * 9,
        check_vma=False,
    )
```

time: 851 us -> 881 us (1.035)
  blocking collectives: 75.9 us -> 0 us
  starting transfers between devices: 149 us -> 215 us
  matrix products: 126 us -> 186 us
  local copies, waits for them, and re-layouts: 200 us -> 166 us
  waiting for transfers between devices: 160 us -> 177 us
    ppermute x2 -> x84, waiting for transfers between devices: 10.2 us -> 162 us  [the longest x54 120 us: shift(): lax.ppermute(x, RING[axis], [(number[i], number[(i + k) % 4]) for i in ra...]
    ppermute x2 -> x84, starting transfers between devices: 10.3 us -> 149 us  [the longest x54 97.6 us: shift(): lax.ppermute(x, RING[axis], [(number[i], number[(i + k) % 4]) for i in ra...]
    all_to_all x16 -> x4, waiting for transfers between devices: 142 us -> 13.6 us  [exchange(): return lax.all_to_all(x, axes, split_axis=0, concat_axis=0, tiled=True)]
    all_to_all x16 -> x4, starting transfers between devices: 119 us -> 39.3 us  [exchange(): return lax.all_to_all(x, axes, split_axis=0, concat_axis=0, tiled=True)]
    all_to_all x2 -> x0, blocking collectives: 75.9 us -> none  [exchange(): return lax.all_to_all(x, axes, split_axis=0, concat_axis=0, tiled=True)]
    dot_general x14 -> x40, matrix products: 44.3 us -> 77.8 us  [dot_tr(): lax.dot_general(a, b, (((1,), (1,)), ((), ())), preferred_element_type=F32)]
    squeeze x12 -> x5, local copies, waits for them, and re-layouts: 21.8 us -> 3.06 us  [the longest x3 1.71 us: scatter_zx(): out = out + shift(line[k], second, 4 - k).astype(F32)]
    dot_general x14 -> x35, matrix products: 39 us -> 54.7 us  [dot(): return jnp.dot(a, b, preferred_element_type=F32)]
  transfers between devices with their start and end apart: 34 -> 114, of which waited for: 14 -> 35; matrix products, arithmetic and copies ran while one was open for 45% -> 38% of each run, Pallas kernels for 0% -> 0%
where the time goes in v2:
time: 881 us; the launch traced here: 867 us
  starting transfers between devices  215 us (24%)
  matrix products  186 us (21%)
  waiting for transfers between devices  177 us (20%)
  local copies, waits for them, and re-layouts  166 us (19%)
  other arithmetic  113 us (13%)
  between operations  9.44 us (1%)
    ppermute x54, waiting for transfers between devices, shift(): lax.ppermute(x, RING[axis], [(number[i], number[(i + k) % 4]) for i in ra...  120 us
    ppermute x54, starting transfers between devices, shift(): lax.ppermute(x, RING[axis], [(number[i], number[(i + k) % 4]) for i in ra...  97.6 us
    dot_general x40, matrix products, dot_tr(): lax.dot_general(a, b, (((1,), (1,)), ((), ())), preferred_element_type=F32)  77.8 us
    dot_general x35, matrix products, dot(): return jnp.dot(a, b, preferred_element_type=F32)  54.7 us
    dot_general x19, matrix products, dot_tl(): lax.dot_general(a, b, (((0,), (0,)), ((), ())), preferred_element_type=F32)  53.9 us
    all_to_all x4, starting transfers between devices, exchange(): return lax.all_to_all(x, axes, split_axis=0, concat_axis=0, tiled=True)  39.3 us
    unnamed x419, local copies, waits for them, and re-layouts  31.8 us
    ppermute x26, starting transfers between devices, other_core(): return lax.ppermute(x, 'c', [(0, 1), (1, 0)])  26.9 us
  transfers between devices with their start and end apart: 114, of which 35 were waited for; matrix products, arithmetic and copies ran while one was open for 38% of the time, Pallas kernels for 0%

profile of v2, /device:TPU:1, one launch (start us, length us, event | category | flops | bytes accessed | tf_op | source)
XLA Modules:
  0.0 866.9 jit_solution(15297122112117870590)
XLA Ops:
  42.4 10.4 %all-to-all-start = ((bf16[64,24,1152]{2,1,0:T(8,128)(2,1)}), bf16[64,24,1152]{2,1,0:T(8,128)(2,1)S(1)}, u32[]{:S(2)}, u32[]{:S(2)}) async-start(bf16[64,24,1152]{2,1,0:T(8,128)(2,1)} %broadcast_in_dim.184), calls=%async_computation | async-start | bytes 7077888 | tf_op jit(solution)/shard_map/all_to_all | solution.py:34
  82.3 19.4 %collective-permute-done.23 = bf16[31,864]{1,0:T(8,128)(2,1)S(1)} collective-permute-done((bf16[31,864]{1,0:T(8,128)(2,1)}, bf16[31,864]{1,0:T(8,128)(2,1)S(1)}, u32[]{:S(2)}, u32[]{:S(2)}) %collective-permute-start.23) | collective-permute-done | bytes 53600 | tf_op jit(solution)/shard_map/ppermute | solution.py:238
  136.9 5.6 collective-permute-start.41
  144.8 5.6 all-to-all-start.1
  160.2 22.4 %collective-permute-done.40 = bf16[88,864]{1,0:T(8,128)(2,1)S(1)} collective-permute-done((bf16[88,864]{1,0:T(8,128)(2,1)}, bf16[88,864]{1,0:T(8,128)(2,1)S(1)}, u32[]{:S(2)}, u32[]{:S(2)}) %collective-permute-start.40) | collective-permute-done | bytes 152096 | tf_op jit(solution)/shard_map/ppermute | solution.py:47
  221.5 11.3 %collective-permute-done.30 = bf16[4,88,864]{2,1,0:T(8,128)(2,1)S(1)} collective-permute-done((bf16[4,88,864]{2,1,0:T(8,128)(2,1)S(1)}, bf16[4,88,864]{2,1,0:T(8,128)(2,1)S(1)}, u32[]{:S(2)}, u32[]{:S(2)}) %collective-permute-start.30) | collective-permute-done | bytes 608288 | tf_op jit(solution)/shard_map/ppermute | solution.py:47
  232.8 13.3 %collective-permute-start.50 = (bf16[4,56,1408]{2,1,0:T(8,128)(2,1)}, bf16[4,56,1408]{2,1,0:T(8,128)(2,1)}, u32[]{:S(2)}, u32[]{:S(2)}) collective-permute-start(bf16[4,56,1408]{2,1,0:T(8,128)(2,1)} %get-tuple-element.107), channel_id=1, source_target_pairs={{0,24},{16,0},{8,16},{24,8},{1,25},{17,1},{9,17},{25,9},{2,26},{18... | collective-permute-start | bytes 1892360 | tf_op jit(solution)/shard_map/ppermute | solution.py:47
  252.6 5.7 copy.144
  262.4 5.6 copy.147
  312.6 5.4 collective-permute-done.7
  347.7 6.2 collective-permute-done.12
  354.6 8.0 collective-permute-done.13
  389.5 7.7 collective-permute-done.56
  397.1 8.0 collective-permute-done.52
  434.5 6.6 convolution_convert_fusion.3
  441.1 6.8 fusion.41
  447.9 5.4 fusion.714
  464.8 7.6 convolution_convert_fusion.1
  478.9 8.5 convolution_add_fusion
  514.4 9.1 %collective-permute-done.105 = bf16[4,56,1152]{2,1,0:T(8,128)(2,1)S(1)} collective-permute-done((bf16[4,56,1152]{2,1,0:T(8,128)(2,1)S(1)}, bf16[4,56,1152]{2,1,0:T(8,128)(2,1)S(1)}, u32[]{:S(2)}, u32[]{:S(2)}) %collective-permute-start.105) | collective-permute-done | bytes 516128 | tf_op jit(solution)/shard_map/ppermute | solution.py:47
  525.3 7.4 collective-permute-done.104
  541.2 5.9 collective-permute-done.84
  551.8 6.6 collective-permute-done.91
  558.4 6.7 collective-permute-start.107
  604.2 5.9 multiply_convert_fusion
  631.2 5.2 collective-permute-start.109
  660.8 10.9 %concatenate.280 = bf16[8,31,864]{2,1,0:T(8,128)(2,1)} concatenate(bf16[8,9,864]{2,1,0:T(8,128)(2,1)} %reshape.928, bf16[8,9,864]{2,1,0:T(8,128)(2,1)} %reshape.931, bf16[8,2,864]{2,1,0:T(2,128)(2,1)} %reshape.932, bf16[8,2,864]{2,1,0:T(2,128)(2,1)} %reshape.933, bf16[8,9,864]{2,1,0:T(8,128)(2,1)} %maximum_maximum_fusion.1), dimensions={1} | concatenate | bytes 857088 | tf_op jit(solution)/shard_map/concatenate | solution.py:387
  693.7 5.6 collective-permute-start.78
  731.9 8.9 %concatenate.259 = bf16[192,1536]{1,0:T(8,128)(2,1)} concatenate(bf16[160,1536]{1,0:T(8,128)(2,1)} %copy-done.73, bf16[9,1536]{1,0:T(8,128)(2,1)} %fusion.106, bf16[9,1536]{1,0:T(8,128)(2,1)} %fusion.109, bf16[1,1536]{1,0:T(2,128)(2,1)} %broadcast_select_fusion.30, bf16[1,1536]{1,0:T(2,128)(2,1)} %broadcast_select_fusion.29, bf16[1,1536]{1,0:T(2,128)(2,1)} %broadcast_select_fusion.28, ...), dimensions={0} | concatenate | bytes 1179648 | tf_op jit(solution)/shard_map/concatenate | solution.py:507
  753.0 13.1 %all-to-all-start.3 = ((bf16[64,24,640]{2,1,0:T(8,128)(2,1)}), bf16[64,24,640]{2,1,0:T(8,128)(2,1)}, u32[]{:S(2)}, u32[]{:S(2)}) async-start(bf16[64,24,640]{2,1,0:T(8,128)(2,1)} %bitcast.403), calls=%async_computation.3 | async-start | bytes 3932160 | tf_op jit(solution)/shard_map/all_to_all | solution.py:34
  794.5 10.2 %all-to-all-start.2 = ((bf16[64,24,768]{2,1,0:T(8,128)(2,1)}), bf16[64,24,768]{2,1,0:T(8,128)(2,1)}, u32[]{:S(2)}, u32[]{:S(2)}) async-start(bf16[64,24,768]{2,1,0:T(8,128)(2,1)} %bitcast.402), calls=%async_computation.2 | async-start | bytes 4718592 | tf_op jit(solution)/shard_map/all_to_all | solution.py:34
  821.9 13.6 %all-to-all-done.2 = bf16[64,24,768]{2,1,0:T(8,128)(2,1)} async-done(((bf16[64,24,768]{2,1,0:T(8,128)(2,1)}), bf16[64,24,768]{2,1,0:T(8,128)(2,1)}, u32[]{:S(2)}, u32[]{:S(2)}) %all-to-all-start.2) | async-done | bytes 2359328 | tf_op jit(solution)/shard_map/all_to_all | solution.py:34
  (942 shorter events, 579.1 us)
Async XLA Ops:
  15.8 50.1 %collective-permute-start.10 = (bf16[12,768]{1,0:T(8,128)(2,1)}, bf16[12,768]{1,0:T(8,128)(2,1)}, u32[]{:S(2)}, u32[]{:S(2)}) collective-permute-start(bf16[12,768]{1,0:T(8,128)(2,1)} %broadcast_select_fusion.16), channel_id=1, source_target_pairs={{0,1},{1,0},{2,3},{3,2},{4,5},{5,4},{6,7},{7,6},{8,9},{9,8},{10,11... | collective-permute-start | bytes 55304 | tf_op jit(solution)/shard_map/ppermute | solution.py:42
  21.2 49.6 %collective-permute-start.19 = (bf16[31,864]{1,0:T(8,128)(2,1)}, bf16[31,864]{1,0:T(8,128)(2,1)}, u32[]{:S(2)}, u32[]{:S(2)}) collective-permute-start(bf16[31,864]{1,0:T(8,128)(2,1)} %bitcast.373), channel_id=1, source_target_pairs={{0,1},{1,0},{2,3},{3,2},{4,5},{5,4},{6,7},{7,6},{8,9},{9,8},{10,11... | collective-permute-start | bytes 160712 | tf_op jit(solution)/shard_map/ppermute | solution.py:238
  22.4 50.8 %collective-permute-start.20 = (bf16[31,864]{1,0:T(8,128)(2,1)}, bf16[31,864]{1,0:T(8,128)(2,1)}, u32[]{:S(2)}, u32[]{:S(2)}) collective-permute-start(bf16[31,864]{1,0:T(8,128)(2,1)} %bitcast.372), channel_id=1, source_target_pairs={{0,2},{1,3},{2,4},{3,5},{4,6},{5,7},{6,0},{7,1},{8,10},{9,11},{10,... | collective-permute-start | bytes 160712 | tf_op jit(solution)/shard_map/ppermute | solution.py:238
  24.4 50.2 %collective-permute-start.21 = (bf16[31,864]{1,0:T(8,128)(2,1)}, bf16[31,864]{1,0:T(8,128)(2,1)}, u32[]{:S(2)}, u32[]{:S(2)}) collective-permute-start(bf16[31,864]{1,0:T(8,128)(2,1)} %bitcast.371), channel_id=1, source_target_pairs={{0,3},{1,2},{2,5},{3,4},{4,7},{5,6},{6,1},{7,0},{8,11},{9,10},{10,... | collective-permute-start | bytes 160712 | tf_op jit(solution)/shard_map/ppermute | solution.py:238
  39.0 41.9 %collective-permute-start.22 = (bf16[31,864]{1,0:T(8,128)(2,1)}, bf16[31,864]{1,0:T(8,128)(2,1)}, u32[]{:S(2)}, u32[]{:S(2)}) collective-permute-start(bf16[31,864]{1,0:T(8,128)(2,1)} %bitcast.370), channel_id=1, source_target_pairs={{0,4},{1,5},{2,6},{3,7},{4,0},{5,1},{6,2},{7,3},{8,12},{9,13},{10,... | collective-permute-start | bytes 160712 | tf_op jit(solution)/shard_map/ppermute | solution.py:238
  42.4 75.7 %all-to-all-start = ((bf16[64,24,1152]{2,1,0:T(8,128)(2,1)}), bf16[64,24,1152]{2,1,0:T(8,128)(2,1)S(1)}, u32[]{:S(2)}, u32[]{:S(2)}) async-start(bf16[64,24,1152]{2,1,0:T(8,128)(2,1)} %broadcast_in_dim.184), calls=%async_computation | async-start | bytes 7077888 | tf_op jit(solution)/shard_map/all_to_all | solution.py:34
  65.9 35.9 %collective-permute-start.23 = (bf16[31,864]{1,0:T(8,128)(2,1)}, bf16[31,864]{1,0:T(8,128)(2,1)S(1)}, u32[]{:S(2)}, u32[]{:S(2)}) collective-permute-start(bf16[31,864]{1,0:T(8,128)(2,1)} %bitcast.452), channel_id=1, source_target_pairs={{0,5},{1,4},{2,7},{3,6},{4,1},{5,0},{6,3},{7,2},{8,13},{9,12},{10,... | collective-permute-start | bytes 160712 | tf_op jit(solution)/shard_map/ppermute | solution.py:238
  74.6 43.5 %collective-permute-start.26 = (bf16[56,1408]{1,0:T(8,128)(2,1)}, bf16[56,1408]{1,0:T(8,128)(2,1)}, u32[]{:S(2)}, u32[]{:S(2)}) collective-permute-start(bf16[56,1408]{1,0:T(8,128)(2,1)} %fusion.393), channel_id=1, source_target_pairs={{0,0},{1,8},{2,16},{3,24},{4,32},{5,40},{6,48},{7,56},{8,64},{9,72... | collective-permute-start | bytes 473096 | tf_op jit(solution)/shard_map/ppermute | solution.py:243
  118.2 36.4 %collective-permute-start.29 = (bf16[88,864]{1,0:T(8,128)(2,1)}, bf16[88,864]{1,0:T(8,128)(2,1)}, u32[]{:S(2)}, u32[]{:S(2)}) collective-permute-start(bf16[88,864]{1,0:T(8,128)(2,1)} %get-tuple-element.32), channel_id=1, source_target_pairs={{0,24},{16,0},{8,16},{24,8},{1,25},{17,1},{9,17},{25,9},{2,26},{18... | collective-permute-start | bytes 456200 | tf_op jit(solution)/shard_map/ppermute | solution.py:47
  121.4 33.5 %collective-permute-start.28 = (bf16[88,864]{1,0:T(8,128)(2,1)}, bf16[88,864]{1,0:T(8,128)(2,1)}, u32[]{:S(2)}, u32[]{:S(2)}) collective-permute-start(bf16[88,864]{1,0:T(8,128)(2,1)} %get-tuple-element.32), channel_id=1, source_target_pairs={{0,8},{16,24},{8,0},{24,16},{1,9},{17,25},{9,1},{25,17},{2,10},{18... | collective-permute-start | bytes 456200 | tf_op jit(solution)/shard_map/ppermute | solution.py:47
  122.3 36.0 %collective-permute-start.27 = (bf16[88,864]{1,0:T(8,128)(2,1)}, bf16[88,864]{1,0:T(8,128)(2,1)}, u32[]{:S(2)}, u32[]{:S(2)}) collective-permute-start(bf16[88,864]{1,0:T(8,128)(2,1)} %get-tuple-element.32), channel_id=1, source_target_pairs={{0,16},{16,8},{8,24},{24,0},{1,17},{17,9},{9,25},{25,1},{2,18},{18... | collective-permute-start | bytes 456200 | tf_op jit(solution)/shard_map/ppermute | solution.py:47
  144.8 143.2 %all-to-all-start.1 = ((bf16[64,24,768]{2,1,0:T(8,128)(2,1)}), bf16[64,24,768]{2,1,0:T(8,128)(2,1)}, u32[]{:S(2)}, u32[]{:S(2)}) async-start(bf16[64,24,768]{2,1,0:T(8,128)(2,1)} %broadcast_in_dim.186), calls=%async_computation.1 | async-start | bytes 4718592 | tf_op jit(solution)/shard_map/all_to_all | solution.py:34
  158.4 35.4 %collective-permute-start.45 = (bf16[56,1408]{1,0:T(8,128)(2,1)}, bf16[56,1408]{1,0:T(8,128)(2,1)S(1)}, u32[]{:S(2)}, u32[]{:S(2)}) collective-permute-start(bf16[56,1408]{1,0:T(8,128)(2,1)} %collective-permute-done.26), channel_id=1, source_target_pairs={{0,32},{32,64},{64,96},{96,0},{1,33},{33,65},{65,97},{97,1},{2,34}... | collective-permute-start | bytes 473096 | tf_op jit(solution)/shard_map/ppermute | solution.py:47
  189.7 99.0 %collective-permute-start.1 = (bf16[64,24,1152]{2,1,0:T(8,128)(2,1)S(1)}, bf16[64,24,1152]{2,1,0:T(8,128)(2,1)}, u32[]{:S(2)}, u32[]{:S(2)}) collective-permute-start(bf16[64,24,1152]{2,1,0:T(8,128)(2,1)S(1)} %all-to-all-done), channel_id=1, source_target_pairs={{0,1},{1,0},{2,3},{3,2},{4,5},{5,4},{6,7},{7,6},{8,9},{9,8},{10,11... | collective-permute-start | bytes 10616840 | tf_op jit(solution)/shard_map/ppermute | solution.py:42
  206.3 43.0 %collective-permute-start.44 = (bf16[4,88,864]{2,1,0:T(8,128)(2,1)S(1)}, bf16[4,88,864]{2,1,0:T(8,128)(2,1)S(1)}, u32[]{:S(2)}, u32[]{:S(2)}) collective-permute-start(bf16[4,88,864]{2,1,0:T(8,128)(2,1)S(1)} %get-tuple-element.111), channel_id=1, source_target_pairs={{0,24},{16,0},{8,16},{24,8},{1,25},{17,1},{9,17},{25,9},{2,26},{18... | collective-permute-start | bytes 1824776 | tf_op jit(solution)/shard_map/ppermute | solution.py:47
  214.6 34.7 %collective-permute-start.43 = (bf16[4,88,864]{2,1,0:T(8,128)(2,1)S(1)}, bf16[4,88,864]{2,1,0:T(8,128)(2,1)S(1)}, u32[]{:S(2)}, u32[]{:S(2)}) collective-permute-start(bf16[4,88,864]{2,1,0:T(8,128)(2,1)S(1)} %get-tuple-element.111), channel_id=1, source_target_pairs={{0,8},{16,24},{8,0},{24,16},{1,9},{17,25},{9,1},{25,17},{2,10},{18... | collective-permute-start | bytes 1824776 | tf_op jit(solution)/shard_map/ppermute | solution.py:47
  232.8 43.4 %collective-permute-start.50 = (bf16[4,56,1408]{2,1,0:T(8,128)(2,1)}, bf16[4,56,1408]{2,1,0:T(8,128)(2,1)}, u32[]{:S(2)}, u32[]{:S(2)}) collective-permute-start(bf16[4,56,1408]{2,1,0:T(8,128)(2,1)} %get-tuple-element.107), channel_id=1, source_target_pairs={{0,24},{16,0},{8,16},{24,8},{1,25},{17,1},{9,17},{25,9},{2,26},{18... | collective-permute-start | bytes 1892360 | tf_op jit(solution)/shard_map/ppermute | solution.py:47
  288.0 36.4 %collective-permute-start.11 = (bf16[64,24,768]{2,1,0:T(8,128)(2,1)}, bf16[64,24,768]{2,1,0:T(8,128)(2,1)S(1)}, u32[]{:S(2)}, u32[]{:S(2)}) collective-permute-start(bf16[64,24,768]{2,1,0:T(8,128)(2,1)} %all-to-all-done.1), channel_id=1, source_target_pairs={{0,1},{1,0},{2,3},{3,2},{4,5},{5,4},{6,7},{7,6},{8,9},{9,8},{10,11... | collective-permute-start | bytes 7077896 | tf_op jit(solution)/shard_map/ppermute | solution.py:42
  496.8 39.3 %collective-permute-start.86 = (bf16[4,88,864]{2,1,0:T(8,128)(2,1)}, bf16[4,88,864]{2,1,0:T(8,128)(2,1)}, u32[]{:S(2)}, u32[]{:S(2)}) collective-permute-start(bf16[4,88,864]{2,1,0:T(8,128)(2,1)} %get-tuple-element.75), channel_id=1, source_target_pairs={{0,32},{32,64},{64,96},{96,0},{1,33},{33,65},{65,97},{97,1},{2,34}... | collective-permute-start | bytes 1824776 | tf_op jit(solution)/shard_map/ppermute | solution.py:47
  498.1 40.7 %collective-permute-start.85 = (bf16[4,88,864]{2,1,0:T(8,128)(2,1)}, bf16[4,88,864]{2,1,0:T(8,128)(2,1)}, u32[]{:S(2)}, u32[]{:S(2)}) collective-permute-start(bf16[4,88,864]{2,1,0:T(8,128)(2,1)} %get-tuple-element.76), channel_id=1, source_target_pairs={{0,64},{32,96},{64,0},{96,32},{1,65},{33,97},{65,1},{97,33},{2,66}... | collective-permute-start | bytes 1824776 | tf_op jit(solution)/shard_map/ppermute | solution.py:47
  538.9 33.6 %collective-permute-start.71 = (bf16[160,1152]{1,0:T(8,128)(2,1)S(1)}, bf16[160,1152]{1,0:T(8,128)(2,1)S(1)}, u32[]{:S(2)}, u32[]{:S(2)}) collective-permute-start(bf16[160,1152]{1,0:T(8,128)(2,1)S(1)} %copy-done.74), channel_id=1, source_target_pairs={{0,1},{1,0},{2,3},{3,2},{4,5},{5,4},{6,7},{7,6},{8,9},{9,8},{10,11... | collective-permute-start | bytes 1105928 | tf_op jit(solution)/shard_map/ppermute | solution.py:42
  571.1 70.8 %collective-permute-start.89 = (bf16[88,864]{1,0:T(8,128)(2,1)}, bf16[88,864]{1,0:T(8,128)(2,1)}, u32[]{:S(2)}, u32[]{:S(2)}) collective-permute-start(bf16[88,864]{1,0:T(8,128)(2,1)} %get-tuple-element.104), channel_id=1, source_target_pairs={{0,16},{16,8},{8,24},{24,0},{1,17},{17,9},{9,25},{25,1},{2,18},{18... | collective-permute-start | bytes 456200 | tf_op jit(solution)/shard_map/ppermute | solution.py:47
  572.5 69.4 %collective-permute-start.88 = (bf16[88,864]{1,0:T(8,128)(2,1)}, bf16[88,864]{1,0:T(8,128)(2,1)}, u32[]{:S(2)}, u32[]{:S(2)}) collective-permute-start(bf16[88,864]{1,0:T(8,128)(2,1)} %get-tuple-element.105), channel_id=1, source_target_pairs={{0,8},{16,24},{8,0},{24,16},{1,9},{17,25},{9,1},{25,17},{2,10},{18... | collective-permute-start | bytes 456200 | tf_op jit(solution)/shard_map/ppermute | solution.py:47
  575.0 52.4 %collective-permute-start.95 = (bf16[88,864]{1,0:T(8,128)(2,1)}, bf16[88,864]{1,0:T(8,128)(2,1)}, u32[]{:S(2)}, u32[]{:S(2)}) collective-permute-start(bf16[88,864]{1,0:T(8,128)(2,1)} %get-tuple-element.101), channel_id=1, source_target_pairs={{0,32},{32,64},{64,96},{96,0},{1,33},{33,65},{65,97},{97,1},{2,34}... | collective-permute-start | bytes 456200 | tf_op jit(solution)/shard_map/ppermute | solution.py:47
  577.7 53.5 %collective-permute-start.94 = (bf16[88,864]{1,0:T(8,128)(2,1)}, bf16[88,864]{1,0:T(8,128)(2,1)}, u32[]{:S(2)}, u32[]{:S(2)}) collective-permute-start(bf16[88,864]{1,0:T(8,128)(2,1)} %get-tuple-element.102), channel_id=1, source_target_pairs={{0,64},{32,96},{64,0},{96,32},{1,65},{33,97},{65,1},{97,33},{2,66}... | collective-permute-start | bytes 456200 | tf_op jit(solution)/shard_map/ppermute | solution.py:47
  579.4 56.9 %collective-permute-start.93 = (bf16[88,864]{1,0:T(8,128)(2,1)}, bf16[88,864]{1,0:T(8,128)(2,1)}, u32[]{:S(2)}, u32[]{:S(2)}) collective-permute-start(bf16[88,864]{1,0:T(8,128)(2,1)} %get-tuple-element.100), channel_id=1, source_target_pairs={{0,96},{32,0},{64,32},{96,64},{1,97},{33,1},{65,33},{97,65},{2,98}... | collective-permute-start | bytes 456200 | tf_op jit(solution)/shard_map/ppermute | solution.py:47
  631.2 47.0 %collective-permute-start.109 = (bf16[56,1152]{1,0:T(8,128)(2,1)}, bf16[56,1152]{1,0:T(8,128)(2,1)}, u32[]{:S(2)}, u32[]{:S(2)}) collective-permute-start(bf16[56,1152]{1,0:T(8,128)(2,1)} %fusion.347), channel_id=1, source_target_pairs={{0,0},{8,1},{16,2},{24,3},{32,4},{40,5},{48,6},{56,7},{64,8},{72,9... | collective-permute-start | bytes 387080 | tf_op jit(solution)/shard_map/ppermute | solution.py:412
  636.4 54.8 %collective-permute-start.72 = (bf16[1280,512]{1,0:T(8,128)(2,1)}, bf16[1280,512]{1,0:T(8,128)(2,1)}, u32[]{:S(2)}, u32[]{:S(2)}) collective-permute-start(bf16[1280,512]{1,0:T(8,128)(2,1)} %fusion.66), channel_id=1, source_target_pairs={{0,1},{1,0},{2,3},{3,2},{4,5},{5,4},{6,7},{7,6},{8,9},{9,8},{10,11... | collective-permute-start | bytes 3932168 | tf_op jit(solution)/shard_map/ppermute | solution.py:42
  707.6 41.4 %collective-permute-start.82 = (bf16[1536,640]{1,0:T(8,128)(2,1)}, bf16[1536,640]{1,0:T(8,128)(2,1)}, u32[]{:S(2)}, u32[]{:S(2)}) collective-permute-start(bf16[1536,640]{1,0:T(8,128)(2,1)} %add_convert_fusion.1), channel_id=1, source_target_pairs={{0,1},{1,0},{2,3},{3,2},{4,5},{5,4},{6,7},{7,6},{8,9},{9,8},{10,11... | collective-permute-start | bytes 5898248 | tf_op jit(solution)/shard_map/ppermute | solution.py:42
  746.8 39.6 %collective-permute-start.80 = (bf16[1536,768]{0,1:T(8,128)(2,1)}, bf16[1536,768]{0,1:T(8,128)(2,1)}, u32[]{:S(2)}, u32[]{:S(2)}) collective-permute-start(bf16[1536,768]{0,1:T(8,128)(2,1)} %pad_maximum_fusion.4), channel_id=1, source_target_pairs={{0,1},{1,0},{2,3},{3,2},{4,5},{5,4},{6,7},{7,6},{8,9},{9,8},{10,11... | collective-permute-start | bytes 7077896 | tf_op jit(solution)/shard_map/ppermute | solution.py:42
  753.0 41.5 %all-to-all-start.3 = ((bf16[64,24,640]{2,1,0:T(8,128)(2,1)}), bf16[64,24,640]{2,1,0:T(8,128)(2,1)}, u32[]{:S(2)}, u32[]{:S(2)}) async-start(bf16[64,24,640]{2,1,0:T(8,128)(2,1)} %bitcast.403), calls=%async_computation.3 | async-start | bytes 3932160 | tf_op jit(solution)/shard_map/all_to_all | solution.py:34
  794.5 41.0 %all-to-all-start.2 = ((bf16[64,24,768]{2,1,0:T(8,128)(2,1)}), bf16[64,24,768]{2,1,0:T(8,128)(2,1)}, u32[]{:S(2)}, u32[]{:S(2)}) async-start(bf16[64,24,768]{2,1,0:T(8,128)(2,1)} %bitcast.402), calls=%async_computation.2 | async-start | bytes 4718592 | tf_op jit(solution)/shard_map/all_to_all | solution.py:34
  (276 other events, 3616.8 us)

commit v3 on v2

--- a/solution.py
+++ b/solution.py
@@ -69,11 +69,8 @@
     return pairs
 
 
-def gather_zx(x, first):
-    second = "z" if first == "x" else "x"
-    line = jnp.stack([x] + [shift(x, first, k) for k in (1, 2, 3)])
-    lines = [line] + [shift(line, second, k) for k in (1, 2, 3)]
-    return jnp.stack(lines, axis=0 if first == "x" else 1)
+def gather_line(x, axis):
+    return jnp.stack([x] + [shift(x, axis, k) for k in (1, 2, 3)])
 
 
 def scatter_zx(x, first):
@@ -127,8 +124,29 @@
     return total
 
 
+def after(done, *values):
+    return lax.optimization_barrier(values + (done,))
+
+
 def table(rows, columns):
     return (rows[:, None] == columns[None, :]).astype(BF)
+
+
+def swap_columns(pieces, core, at_y):
+    slab = jnp.zeros(pieces.shape, pieces.dtype)
+    for ky in range(4):
+        for kc in range(2):
+            to = 2 * ((at_y + ky) % 4) + (core + kc) % 2
+            source = 2 * ((at_y - ky) % 4) + (core - kc) % 2
+            piece = lax.dynamic_index_in_dim(pieces, to, 0, keepdims=False)
+            if ky or kc:
+                route = []
+                for y in range(4):
+                    for c in range(2):
+                        route.append((2 * y + c, 2 * ((y + ky) % 4) + (c + kc) % 2))
+                piece = lax.ppermute(piece, ("y", "c"), route)
+            slab = lax.dynamic_update_index_in_dim(slab, piece, source, 0)
+    return slab
 
 
 def on_device(
@@ -167,7 +185,6 @@
     at_x = 2 * at_xh + at_xl
     is_first = core == 0
     score_scale = WIDTH**-0.5
-    hidden = layer_input[0].astype(F32)
     count_here = jnp.sum(loss_token_mask[0]).astype(BF)
 
     extra = jnp.concatenate([gain_one[None], gain_two[None], count_here.reshape(1, 1)], axis=1)
@@ -186,8 +203,15 @@
 
     keep, send = pick(is_first, attention_half(0), attention_half(1))
     lower, upper = pick(is_first, keep, other_core(send))
-    raw_one = gather_chips(jnp.concatenate([lower, upper], axis=0))
+    att_own = jnp.concatenate([lower, upper], axis=0)
+    raw_one = gather_chips(att_own)
     raw_two = other_core(raw_one)
+    (layer_input, wg, wu, bg, bu, wd, ad, ag, au, wo, ao, bo, bd, segment, position, core, at_z, _) = after(
+        att_own,
+        layer_input, wg, wu, bg, bu, wd, ad, ag, au, wo, ao, bo, bd, segment, position, core, at_z,
+    )
+    is_first = core == 0
+    hidden = layer_input[0].astype(F32)
     marks = raw_one.reshape(128, 12, 1152)[:, 9, 768:896]
     gain_one_full = marks[:, :9].reshape(1, 1152).astype(F32)
     gain_two_full = marks[:, 9:18].reshape(1, 1152).astype(F32)
@@ -195,61 +219,33 @@
     raw = [raw_one.reshape(1536, 1152), raw_two.reshape(1536, 1152)]
 
     def output_half(k):
-        zero = jnp.zeros((2, 128), BF)
-        return jnp.concatenate(
-            [
-                jnp.concatenate([wo[:, 512 * k : 512 * k + 640], ao[:, 128 * k : 128 * k + 128]], axis=1),
-                jnp.concatenate([bo[:, 512 * k : 512 * k + 640], zero], axis=1),
-                jnp.concatenate([bd[:, 512 * k : 512 * k + 640], zero], axis=1),
-            ],
-            axis=0,
-        )
+        wide = jnp.concatenate([m[:, 512 * k : 512 * k + 640] for m in (wo, bo, bd)], axis=0)
+        narrow = jnp.pad(ao[:, 128 * k : 128 * k + 128], ((0, 4), (0, 0)))
+        return jnp.concatenate([wide, narrow, jnp.pad((ag, au)[k], ((0, 3), (0, 0)))], axis=1)
 
     keep, send = pick(is_first, output_half(0), output_half(1))
     lower, upper = pick(is_first, keep, other_core(send))
-    out_own = lax.optimization_barrier((jnp.concatenate([lower, upper], axis=0), raw_one))[0]
+    out_own, _ = after(raw_one, jnp.concatenate([lower, upper], axis=0))
     out_one = gather_chips(out_own)
     out_two = other_core(out_one)
-    raw_out = [out_one.reshape(1536, 768), out_two.reshape(1536, 768)]
-
-    rows31 = jnp.concatenate(
+    raw_out = [out_one.reshape(1536, 1024), out_two.reshape(1536, 1024)]
+
+    rows22 = jnp.concatenate([wg, wu, bg, bu], axis=0).reshape(22, 128, 54)
+    rows22 = jnp.pad(rows22, ((0, 0), (0, 0), (0, 2))).reshape(22, 8, 896).transpose(1, 0, 2)
+    slab = swap_columns(rows22, core, at_y)
+    ff_own = jnp.concatenate(
         [
-            wg,
-            wu,
-            bg,
-            bu,
+            slab[:, :9].reshape(72, 896),
+            slab[:, 9:18].reshape(72, 896),
+            slab[:, 18:20].reshape(16, 896),
+            slab[:, 20:22].reshape(16, 896),
         ],
         axis=0,
     )
-    rows31 = rows31.reshape(22, 8, 864).transpose(1, 0, 2)
-    inner_rows = jnp.concatenate([ag, au, jnp.zeros((9, 352), BF)], axis=1)
-    rows31 = jnp.concatenate([rows31, jnp.broadcast_to(inner_rows[None], (8, 9, 864))], axis=1)
-    slab = jnp.zeros((8, 31, 864), BF)
-    for ky in range(4):
-        for kc in range(2):
-            to = 2 * ((at_y + ky) % 4) + (core + kc) % 2
-            source = 2 * ((at_y - ky) % 4) + (core - kc) % 2
-            piece = lax.dynamic_index_in_dim(rows31, to, 0, keepdims=False)
-            if ky or kc:
-                route = []
-                for y in range(4):
-                    for c in range(2):
-                        route.append((2 * y + c, 2 * ((y + ky) % 4) + (c + kc) % 2))
-                piece = lax.ppermute(piece, ("y", "c"), route)
-            slab = lax.dynamic_update_index_in_dim(slab, piece, source, 0)
-    gate_own = jnp.concatenate([slab[:, :9].reshape(72, 864), slab[:, 18:20].reshape(16, 864)], axis=0)
-    up_own = jnp.concatenate([slab[:, 9:18].reshape(72, 864), slab[:, 20:22].reshape(16, 864)], axis=0)
-    inner_own = slab[:, 22:, :512].reshape(72, 512)
     down_own = lax.ppermute(
         jnp.pad(jnp.concatenate([wd, ad], axis=1), ((0, 2), (0, 0))), EVERY, down_route()
     )
-    gate_own, up_own, inner_own, down_own, _ = lax.optimization_barrier(
-        (gate_own, up_own, inner_own, down_own, raw_one)
-    )
-    gate_raw = gather_zx(gate_own, "x")
-    up_raw = gather_zx(up_own, "z")
-    inner_raw = gather_zx(inner_own, "x").reshape(1152, 512)
-    down_raw = gather_zx(down_own, "z").reshape(896, 1408)
+    down_own, _ = after(raw_one, down_own)
 
     ids = jnp.arange(1536, dtype=jnp.int32)
     dev, j = 2 * (ids // 24) + (ids % 24) // 12, ids % 12
@@ -270,13 +266,8 @@
         x = (at_x - kx) % 4
         return (((at_z - kz) % 4) * 2 + x % 2) * 2 + x // 2
 
-    put_feature = table(features, 72 * plane(features // 72) + features % 72)
-    put_b = table(halves, 16 * plane(halves // 16) + halves % 16)
-    hidden_ids = jnp.arange(864, dtype=jnp.int32)
-    down_ids = jnp.arange(896, dtype=jnp.int32)
-    put_down = table(
-        hidden_ids, jnp.where(down_ids % 56 < 54, 54 * plane(down_ids // 56) + down_ids % 56, -1)
-    )
+    hidden_ids = jnp.arange(896, dtype=jnp.int32)
+    put_down = table(hidden_ids, 56 * plane(hidden_ids // 56) + hidden_ids % 56)
 
     seq = (at_xh * 4 + at_y) * 2 + core
     tree_seg = segment[0]
@@ -309,6 +300,10 @@
     vv = pick(is_first, *[dot(sides[2], raw[i][:, 640:768]) for i in (0, 1)])
     kv_own = jnp.concatenate([turn(jnp.concatenate(kk, axis=1), cos, sin), vv[0], vv[1]], axis=1).astype(BF)
 
+    down_line = gather_line(down_own, "z")
+    ff_own, _ = after(kv_own, ff_own)
+    ff_all = exchange(jnp.broadcast_to(ff_own[None], (16, 176, 896)), ("z", "xl", "xh"))
+
     def tree_shift(x, kh, ky):
         route = []
         for h in range(2):
@@ -320,6 +315,9 @@
     kv_mine = jnp.concatenate(kv_mine, axis=0)
     kv = jnp.concatenate([kv_mine, other_core(kv_mine)], axis=0)
     keys, values = kv[:, :256], kv[:, 256:]
+    down_line, _ = after(kv, down_line)
+    down_raw = jnp.stack([down_line] + [shift(down_line, "x", k) for k in (1, 2, 3)], axis=1)
+    down_raw = down_raw.reshape(896, 1408)
     queries = [dot(sides[0], raw[i][:, :512]) for i in (0, 1)]
     q_rows = jnp.concatenate(
         [turn(queries[h // 2][:, WIDTH * (h % 2) : WIDTH * (h % 2 + 1)], cos, sin) for h in range(HEADS)],
@@ -333,29 +331,28 @@
     mix_rows = dot((ex / total).astype(BF), values).astype(BF)
     mix = jnp.concatenate([mix_rows[TOKENS * h : TOKENS * (h + 1)] for h in range(HEADS)], axis=1)
     mix_placed = dot(mix, put_mix).astype(BF)
-    inner_out = jnp.concatenate([dot(mix_placed, raw_out[i][:, 640:]) for i in (0, 1)], axis=1).astype(BF)
+    inner_out = jnp.concatenate([dot(mix_placed, raw_out[i][:, 640:768]) for i in (0, 1)], axis=1).astype(BF)
     side_out = mix_placed + dot(inner_out, put_inner_out).astype(BF)
     left, right = pick(is_first, *[dot(side_out, raw_out[i][:, :640]) for i in (0, 1)])
-    after = hidden + jnp.concatenate([left, right[:, 128:]], axis=1)
-
-    a_gate = dot(inner_raw[:, :256], put_b).astype(BF)
-    a_up = dot(inner_raw[:, 256:], put_b).astype(BF)
-    b_gate = gate_raw[:, :, 72:].reshape(256, 864)
-    b_up = up_raw[:, :, 72:].reshape(256, 864)
-    w_gate = (gate_raw[:, :, :72].reshape(1152, 864).astype(F32) + dot(a_gate, b_gate)).astype(BF)
-    w_up = (up_raw[:, :, :72].reshape(1152, 864).astype(F32) + dot(a_up, b_up)).astype(BF)
+    after_att = hidden + jnp.concatenate([left, right[:, 128:]], axis=1)
+
+    a_gate, a_up = pick(is_first, *[dot(put_rows, raw_out[i][:, 768:]).astype(BF) for i in (0, 1)])
+    b_gate = ff_all[:, 144:160].reshape(256, 896)
+    b_up = ff_all[:, 160:].reshape(256, 896)
+    w_gate = (ff_all[:, :72].reshape(1152, 896).astype(F32) + dot(a_gate, b_gate)).astype(BF)
+    w_up = (ff_all[:, 72:144].reshape(1152, 896).astype(F32) + dot(a_up, b_up)).astype(BF)
     left, right = pick(is_first, *[dot(put_inner_down, raw_out[i][:, :640]).astype(BF) for i in (0, 1)])
     b_down = jnp.concatenate([left, right[:, 128:]], axis=1)
     a_down = dot(put_down, down_raw[:, 1152:]).astype(BF)
     w_down = (dot(put_down, down_raw[:, :1152]) + dot(a_down, b_down)).astype(BF)
 
-    scale_two, n_two, u_two = norm_parts(after, gain_two_full)
-    u_all = gather_tokens(dot(u_two, put_feature).astype(BF))
+    scale_two, n_two, u_two = norm_parts(after_att, gain_two_full)
+    u_all = gather_tokens(u_two)
     gate = dot(u_all, w_gate)
     up = dot(u_all, w_up)
     act, act_pull = jax.vjp(lambda g, u: jax.nn.gelu(g, approximate=True) * u, gate, up)
     act = act.astype(BF)
-    result = after + scatter_tokens(dot(act, w_down))
+    result = after_att + scatter_tokens(dot(act, w_down))
 
     valid = loss_token_mask[0].astype(F32)[:, None]
     error = result - teacher[0].astype(F32)
@@ -366,48 +363,42 @@
     g_act = dot_tr(g_all, w_down).astype(BF)
     g_gate, g_up = act_pull(g_act.astype(F32))
     g_gate, g_up = g_gate.astype(BF), g_up.astype(BF)
-    g_u_two = select_back(scatter_tokens(dot_tr(g_gate, w_gate) + dot_tr(g_up, w_up)), put_feature)
+    g_u_part = dot_tr(g_gate, w_gate) + dot_tr(g_up, w_up)
+    g_u_two = scatter_tokens(g_u_part)
+    u_all, act, g_all, g_gate, g_up, _ = after(g_u_part, u_all, act, g_all, g_gate, g_up)
     gw_gate = dot_tl(u_all, g_gate).astype(BF)
     gw_up = dot_tl(u_all, g_up).astype(BF)
-    gw_down = dot_tl(act, g_all).astype(BF)
     gb_gate = dot_tl(a_gate, gw_gate).astype(BF)
     gb_up = dot_tl(a_up, gw_up).astype(BF)
+    ff_grads = jnp.concatenate(
+        [
+            gw_gate.reshape(16, 72, 896),
+            gw_up.reshape(16, 72, 896),
+            gb_gate.reshape(16, 16, 896),
+            gb_up.reshape(16, 16, 896),
+        ],
+        axis=1,
+    )
+    ff_sum = jnp.sum(exchange(ff_grads, ("z", "xl", "xh")).astype(F32), axis=0).astype(BF)
+    gw_down = dot_tl(act, g_all).astype(BF)
     gb_down = dot_tl(a_down, gw_down).astype(BF)
     gw_down = dot_tl(put_down, gw_down).astype(BF)
-    gate_sum = scatter_zx(
-        jnp.concatenate([gw_gate.reshape(4, 4, 72, 864), gb_gate.reshape(4, 4, 16, 864)], axis=2), "z"
+    down_sum = scatter_zx(gw_down.reshape(4, 4, 56, 1152), "x").astype(BF)
+    ga_part = jnp.concatenate(
+        [dot_tr(ff_sum[:72], b_gate), dot_tr(ff_sum[72:144], b_up), jnp.zeros((72, 384), F32)], axis=1
     ).astype(BF)
-    up_sum = scatter_zx(
-        jnp.concatenate([gw_up.reshape(4, 4, 72, 864), gb_up.reshape(4, 4, 16, 864)], axis=2), "x"
-    ).astype(BF)
-    down_sum = scatter_zx(gw_down.reshape(4, 4, 56, 1152), "x").astype(BF)
-    ga_gate = dot_tr(dot_tr(gate_sum[:72], b_gate).astype(BF), put_b)
-    ga_up = dot_tr(dot_tr(up_sum[:72], b_up).astype(BF), put_b)
-    ga_part = jnp.concatenate([ga_gate, ga_up, jnp.zeros((72, 352), F32)], axis=1).astype(BF)
     leaving = jnp.concatenate(
         [
-            gate_sum[:72].reshape(8, 9, 864),
-            up_sum[:72].reshape(8, 9, 864),
-            gate_sum[72:].reshape(8, 2, 864),
-            up_sum[72:].reshape(8, 2, 864),
-            ga_part.reshape(8, 9, 864),
+            ff_sum[:72].reshape(8, 9, 896),
+            ff_sum[72:144].reshape(8, 9, 896),
+            ff_sum[144:160].reshape(8, 2, 896),
+            ff_sum[160:].reshape(8, 2, 896),
+            ga_part.reshape(8, 9, 896),
         ],
         axis=1,
     )
-    slab = jnp.zeros((8, 31, 864), BF)
-    for ky in range(4):
-        for kc in range(2):
-            to = 2 * ((at_y + ky) % 4) + (core + kc) % 2
-            source = 2 * ((at_y - ky) % 4) + (core - kc) % 2
-            piece = lax.dynamic_index_in_dim(leaving, to, 0, keepdims=False)
-            if ky or kc:
-                route = []
-                for y in range(4):
-                    for c in range(2):
-                        route.append((2 * y + c, 2 * ((y + ky) % 4) + (c + kc) % 2))
-                piece = lax.ppermute(piece, ("y", "c"), route)
-            slab = lax.dynamic_update_index_in_dim(slab, piece, source, 0)
-    wide = slab[:, :22].transpose(1, 0, 2).reshape(22, 6912).astype(F32)
+    slab = swap_columns(leaving, core, at_y)
+    wide = slab[:, :22].transpose(1, 0, 2).reshape(22, 128, 56)[:, :, :54].reshape(22, 6912).astype(F32)
     ga = jnp.sum(slab[:, 22:, :512].astype(F32), axis=0)
     gw_down_own = lax.ppermute(down_sum, EVERY, [(b, a) for a, b in down_route()])[:54]
     ga_down_own = dot_tr(gw_down_own, b_down)
@@ -422,8 +413,8 @@
     gi_out = dot_tr(d_out.astype(BF), put_inner_out).astype(BF)
     d_out = (
         d_out
-        + dot_tr(gi_out[:, :128], raw_out[0][:, 640:])
-        + dot_tr(gi_out[:, 128:], raw_out[1][:, 640:])
+        + dot_tr(gi_out[:, :128], raw_out[0][:, 640:768])
+        + dot_tr(gi_out[:, 128:], raw_out[1][:, 640:768])
     )
     g_mix = dot_tr(d_out.astype(BF), put_mix).astype(BF)
     g_rows = jnp.concatenate([g_mix[:, WIDTH * h : WIDTH * (h + 1)] for h in range(HEADS)], axis=0)
@@ -441,6 +432,7 @@
     for k in range(1, 8):
         away = g_kv_b[TOKENS * k : TOKENS * (k + 1)]
         g_kv_own = g_kv_own + tree_shift(away, k // 4, (4 - k % 4) % 4).astype(F32)
+    g_scores, side_out, _ = after(g_kv_b, g_scores, side_out)
     g_q_rows = dot(g_scores, keys) * score_scale
     g_q = [
         jnp.concatenate(

time: 881 us -> 881 us (level)
  starting transfers between devices: 215 us -> 165 us
  waiting for transfers between devices: 177 us -> 224 us
  local copies, waits for them, and re-layouts: 166 us -> 193 us
  other arithmetic: 113 us -> 97.7 us
  matrix products: 186 us -> 177 us
    ppermute x54 -> x24, starting transfers between devices: 97.6 us -> 25.7 us  [shift(): lax.ppermute(x, RING[axis], [(number[i], number[(i + k) % 4]) for i in ra...]
    ppermute x54 -> x24, waiting for transfers between devices: 120 us -> 180 us  [shift(): lax.ppermute(x, RING[axis], [(number[i], number[(i + k) % 4]) for i in ra...]
    dynamic_update_slice x15 -> x16, local copies, waits for them, and re-layouts: 8.38 us -> 33.3 us  [swap_columns(): slab = lax.dynamic_update_index_in_dim(slab, piece, source, 0)]
    convert_element_type x7 -> x0, local copies, waits for them, and re-layouts: 24.7 us -> none  [the longest x2 7.89 us: on_device(): up_raw[:, :, :72].reshape(1152, 864).astype(F32) + dot(a_up, b_up)]
    ppermute x14, waiting for transfers between devices: 21.3 us -> 1.2 us  [swap_columns(): piece = lax.ppermute(piece, ('y', 'c'), route)]
    broadcast_in_dim x2 -> x11, local copies, waits for them, and re-layouts: 0.02 us -> 15 us  [the longest x7 10.8 us: swap_columns(): slab = lax.dynamic_update_index_in_dim(slab, piece, source, 0)]
    ppermute x14, waiting for transfers between devices: 21 us -> 33.4 us  [tree_shift(): return lax.ppermute(x, ('xh', 'y'), route)]
    all_to_all x4 -> x6, starting transfers between devices: 39.3 us -> 51.6 us  [exchange(): return lax.all_to_all(x, axes, split_axis=0, concat_axis=0, tiled=True)]
  transfers between devices with their start and end apart: 114 -> 86, of which waited for: 35 -> 19; matrix products, arithmetic and copies ran while one was open for 38% -> 43% of each run, Pallas kernels for 0% -> 0%
where the time goes in v3:
time: 881 us; the launch traced here: 865 us
  waiting for transfers between devices  224 us (25%)
  local copies, waits for them, and re-layouts  193 us (22%)
  matrix products  177 us (20%)
  starting transfers between devices  165 us (19%)
  other arithmetic  97.7 us (11%)
    ppermute x24, waiting for transfers between devices, shift(): lax.ppermute(x, RING[axis], [(number[i], number[(i + k) % 4]) for i in ra...  180 us
    dot_general x38, matrix products, dot_tr(): lax.dot_general(a, b, (((1,), (1,)), ((), ())), preferred_element_type=F32)  71.3 us
    dot_general x34, matrix products, dot(): return jnp.dot(a, b, preferred_element_type=F32)  63.1 us
    all_to_all x6, starting transfers between devices, exchange(): return lax.all_to_all(x, axes, split_axis=0, concat_axis=0, tiled=True)  51.6 us
    dot_general x19, matrix products, dot_tl(): lax.dot_general(a, b, (((0,), (0,)), ((), ())), preferred_element_type=F32)  42.6 us
    unnamed x315, local copies, waits for them, and re-layouts  39.3 us
    ppermute x26, starting transfers between devices, other_core(): return lax.ppermute(x, 'c', [(0, 1), (1, 0)])  35.6 us
    ppermute x14, waiting for transfers between devices, tree_shift(): return lax.ppermute(x, ('xh', 'y'), route)  33.4 us
  transfers between devices with their start and end apart: 86, of which 19 were waited for; matrix products, arithmetic and copies ran while one was open for 43% of the time, Pallas kernels for 0%

profile of v3, /device:TPU:1, one launch (start us, length us, event | category | flops | bytes accessed | tf_op | source)
XLA Modules:
  0.0 865.5 jit_solution(3243457801133208655)
XLA Ops:
  19.2 11.3 %all-to-all-start = ((bf16[64,24,1152]{2,1,0:T(8,128)(2,1)}), bf16[64,24,1152]{2,1,0:T(8,128)(2,1)S(1)}, u32[]{:S(2)}, u32[]{:S(2)}) async-start(bf16[64,24,1152]{2,1,0:T(8,128)(2,1)} %broadcast_in_dim.182), calls=%async_computation | async-start | bytes 7077888 | tf_op jit(solution)/shard_map/all_to_all | solution.py:34
  33.5 4.9 collective-permute-start.26
  53.6 4.3 constant_dynamic-slice_fusion.1
  113.9 12.9 %all-to-all-start.1 = ((bf16[64,24,1024]{2,1,0:T(8,128)(2,1)}), bf16[64,24,1024]{2,1,0:T(8,128)(2,1)}, u32[]{:S(2)}, u32[]{:S(2)}) async-start(bf16[64,24,1024]{2,1,0:T(8,128)(2,1)} %broadcast_in_dim.184), calls=%async_computation.1 | async-start | bytes 6291456 | tf_op jit(solution)/shard_map/all_to_all | solution.py:34
  147.5 18.0 %collective-permute-done.2 = bf16[160,512]{1,0:T(8,128)(2,1)S(1)} collective-permute-done((bf16[160,512]{1,0:T(8,128)(2,1)S(1)}, bf16[160,512]{1,0:T(8,128)(2,1)S(1)}, u32[]{:S(2)}, u32[]{:S(2)}) %collective-permute-start.2) | collective-permute-done | bytes 163872 | tf_op jit(solution)/shard_map/ppermute | solution.py:312
  189.7 5.8 collective-permute-start.9
  203.7 5.7 all-to-all-start.2
  225.3 65.8 %collective-permute-done.30 = bf16[4,56,1408]{2,1,0:T(8,128)(2,1)S(1)} collective-permute-done((bf16[4,56,1408]{2,1,0:T(8,128)(2,1)S(1)}, bf16[4,56,1408]{2,1,0:T(8,128)(2,1)S(1)}, u32[]{:S(2)}, u32[]{:S(2)}) %collective-permute-start.30) | collective-permute-done | bytes 630816 | tf_op jit(solution)/shard_map/ppermute | solution.py:47
  291.1 18.8 %collective-permute-done.31 = bf16[4,56,1408]{2,1,0:T(8,128)(2,1)S(1)} collective-permute-done((bf16[4,56,1408]{2,1,0:T(8,128)(2,1)S(1)}, bf16[4,56,1408]{2,1,0:T(8,128)(2,1)S(1)}, u32[]{:S(2)}, u32[]{:S(2)}) %collective-permute-start.31) | collective-permute-done | bytes 630816 | tf_op jit(solution)/shard_map/ppermute | solution.py:47
  334.9 6.0 collective-permute-start.16
  352.4 6.1 fusion.637
  358.5 9.9 %multiply_convert_fusion.1 = (bf16[1280,896]{1,0:T(8,128)(2,1)S(1)}, f32[1280,896]{1,0:T(8,128)}) fusion(f32[1280,896]{1,0:T(8,128)S(1)} %fusion.637, bf16[1280,1152]{1,0:T(8,128)(2,1)} %constant_dynamic-update-slice_fusion.29, bf16[1152,896]{1,0:T(8,128)(2,1)S(1)} %fusion.42), kind=kOutput, calls=%fused_computation.59 | convolution fusion | flops 2653880320 | bytes 16482304 | tf_op jit(solution)/shard_map/dot_general | solution.py:22
  384.7 8.4 collective-permute-done.34
  393.2 7.6 collective-permute-done.36
  417.3 6.9 collective-permute-done.41
  434.9 11.2 %fusion.33 = (bf16[1280,896]{1,0:T(8,128)(2,1)S(1)}, bf16[1280,896]{1,0:T(8,128)(2,1)S(1)}) fusion(f32[1280,896]{1,0:T(8,128)} %copy-done.137, f32[1280,896]{1,0:T(8,128)} %get-tuple-element.284, bf16[1280,1152]{1,0:T(8,128)(2,1)} %constant_dynamic-update-slice_fusion.37, bf16[896,1152]{1,0:T(8,128)(2,1)S(1)} %copy-done.22), kind=kOutput, calls=%fused_computation.51 | convolution fusion | flops 2672230400 | bytes 18776064 | tf_op jit(solution)/shard_map/dot_general | solution.py:30
  461.4 5.1 convolution_convert_fusion.2
  467.4 5.1 convolution_convert_fusion.1
  478.4 7.1 all-to-all-start.5
  495.5 68.7 %collective-permute-done.75 = bf16[4,56,1152]{2,1,0:T(8,128)(2,1)S(1)} collective-permute-done((bf16[4,56,1152]{2,1,0:T(8,128)(2,1)S(1)}, bf16[4,56,1152]{2,1,0:T(8,128)(2,1)S(1)}, u32[]{:S(2)}, u32[]{:S(2)}) %collective-permute-start.75) | collective-permute-done | bytes 516128 | tf_op jit(solution)/shard_map/ppermute | solution.py:47
  586.4 4.7 multiply_reduce_fusion
  593.0 5.7 multiply_convert_fusion
  607.5 4.3 collective-permute-done.79
  625.5 4.7 collective-permute-start.58
  637.7 4.4 collective-permute-start.60
  645.9 4.8 collective-permute-done.61
  669.5 8.9 %concatenate.224 = bf16[192,1536]{1,0:T(8,128)(2,1)} concatenate(bf16[160,1536]{1,0:T(8,128)(2,1)} %copy-done.49, bf16[9,1536]{1,0:T(8,128)(2,1)} %fusion.104, bf16[9,1536]{1,0:T(8,128)(2,1)} %fusion.107, bf16[1,1536]{1,0:T(2,128)(2,1)} %broadcast_select_fusion.34, bf16[1,1536]{1,0:T(2,128)(2,1)} %broadcast_select_fusion.33, bf16[1,1536]{1,0:T(2,128)(2,1)} %broadcast_select_fusion.32, ...), dimensions={0} | concatenate | bytes 1179648 | tf_op jit(solution)/shard_map/concatenate | solution.py:499
  696.0 5.7 all-to-all-start.4
  718.5 10.9 %concatenate.242 = bf16[8,31,896]{2,1,0:T(8,128)(2,1)} concatenate(bf16[8,9,896]{2,1,0:T(8,128)(2,1)} %reshape.733, bf16[8,9,896]{2,1,0:T(8,128)(2,1)} %reshape.734, bf16[8,2,896]{2,1,0:T(2,128)(2,1)} %reshape.735, bf16[8,2,896]{2,1,0:T(2,128)(2,1)} %reshape.736, bf16[8,9,896]{2,1,0:T(8,128)(2,1)} %maximum_maximum_fusion.1), dimensions={1} | concatenate | bytes 888832 | tf_op jit(solution)/shard_map/concatenate | solution.py:390
  741.6 5.0 fusion.32
  799.3 8.8 %all-to-all-start.3 = ((bf16[64,24,768]{2,1,0:T(8,128)(2,1)}), bf16[64,24,768]{2,1,0:T(8,128)(2,1)}, u32[]{:S(2)}, u32[]{:S(2)}) async-start(bf16[64,24,768]{2,1,0:T(8,128)(2,1)} %bitcast.310), calls=%async_computation.3 | async-start | bytes 4718592 | tf_op jit(solution)/shard_map/all_to_all | solution.py:34
  834.0 5.0 all-to-all-done.3
  (757 shorter events, 494.2 us)
Async XLA Ops:
  19.2 57.4 %all-to-all-start = ((bf16[64,24,1152]{2,1,0:T(8,128)(2,1)}), bf16[64,24,1152]{2,1,0:T(8,128)(2,1)S(1)}, u32[]{:S(2)}, u32[]{:S(2)}) async-start(bf16[64,24,1152]{2,1,0:T(8,128)(2,1)} %broadcast_in_dim.182), calls=%async_computation | async-start | bytes 7077888 | tf_op jit(solution)/shard_map/all_to_all | solution.py:34
  33.5 109.1 %collective-permute-start.26 = (bf16[56,1408]{1,0:T(8,128)(2,1)}, bf16[56,1408]{1,0:T(8,128)(2,1)}, u32[]{:S(2)}, u32[]{:S(2)}) collective-permute-start(bf16[56,1408]{1,0:T(8,128)(2,1)} %fusion.361), channel_id=1, source_target_pairs={{0,0},{1,8},{2,16},{3,24},{4,32},{5,40},{6,48},{7,56},{8,64},{9,72... | collective-permute-start | bytes 473096 | tf_op jit(solution)/shard_map/ppermute | solution.py:245
  42.8 45.5 %collective-permute-start.10 = (bf16[12,1024]{1,0:T(8,128)(2,1)}, bf16[12,1024]{1,0:T(8,128)(2,1)}, u32[]{:S(2)}, u32[]{:S(2)}) collective-permute-start(bf16[12,1024]{1,0:T(8,128)(2,1)} %broadcast_select_fusion.20), channel_id=1, source_target_pairs={{0,1},{1,0},{2,3},{3,2},{4,5},{5,4},{6,7},{7,6},{8,9},{9,8},{10,11... | collective-permute-start | bytes 73736 | tf_op jit(solution)/shard_map/ppermute | solution.py:42
  58.5 34.4 %collective-permute-start.19 = (bf16[22,896]{1,0:T(8,128)(2,1)}, bf16[22,896]{1,0:T(8,128)(2,1)}, u32[]{:S(2)}, u32[]{:S(2)}) collective-permute-start(bf16[22,896]{1,0:T(8,128)(2,1)} %bitcast.287), channel_id=1, source_target_pairs={{0,1},{1,0},{2,3},{3,2},{4,5},{5,4},{6,7},{7,6},{8,9},{9,8},{10,11... | collective-permute-start | bytes 118280 | tf_op jit(solution)/shard_map/ppermute | solution.py:147
  59.7 35.5 %collective-permute-start.20 = (bf16[22,896]{1,0:T(8,128)(2,1)}, bf16[22,896]{1,0:T(8,128)(2,1)}, u32[]{:S(2)}, u32[]{:S(2)}) collective-permute-start(bf16[22,896]{1,0:T(8,128)(2,1)} %bitcast.286), channel_id=1, source_target_pairs={{0,2},{1,3},{2,4},{3,5},{4,6},{5,7},{6,0},{7,1},{8,10},{9,11},{10,... | collective-permute-start | bytes 118280 | tf_op jit(solution)/shard_map/ppermute | solution.py:147
  76.6 53.4 %collective-permute-start.1 = (bf16[64,24,1152]{2,1,0:T(8,128)(2,1)S(1)}, bf16[64,24,1152]{2,1,0:T(8,128)(2,1)}, u32[]{:S(2)}, u32[]{:S(2)}) collective-permute-start(bf16[64,24,1152]{2,1,0:T(8,128)(2,1)S(1)} %all-to-all-done), channel_id=1, source_target_pairs={{0,1},{1,0},{2,3},{3,2},{4,5},{5,4},{6,7},{7,6},{8,9},{9,8},{10,11... | collective-permute-start | bytes 10616840 | tf_op jit(solution)/shard_map/ppermute | solution.py:42
  113.9 84.1 %all-to-all-start.1 = ((bf16[64,24,1024]{2,1,0:T(8,128)(2,1)}), bf16[64,24,1024]{2,1,0:T(8,128)(2,1)}, u32[]{:S(2)}, u32[]{:S(2)}) async-start(bf16[64,24,1024]{2,1,0:T(8,128)(2,1)} %broadcast_in_dim.184), calls=%async_computation.1 | async-start | bytes 6291456 | tf_op jit(solution)/shard_map/all_to_all | solution.py:34
  138.1 27.4 %collective-permute-start.2 = (bf16[160,512]{1,0:T(8,128)(2,1)S(1)}, bf16[160,512]{1,0:T(8,128)(2,1)S(1)}, u32[]{:S(2)}, u32[]{:S(2)}) collective-permute-start(bf16[160,512]{1,0:T(8,128)(2,1)S(1)} %get-tuple-element.212), channel_id=1, source_target_pairs={{0,2},{2,4},{4,6},{6,0},{8,10},{10,12},{12,14},{14,8},{1,3},{3,5},... | collective-permute-start | bytes 491528 | tf_op jit(solution)/shard_map/ppermute | solution.py:312
  139.1 30.3 %collective-permute-start.3 = (bf16[160,512]{1,0:T(8,128)(2,1)S(1)}, bf16[160,512]{1,0:T(8,128)(2,1)S(1)}, u32[]{:S(2)}, u32[]{:S(2)}) collective-permute-start(bf16[160,512]{1,0:T(8,128)(2,1)S(1)} %get-tuple-element.212), channel_id=1, source_target_pairs={{0,4},{2,6},{4,0},{6,2},{8,12},{10,14},{12,8},{14,10},{1,5},{3,7},... | collective-permute-start | bytes 491528 | tf_op jit(solution)/shard_map/ppermute | solution.py:312
  142.6 54.4 %collective-permute-start.27 = (bf16[56,1408]{1,0:T(8,128)(2,1)}, bf16[56,1408]{1,0:T(8,128)(2,1)S(1)}, u32[]{:S(2)}, u32[]{:S(2)}) collective-permute-start(bf16[56,1408]{1,0:T(8,128)(2,1)} %collective-permute-done.26), channel_id=1, source_target_pairs={{0,32},{32,64},{64,96},{96,0},{1,33},{33,65},{65,97},{97,1},{2,34}... | collective-permute-start | bytes 473096 | tf_op jit(solution)/shard_map/ppermute | solution.py:47
  143.8 53.2 %collective-permute-start.28 = (bf16[56,1408]{1,0:T(8,128)(2,1)}, bf16[56,1408]{1,0:T(8,128)(2,1)S(1)}, u32[]{:S(2)}, u32[]{:S(2)}) collective-permute-start(bf16[56,1408]{1,0:T(8,128)(2,1)} %collective-permute-done.26), channel_id=1, source_target_pairs={{0,64},{32,96},{64,0},{96,32},{1,65},{33,97},{65,1},{97,33},{2,66}... | collective-permute-start | bytes 473096 | tf_op jit(solution)/shard_map/ppermute | solution.py:47
  146.5 50.6 %collective-permute-start.29 = (bf16[56,1408]{1,0:T(8,128)(2,1)}, bf16[56,1408]{1,0:T(8,128)(2,1)S(1)}, u32[]{:S(2)}, u32[]{:S(2)}) collective-permute-start(bf16[56,1408]{1,0:T(8,128)(2,1)} %collective-permute-done.26), channel_id=1, source_target_pairs={{0,96},{32,0},{64,32},{96,64},{1,97},{33,1},{65,33},{97,65},{2,98}... | collective-permute-start | bytes 473096 | tf_op jit(solution)/shard_map/ppermute | solution.py:47
  198.1 115.5 %collective-permute-start.11 = (bf16[64,24,1024]{2,1,0:T(8,128)(2,1)}, bf16[64,24,1024]{2,1,0:T(8,128)(2,1)}, u32[]{:S(2)}, u32[]{:S(2)}) collective-permute-start(bf16[64,24,1024]{2,1,0:T(8,128)(2,1)} %all-to-all-done.1), channel_id=1, source_target_pairs={{0,1},{1,0},{2,3},{3,2},{4,5},{5,4},{6,7},{7,6},{8,9},{9,8},{10,11... | collective-permute-start | bytes 9437192 | tf_op jit(solution)/shard_map/ppermute | solution.py:42
  203.7 143.3 %all-to-all-start.2 = ((bf16[16,176,896]{2,1,0:T(8,128)(2,1)}), bf16[16,176,896]{2,1,0:T(8,128)(2,1)}, u32[]{:S(2)}, u32[]{:S(2)}) async-start(bf16[16,176,896]{2,1,0:T(8,128)(2,1)} %broadcast_in_dim.193), calls=%async_computation.2 | async-start | bytes 10092544 | tf_op jit(solution)/shard_map/all_to_all | solution.py:34
  212.1 79.0 %collective-permute-start.30 = (bf16[4,56,1408]{2,1,0:T(8,128)(2,1)S(1)}, bf16[4,56,1408]{2,1,0:T(8,128)(2,1)S(1)}, u32[]{:S(2)}, u32[]{:S(2)}) collective-permute-start(bf16[4,56,1408]{2,1,0:T(8,128)(2,1)S(1)} %pad_maximum_fusion.4), channel_id=1, source_target_pairs={{0,16},{16,8},{8,24},{24,0},{1,17},{17,9},{9,25},{25,1},{2,18},{18... | collective-permute-start | bytes 1892360 | tf_op jit(solution)/shard_map/ppermute | solution.py:47
  213.4 96.4 %collective-permute-start.31 = (bf16[4,56,1408]{2,1,0:T(8,128)(2,1)S(1)}, bf16[4,56,1408]{2,1,0:T(8,128)(2,1)S(1)}, u32[]{:S(2)}, u32[]{:S(2)}) collective-permute-start(bf16[4,56,1408]{2,1,0:T(8,128)(2,1)S(1)} %pad_maximum_fusion.4), channel_id=1, source_target_pairs={{0,8},{16,24},{8,0},{24,16},{1,9},{17,25},{9,1},{25,17},{2,10},{18... | collective-permute-start | bytes 1892360 | tf_op jit(solution)/shard_map/ppermute | solution.py:47
  215.8 94.0 %collective-permute-start.32 = (bf16[4,56,1408]{2,1,0:T(8,128)(2,1)S(1)}, bf16[4,56,1408]{2,1,0:T(8,128)(2,1)S(1)}, u32[]{:S(2)}, u32[]{:S(2)}) collective-permute-start(bf16[4,56,1408]{2,1,0:T(8,128)(2,1)S(1)} %pad_maximum_fusion.4), channel_id=1, source_target_pairs={{0,24},{16,0},{8,16},{24,8},{1,25},{17,1},{9,17},{25,9},{2,26},{18... | collective-permute-start | bytes 1892360 | tf_op jit(solution)/shard_map/ppermute | solution.py:47
  460.4 33.6 %collective-permute-start.73 = (bf16[4,56,1152]{2,1,0:T(8,128)(2,1)}, bf16[4,56,1152]{2,1,0:T(8,128)(2,1)}, u32[]{:S(2)}, u32[]{:S(2)}) collective-permute-start(bf16[4,56,1152]{2,1,0:T(8,128)(2,1)} %get-tuple-element.126), channel_id=1, source_target_pairs={{0,24},{16,0},{8,16},{24,8},{1,25},{17,1},{9,17},{25,9},{2,26},{18... | collective-permute-start | bytes 1548296 | tf_op jit(solution)/shard_map/ppermute | solution.py:47
  461.0 33.1 %collective-permute-start.74 = (bf16[4,56,1152]{2,1,0:T(8,128)(2,1)}, bf16[4,56,1152]{2,1,0:T(8,128)(2,1)}, u32[]{:S(2)}, u32[]{:S(2)}) collective-permute-start(bf16[4,56,1152]{2,1,0:T(8,128)(2,1)} %get-tuple-element.127), channel_id=1, source_target_pairs={{0,8},{16,24},{8,0},{24,16},{1,9},{17,25},{9,1},{25,17},{2,10},{18... | collective-permute-start | bytes 1548296 | tf_op jit(solution)/shard_map/ppermute | solution.py:47
  478.4 217.6 %all-to-all-start.5 = ((bf16[16,176,896]{2,1,0:T(8,128)(2,1)}), bf16[16,176,896]{2,1,0:T(8,128)(2,1)}, u32[]{:S(2)}, u32[]{:S(2)}) async-start(bf16[16,176,896]{2,1,0:T(8,128)(2,1)} %pad_maximum_fusion), calls=%async_computation.5 | async-start | bytes 10092544 | tf_op jit(solution)/shard_map/all_to_all | solution.py:34
  489.6 74.6 %collective-permute-start.75 = (bf16[4,56,1152]{2,1,0:T(8,128)(2,1)S(1)}, bf16[4,56,1152]{2,1,0:T(8,128)(2,1)S(1)}, u32[]{:S(2)}, u32[]{:S(2)}) collective-permute-start(bf16[4,56,1152]{2,1,0:T(8,128)(2,1)S(1)} %copy-done.48), channel_id=1, source_target_pairs={{0,16},{16,8},{8,24},{24,0},{1,17},{17,9},{9,25},{25,1},{2,18},{18... | collective-permute-start | bytes 1548296 | tf_op jit(solution)/shard_map/ppermute | solution.py:47
  491.0 75.8 %collective-permute-start.53 = (bf16[160,1152]{1,0:T(8,128)(2,1)S(1)}, bf16[160,1152]{1,0:T(8,128)(2,1)S(1)}, u32[]{:S(2)}, u32[]{:S(2)}) collective-permute-start(bf16[160,1152]{1,0:T(8,128)(2,1)S(1)} %copy-done.51), channel_id=1, source_target_pairs={{0,1},{1,0},{2,3},{3,2},{4,5},{5,4},{6,7},{7,6},{8,9},{9,8},{10,11... | collective-permute-start | bytes 1105928 | tf_op jit(solution)/shard_map/ppermute | solution.py:42
  493.9 75.8 %collective-permute-start.48 = (bf16[160,1152]{1,0:T(8,128)(2,1)S(1)}, bf16[160,1152]{1,0:T(8,128)(2,1)S(1)}, u32[]{:S(2)}, u32[]{:S(2)}) collective-permute-start(bf16[160,1152]{1,0:T(8,128)(2,1)S(1)} %get-tuple-element.108), channel_id=1, source_target_pairs={{0,4},{2,6},{4,0},{6,2},{1,5},{3,7},{5,1},{7,3},{8,12},{10,14},{12... | collective-permute-start | bytes 1105928 | tf_op jit(solution)/shard_map/ppermute | solution.py:47
  494.0 76.5 %collective-permute-start.50 = (bf16[160,1152]{1,0:T(8,128)(2,1)S(1)}, bf16[160,1152]{1,0:T(8,128)(2,1)S(1)}, u32[]{:S(2)}, u32[]{:S(2)}) collective-permute-start(bf16[160,1152]{1,0:T(8,128)(2,1)S(1)} %get-tuple-element.110), channel_id=1, source_target_pairs={{0,6},{2,0},{4,2},{6,4},{1,7},{3,1},{5,3},{7,5},{8,14},{10,8},{12,... | collective-permute-start | bytes 1105928 | tf_op jit(solution)/shard_map/ppermute | solution.py:47
  494.1 76.4 %collective-permute-start.52 = (bf16[160,1152]{1,0:T(8,128)(2,1)S(1)}, bf16[160,1152]{1,0:T(8,128)(2,1)S(1)}, u32[]{:S(2)}, u32[]{:S(2)}) collective-permute-start(bf16[160,1152]{1,0:T(8,128)(2,1)S(1)} %get-tuple-element.109), channel_id=1, source_target_pairs={{0,2},{2,4},{4,6},{6,0},{1,3},{3,5},{5,7},{7,1},{8,10},{10,12},{12... | collective-permute-start | bytes 1105928 | tf_op jit(solution)/shard_map/ppermute | solution.py:47
  566.6 35.7 %collective-permute-start.76 = (bf16[56,1152]{1,0:T(8,128)(2,1)}, bf16[56,1152]{1,0:T(8,128)(2,1)}, u32[]{:S(2)}, u32[]{:S(2)}) collective-permute-start(bf16[56,1152]{1,0:T(8,128)(2,1)} %get-tuple-element.149), channel_id=1, source_target_pairs={{0,96},{32,0},{64,32},{96,64},{1,97},{33,1},{65,33},{97,65},{2,98}... | collective-permute-start | bytes 387080 | tf_op jit(solution)/shard_map/ppermute | solution.py:47
  566.8 35.5 %collective-permute-start.77 = (bf16[56,1152]{1,0:T(8,128)(2,1)}, bf16[56,1152]{1,0:T(8,128)(2,1)}, u32[]{:S(2)}, u32[]{:S(2)}) collective-permute-start(bf16[56,1152]{1,0:T(8,128)(2,1)} %get-tuple-element.151), channel_id=1, source_target_pairs={{0,64},{32,96},{64,0},{96,32},{1,65},{33,97},{65,1},{97,33},{2,66}... | collective-permute-start | bytes 387080 | tf_op jit(solution)/shard_map/ppermute | solution.py:47
  569.7 32.6 %collective-permute-start.78 = (bf16[56,1152]{1,0:T(8,128)(2,1)}, bf16[56,1152]{1,0:T(8,128)(2,1)}, u32[]{:S(2)}, u32[]{:S(2)}) collective-permute-start(bf16[56,1152]{1,0:T(8,128)(2,1)} %get-tuple-element.150), channel_id=1, source_target_pairs={{0,32},{32,64},{64,96},{96,0},{1,33},{33,65},{65,97},{97,1},{2,34}... | collective-permute-start | bytes 387080 | tf_op jit(solution)/shard_map/ppermute | solution.py:47
  642.5 48.5 %collective-permute-start.64 = (bf16[1536,640]{1,0:T(8,128)(2,1)}, bf16[1536,640]{1,0:T(8,128)(2,1)}, u32[]{:S(2)}, u32[]{:S(2)}) collective-permute-start(bf16[1536,640]{1,0:T(8,128)(2,1)} %add_convert_fusion.1), channel_id=1, source_target_pairs={{0,1},{1,0},{2,3},{3,2},{4,5},{5,4},{6,7},{7,6},{8,9},{9,8},{10,11... | collective-permute-start | bytes 5898248 | tf_op jit(solution)/shard_map/ppermute | solution.py:42
  683.1 54.1 %collective-permute-start.62 = (bf16[1536,768]{0,1:T(8,128)(2,1)}, bf16[1536,768]{0,1:T(8,128)(2,1)}, u32[]{:S(2)}, u32[]{:S(2)}) collective-permute-start(bf16[1536,768]{0,1:T(8,128)(2,1)} %pad_maximum_fusion.3), channel_id=1, source_target_pairs={{0,1},{1,0},{2,3},{3,2},{4,5},{5,4},{6,7},{7,6},{8,9},{9,8},{10,11... | collective-permute-start | bytes 7077896 | tf_op jit(solution)/shard_map/ppermute | solution.py:42
  696.0 103.3 %all-to-all-start.4 = ((bf16[64,24,640]{2,1,0:T(8,128)(2,1)}), bf16[64,24,640]{2,1,0:T(8,128)(2,1)}, u32[]{:S(2)}, u32[]{:S(2)}) async-start(bf16[64,24,640]{2,1,0:T(8,128)(2,1)} %bitcast.315), calls=%async_computation.4 | async-start | bytes 3932160 | tf_op jit(solution)/shard_map/all_to_all | solution.py:34
  799.3 39.6 %all-to-all-start.3 = ((bf16[64,24,768]{2,1,0:T(8,128)(2,1)}), bf16[64,24,768]{2,1,0:T(8,128)(2,1)}, u32[]{:S(2)}, u32[]{:S(2)}) async-start(bf16[64,24,768]{2,1,0:T(8,128)(2,1)} %bitcast.310), calls=%async_computation.3 | async-start | bytes 4718592 | tf_op jit(solution)/shard_map/all_to_all | solution.py:34
  (196 other events, 2058.9 us)

commit v4 on v3

--- a/solution.py
+++ b/solution.py
@@ -71,19 +71,6 @@
 
 def gather_line(x, axis):
     return jnp.stack([x] + [shift(x, axis, k) for k in (1, 2, 3)])
-
-
-def scatter_zx(x, first):
-    second = "z" if first == "x" else "x"
-    x = [x[k] if first == "z" else x[:, k] for k in range(4)]
-    line = x[0].astype(F32)
-    for k in (1, 2, 3):
-        line = line + shift(x[k], first, 4 - k).astype(F32)
-    line = line.astype(BF)
-    out = line[0].astype(F32)
-    for k in (1, 2, 3):
-        out = out + shift(line[k], second, 4 - k).astype(F32)
-    return out
 
 
 def norm_parts(values, gain):
@@ -130,23 +117,6 @@
 
 def table(rows, columns):
     return (rows[:, None] == columns[None, :]).astype(BF)
-
-
-def swap_columns(pieces, core, at_y):
-    slab = jnp.zeros(pieces.shape, pieces.dtype)
-    for ky in range(4):
-        for kc in range(2):
-            to = 2 * ((at_y + ky) % 4) + (core + kc) % 2
-            source = 2 * ((at_y - ky) % 4) + (core - kc) % 2
-            piece = lax.dynamic_index_in_dim(pieces, to, 0, keepdims=False)
-            if ky or kc:
-                route = []
-                for y in range(4):
-                    for c in range(2):
-                        route.append((2 * y + c, 2 * ((y + ky) % 4) + (c + kc) % 2))
-                piece = lax.ppermute(piece, ("y", "c"), route)
-            slab = lax.dynamic_update_index_in_dim(slab, piece, source, 0)
-    return slab
 
 
 def on_device(
@@ -225,27 +195,31 @@
 
     keep, send = pick(is_first, output_half(0), output_half(1))
     lower, upper = pick(is_first, keep, other_core(send))
-    out_own, _ = after(raw_one, jnp.concatenate([lower, upper], axis=0))
-    out_one = gather_chips(out_own)
-    out_two = other_core(out_one)
-    raw_out = [out_one.reshape(1536, 1024), out_two.reshape(1536, 1024)]
-
-    rows22 = jnp.concatenate([wg, wu, bg, bu], axis=0).reshape(22, 128, 54)
-    rows22 = jnp.pad(rows22, ((0, 0), (0, 0), (0, 2))).reshape(22, 8, 896).transpose(1, 0, 2)
-    slab = swap_columns(rows22, core, at_y)
-    ff_own = jnp.concatenate(
-        [
-            slab[:, :9].reshape(72, 896),
-            slab[:, 9:18].reshape(72, 896),
-            slab[:, 18:20].reshape(16, 896),
-            slab[:, 20:22].reshape(16, 896),
-        ],
-        axis=0,
-    )
+    out_own = jnp.concatenate([lower, upper], axis=0)
+
+    rows22 = jnp.pad(jnp.concatenate([wg, wu, bg, bu], axis=0), ((0, 2), (0, 0)))
+    rows22 = jnp.concatenate([rows22[:, 864 * t : 864 * (t + 1)] for t in range(8)], axis=0)
+    wider = jnp.arange(896, dtype=jnp.int32)
+    wider = table(jnp.arange(864, dtype=jnp.int32), jnp.where(wider % 56 < 54, wider // 56 * 54 + wider % 56, -1))
+    slab = exchange(dot(rows22, wider).astype(BF).reshape(8, 24, 896), ("y", "c"))
+    row = jnp.arange(176, dtype=jnp.int32)
+    low = row - 144
+    at_row = jnp.where(
+        row < 72,
+        row // 9 * 24 + row % 9,
+        jnp.where(
+            row < 144,
+            (row - 72) // 9 * 24 + 9 + (row - 72) % 9,
+            low % 16 // 2 * 24 + 18 + low // 16 * 2 + low % 2,
+        ),
+    )
+    ff_own = dot(table(at_row, jnp.arange(192, dtype=jnp.int32)), slab.reshape(192, 896)).astype(BF)
     down_own = lax.ppermute(
         jnp.pad(jnp.concatenate([wd, ad], axis=1), ((0, 2), (0, 0))), EVERY, down_route()
     )
-    down_own, _ = after(raw_one, down_own)
+    down_line = gather_line(down_own, "z")
+    down_line, _ = after(raw_one, down_line)
+    down_lines = [down_line] + [shift(down_line, "x", k) for k in (1, 2, 3)]
 
     ids = jnp.arange(1536, dtype=jnp.int32)
     dev, j = 2 * (ids // 24) + (ids % 24) // 12, ids % 12
@@ -262,7 +236,7 @@
     put_inner_down = table(halves, jnp.where(j >= 10, 2 * dev + j - 10, -1))
 
     def plane(block):
-        kz, kx = block // 4, block % 4
+        kx, kz = block // 4, block % 4
         x = (at_x - kx) % 4
         return (((at_z - kz) % 4) * 2 + x % 2) * 2 + x // 2
 
@@ -300,10 +274,6 @@
     vv = pick(is_first, *[dot(sides[2], raw[i][:, 640:768]) for i in (0, 1)])
     kv_own = jnp.concatenate([turn(jnp.concatenate(kk, axis=1), cos, sin), vv[0], vv[1]], axis=1).astype(BF)
 
-    down_line = gather_line(down_own, "z")
-    ff_own, _ = after(kv_own, ff_own)
-    ff_all = exchange(jnp.broadcast_to(ff_own[None], (16, 176, 896)), ("z", "xl", "xh"))
-
     def tree_shift(x, kh, ky):
         route = []
         for h in range(2):
@@ -311,13 +281,16 @@
                 route.append((4 * h + y, 4 * ((h + kh) % 2) + (y + ky) % 4))
         return lax.ppermute(x, ("xh", "y"), route)
 
+    out_own, _ = after(kv_own, out_own)
+    out_one = gather_chips(out_own)
+    out_two = other_core(out_one)
+    raw_out = [out_one.reshape(1536, 1024), out_two.reshape(1536, 1024)]
     kv_mine = [kv_own] + [tree_shift(kv_own, k // 4, k % 4) for k in range(1, 8)]
     kv_mine = jnp.concatenate(kv_mine, axis=0)
     kv = jnp.concatenate([kv_mine, other_core(kv_mine)], axis=0)
     keys, values = kv[:, :256], kv[:, 256:]
-    down_line, _ = after(kv, down_line)
-    down_raw = jnp.stack([down_line] + [shift(down_line, "x", k) for k in (1, 2, 3)], axis=1)
-    down_raw = down_raw.reshape(896, 1408)
+    ff_own, _ = after(kv, ff_own)
+    ff_all = exchange(jnp.broadcast_to(ff_own[None], (16, 176, 896)), ("z", "xl", "xh"))
     queries = [dot(sides[0], raw[i][:, :512]) for i in (0, 1)]
     q_rows = jnp.concatenate(
         [turn(queries[h // 2][:, WIDTH * (h % 2) : WIDTH * (h % 2 + 1)], cos, sin) for h in range(HEADS)],
@@ -336,6 +309,11 @@
     left, right = pick(is_first, *[dot(side_out, raw_out[i][:, :640]) for i in (0, 1)])
     after_att = hidden + jnp.concatenate([left, right[:, 128:]], axis=1)
 
+    scale_two, n_two, u_two = norm_parts(after_att, gain_two_full)
+    u_all = gather_tokens(u_two)
+
+    ff_all, down_lines, _ = after(u_two, ff_all, down_lines)
+    down_raw = jnp.concatenate(down_lines, axis=0).reshape(896, 1408)
     a_gate, a_up = pick(is_first, *[dot(put_rows, raw_out[i][:, 768:]).astype(BF) for i in (0, 1)])
     b_gate = ff_all[:, 144:160].reshape(256, 896)
     b_up = ff_all[:, 160:].reshape(256, 896)
@@ -346,8 +324,6 @@
     a_down = dot(put_down, down_raw[:, 1152:]).astype(BF)
     w_down = (dot(put_down, down_raw[:, :1152]) + dot(a_down, b_down)).astype(BF)
 
-    scale_two, n_two, u_two = norm_parts(after_att, gain_two_full)
-    u_all = gather_tokens(u_two)
     gate = dot(u_all, w_gate)
     up = dot(u_all, w_up)
     act, act_pull = jax.vjp(lambda g, u: jax.nn.gelu(g, approximate=True) * u, gate, up)
@@ -379,29 +355,12 @@
         ],
         axis=1,
     )
-    ff_sum = jnp.sum(exchange(ff_grads, ("z", "xl", "xh")).astype(F32), axis=0).astype(BF)
+    ff_parts = exchange(ff_grads, ("z", "xl", "xh"))
     gw_down = dot_tl(act, g_all).astype(BF)
     gb_down = dot_tl(a_down, gw_down).astype(BF)
     gw_down = dot_tl(put_down, gw_down).astype(BF)
-    down_sum = scatter_zx(gw_down.reshape(4, 4, 56, 1152), "x").astype(BF)
-    ga_part = jnp.concatenate(
-        [dot_tr(ff_sum[:72], b_gate), dot_tr(ff_sum[72:144], b_up), jnp.zeros((72, 384), F32)], axis=1
-    ).astype(BF)
-    leaving = jnp.concatenate(
-        [
-            ff_sum[:72].reshape(8, 9, 896),
-            ff_sum[72:144].reshape(8, 9, 896),
-            ff_sum[144:160].reshape(8, 2, 896),
-            ff_sum[160:].reshape(8, 2, 896),
-            ga_part.reshape(8, 9, 896),
-        ],
-        axis=1,
-    )
-    slab = swap_columns(leaving, core, at_y)
-    wide = slab[:, :22].transpose(1, 0, 2).reshape(22, 128, 56)[:, :, :54].reshape(22, 6912).astype(F32)
-    ga = jnp.sum(slab[:, 22:, :512].astype(F32), axis=0)
-    gw_down_own = lax.ppermute(down_sum, EVERY, [(b, a) for a, b in down_route()])[:54]
-    ga_down_own = dot_tr(gw_down_own, b_down)
+    down_pieces = gw_down.reshape(4, 4, 56, 1152)
+    down_first = [down_pieces[0]] + [shift(down_pieces[k], "x", 4 - k) for k in (1, 2, 3)]
 
     norm_two_back, g_gain_two = norm_back(scale_two, n_two, gain_two_full, g_u_two)
     g_after = grad_result + norm_two_back
@@ -432,7 +391,9 @@
     for k in range(1, 8):
         away = g_kv_b[TOKENS * k : TOKENS * (k + 1)]
         g_kv_own = g_kv_own + tree_shift(away, k // 4, (4 - k % 4) % 4).astype(F32)
-    g_scores, side_out, _ = after(g_kv_b, g_scores, side_out)
+    g_scores, side_out, ff_parts, down_first, gb_down, _ = after(
+        g_kv_b, g_scores, side_out, ff_parts, down_first, gb_down
+    )
     g_q_rows = dot(g_scores, keys) * score_scale
     g_q = [
         jnp.concatenate(
@@ -441,6 +402,31 @@
         ).astype(BF)
         for i in (0, 1)
     ]
+    down_line = sum(m.astype(F32) for m in down_first).astype(BF)
+    down_second = [down_line[0]] + [shift(down_line[k], "z", 4 - k) for k in (1, 2, 3)]
+    ff_sum = jnp.sum(ff_parts.astype(F32), axis=0).astype(BF)
+    ga_part = jnp.concatenate(
+        [dot_tr(ff_sum[:72], b_gate), dot_tr(ff_sum[72:144], b_up), jnp.zeros((72, 384), F32)], axis=1
+    ).astype(BF)
+    back_row = jnp.arange(256, dtype=jnp.int32)
+    group, line = back_row // 32, back_row % 32
+    take = jnp.where(
+        line < 9,
+        9 * group + line,
+        jnp.where(
+            line < 18,
+            72 + 9 * group + line - 9,
+            jnp.where(
+                line < 22,
+                144 + 16 * ((line - 18) // 2) + 2 * group + line % 2,
+                jnp.where(line < 31, 176 + 9 * group + line - 22, -1),
+            ),
+        ),
+    )
+    leaving = dot(
+        table(take, jnp.arange(248, dtype=jnp.int32)), jnp.concatenate([ff_sum, ga_part], axis=0)
+    ).astype(BF)
+    slab = exchange(leaving.reshape(8, 32, 896), ("y", "c"))
     g_k = turn_back(g_kv_own[:, :256], cos, sin).astype(BF)
     g_v = g_kv_own[:, 256:].astype(BF)
     g_k = pick(is_first, g_k[:, :128], g_k[:, 128:])
@@ -457,27 +443,18 @@
     norm_one_back, g_gain_one = norm_back(scale_one, n_one, gain_one_full, g_u_one)
     grad_hidden = (g_after + norm_one_back).astype(BF)
 
-    def to_owners(own, away):
-        summed = (own + other_core(away.astype(BF)).astype(F32)).astype(BF)
-        return jnp.sum(exchange(summed.reshape(64, 24, -1), CHIPS).astype(F32), axis=0)
+    def of_chip(own, away):
+        return (own.astype(F32) + other_core(away.astype(BF)).astype(F32)).astype(BF).reshape(64, 24, -1)
 
     def both_halves(owned):
         mine, away = pick(is_first, owned[:12], owned[12:])
         return pick(is_first, mine, other_core(away.astype(BF)).astype(F32))
 
     left, right = pick(is_first, gb_down[:, :640], gb_down[:, 512:])
-    owned_out = to_owners(
+    chip_out = of_chip(
         dot_tl(side_out, g_half[0]) + dot_tl(put_inner_down, left),
         dot_tl(side_out, g_half[1]) + dot_tl(put_inner_down, right),
     )
-    left, right = both_halves(owned_out)
-    own_out = jnp.concatenate([left, right[:, 128:]], axis=1)
-    d = dot_tr(own_out[:8, :640].astype(BF), pick(is_first, *raw_out)[0][:, :640]) + dot_tr(
-        own_out[:8, 640:].astype(BF), pick(is_first, *raw_out)[1][:, 128:640]
-    )
-    ga_out_own = dot_tr(d.astype(BF), put_inner_out)
-    ga_out_own = jnp.concatenate(pick(is_first, ga_out_own[:, :128], ga_out_own[:, 128:]), axis=1)
-
     nines = jnp.arange(9, dtype=jnp.int32)[:, None] == features[None, :] % 9
     loss_high, loss_rest = split_in_two(loss_here)
     loss_mid, loss_low = split_in_two(loss_here - loss_high.astype(F32))
@@ -500,15 +477,33 @@
     sums = [
         jnp.concatenate(
             [
-                dot_tl(side_q, jnp.concatenate([g_q[i], more_grad], axis=0)),
-                dot_tl(sides[1], g_k[i]),
-                dot_tl(sides[2], g_v[i]),
+                dot_tl(side_q, jnp.concatenate([g_q[i], more_grad], axis=0)).astype(BF),
+                dot_tl(sides[1], g_k[i]).astype(BF),
+                dot_tl(sides[2], g_v[i]).astype(BF),
             ],
             axis=1,
         )
         for i in (0, 1)
     ]
-    owned = to_owners(sums[0], sums[1])
+    chip_sums = jnp.concatenate([of_chip(sums[0], sums[1]), chip_out], axis=2)
+    parts = exchange(chip_sums, CHIPS)
+    slab, down_second, _ = after(chip_sums, slab, down_second)
+
+    narrow = dot_tr(slab.reshape(256, 896), wider).reshape(8, 32, 864)
+    wide = jnp.concatenate([narrow[t] for t in range(8)], axis=1)
+    ga = jnp.sum(slab[:, 22:31, :512].astype(F32), axis=0)
+    down_sum = sum(m.astype(F32) for m in down_second).astype(BF)
+    gw_down_own = lax.ppermute(down_sum, EVERY, [(b, a) for a, b in down_route()])[:54]
+    ga_down_own = dot_tr(gw_down_own, b_down)
+    all_owned = jnp.sum(parts.astype(F32), axis=0)
+    owned, owned_out = all_owned[:, :768], all_owned[:, 768:]
+    left, right = both_halves(owned_out)
+    own_out = jnp.concatenate([left, right[:, 128:]], axis=1)
+    d = dot_tr(own_out[:8, :640].astype(BF), pick(is_first, *raw_out)[0][:, :640]) + dot_tr(
+        own_out[:8, 640:].astype(BF), pick(is_first, *raw_out)[1][:, 128:640]
+    )
+    ga_out_own = dot_tr(d.astype(BF), put_inner_out)
+    ga_out_own = jnp.concatenate(pick(is_first, ga_out_own[:, :128], ga_out_own[:, 128:]), axis=1)
     loss_value = jnp.sum(owned[11, 18:24]) / (1152.0 * valid_count)
     left, right = both_halves(owned)
     gains = left[11]
@@ -551,7 +546,7 @@
         ga[:, :256],
         wide[18:20],
         ga[:, 256:],
-        wide[20:],
+        wide[20:22],
         ga_down_own,
         own_out[10:],
     )

time: 881 us -> 755 us (0.86)
  the two profiles are of different devices: /device:TPU:1 before, /device:TPU:13 now
where the time goes in v4:
time: 755 us; the launch traced here: 741 us
  waiting for transfers between devices  191 us (25%)
  matrix products  160 us (21%)
  starting transfers between devices  151 us (20%)
  local copies, waits for them, and re-layouts  123 us (16%)
  other arithmetic  107 us (14%)
  between operations  8.77 us (1%)
    dot_general x39, matrix products, dot_tr(): lax.dot_general(a, b, (((1,), (1,)), ((), ())), preferred_element_type=F32)  74.5 us
    all_to_all x7, waiting for transfers between devices, exchange(): return lax.all_to_all(x, axes, split_axis=0, concat_axis=0, tiled=True)  70.8 us
    all_to_all x7, starting transfers between devices, exchange(): return lax.all_to_all(x, axes, split_axis=0, concat_axis=0, tiled=True)  58.2 us
    ppermute x14, waiting for transfers between devices, tree_shift(): return lax.ppermute(x, ('xh', 'y'), route)  54.5 us
    dot_general x37, matrix products, dot(): return jnp.dot(a, b, preferred_element_type=F32)  54 us
    unnamed x327, local copies, waits for them, and re-layouts  39.4 us
    ppermute x24, starting transfers between devices, shift(): lax.ppermute(x, RING[axis], [(number[i], number[(i + k) % 4]) for i in ra...  38.4 us
    ppermute x24, waiting for transfers between devices, shift(): lax.ppermute(x, RING[axis], [(number[i], number[(i + k) % 4]) for i in ra...  38.3 us
  transfers between devices with their start and end apart: 73, of which 21 were waited for; matrix products, arithmetic and copies ran while one was open for 39% of the time, Pallas kernels for 0%

profile of v4, /device:TPU:13, one launch (start us, length us, event | category | flops | bytes accessed | tf_op | source)
XLA Modules:
  0.0 741.0 jit_solution(16290572777951037235)
XLA Ops:
  20.7 10.9 %all-to-all-start = ((bf16[64,24,1152]{2,1,0:T(8,128)(2,1)}), bf16[64,24,1152]{2,1,0:T(8,128)(2,1)S(1)}, u32[]{:S(2)}, u32[]{:S(2)}) async-start(bf16[64,24,1152]{2,1,0:T(8,128)(2,1)} %broadcast_in_dim.74), calls=%async_computation | async-start | bytes 7077888 | tf_op jit(solution)/shard_map/all_to_all | solution.py:34
  49.8 24.2 %all-to-all-done = bf16[64,24,1152]{2,1,0:T(8,128)(2,1)S(1)} async-done(((bf16[64,24,1152]{2,1,0:T(8,128)(2,1)}), bf16[64,24,1152]{2,1,0:T(8,128)(2,1)S(1)}, u32[]{:S(2)}, u32[]{:S(2)}) %all-to-all-start) | async-done | bytes 3538976 | tf_op jit(solution)/shard_map/all_to_all | solution.py:34
  81.2 6.9 all-to-all-start.2
  122.0 9.4 %all-to-all-start.1 = ((bf16[64,24,1024]{2,1,0:T(8,128)(2,1)}), bf16[64,24,1024]{2,1,0:T(8,128)(2,1)S(1)}, u32[]{:S(2)}, u32[]{:S(2)}) async-start(bf16[64,24,1024]{2,1,0:T(8,128)(2,1)} %broadcast_in_dim.76), calls=%async_computation.1 | async-start | bytes 6291456 | tf_op jit(solution)/shard_map/all_to_all | solution.py:34
  132.7 6.9 collective-permute-start.19
  139.7 4.0 collective-permute-start.6
  149.1 21.4 %collective-permute-done.4 = bf16[160,512]{1,0:T(8,128)(2,1)S(1)} collective-permute-done((bf16[160,512]{1,0:T(8,128)(2,1)S(1)}, bf16[160,512]{1,0:T(8,128)(2,1)S(1)}, u32[]{:S(2)}, u32[]{:S(2)}) %collective-permute-start.4) | collective-permute-done | bytes 163872 | tf_op jit(solution)/shard_map/ppermute | solution.py:282
  179.0 6.7 collective-permute-done.8
  193.0 4.9 collective-permute-start.21
  221.3 7.2 all-to-all-start.3
  247.0 4.9 collective-permute-start.13
  254.9 46.6 %all-to-all-done.3 = bf16[16,176,896]{2,1,0:T(8,128)(2,1)} async-done(((bf16[16,176,896]{2,1,0:T(8,128)(2,1)}), bf16[16,176,896]{2,1,0:T(8,128)(2,1)}, u32[]{:S(2)}, u32[]{:S(2)}) %all-to-all-start.3) | async-done | bytes 5046304 | tf_op jit(solution)/shard_map/all_to_all | solution.py:34
  327.2 5.5 multiply_convert_fusion.1
  350.0 6.1 collective-permute-done.31
  357.2 8.8 %collective-permute-done.27 = bf16[160,1152]{1,0:T(8,128)(2,1)S(1)} collective-permute-done((bf16[160,1152]{1,0:T(8,128)(2,1)S(1)}, bf16[160,1152]{1,0:T(8,128)(2,1)S(1)}, u32[]{:S(2)}, u32[]{:S(2)}) %collective-permute-start.27) | collective-permute-done | bytes 368672 | tf_op jit(solution)/shard_map/ppermute | solution.py:47
  397.4 11.0 %fusion.32 = (bf16[1280,896]{1,0:T(8,128)(2,1)S(1)}, bf16[1280,896]{1,0:T(8,128)(2,1)S(1)}) fusion(f32[1280,896]{1,0:T(8,128)} %copy-done.143, f32[1280,896]{1,0:T(8,128)} %get-tuple-element.352, bf16[1280,1152]{1,0:T(8,128)(2,1)} %constant_dynamic-update-slice_fusion.45, bf16[896,1152]{1,0:T(8,128)(2,1)S(1)} %copy-done.34), kind=kOutput, calls=%fused_computation.50 | convolution fusion | flops 2672230400 | bytes 18776064 | tf_op jit(solution)/shard_map/dot_general | solution.py:30
  436.2 9.2 %all-to-all-start.4 = ((bf16[16,176,896]{2,1,0:T(8,128)(2,1)}), bf16[16,176,896]{2,1,0:T(8,128)(2,1)}, u32[]{:S(2)}, u32[]{:S(2)}) async-start(bf16[16,176,896]{2,1,0:T(8,128)(2,1)} %pad_maximum_fusion), calls=%async_computation.4 | async-start | bytes 10092544 | tf_op jit(solution)/shard_map/all_to_all | solution.py:34
  446.1 4.0 collective-permute-done.41
  463.4 4.7 multiply_reduce_fusion
  470.0 5.7 multiply_convert_fusion
  494.9 4.4 collective-permute-start.55
  499.4 14.5 %collective-permute-done.57 = bf16[160,512]{1,0:T(8,128)(2,1)S(1)} collective-permute-done((bf16[160,512]{1,0:T(8,128)(2,1)S(1)}, bf16[160,512]{1,0:T(8,128)(2,1)S(1)}, u32[]{:S(2)}, u32[]{:S(2)}) %collective-permute-start.57) | collective-permute-done | bytes 163872 | tf_op jit(solution)/shard_map/ppermute | solution.py:282
  542.5 9.0 %collective-permute-done.49 = bf16[4,56,1152]{2,1,0:T(8,128)(2,1)} collective-permute-done((bf16[4,56,1152]{2,1,0:T(8,128)(2,1)S(1)}, bf16[4,56,1152]{2,1,0:T(8,128)(2,1)}, u32[]{:S(2)}, u32[]{:S(2)}) %collective-permute-start.49) | collective-permute-done | bytes 516128 | tf_op jit(solution)/shard_map/ppermute | solution.py:47
  551.5 4.0 reduce_sum.171
  580.0 8.9 %concatenate.233 = bf16[192,1536]{1,0:T(8,128)(2,1)} concatenate(bf16[160,1536]{1,0:T(8,128)(2,1)} %copy-done.52, bf16[9,1536]{1,0:T(8,128)(2,1)} %fusion.105, bf16[9,1536]{1,0:T(8,128)(2,1)} %fusion.108, bf16[1,1536]{1,0:T(2,128)(2,1)} %broadcast_select_fusion.34, bf16[1,1536]{1,0:T(2,128)(2,1)} %broadcast_select_fusion.33, bf16[1,1536]{1,0:T(2,128)(2,1)} %broadcast_select_fusion.32, ...), dimensions={0} | concatenate | bytes 1179648 | tf_op jit(solution)/shard_map/concatenate | solution.py:476
  595.2 5.3 all-to-all-start.6
  611.5 3.8 add_convert_fusion.1
  619.0 4.3 copy.81
  623.2 4.6 pad_maximum_fusion.1
  627.9 9.2 %all-to-all-start.5 = ((bf16[64,24,1408]{2,1,0:T(8,128)(2,1)}), bf16[64,24,1408]{2,1,0:T(8,128)(2,1)}, u32[]{:S(2)}, u32[]{:S(2)}) async-start(bf16[64,24,1408]{2,1,0:T(8,128)(2,1)} %pad_maximum_fusion.1), calls=%async_computation.5 | async-start | bytes 8650752 | tf_op jit(solution)/shard_map/all_to_all | solution.py:34
  668.8 26.9 %collective-permute-done.65 = bf16[56,1152]{1,0:T(8,128)(2,1)} collective-permute-done((bf16[56,1152]{1,0:T(8,128)(2,1)}, bf16[56,1152]{1,0:T(8,128)(2,1)}, u32[]{:S(2)}, u32[]{:S(2)}) %collective-permute-start.65) | collective-permute-done | bytes 129056 | tf_op jit(solution)/shard_map/ppermute | solution.py:496
  711.0 3.7 fusion.85
  (709 shorter events, 424.9 us)
Async XLA Ops:
  20.7 53.3 %all-to-all-start = ((bf16[64,24,1152]{2,1,0:T(8,128)(2,1)}), bf16[64,24,1152]{2,1,0:T(8,128)(2,1)S(1)}, u32[]{:S(2)}, u32[]{:S(2)}) async-start(bf16[64,24,1152]{2,1,0:T(8,128)(2,1)} %broadcast_in_dim.74), calls=%async_computation | async-start | bytes 7077888 | tf_op jit(solution)/shard_map/all_to_all | solution.py:34
  43.8 52.2 %collective-permute-start.10 = (bf16[12,1024]{1,0:T(8,128)(2,1)}, bf16[12,1024]{1,0:T(8,128)(2,1)}, u32[]{:S(2)}, u32[]{:S(2)}) collective-permute-start(bf16[12,1024]{1,0:T(8,128)(2,1)} %broadcast_select_fusion.20), channel_id=1, source_target_pairs={{0,1},{1,0},{2,3},{3,2},{4,5},{5,4},{6,7},{7,6},{8,9},{9,8},{10,11... | collective-permute-start | bytes 73736 | tf_op jit(solution)/shard_map/ppermute | solution.py:42
  74.0 33.8 %collective-permute-start.1 = (bf16[64,24,1152]{2,1,0:T(8,128)(2,1)S(1)}, bf16[64,24,1152]{2,1,0:T(8,128)(2,1)}, u32[]{:S(2)}, u32[]{:S(2)}) collective-permute-start(bf16[64,24,1152]{2,1,0:T(8,128)(2,1)S(1)} %all-to-all-done), channel_id=1, source_target_pairs={{0,1},{1,0},{2,3},{3,2},{4,5},{5,4},{6,7},{7,6},{8,9},{9,8},{10,11... | collective-permute-start | bytes 10616840 | tf_op jit(solution)/shard_map/ppermute | solution.py:42
  81.2 37.9 %all-to-all-start.2 = ((bf16[8,24,896]{2,1,0:T(8,128)(2,1)}), bf16[8,24,896]{2,1,0:T(8,128)(2,1)}, u32[]{:S(2)}, u32[]{:S(2)}) async-start(bf16[8,24,896]{2,1,0:T(8,128)(2,1)} %bitcast.259), calls=%async_computation.2 | async-start | bytes 688128 | tf_op jit(solution)/shard_map/all_to_all | solution.py:34
  118.5 27.0 %collective-permute-start.3 = (bf16[160,512]{1,0:T(8,128)(2,1)S(1)}, bf16[160,512]{1,0:T(8,128)(2,1)S(1)}, u32[]{:S(2)}, u32[]{:S(2)}) collective-permute-start(bf16[160,512]{1,0:T(8,128)(2,1)S(1)} %get-tuple-element.280), channel_id=1, source_target_pairs={{0,4},{2,6},{4,0},{6,2},{8,12},{10,14},{12,8},{14,10},{1,5},{3,7},... | collective-permute-start | bytes 491528 | tf_op jit(solution)/shard_map/ppermute | solution.py:282
  122.0 95.6 %all-to-all-start.1 = ((bf16[64,24,1024]{2,1,0:T(8,128)(2,1)}), bf16[64,24,1024]{2,1,0:T(8,128)(2,1)S(1)}, u32[]{:S(2)}, u32[]{:S(2)}) async-start(bf16[64,24,1024]{2,1,0:T(8,128)(2,1)} %broadcast_in_dim.76), calls=%async_computation.1 | async-start | bytes 6291456 | tf_op jit(solution)/shard_map/all_to_all | solution.py:34
  132.7 57.5 %collective-permute-start.19 = (bf16[56,1408]{1,0:T(8,128)(2,1)}, bf16[56,1408]{1,0:T(8,128)(2,1)}, u32[]{:S(2)}, u32[]{:S(2)}) collective-permute-start(bf16[56,1408]{1,0:T(8,128)(2,1)} %fusion.373), channel_id=1, source_target_pairs={{0,0},{1,8},{2,16},{3,24},{4,32},{5,40},{6,48},{7,56},{8,64},{9,72... | collective-permute-start | bytes 473096 | tf_op jit(solution)/shard_map/ppermute | solution.py:217
  139.5 30.9 %collective-permute-start.4 = (bf16[160,512]{1,0:T(8,128)(2,1)S(1)}, bf16[160,512]{1,0:T(8,128)(2,1)S(1)}, u32[]{:S(2)}, u32[]{:S(2)}) collective-permute-start(bf16[160,512]{1,0:T(8,128)(2,1)S(1)} %get-tuple-element.280), channel_id=1, source_target_pairs={{0,6},{2,0},{4,2},{6,4},{8,14},{10,8},{12,10},{14,12},{1,7},{3,1},... | collective-permute-start | bytes 491528 | tf_op jit(solution)/shard_map/ppermute | solution.py:282
  139.6 31.6 %collective-permute-start.5 = (bf16[160,512]{1,0:T(8,128)(2,1)S(1)}, bf16[160,512]{1,0:T(8,128)(2,1)S(1)}, u32[]{:S(2)}, u32[]{:S(2)}) collective-permute-start(bf16[160,512]{1,0:T(8,128)(2,1)S(1)} %get-tuple-element.280), channel_id=1, source_target_pairs={{0,8},{2,10},{4,12},{6,14},{8,0},{10,2},{12,4},{14,6},{1,9},{3,11}... | collective-permute-start | bytes 491528 | tf_op jit(solution)/shard_map/ppermute | solution.py:282
  139.7 35.8 %collective-permute-start.6 = (bf16[160,512]{1,0:T(8,128)(2,1)S(1)}, bf16[160,512]{1,0:T(8,128)(2,1)S(1)}, u32[]{:S(2)}, u32[]{:S(2)}) collective-permute-start(bf16[160,512]{1,0:T(8,128)(2,1)S(1)} %get-tuple-element.280), channel_id=1, source_target_pairs={{0,10},{2,12},{4,14},{6,8},{8,2},{10,4},{12,6},{14,0},{1,11},{3,13... | collective-permute-start | bytes 491528 | tf_op jit(solution)/shard_map/ppermute | solution.py:282
  145.4 32.9 %collective-permute-start.7 = (bf16[160,512]{1,0:T(8,128)(2,1)S(1)}, bf16[160,512]{1,0:T(8,128)(2,1)S(1)}, u32[]{:S(2)}, u32[]{:S(2)}) collective-permute-start(bf16[160,512]{1,0:T(8,128)(2,1)S(1)} %get-tuple-element.280), channel_id=1, source_target_pairs={{0,12},{2,14},{4,8},{6,10},{8,4},{10,6},{12,0},{14,2},{1,13},{3,15... | collective-permute-start | bytes 491528 | tf_op jit(solution)/shard_map/ppermute | solution.py:282
  186.4 28.7 %collective-permute-start.9 = (bf16[1280,512]{1,0:T(8,128)(2,1)}, bf16[1280,512]{1,0:T(8,128)(2,1)}, u32[]{:S(2)}, u32[]{:S(2)}) collective-permute-start(bf16[1280,512]{1,0:T(8,128)(2,1)} %get-tuple-element.264), channel_id=1, source_target_pairs={{0,1},{1,0},{2,3},{3,2},{4,5},{5,4},{6,7},{7,6},{8,9},{9,8},{10,11... | collective-permute-start | bytes 3932168 | tf_op jit(solution)/shard_map/ppermute | solution.py:42
  207.5 44.3 %collective-permute-start.23 = (bf16[4,56,1408]{2,1,0:T(8,128)(2,1)}, bf16[4,56,1408]{2,1,0:T(8,128)(2,1)}, u32[]{:S(2)}, u32[]{:S(2)}) collective-permute-start(bf16[4,56,1408]{2,1,0:T(8,128)(2,1)} %pad_maximum_fusion.5), channel_id=1, source_target_pairs={{0,16},{16,8},{8,24},{24,0},{1,17},{17,9},{9,25},{25,1},{2,18},{18... | collective-permute-start | bytes 1892360 | tf_op jit(solution)/shard_map/ppermute | solution.py:47
  208.5 45.5 %collective-permute-start.24 = (bf16[4,56,1408]{2,1,0:T(8,128)(2,1)}, bf16[4,56,1408]{2,1,0:T(8,128)(2,1)}, u32[]{:S(2)}, u32[]{:S(2)}) collective-permute-start(bf16[4,56,1408]{2,1,0:T(8,128)(2,1)} %pad_maximum_fusion.5), channel_id=1, source_target_pairs={{0,8},{16,24},{8,0},{24,16},{1,9},{17,25},{9,1},{25,17},{2,10},{18... | collective-permute-start | bytes 1892360 | tf_op jit(solution)/shard_map/ppermute | solution.py:47
  209.7 45.2 %collective-permute-start.25 = (bf16[4,56,1408]{2,1,0:T(8,128)(2,1)}, bf16[4,56,1408]{2,1,0:T(8,128)(2,1)}, u32[]{:S(2)}, u32[]{:S(2)}) collective-permute-start(bf16[4,56,1408]{2,1,0:T(8,128)(2,1)} %pad_maximum_fusion.5), channel_id=1, source_target_pairs={{0,24},{16,0},{8,16},{24,8},{1,25},{17,1},{9,17},{25,9},{2,26},{18... | collective-permute-start | bytes 1892360 | tf_op jit(solution)/shard_map/ppermute | solution.py:47
  221.3 80.3 %all-to-all-start.3 = ((bf16[16,176,896]{2,1,0:T(8,128)(2,1)}), bf16[16,176,896]{2,1,0:T(8,128)(2,1)}, u32[]{:S(2)}, u32[]{:S(2)}) async-start(bf16[16,176,896]{2,1,0:T(8,128)(2,1)} %broadcast_in_dim.81), calls=%async_computation.3 | async-start | bytes 10092544 | tf_op jit(solution)/shard_map/all_to_all | solution.py:34
  246.9 70.8 %collective-permute-start.12 = (bf16[160,1152]{1,0:T(8,128)(2,1)}, bf16[160,1152]{1,0:T(8,128)(2,1)}, u32[]{:S(2)}, u32[]{:S(2)}) collective-permute-start(bf16[160,1152]{1,0:T(8,128)(2,1)} %get-tuple-element.185), channel_id=1, source_target_pairs={{0,2},{2,4},{4,6},{6,0},{1,3},{3,5},{5,7},{7,1},{8,10},{10,12},{12... | collective-permute-start | bytes 1105928 | tf_op jit(solution)/shard_map/ppermute | solution.py:47
  247.0 71.6 %collective-permute-start.13 = (bf16[160,1152]{1,0:T(8,128)(2,1)}, bf16[160,1152]{1,0:T(8,128)(2,1)S(1)}, u32[]{:S(2)}, u32[]{:S(2)}) collective-permute-start(bf16[160,1152]{1,0:T(8,128)(2,1)} %get-tuple-element.185), channel_id=1, source_target_pairs={{0,4},{2,6},{4,0},{6,2},{1,5},{3,7},{5,1},{7,3},{8,12},{10,14},{12... | collective-permute-start | bytes 1105928 | tf_op jit(solution)/shard_map/ppermute | solution.py:47
  251.8 69.4 %collective-permute-start.14 = (bf16[160,1152]{1,0:T(8,128)(2,1)}, bf16[160,1152]{1,0:T(8,128)(2,1)S(1)}, u32[]{:S(2)}, u32[]{:S(2)}) collective-permute-start(bf16[160,1152]{1,0:T(8,128)(2,1)} %get-tuple-element.185), channel_id=1, source_target_pairs={{0,6},{2,0},{4,2},{6,4},{1,7},{3,1},{5,3},{7,5},{8,14},{10,8},{12,... | collective-permute-start | bytes 1105928 | tf_op jit(solution)/shard_map/ppermute | solution.py:47
  253.9 68.5 %collective-permute-start.15 = (bf16[160,1152]{1,0:T(8,128)(2,1)}, bf16[160,1152]{1,0:T(8,128)(2,1)}, u32[]{:S(2)}, u32[]{:S(2)}) collective-permute-start(bf16[160,1152]{1,0:T(8,128)(2,1)} %get-tuple-element.185), channel_id=1, source_target_pairs={{0,1},{1,0},{2,3},{3,2},{4,5},{5,4},{6,7},{7,6},{8,9},{9,8},{10,11... | collective-permute-start | bytes 1105928 | tf_op jit(solution)/shard_map/ppermute | solution.py:42
  416.7 28.7 %collective-permute-start.46 = (bf16[160,1152]{1,0:T(8,128)(2,1)}, bf16[160,1152]{1,0:T(8,128)(2,1)}, u32[]{:S(2)}, u32[]{:S(2)}) collective-permute-start(bf16[160,1152]{1,0:T(8,128)(2,1)} %get-tuple-element.201), channel_id=1, source_target_pairs={{0,1},{1,0},{2,3},{3,2},{4,5},{5,4},{6,7},{7,6},{8,9},{9,8},{10,11... | collective-permute-start | bytes 1105928 | tf_op jit(solution)/shard_map/ppermute | solution.py:42
  436.2 115.3 %all-to-all-start.4 = ((bf16[16,176,896]{2,1,0:T(8,128)(2,1)}), bf16[16,176,896]{2,1,0:T(8,128)(2,1)}, u32[]{:S(2)}, u32[]{:S(2)}) async-start(bf16[16,176,896]{2,1,0:T(8,128)(2,1)} %pad_maximum_fusion), calls=%async_computation.4 | async-start | bytes 10092544 | tf_op jit(solution)/shard_map/all_to_all | solution.py:34
  487.4 26.5 %collective-permute-start.57 = (bf16[160,512]{1,0:T(8,128)(2,1)S(1)}, bf16[160,512]{1,0:T(8,128)(2,1)S(1)}, u32[]{:S(2)}, u32[]{:S(2)}) collective-permute-start(bf16[160,512]{1,0:T(8,128)(2,1)S(1)} %get-tuple-element.213), channel_id=1, source_target_pairs={{0,10},{2,12},{4,14},{6,8},{8,2},{10,4},{12,6},{14,0},{1,11},{3,13... | collective-permute-start | bytes 491528 | tf_op jit(solution)/shard_map/ppermute | solution.py:282
  489.7 27.6 %collective-permute-start.56 = (bf16[160,512]{1,0:T(8,128)(2,1)S(1)}, bf16[160,512]{1,0:T(8,128)(2,1)S(1)}, u32[]{:S(2)}, u32[]{:S(2)}) collective-permute-start(bf16[160,512]{1,0:T(8,128)(2,1)S(1)} %get-tuple-element.214), channel_id=1, source_target_pairs={{0,12},{2,14},{4,8},{6,10},{8,4},{10,6},{12,0},{14,2},{1,13},{3,15... | collective-permute-start | bytes 491528 | tf_op jit(solution)/shard_map/ppermute | solution.py:282
  499.4 28.7 %collective-permute-start.53 = (bf16[160,512]{1,0:T(8,128)(2,1)S(1)}, bf16[160,512]{1,0:T(8,128)(2,1)S(1)}, u32[]{:S(2)}, u32[]{:S(2)}) collective-permute-start(bf16[160,512]{1,0:T(8,128)(2,1)S(1)} %get-tuple-element.217), channel_id=1, source_target_pairs={{0,2},{2,4},{4,6},{6,0},{8,10},{10,12},{12,14},{14,8},{1,3},{3,5},... | collective-permute-start | bytes 491528 | tf_op jit(solution)/shard_map/ppermute | solution.py:282
  563.9 47.7 %collective-permute-start.59 = (bf16[1536,640]{1,0:T(8,128)(2,1)}, bf16[1536,640]{1,0:T(8,128)(2,1)}, u32[]{:S(2)}, u32[]{:S(2)}) collective-permute-start(bf16[1536,640]{1,0:T(8,128)(2,1)} %add_convert_fusion.2), channel_id=1, source_target_pairs={{0,1},{1,0},{2,3},{3,2},{4,5},{5,4},{6,7},{7,6},{8,9},{9,8},{10,11... | collective-permute-start | bytes 5898248 | tf_op jit(solution)/shard_map/ppermute | solution.py:42
  595.2 32.7 %all-to-all-start.6 = ((bf16[8,32,896]{2,1,0:T(8,128)(2,1)}), bf16[8,32,896]{2,1,0:T(8,128)(2,1)}, u32[]{:S(2)}, u32[]{:S(2)}) async-start(bf16[8,32,896]{2,1,0:T(8,128)(2,1)} %bitcast.258), calls=%async_computation.6 | async-start | bytes 917504 | tf_op jit(solution)/shard_map/all_to_all | solution.py:34
  603.2 33.9 %collective-permute-start.62 = (bf16[56,1152]{1,0:T(8,128)(2,1)}, bf16[56,1152]{1,0:T(8,128)(2,1)}, u32[]{:S(2)}, u32[]{:S(2)}) collective-permute-start(bf16[56,1152]{1,0:T(8,128)(2,1)} %get-tuple-element.242), channel_id=1, source_target_pairs={{0,96},{32,0},{64,32},{96,64},{1,97},{33,1},{65,33},{97,65},{2,98}... | collective-permute-start | bytes 387080 | tf_op jit(solution)/shard_map/ppermute | solution.py:47
  603.2 34.0 %collective-permute-start.63 = (bf16[56,1152]{1,0:T(8,128)(2,1)}, bf16[56,1152]{1,0:T(8,128)(2,1)}, u32[]{:S(2)}, u32[]{:S(2)}) collective-permute-start(bf16[56,1152]{1,0:T(8,128)(2,1)} %get-tuple-element.241), channel_id=1, source_target_pairs={{0,64},{32,96},{64,0},{96,32},{1,65},{33,97},{65,1},{97,33},{2,66}... | collective-permute-start | bytes 387080 | tf_op jit(solution)/shard_map/ppermute | solution.py:47
  606.2 30.9 %collective-permute-start.64 = (bf16[56,1152]{1,0:T(8,128)(2,1)}, bf16[56,1152]{1,0:T(8,128)(2,1)}, u32[]{:S(2)}, u32[]{:S(2)}) collective-permute-start(bf16[56,1152]{1,0:T(8,128)(2,1)} %get-tuple-element.240), channel_id=1, source_target_pairs={{0,32},{32,64},{64,96},{96,0},{1,33},{33,65},{65,97},{97,1},{2,34}... | collective-permute-start | bytes 387080 | tf_op jit(solution)/shard_map/ppermute | solution.py:47
  627.9 71.5 %all-to-all-start.5 = ((bf16[64,24,1408]{2,1,0:T(8,128)(2,1)}), bf16[64,24,1408]{2,1,0:T(8,128)(2,1)}, u32[]{:S(2)}, u32[]{:S(2)}) async-start(bf16[64,24,1408]{2,1,0:T(8,128)(2,1)} %pad_maximum_fusion.1), calls=%async_computation.5 | async-start | bytes 8650752 | tf_op jit(solution)/shard_map/all_to_all | solution.py:34
  657.8 37.9 %collective-permute-start.65 = (bf16[56,1152]{1,0:T(8,128)(2,1)}, bf16[56,1152]{1,0:T(8,128)(2,1)}, u32[]{:S(2)}, u32[]{:S(2)}) collective-permute-start(bf16[56,1152]{1,0:T(8,128)(2,1)} %add_convert_fusion.4), channel_id=1, source_target_pairs={{0,0},{8,1},{16,2},{24,3},{32,4},{40,5},{48,6},{56,7},{64,8},{72,9... | collective-permute-start | bytes 387080 | tf_op jit(solution)/shard_map/ppermute | solution.py:496
  (189 other events, 1645.9 us)

commit v5 on v4

--- a/solution.py
+++ b/solution.py
@@ -42,6 +42,10 @@
     return lax.ppermute(x, "c", [(0, 1), (1, 0)])
 
 
+def other_half(x):
+    return lax.ppermute(x, "xh", [(0, 1), (1, 0)])
+
+
 def shift(x, axis, k):
     number = [0, 2, 1, 3] if axis == "x" else [0, 1, 2, 3]
     return lax.ppermute(x, RING[axis], [(number[i], number[(i + k) % 4]) for i in range(4)])
@@ -53,12 +57,12 @@
 
 def split_in_two(x):
     high = x.astype(BF)
-    return high, (x - high.astype(F32)).astype(BF)
+    return high, x - high.astype(F32)
 
 
 def select_back(x, table):
     high, low = split_in_two(x)
-    return dot_tr(high, table) + dot_tr(low, table)
+    return dot_tr(high, table) + dot_tr(low.astype(BF), table)
 
 
 def down_route():
@@ -197,11 +201,28 @@
     lower, upper = pick(is_first, keep, other_core(send))
     out_own = jnp.concatenate([lower, upper], axis=0)
 
+    def column_of(k):
+        return 2 * ((at_y + k // 2) % 4) + (core + k) % 2
+
+    def column_shift(x, k):
+        route = []
+        for y in range(4):
+            for c in range(2):
+                route.append((2 * y + c, 2 * ((y + k // 2) % 4) + (c + k) % 2))
+        return lax.ppermute(x, ("y", "c"), route)
+
     rows22 = jnp.pad(jnp.concatenate([wg, wu, bg, bu], axis=0), ((0, 2), (0, 0)))
     rows22 = jnp.concatenate([rows22[:, 864 * t : 864 * (t + 1)] for t in range(8)], axis=0)
     wider = jnp.arange(896, dtype=jnp.int32)
     wider = table(jnp.arange(864, dtype=jnp.int32), jnp.where(wider % 56 < 54, wider // 56 * 54 + wider % 56, -1))
-    slab = exchange(dot(rows22, wider).astype(BF).reshape(8, 24, 896), ("y", "c"))
+    rows22 = dot(rows22, wider).astype(BF).reshape(8, 24, 896)
+    slab = []
+    for k in range(8):
+        piece = lax.dynamic_index_in_dim(rows22, column_of(k), 0, keepdims=False)
+        slab.append(column_shift(piece, k) if k else piece)
+    slab = jnp.concatenate(slab, axis=0)
+    back = jnp.arange(8, dtype=jnp.int32)
+    sources = 2 * ((at_y - back // 2) % 4) + (core - back) % 2
     row = jnp.arange(176, dtype=jnp.int32)
     low = row - 144
     at_row = jnp.where(
@@ -213,13 +234,22 @@
             low % 16 // 2 * 24 + 18 + low // 16 * 2 + low % 2,
         ),
     )
-    ff_own = dot(table(at_row, jnp.arange(192, dtype=jnp.int32)), slab.reshape(192, 896)).astype(BF)
+    in_slab = jnp.arange(192, dtype=jnp.int32)
+    in_slab = jnp.repeat(sources, 24) * 24 + in_slab % 24
+    ff_own = dot(table(at_row, in_slab), slab).astype(BF)
     down_own = lax.ppermute(
         jnp.pad(jnp.concatenate([wd, ad], axis=1), ((0, 2), (0, 0))), EVERY, down_route()
     )
     down_line = gather_line(down_own, "z")
     down_line, _ = after(raw_one, down_line)
     down_lines = [down_line] + [shift(down_line, "x", k) for k in (1, 2, 3)]
+
+    out_own, _ = after(raw_one, out_own)
+    out_one = gather_chips(out_own)
+    out_two = other_core(out_one)
+    raw_out = [out_one.reshape(1536, 1024), out_two.reshape(1536, 1024)]
+    ff_own, _ = after(out_one, ff_own)
+    ff_all = exchange(jnp.broadcast_to(ff_own[None], (16, 176, 896)), ("z", "xl", "xh"))
 
     ids = jnp.arange(1536, dtype=jnp.int32)
     dev, j = 2 * (ids // 24) + (ids % 24) // 12, ids % 12
@@ -274,23 +304,10 @@
     vv = pick(is_first, *[dot(sides[2], raw[i][:, 640:768]) for i in (0, 1)])
     kv_own = jnp.concatenate([turn(jnp.concatenate(kk, axis=1), cos, sin), vv[0], vv[1]], axis=1).astype(BF)
 
-    def tree_shift(x, kh, ky):
-        route = []
-        for h in range(2):
-            for y in range(4):
-                route.append((4 * h + y, 4 * ((h + kh) % 2) + (y + ky) % 4))
-        return lax.ppermute(x, ("xh", "y"), route)
-
-    out_own, _ = after(kv_own, out_own)
-    out_one = gather_chips(out_own)
-    out_two = other_core(out_one)
-    raw_out = [out_one.reshape(1536, 1024), out_two.reshape(1536, 1024)]
-    kv_mine = [kv_own] + [tree_shift(kv_own, k // 4, k % 4) for k in range(1, 8)]
-    kv_mine = jnp.concatenate(kv_mine, axis=0)
+    kv_line = gather_line(kv_own, "y").reshape(640, 512)
+    kv_mine = jnp.concatenate([kv_line, other_half(kv_line)], axis=0)
     kv = jnp.concatenate([kv_mine, other_core(kv_mine)], axis=0)
     keys, values = kv[:, :256], kv[:, 256:]
-    ff_own, _ = after(kv, ff_own)
-    ff_all = exchange(jnp.broadcast_to(ff_own[None], (16, 176, 896)), ("z", "xl", "xh"))
     queries = [dot(sides[0], raw[i][:, :512]) for i in (0, 1)]
     q_rows = jnp.concatenate(
         [turn(queries[h // 2][:, WIDTH * (h % 2) : WIDTH * (h % 2 + 1)], cos, sin) for h in range(HEADS)],
@@ -312,17 +329,18 @@
     scale_two, n_two, u_two = norm_parts(after_att, gain_two_full)
     u_all = gather_tokens(u_two)
 
-    ff_all, down_lines, _ = after(u_two, ff_all, down_lines)
+    down_lines, _ = after(u_two, down_lines)
     down_raw = jnp.concatenate(down_lines, axis=0).reshape(896, 1408)
+    left, right = pick(is_first, *[dot(put_inner_down, raw_out[i][:, :640]).astype(BF) for i in (0, 1)])
+    b_down = jnp.concatenate([left, right[:, 128:]], axis=1)
+    a_down = dot(put_down, down_raw[:, 1152:]).astype(BF)
+    w_down = (dot(put_down, down_raw[:, :1152]) + dot(a_down, b_down)).astype(BF)
     a_gate, a_up = pick(is_first, *[dot(put_rows, raw_out[i][:, 768:]).astype(BF) for i in (0, 1)])
+    ff_all, _ = after(w_down, ff_all)
     b_gate = ff_all[:, 144:160].reshape(256, 896)
     b_up = ff_all[:, 160:].reshape(256, 896)
     w_gate = (ff_all[:, :72].reshape(1152, 896).astype(F32) + dot(a_gate, b_gate)).astype(BF)
     w_up = (ff_all[:, 72:144].reshape(1152, 896).astype(F32) + dot(a_up, b_up)).astype(BF)
-    left, right = pick(is_first, *[dot(put_inner_down, raw_out[i][:, :640]).astype(BF) for i in (0, 1)])
-    b_down = jnp.concatenate([left, right[:, 128:]], axis=1)
-    a_down = dot(put_down, down_raw[:, 1152:]).astype(BF)
-    w_down = (dot(put_down, down_raw[:, :1152]) + dot(a_down, b_down)).astype(BF)
 
     gate = dot(u_all, w_gate)
     up = dot(u_all, w_up)
@@ -387,10 +405,11 @@
     n_mine = 8 * TOKENS
     g_kv_sum = g_kv[:n_mine] + other_core(g_kv[n_mine:].astype(BF)).astype(F32)
     g_kv_b = g_kv_sum.astype(BF)
-    g_kv_own = g_kv_sum[:TOKENS]
-    for k in range(1, 8):
-        away = g_kv_b[TOKENS * k : TOKENS * (k + 1)]
-        g_kv_own = g_kv_own + tree_shift(away, k // 4, (4 - k % 4) % 4).astype(F32)
+    g_line = g_kv_sum[:640] + other_half(g_kv_b[640:]).astype(F32)
+    g_kv_own = g_line[:TOKENS]
+    g_line = g_line.astype(BF)
+    for k in (1, 2, 3):
+        g_kv_own = g_kv_own + shift(g_line[TOKENS * k : TOKENS * (k + 1)], "y", 4 - k).astype(F32)
     g_scores, side_out, ff_parts, down_first, gb_down, _ = after(
         g_kv_b, g_scores, side_out, ff_parts, down_first, gb_down
     )
@@ -455,29 +474,23 @@
         dot_tl(side_out, g_half[0]) + dot_tl(put_inner_down, left),
         dot_tl(side_out, g_half[1]) + dot_tl(put_inner_down, right),
     )
-    nines = jnp.arange(9, dtype=jnp.int32)[:, None] == features[None, :] % 9
     loss_high, loss_rest = split_in_two(loss_here)
-    loss_mid, loss_low = split_in_two(loss_here - loss_high.astype(F32))
-    at_marks = (j == 11).astype(BF)[None, :]
-    more_side = jnp.concatenate(
-        [
-            dot(jnp.where(nines, g_gain_one, 0.0).astype(BF), put_marks).astype(BF),
-            dot(jnp.where(nines, g_gain_two, 0.0).astype(BF), put_marks).astype(BF),
-            loss_high * at_marks,
-            loss_mid * at_marks,
-            loss_low * at_marks,
-            jnp.zeros((11, 1536), BF),
-        ],
-        axis=0,
-    )
+    loss_mid, loss_low = split_in_two(loss_rest)
+    loss_low = loss_low.astype(BF)
+    at_row = jnp.arange(32, dtype=jnp.int32)[:, None]
+    nines = (features[None, :] % 9 == at_row % 9) & (at_row < 18)
+    gain_rows = jnp.where(nines, jnp.where(at_row < 9, g_gain_one, g_gain_two), 0.0).astype(BF)
+    loss_rows = jnp.where(
+        at_row == 18, loss_high, jnp.where(at_row == 19, loss_mid, jnp.where(at_row == 20, loss_low, 0))
+    ).astype(F32)
+    more_side = (dot(gain_rows, put_marks) + loss_rows * (j == 11)[None, :]).astype(BF)
     lines = jnp.arange(32, dtype=jnp.int32)
     line_at = jnp.where(lines < 18, lines, jnp.where(lines < 21, lines + 3 * core, -1))
     more_grad = table(line_at, jnp.arange(512, dtype=jnp.int32))
-    side_q = jnp.concatenate([sides[0], more_side], axis=0)
     sums = [
         jnp.concatenate(
             [
-                dot_tl(side_q, jnp.concatenate([g_q[i], more_grad], axis=0)).astype(BF),
+                (dot_tl(sides[0], g_q[i]) + dot_tl(more_side, more_grad)).astype(BF),
                 dot_tl(sides[1], g_k[i]).astype(BF),
                 dot_tl(sides[2], g_v[i]).astype(BF),
             ],

time: 755 us -> 756 us (level)
  the two profiles are of different devices: /device:TPU:13 before, /device:TPU:1 now
where the time goes in v5:
time: 756 us; the launch traced here: 742 us
  waiting for transfers between devices  212 us (28%)
  matrix products  184 us (24%)
  starting transfers between devices  134 us (18%)
  other arithmetic  109 us (14%)
  local copies, waits for them, and re-layouts  93.8 us (12%)
  between operations  8.77 us (1%)
    dot_general x39, matrix products, dot_tr(): lax.dot_general(a, b, (((1,), (1,)), ((), ())), preferred_element_type=F32)  75.5 us
    ppermute x2, waiting for transfers between devices, other_half(): return lax.ppermute(x, 'xh', [(0, 1), (1, 0)])  73.2 us
    ppermute x30, waiting for transfers between devices, shift(): lax.ppermute(x, RING[axis], [(number[i], number[(i + k) % 4]) for i in ra...  70 us
    dot_general x35, matrix products, dot(): return jnp.dot(a, b, preferred_element_type=F32)  56.9 us
    dot_general x20, matrix products, dot_tl(): lax.dot_general(a, b, (((0,), (0,)), ((), ())), preferred_element_type=F32)  51.6 us
    all_to_all x6, waiting for transfers between devices, exchange(): return lax.all_to_all(x, axes, split_axis=0, concat_axis=0, tiled=True)  48.3 us
    all_to_all x6, starting transfers between devices, exchange(): return lax.all_to_all(x, axes, split_axis=0, concat_axis=0, tiled=True)  42.5 us
    ppermute x30, starting transfers between devices, shift(): lax.ppermute(x, RING[axis], [(number[i], number[(i + k) % 4]) for i in ra...  38.3 us
  transfers between devices with their start and end apart: 73, of which 19 were waited for; matrix products, arithmetic and copies ran while one was open for 33% of the time, Pallas kernels for 0%

profile of v5, /device:TPU:1, one launch (start us, length us, event | category | flops | bytes accessed | tf_op | source)
XLA Modules:
  0.0 741.6 jit_solution(1920247662111773358)
XLA Ops:
  20.2 11.3 %all-to-all-start = ((bf16[64,24,1152]{2,1,0:T(8,128)(2,1)}), bf16[64,24,1152]{2,1,0:T(8,128)(2,1)S(1)}, u32[]{:S(2)}, u32[]{:S(2)}) async-start(bf16[64,24,1152]{2,1,0:T(8,128)(2,1)} %broadcast_in_dim.104), calls=%async_computation | async-start | bytes 7077888 | tf_op jit(solution)/shard_map/all_to_all | solution.py:34
  58.3 17.4 %all-to-all-done = bf16[64,24,1152]{2,1,0:T(8,128)(2,1)S(1)} async-done(((bf16[64,24,1152]{2,1,0:T(8,128)(2,1)}), bf16[64,24,1152]{2,1,0:T(8,128)(2,1)S(1)}, u32[]{:S(2)}, u32[]{:S(2)}) %all-to-all-start) | async-done | bytes 3538976 | tf_op jit(solution)/shard_map/all_to_all | solution.py:34
  99.6 7.6 %all-to-all-start.1 = ((bf16[64,24,1024]{2,1,0:T(8,128)(2,1)}), bf16[64,24,1024]{2,1,0:T(8,128)(2,1)}, u32[]{:S(2)}, u32[]{:S(2)}) async-start(bf16[64,24,1024]{2,1,0:T(8,128)(2,1)} %broadcast_in_dim.167), calls=%async_computation.1 | async-start | bytes 6291456 | tf_op jit(solution)/shard_map/all_to_all | solution.py:34
  122.4 24.8 %collective-permute-done.4 = bf16[160,512]{1,0:T(8,128)(2,1)S(1)} collective-permute-done((bf16[160,512]{1,0:T(8,128)(2,1)S(1)}, bf16[160,512]{1,0:T(8,128)(2,1)S(1)}, u32[]{:S(2)}, u32[]{:S(2)}) %collective-permute-start.4) | collective-permute-done | bytes 163872 | tf_op jit(solution)/shard_map/ppermute | solution.py:51
  165.2 6.5 collective-permute-done.5
  174.5 5.8 collective-permute-start.26
  181.1 6.0 collective-permute-done.26
  197.2 4.7 all-to-all-start.2
  250.3 30.9 %all-to-all-done.2 = bf16[16,176,896]{2,1,0:T(8,128)(2,1)} async-done(((bf16[16,176,896]{2,1,0:T(8,128)(2,1)}), bf16[16,176,896]{2,1,0:T(8,128)(2,1)}, u32[]{:S(2)}, u32[]{:S(2)}) %all-to-all-start.2) | async-done | bytes 5046304 | tf_op jit(solution)/shard_map/all_to_all | solution.py:34
  286.1 6.1 fusion.667
  293.0 9.7 %multiply_convert_fusion.1 = (bf16[1280,896]{1,0:T(8,128)(2,1)S(1)}, f32[1280,896]{1,0:T(8,128)}) fusion(f32[1280,896]{1,0:T(8,128)S(1)} %fusion.667, bf16[1280,1152]{1,0:T(8,128)(2,1)} %constant_dynamic-update-slice_fusion.12, bf16[1152,896]{1,0:T(8,128)(2,1)S(1)} %fusion.39), kind=kOutput, calls=%fused_computation.56 | convolution fusion | flops 2653880320 | bytes 16482304 | tf_op jit(solution)/shard_map/dot_general | solution.py:22
  320.4 5.5 collective-permute-done.35
  325.9 8.3 %collective-permute-done.31 = bf16[160,1152]{1,0:T(8,128)(2,1)} collective-permute-done((bf16[160,1152]{1,0:T(8,128)(2,1)}, bf16[160,1152]{1,0:T(8,128)(2,1)}, u32[]{:S(2)}, u32[]{:S(2)}) %collective-permute-start.31) | collective-permute-done | bytes 368672 | tf_op jit(solution)/shard_map/ppermute | solution.py:51
  351.5 5.0 collective-permute-done.38
  367.9 11.0 %fusion.30 = (bf16[1280,896]{1,0:T(8,128)(2,1)S(1)}, bf16[1280,896]{1,0:T(8,128)(2,1)S(1)}) fusion(f32[1280,896]{1,0:T(8,128)} %copy-done.144, f32[1280,896]{1,0:T(8,128)} %get-tuple-element.342, bf16[1280,1152]{1,0:T(8,128)(2,1)} %constant_dynamic-update-slice_fusion.36, bf16[896,1152]{1,0:T(8,128)(2,1)S(1)} %copy-done.34), kind=kOutput, calls=%fused_computation.48 | convolution fusion | flops 2672230400 | bytes 18776064 | tf_op jit(solution)/shard_map/dot_general | solution.py:30
  388.1 5.1 convolution_convert_fusion.2
  396.3 6.3 convolution_convert_fusion.3
  405.0 7.1 collective-permute-done.45
  423.6 5.0 multiply_reduce_fusion
  430.6 6.0 multiply_convert_fusion
  444.7 7.3 all-to-all-start.3
  452.0 5.9 convolution_convert_fusion.1
  468.2 66.8 %collective-permute-done.55 = bf16[640,512]{1,0:T(8,128)(2,1)S(1)} collective-permute-done((bf16[640,512]{1,0:T(8,128)(2,1)S(1)}, bf16[640,512]{1,0:T(8,128)(2,1)S(1)}, u32[]{:S(2)}, u32[]{:S(2)}) %collective-permute-start.55) | collective-permute-done | bytes 655392 | tf_op jit(solution)/shard_map/ppermute | solution.py:46
  573.1 4.7 add_convert_fusion.2
  577.8 5.6 collective-permute-start.60
  595.2 4.3 fusion.186
  605.1 4.5 all-to-all-start.5
  626.8 4.3 copy.81
  631.1 4.6 pad_maximum_fusion.1
  635.7 7.1 all-to-all-start.4
  663.4 4.2 collective-permute-start.66
  675.6 18.8 %collective-permute-done.66 = bf16[56,1152]{1,0:T(8,128)(2,1)} collective-permute-done((bf16[56,1152]{1,0:T(8,128)(2,1)}, bf16[56,1152]{1,0:T(8,128)(2,1)}, u32[]{:S(2)}, u32[]{:S(2)}) %collective-permute-start.66) | collective-permute-done | bytes 129056 | tf_op jit(solution)/shard_map/ppermute | solution.py:509
  (716 shorter events, 404.8 us)
Async XLA Ops:
  20.2 55.6 %all-to-all-start = ((bf16[64,24,1152]{2,1,0:T(8,128)(2,1)}), bf16[64,24,1152]{2,1,0:T(8,128)(2,1)S(1)}, u32[]{:S(2)}, u32[]{:S(2)}) async-start(bf16[64,24,1152]{2,1,0:T(8,128)(2,1)} %broadcast_in_dim.104), calls=%async_computation | async-start | bytes 7077888 | tf_op jit(solution)/shard_map/all_to_all | solution.py:34
  46.3 41.8 %collective-permute-start.7 = (bf16[12,1024]{1,0:T(8,128)(2,1)}, bf16[12,1024]{1,0:T(8,128)(2,1)}, u32[]{:S(2)}, u32[]{:S(2)}) collective-permute-start(bf16[12,1024]{1,0:T(8,128)(2,1)} %broadcast_select_fusion.20), channel_id=1, source_target_pairs={{0,1},{1,0},{2,3},{3,2},{4,5},{5,4},{6,7},{7,6},{8,9},{9,8},{10,11... | collective-permute-start | bytes 73736 | tf_op jit(solution)/shard_map/ppermute | solution.py:42
  51.4 102.8 %collective-permute-start.16 = (bf16[24,896]{1,0:T(8,128)(2,1)}, bf16[24,896]{1,0:T(8,128)(2,1)}, u32[]{:S(2)}, u32[]{:S(2)}) collective-permute-start(bf16[24,896]{1,0:T(8,128)(2,1)} %get-tuple-element.248), channel_id=1, source_target_pairs={{0,1},{1,0},{2,3},{3,2},{4,5},{5,4},{6,7},{7,6},{8,9},{9,8},{10,11... | collective-permute-start | bytes 129032 | tf_op jit(solution)/shard_map/ppermute | solution.py:212
  51.6 105.2 %collective-permute-start.17 = (bf16[24,896]{1,0:T(8,128)(2,1)}, bf16[24,896]{1,0:T(8,128)(2,1)}, u32[]{:S(2)}, u32[]{:S(2)}) collective-permute-start(bf16[24,896]{1,0:T(8,128)(2,1)} %get-tuple-element.247), channel_id=1, source_target_pairs={{0,2},{1,3},{2,4},{3,5},{4,6},{5,7},{6,0},{7,1},{8,10},{9,11},{10,... | collective-permute-start | bytes 129032 | tf_op jit(solution)/shard_map/ppermute | solution.py:212
  75.8 34.6 %collective-permute-start.1 = (bf16[64,24,1152]{2,1,0:T(8,128)(2,1)S(1)}, bf16[64,24,1152]{2,1,0:T(8,128)(2,1)}, u32[]{:S(2)}, u32[]{:S(2)}) collective-permute-start(bf16[64,24,1152]{2,1,0:T(8,128)(2,1)S(1)} %all-to-all-done), channel_id=1, source_target_pairs={{0,1},{1,0},{2,3},{3,2},{4,5},{5,4},{6,7},{7,6},{8,9},{9,8},{10,11... | collective-permute-start | bytes 10616840 | tf_op jit(solution)/shard_map/ppermute | solution.py:42
  99.6 95.0 %all-to-all-start.1 = ((bf16[64,24,1024]{2,1,0:T(8,128)(2,1)}), bf16[64,24,1024]{2,1,0:T(8,128)(2,1)}, u32[]{:S(2)}, u32[]{:S(2)}) async-start(bf16[64,24,1024]{2,1,0:T(8,128)(2,1)} %broadcast_in_dim.167), calls=%async_computation.1 | async-start | bytes 6291456 | tf_op jit(solution)/shard_map/all_to_all | solution.py:34
  118.0 29.2 %collective-permute-start.4 = (bf16[160,512]{1,0:T(8,128)(2,1)S(1)}, bf16[160,512]{1,0:T(8,128)(2,1)S(1)}, u32[]{:S(2)}, u32[]{:S(2)}) collective-permute-start(bf16[160,512]{1,0:T(8,128)(2,1)S(1)} %pad_maximum_fusion.13), channel_id=1, source_target_pairs={{0,6},{2,0},{4,2},{6,4},{1,7},{3,1},{5,3},{7,5},{8,14},{10,8},{12,... | collective-permute-start | bytes 491528 | tf_op jit(solution)/shard_map/ppermute | solution.py:51
  120.4 27.8 %collective-permute-start.3 = (bf16[160,512]{1,0:T(8,128)(2,1)S(1)}, bf16[160,512]{1,0:T(8,128)(2,1)S(1)}, u32[]{:S(2)}, u32[]{:S(2)}) collective-permute-start(bf16[160,512]{1,0:T(8,128)(2,1)S(1)} %pad_maximum_fusion.13), channel_id=1, source_target_pairs={{0,4},{2,6},{4,0},{6,2},{1,5},{3,7},{5,1},{7,3},{8,12},{10,14},{12... | collective-permute-start | bytes 491528 | tf_op jit(solution)/shard_map/ppermute | solution.py:51
  121.0 29.3 %collective-permute-start.2 = (bf16[160,512]{1,0:T(8,128)(2,1)S(1)}, bf16[160,512]{1,0:T(8,128)(2,1)S(1)}, u32[]{:S(2)}, u32[]{:S(2)}) collective-permute-start(bf16[160,512]{1,0:T(8,128)(2,1)S(1)} %pad_maximum_fusion.13), channel_id=1, source_target_pairs={{0,2},{2,4},{4,6},{6,0},{1,3},{3,5},{5,7},{7,1},{8,10},{10,12},{12... | collective-permute-start | bytes 491528 | tf_op jit(solution)/shard_map/ppermute | solution.py:51
  172.9 36.1 %collective-permute-start.6 = (bf16[1280,512]{1,0:T(8,128)(2,1)}, bf16[1280,512]{1,0:T(8,128)(2,1)}, u32[]{:S(2)}, u32[]{:S(2)}) collective-permute-start(bf16[1280,512]{1,0:T(8,128)(2,1)} %pad_maximum_fusion.6), channel_id=1, source_target_pairs={{0,1},{1,0},{2,3},{3,2},{4,5},{5,4},{6,7},{7,6},{8,9},{9,8},{10,11... | collective-permute-start | bytes 3932168 | tf_op jit(solution)/shard_map/ppermute | solution.py:42
  190.6 36.1 %collective-permute-start.27 = (bf16[4,56,1408]{2,1,0:T(8,128)(2,1)S(1)}, bf16[4,56,1408]{2,1,0:T(8,128)(2,1)}, u32[]{:S(2)}, u32[]{:S(2)}) collective-permute-start(bf16[4,56,1408]{2,1,0:T(8,128)(2,1)S(1)} %pad_maximum_fusion.8), channel_id=1, source_target_pairs={{0,16},{16,8},{8,24},{24,0},{1,17},{17,9},{9,25},{25,1},{2,18},{18... | collective-permute-start | bytes 1892360 | tf_op jit(solution)/shard_map/ppermute | solution.py:51
  191.5 36.5 %collective-permute-start.28 = (bf16[4,56,1408]{2,1,0:T(8,128)(2,1)S(1)}, bf16[4,56,1408]{2,1,0:T(8,128)(2,1)}, u32[]{:S(2)}, u32[]{:S(2)}) collective-permute-start(bf16[4,56,1408]{2,1,0:T(8,128)(2,1)S(1)} %pad_maximum_fusion.8), channel_id=1, source_target_pairs={{0,8},{16,24},{8,0},{24,16},{1,9},{17,25},{9,1},{25,17},{2,10},{18... | collective-permute-start | bytes 1892360 | tf_op jit(solution)/shard_map/ppermute | solution.py:51
  192.5 36.6 %collective-permute-start.29 = (bf16[4,56,1408]{2,1,0:T(8,128)(2,1)S(1)}, bf16[4,56,1408]{2,1,0:T(8,128)(2,1)}, u32[]{:S(2)}, u32[]{:S(2)}) collective-permute-start(bf16[4,56,1408]{2,1,0:T(8,128)(2,1)S(1)} %pad_maximum_fusion.8), channel_id=1, source_target_pairs={{0,24},{16,0},{8,16},{24,8},{1,25},{17,1},{9,17},{25,9},{2,26},{18... | collective-permute-start | bytes 1892360 | tf_op jit(solution)/shard_map/ppermute | solution.py:51
  197.2 83.9 %all-to-all-start.2 = ((bf16[16,176,896]{2,1,0:T(8,128)(2,1)}), bf16[16,176,896]{2,1,0:T(8,128)(2,1)}, u32[]{:S(2)}, u32[]{:S(2)}) async-start(bf16[16,176,896]{2,1,0:T(8,128)(2,1)} %broadcast_in_dim.169), calls=%async_computation.2 | async-start | bytes 10092544 | tf_op jit(solution)/shard_map/all_to_all | solution.py:34
  225.0 18.5 %collective-permute-start.10 = (bf16[160,1152]{1,0:T(8,128)(2,1)S(1)}, bf16[160,1152]{1,0:T(8,128)(2,1)S(1)}, u32[]{:S(2)}, u32[]{:S(2)}) collective-permute-start(bf16[160,1152]{1,0:T(8,128)(2,1)S(1)} %get-tuple-element.187), channel_id=1, source_target_pairs={{0,4},{2,6},{4,0},{6,2},{1,5},{3,7},{5,1},{7,3},{8,12},{10,14},{12... | collective-permute-start | bytes 1105928 | tf_op jit(solution)/shard_map/ppermute | solution.py:51
  228.0 19.2 %collective-permute-start.12 = (bf16[160,1152]{1,0:T(8,128)(2,1)S(1)}, bf16[160,1152]{1,0:T(8,128)(2,1)S(1)}, u32[]{:S(2)}, u32[]{:S(2)}) collective-permute-start(bf16[160,1152]{1,0:T(8,128)(2,1)S(1)} %get-tuple-element.187), channel_id=1, source_target_pairs={{0,1},{1,0},{2,3},{3,2},{4,5},{5,4},{6,7},{7,6},{8,9},{9,8},{10,11... | collective-permute-start | bytes 1105928 | tf_op jit(solution)/shard_map/ppermute | solution.py:42
  338.4 18.1 %collective-permute-start.38 = (bf16[160,1152]{1,0:T(8,128)(2,1)}, bf16[160,1152]{1,0:T(8,128)(2,1)}, u32[]{:S(2)}, u32[]{:S(2)}) collective-permute-start(bf16[160,1152]{1,0:T(8,128)(2,1)} %get-tuple-element.185), channel_id=1, source_target_pairs={{0,4},{2,6},{4,0},{6,2},{1,5},{3,7},{5,1},{7,3},{8,12},{10,14},{12... | collective-permute-start | bytes 1105928 | tf_op jit(solution)/shard_map/ppermute | solution.py:51
  342.0 18.3 %collective-permute-start.39 = (bf16[160,1152]{1,0:T(8,128)(2,1)}, bf16[160,1152]{1,0:T(8,128)(2,1)}, u32[]{:S(2)}, u32[]{:S(2)}) collective-permute-start(bf16[160,1152]{1,0:T(8,128)(2,1)} %get-tuple-element.185), channel_id=1, source_target_pairs={{0,6},{2,0},{4,2},{6,4},{1,7},{3,1},{5,3},{7,5},{8,14},{10,8},{12,... | collective-permute-start | bytes 1105928 | tf_op jit(solution)/shard_map/ppermute | solution.py:51
  342.3 21.5 %collective-permute-start.40 = (bf16[160,1152]{1,0:T(8,128)(2,1)}, bf16[160,1152]{1,0:T(8,128)(2,1)}, u32[]{:S(2)}, u32[]{:S(2)}) collective-permute-start(bf16[160,1152]{1,0:T(8,128)(2,1)} %get-tuple-element.185), channel_id=1, source_target_pairs={{0,1},{1,0},{2,3},{3,2},{4,5},{5,4},{6,7},{7,6},{8,9},{9,8},{10,11... | collective-permute-start | bytes 1105928 | tf_op jit(solution)/shard_map/ppermute | solution.py:42
  439.6 18.3 %collective-permute-start.54 = (bf16[1280,512]{1,0:T(8,128)(2,1)}, bf16[1280,512]{1,0:T(8,128)(2,1)}, u32[]{:S(2)}, u32[]{:S(2)}) collective-permute-start(bf16[1280,512]{1,0:T(8,128)(2,1)} %fusion.63), channel_id=1, source_target_pairs={{0,1},{1,0},{2,3},{3,2},{4,5},{5,4},{6,7},{7,6},{8,9},{9,8},{10,11... | collective-permute-start | bytes 3932168 | tf_op jit(solution)/shard_map/ppermute | solution.py:42
  444.7 113.5 %all-to-all-start.3 = ((bf16[16,176,896]{2,1,0:T(8,128)(2,1)}), bf16[16,176,896]{2,1,0:T(8,128)(2,1)}, u32[]{:S(2)}, u32[]{:S(2)}) async-start(bf16[16,176,896]{2,1,0:T(8,128)(2,1)} %pad_maximum_fusion), calls=%async_computation.3 | async-start | bytes 10092544 | tf_op jit(solution)/shard_map/all_to_all | solution.py:34
  459.7 75.2 %collective-permute-start.55 = (bf16[640,512]{1,0:T(8,128)(2,1)S(1)}, bf16[640,512]{1,0:T(8,128)(2,1)S(1)}, u32[]{:S(2)}, u32[]{:S(2)}) collective-permute-start(bf16[640,512]{1,0:T(8,128)(2,1)S(1)} %slice.1025), channel_id=1, source_target_pairs={{0,8},{8,0},{1,9},{9,1},{2,10},{10,2},{3,11},{11,3},{4,12},{12,4},... | collective-permute-start | bytes 1966088 | tf_op jit(solution)/shard_map/ppermute | solution.py:46
  466.1 92.1 %collective-permute-start.51 = (bf16[4,56,1152]{2,1,0:T(8,128)(2,1)S(1)}, bf16[4,56,1152]{2,1,0:T(8,128)(2,1)}, u32[]{:S(2)}, u32[]{:S(2)}) collective-permute-start(bf16[4,56,1152]{2,1,0:T(8,128)(2,1)S(1)} %bitcast.275), channel_id=1, source_target_pairs={{0,24},{16,0},{8,16},{24,8},{1,25},{17,1},{9,17},{25,9},{2,26},{18... | collective-permute-start | bytes 1548296 | tf_op jit(solution)/shard_map/ppermute | solution.py:51
  467.0 91.2 %collective-permute-start.52 = (bf16[4,56,1152]{2,1,0:T(8,128)(2,1)S(1)}, bf16[4,56,1152]{2,1,0:T(8,128)(2,1)}, u32[]{:S(2)}, u32[]{:S(2)}) collective-permute-start(bf16[4,56,1152]{2,1,0:T(8,128)(2,1)S(1)} %bitcast.274), channel_id=1, source_target_pairs={{0,8},{16,24},{8,0},{24,16},{1,9},{17,25},{9,1},{25,17},{2,10},{18... | collective-permute-start | bytes 1548296 | tf_op jit(solution)/shard_map/ppermute | solution.py:51
  577.8 41.4 %collective-permute-start.60 = (bf16[1536,640]{1,0:T(8,128)(2,1)}, bf16[1536,640]{1,0:T(8,128)(2,1)}, u32[]{:S(2)}, u32[]{:S(2)}) collective-permute-start(bf16[1536,640]{1,0:T(8,128)(2,1)} %add_convert_fusion.2), channel_id=1, source_target_pairs={{0,1},{1,0},{2,3},{3,2},{4,5},{5,4},{6,7},{7,6},{8,9},{9,8},{10,11... | collective-permute-start | bytes 5898248 | tf_op jit(solution)/shard_map/ppermute | solution.py:42
  603.9 19.2 %collective-permute-start.59 = (bf16[1536,768]{0,1:T(8,128)(2,1)}, bf16[1536,768]{0,1:T(8,128)(2,1)}, u32[]{:S(2)}, u32[]{:S(2)}) collective-permute-start(bf16[1536,768]{0,1:T(8,128)(2,1)} %pad_maximum_fusion.5), channel_id=1, source_target_pairs={{0,1},{1,0},{2,3},{3,2},{4,5},{5,4},{6,7},{7,6},{8,9},{9,8},{10,11... | collective-permute-start | bytes 7077896 | tf_op jit(solution)/shard_map/ppermute | solution.py:42
  605.1 30.6 %all-to-all-start.5 = ((bf16[8,32,896]{2,1,0:T(8,128)(2,1)}), bf16[8,32,896]{2,1,0:T(8,128)(2,1)}, u32[]{:S(2)}, u32[]{:S(2)}) async-start(bf16[8,32,896]{2,1,0:T(8,128)(2,1)} %bitcast.276), calls=%async_computation.5 | async-start | bytes 917504 | tf_op jit(solution)/shard_map/all_to_all | solution.py:34
  612.3 30.5 %collective-permute-start.63 = (bf16[56,1152]{1,0:T(8,128)(2,1)}, bf16[56,1152]{1,0:T(8,128)(2,1)}, u32[]{:S(2)}, u32[]{:S(2)}) collective-permute-start(bf16[56,1152]{1,0:T(8,128)(2,1)} %get-tuple-element.240), channel_id=1, source_target_pairs={{0,96},{32,0},{64,32},{96,64},{1,97},{33,1},{65,33},{97,65},{2,98}... | collective-permute-start | bytes 387080 | tf_op jit(solution)/shard_map/ppermute | solution.py:51
  612.3 30.5 %collective-permute-start.64 = (bf16[56,1152]{1,0:T(8,128)(2,1)}, bf16[56,1152]{1,0:T(8,128)(2,1)}, u32[]{:S(2)}, u32[]{:S(2)}) collective-permute-start(bf16[56,1152]{1,0:T(8,128)(2,1)} %get-tuple-element.239), channel_id=1, source_target_pairs={{0,64},{32,96},{64,0},{96,32},{1,65},{33,97},{65,1},{97,33},{2,66}... | collective-permute-start | bytes 387080 | tf_op jit(solution)/shard_map/ppermute | solution.py:51
  615.0 27.8 %collective-permute-start.65 = (bf16[56,1152]{1,0:T(8,128)(2,1)}, bf16[56,1152]{1,0:T(8,128)(2,1)}, u32[]{:S(2)}, u32[]{:S(2)}) collective-permute-start(bf16[56,1152]{1,0:T(8,128)(2,1)} %get-tuple-element.238), channel_id=1, source_target_pairs={{0,32},{32,64},{64,96},{96,0},{1,33},{33,65},{65,97},{97,1},{2,34}... | collective-permute-start | bytes 387080 | tf_op jit(solution)/shard_map/ppermute | solution.py:51
  635.7 62.4 %all-to-all-start.4 = ((bf16[64,24,1408]{2,1,0:T(8,128)(2,1)}), bf16[64,24,1408]{2,1,0:T(8,128)(2,1)}, u32[]{:S(2)}, u32[]{:S(2)}) async-start(bf16[64,24,1408]{2,1,0:T(8,128)(2,1)} %pad_maximum_fusion.1), calls=%async_computation.4 | async-start | bytes 8650752 | tf_op jit(solution)/shard_map/all_to_all | solution.py:34
  663.4 31.0 %collective-permute-start.66 = (bf16[56,1152]{1,0:T(8,128)(2,1)}, bf16[56,1152]{1,0:T(8,128)(2,1)}, u32[]{:S(2)}, u32[]{:S(2)}) collective-permute-start(bf16[56,1152]{1,0:T(8,128)(2,1)} %add_convert_fusion.4), channel_id=1, source_target_pairs={{0,0},{8,1},{16,2},{24,3},{32,4},{40,5},{48,6},{56,7},{64,8},{72,9... | collective-permute-start | bytes 387080 | tf_op jit(solution)/shard_map/ppermute | solution.py:509
  (189 other events, 2082.8 us)

commit v6 on v5

--- a/solution.py
+++ b/solution.py
@@ -9,6 +9,7 @@
 BF = jnp.bfloat16
 F32 = jnp.float32
 
+PLANE = ("z", "xl", "xh")
 CHIPS = ("z", "xl", "xh", "y")
 EVERY = ("z", "xl", "xh", "y", "c")
 SIZES = dict(z=4, xl=2, xh=2, y=4, c=2)
@@ -77,6 +78,22 @@
     return jnp.stack([x] + [shift(x, axis, k) for k in (1, 2, 3)])
 
 
+def leave(x, axis, dim, at_z, at_x):
+    parts = []
+    for k in range(4):
+        place = (at_z - k) % 4 if axis == "z" else (at_x - k) % 4 % 2 * 2 + (at_x - k) % 4 // 2
+        block = lax.dynamic_index_in_dim(x, place, dim, keepdims=False)
+        parts.append(shift(block, axis, 4 - k) if k else block)
+    return parts
+
+
+def add(parts):
+    total = parts[0].astype(F32)
+    for p in parts[1:]:
+        total = total + p.astype(F32)
+    return total
+
+
 def norm_parts(values, gain):
     scale = lax.rsqrt(jnp.mean(values * values, axis=-1, keepdims=True) + EPSILON)
     n = values * scale
@@ -86,7 +103,7 @@
 def norm_back(scale, n, gain, grad):
     m = grad * (1.0 + gain)
     back = scale * (m - n * jnp.mean(m * n, axis=-1, keepdims=True))
-    return back, jnp.sum(grad * n, axis=0, keepdims=True)
+    return back
 
 
 def turn(x, cos, sin):
@@ -116,7 +133,7 @@
 
 
 def after(done, *values):
-    return lax.optimization_barrier(values + (done,))
+    return tuple(lax.optimization_barrier((v, done))[0] for v in values) + (done,)
 
 
 def table(rows, columns):
@@ -179,18 +196,12 @@
     lower, upper = pick(is_first, keep, other_core(send))
     att_own = jnp.concatenate([lower, upper], axis=0)
     raw_one = gather_chips(att_own)
-    raw_two = other_core(raw_one)
     (layer_input, wg, wu, bg, bu, wd, ad, ag, au, wo, ao, bo, bd, segment, position, core, at_z, _) = after(
         att_own,
         layer_input, wg, wu, bg, bu, wd, ad, ag, au, wo, ao, bo, bd, segment, position, core, at_z,
     )
     is_first = core == 0
     hidden = layer_input[0].astype(F32)
-    marks = raw_one.reshape(128, 12, 1152)[:, 9, 768:896]
-    gain_one_full = marks[:, :9].reshape(1, 1152).astype(F32)
-    gain_two_full = marks[:, 9:18].reshape(1, 1152).astype(F32)
-    valid_count = jnp.sum(marks[:, 18].astype(F32))
-    raw = [raw_one.reshape(1536, 1152), raw_two.reshape(1536, 1152)]
 
     def output_half(k):
         wide = jnp.concatenate([m[:, 512 * k : 512 * k + 640] for m in (wo, bo, bd)], axis=0)
@@ -240,16 +251,22 @@
     down_own = lax.ppermute(
         jnp.pad(jnp.concatenate([wd, ad], axis=1), ((0, 2), (0, 0))), EVERY, down_route()
     )
-    down_line = gather_line(down_own, "z")
-    down_line, _ = after(raw_one, down_line)
-    down_lines = [down_line] + [shift(down_line, "x", k) for k in (1, 2, 3)]
-
+    raw_one, _ = after(ff_own, raw_one)
+    raw_two = other_core(raw_one)
+    marks = raw_one.reshape(128, 12, 1152)[:, 9, 768:896]
+    gain_one_full = marks[:, :9].reshape(1, 1152).astype(F32)
+    gain_two_full = marks[:, 9:18].reshape(1, 1152).astype(F32)
+    valid_count = jnp.sum(marks[:, 18].astype(F32))
     out_own, _ = after(raw_one, out_own)
-    out_one = gather_chips(out_own)
+    out_wide = jnp.broadcast_to(out_own[None], (64, 24, 1024))
+    out_one = exchange(out_wide, CHIPS)
     out_two = other_core(out_one)
     raw_out = [out_one.reshape(1536, 1024), out_two.reshape(1536, 1024)]
+    raw_one, raw_two, _ = after(out_wide, raw_one, raw_two)
+    raw = [raw_one.reshape(1536, 1152), raw_two.reshape(1536, 1152)]
     ff_own, _ = after(out_one, ff_own)
-    ff_all = exchange(jnp.broadcast_to(ff_own[None], (16, 176, 896)), ("z", "xl", "xh"))
+    ff_wide = jnp.broadcast_to(ff_own[None], (16, 176, 896))
+    ff_all = exchange(ff_wide, PLANE)
 
     ids = jnp.arange(1536, dtype=jnp.int32)
     dev, j = 2 * (ids // 24) + (ids % 24) // 12, ids % 12
@@ -260,18 +277,11 @@
     features = jnp.arange(1152, dtype=jnp.int32)
     put_rows = table(features, jnp.where(j < 9, 9 * dev + j, -1))
     put_inner = table(inner_ids, jnp.where((j >= 9) & (j < 11), 2 * dev + j - 9, -1))
-    put_marks = table(features // 9, jnp.where(j == 11, dev, -1))
+    take_b = table(halves, jnp.where((j >= 9) & (j < 11), 2 * dev + j - 9, -1))
+    take_b_out = table(halves, jnp.where((j >= 8) & (j < 10), 2 * dev + j - 8, -1))
     put_mix = table(head_ids, jnp.where(j < 8, 8 * dev + j, -1))
     put_inner_out = table(inner_ids, jnp.where((j >= 8) & (j < 10), 2 * dev + j - 8, -1))
     put_inner_down = table(halves, jnp.where(j >= 10, 2 * dev + j - 10, -1))
-
-    def plane(block):
-        kx, kz = block // 4, block % 4
-        x = (at_x - kx) % 4
-        return (((at_z - kz) % 4) * 2 + x % 2) * 2 + x // 2
-
-    hidden_ids = jnp.arange(896, dtype=jnp.int32)
-    put_down = table(hidden_ids, 56 * plane(hidden_ids // 56) + hidden_ids % 56)
 
     seq = (at_xh * 4 + at_y) * 2 + core
     tree_seg = segment[0]
@@ -307,6 +317,7 @@
     kv_line = gather_line(kv_own, "y").reshape(640, 512)
     kv_mine = jnp.concatenate([kv_line, other_half(kv_line)], axis=0)
     kv = jnp.concatenate([kv_mine, other_core(kv_mine)], axis=0)
+    kv, _ = after(ff_wide, kv)
     keys, values = kv[:, :256], kv[:, 256:]
     queries = [dot(sides[0], raw[i][:, :512]) for i in (0, 1)]
     q_rows = jnp.concatenate(
@@ -329,18 +340,22 @@
     scale_two, n_two, u_two = norm_parts(after_att, gain_two_full)
     u_all = gather_tokens(u_two)
 
-    down_lines, _ = after(u_two, down_lines)
-    down_raw = jnp.concatenate(down_lines, axis=0).reshape(896, 1408)
-    left, right = pick(is_first, *[dot(put_inner_down, raw_out[i][:, :640]).astype(BF) for i in (0, 1)])
+    raw_late, out_late, ff_all, _ = after(u_two, raw, raw_out, ff_all)
+    down_own, _ = after(ff_all, down_own)
+    down_raw = exchange(jnp.broadcast_to(down_own[None], (16, 56, 1408)), PLANE).reshape(896, 1408)
+    b_left, b_right = pick(is_first, *[dot(take_b, raw_late[i][:, :768]).astype(BF) for i in (0, 1)])
+    left, right = pick(is_first, *[dot(take_b_out, out_late[i][:, :640]).astype(BF) for i in (0, 1)])
+    b_out = jnp.concatenate([left, right[:, 128:]], axis=1)
+    left, right = pick(is_first, *[dot(put_inner_down, out_late[i][:, :640]).astype(BF) for i in (0, 1)])
     b_down = jnp.concatenate([left, right[:, 128:]], axis=1)
-    a_down = dot(put_down, down_raw[:, 1152:]).astype(BF)
-    w_down = (dot(put_down, down_raw[:, :1152]) + dot(a_down, b_down)).astype(BF)
-    a_gate, a_up = pick(is_first, *[dot(put_rows, raw_out[i][:, 768:]).astype(BF) for i in (0, 1)])
-    ff_all, _ = after(w_down, ff_all)
+    a_gate, a_up = pick(is_first, *[dot(put_rows, out_late[i][:, 768:]).astype(BF) for i in (0, 1)])
     b_gate = ff_all[:, 144:160].reshape(256, 896)
     b_up = ff_all[:, 160:].reshape(256, 896)
     w_gate = (ff_all[:, :72].reshape(1152, 896).astype(F32) + dot(a_gate, b_gate)).astype(BF)
     w_up = (ff_all[:, 72:144].reshape(1152, 896).astype(F32) + dot(a_up, b_up)).astype(BF)
+
+    a_down = down_raw[:, 1152:]
+    w_down = (down_raw[:, :1152].astype(F32) + dot(a_down, b_down)).astype(BF)
 
     gate = dot(u_all, w_gate)
     up = dot(u_all, w_up)
@@ -361,26 +376,24 @@
     g_u_two = scatter_tokens(g_u_part)
     u_all, act, g_all, g_gate, g_up, _ = after(g_u_part, u_all, act, g_all, g_gate, g_up)
     gw_gate = dot_tl(u_all, g_gate).astype(BF)
+    gb_gate = dot_tl(a_gate, gw_gate).astype(BF)
+    gate_grads = jnp.concatenate([gw_gate.reshape(16, 72, 896), gb_gate.reshape(16, 16, 896)], axis=1)
+    gate_first = leave(gate_grads.reshape(4, 4, 88, 896), "z", 0, at_z, at_x)
+    gate_first, _ = after(g_u_two, gate_first)
+    gate_line = add(gate_first).astype(BF)
+    gate_second = leave(gate_line, "x", 0, at_z, at_x)
     gw_up = dot_tl(u_all, g_up).astype(BF)
-    gb_gate = dot_tl(a_gate, gw_gate).astype(BF)
     gb_up = dot_tl(a_up, gw_up).astype(BF)
-    ff_grads = jnp.concatenate(
-        [
-            gw_gate.reshape(16, 72, 896),
-            gw_up.reshape(16, 72, 896),
-            gb_gate.reshape(16, 16, 896),
-            gb_up.reshape(16, 16, 896),
-        ],
-        axis=1,
-    )
-    ff_parts = exchange(ff_grads, ("z", "xl", "xh"))
+    up_grads = jnp.concatenate([gw_up.reshape(16, 72, 896), gb_up.reshape(16, 16, 896)], axis=1)
+    up_first = leave(up_grads.reshape(4, 4, 88, 896), "x", 1, at_z, at_x)
+    up_first, _ = after(g_u_two, up_first)
+    up_line = add(up_first).astype(BF)
+    up_second = leave(up_line, "z", 0, at_z, at_x)
     gw_down = dot_tl(act, g_all).astype(BF)
     gb_down = dot_tl(a_down, gw_down).astype(BF)
-    gw_down = dot_tl(put_down, gw_down).astype(BF)
-    down_pieces = gw_down.reshape(4, 4, 56, 1152)
-    down_first = [down_pieces[0]] + [shift(down_pieces[k], "x", 4 - k) for k in (1, 2, 3)]
-
-    norm_two_back, g_gain_two = norm_back(scale_two, n_two, gain_two_full, g_u_two)
+    down_first = leave(gw_down.reshape(4, 4, 56, 1152), "z", 0, at_z, at_x)
+
+    norm_two_back = norm_back(scale_two, n_two, gain_two_full, g_u_two)
     g_after = grad_result + norm_two_back
     g_after_b = g_after.astype(BF)
     once = jnp.where(jnp.arange(640) < 128, 0, 1).astype(BF)[None]
@@ -399,6 +412,7 @@
     probs = jnp.where(allowed, jnp.exp(scores_again - lse), 0.0)
     g_probs = dot_tr(g_rows, values)
     g_scores = (probs * (g_probs - jnp.sum(probs * g_probs, axis=-1, keepdims=True))).astype(BF)
+    g_scores, probs, _ = after((gate_line, up_line), g_scores, probs)
     g_keys = dot_tl(g_scores, q_rows) * score_scale
     g_values = dot_tl(probs.astype(BF), g_rows)
     g_kv = jnp.concatenate([g_keys, g_values], axis=1)
@@ -410,8 +424,8 @@
     g_line = g_line.astype(BF)
     for k in (1, 2, 3):
         g_kv_own = g_kv_own + shift(g_line[TOKENS * k : TOKENS * (k + 1)], "y", 4 - k).astype(F32)
-    g_scores, side_out, ff_parts, down_first, gb_down, _ = after(
-        g_kv_b, g_scores, side_out, ff_parts, down_first, gb_down
+    g_scores, side_out, gate_second, up_second, down_first, gb_down, _ = after(
+        g_kv_b, g_scores, side_out, gate_second, up_second, down_first, gb_down
     )
     g_q_rows = dot(g_scores, keys) * score_scale
     g_q = [
@@ -421,11 +435,9 @@
         ).astype(BF)
         for i in (0, 1)
     ]
-    down_line = sum(m.astype(F32) for m in down_first).astype(BF)
-    down_second = [down_line[0]] + [shift(down_line[k], "z", 4 - k) for k in (1, 2, 3)]
-    ff_sum = jnp.sum(ff_parts.astype(F32), axis=0).astype(BF)
+    gate_sum, up_sum = add(gate_second).astype(BF), add(up_second).astype(BF)
     ga_part = jnp.concatenate(
-        [dot_tr(ff_sum[:72], b_gate), dot_tr(ff_sum[72:144], b_up), jnp.zeros((72, 384), F32)], axis=1
+        [dot_tr(gate_sum[:72], b_gate), dot_tr(up_sum[:72], b_up), jnp.zeros((72, 384), F32)], axis=1
     ).astype(BF)
     back_row = jnp.arange(256, dtype=jnp.int32)
     group, line = back_row // 32, back_row % 32
@@ -434,22 +446,60 @@
         9 * group + line,
         jnp.where(
             line < 18,
-            72 + 9 * group + line - 9,
+            88 + 9 * group + line - 9,
             jnp.where(
                 line < 22,
-                144 + 16 * ((line - 18) // 2) + 2 * group + line % 2,
+                72 + 88 * ((line - 18) // 2) + 2 * group + line % 2,
                 jnp.where(line < 31, 176 + 9 * group + line - 22, -1),
             ),
         ),
     )
     leaving = dot(
-        table(take, jnp.arange(248, dtype=jnp.int32)), jnp.concatenate([ff_sum, ga_part], axis=0)
+        table(take, jnp.arange(248, dtype=jnp.int32)), jnp.concatenate([gate_sum, up_sum, ga_part], axis=0)
     ).astype(BF)
     slab = exchange(leaving.reshape(8, 32, 896), ("y", "c"))
+    def of_chip(own, away):
+        return (own.astype(F32) + other_core(away.astype(BF)).astype(F32)).astype(BF).reshape(64, 24, -1)
+
+    def both_halves(owned):
+        mine, away = pick(is_first, owned[:12], owned[12:])
+        return pick(is_first, mine, other_core(away.astype(BF)).astype(F32))
+
+    left, right = pick(is_first, gb_down[:, :640], gb_down[:, 512:])
+    chip_out = of_chip(
+        dot_tl(side_out, g_half[0]) + dot_tl(put_inner_down, left),
+        dot_tl(side_out, g_half[1]) + dot_tl(put_inner_down, right),
+    )
+    loss_high, loss_rest = split_in_two(loss_here)
+    loss_mid, loss_low = split_in_two(loss_rest)
+    lines = jnp.arange(16, dtype=jnp.int32)
+    loss_rows = jnp.where(
+        lines == 0,
+        loss_high.astype(F32),
+        jnp.where(lines == 1, loss_mid.astype(F32), jnp.where(lines == 2, loss_low, 0.0)),
+    )
+    more_side = (loss_rows[:, None] * (j == 11)[None, :]).astype(BF)
+    more_grad = table(jnp.where(lines < 3, lines + 3 * core, -1), jnp.arange(512, dtype=jnp.int32))
+    chip_q = of_chip(
+        *[(dot_tl(sides[0], g_q[i]) + dot_tl(more_side, more_grad)).astype(BF) for i in (0, 1)]
+    )
+    g_kv_own, _ = after((chip_q, chip_out, leaving), g_kv_own)
     g_k = turn_back(g_kv_own[:, :256], cos, sin).astype(BF)
     g_v = g_kv_own[:, 256:].astype(BF)
     g_k = pick(is_first, g_k[:, :128], g_k[:, 128:])
     g_v = pick(is_first, g_v[:, :128], g_v[:, 128:])
+    chip_kv = of_chip(
+        *[
+            jnp.concatenate([dot_tl(sides[1], g_k[i]).astype(BF), dot_tl(sides[2], g_v[i]).astype(BF)], axis=1)
+            for i in (0, 1)
+        ]
+    )
+    chip_sums = jnp.concatenate([chip_q, chip_kv, chip_out], axis=2)
+    parts = exchange(chip_sums, CHIPS)
+    down_first, _ = after(g_kv_own, down_first)
+    down_second = leave(add(down_first).astype(BF), "x", 0, at_z, at_x)
+    slab, down_second, g_q, g_k, g_v, _ = after(chip_sums, slab, down_second, g_q, g_k, g_v)
+
     d_one = None
     for i, (g, first, last) in enumerate(((g_q, 0, 512), (g_k, 512, 640), (g_v, 640, 768))):
         d = dot_tr(g[0], raw[0][:, first:last]) + dot_tr(g[1], raw[1][:, first:last])
@@ -459,90 +509,50 @@
         d = d + dot_tr(gi[:, 128:], raw[1][:, inner_at : inner_at + 128])
         d_one = d if d_one is None else d_one + d
     g_u_one = select_back(d_one, put_rows)
-    norm_one_back, g_gain_one = norm_back(scale_one, n_one, gain_one_full, g_u_one)
-    grad_hidden = (g_after + norm_one_back).astype(BF)
-
-    def of_chip(own, away):
-        return (own.astype(F32) + other_core(away.astype(BF)).astype(F32)).astype(BF).reshape(64, 24, -1)
-
-    def both_halves(owned):
-        mine, away = pick(is_first, owned[:12], owned[12:])
-        return pick(is_first, mine, other_core(away.astype(BF)).astype(F32))
-
-    left, right = pick(is_first, gb_down[:, :640], gb_down[:, 512:])
-    chip_out = of_chip(
-        dot_tl(side_out, g_half[0]) + dot_tl(put_inner_down, left),
-        dot_tl(side_out, g_half[1]) + dot_tl(put_inner_down, right),
-    )
-    loss_high, loss_rest = split_in_two(loss_here)
-    loss_mid, loss_low = split_in_two(loss_rest)
-    loss_low = loss_low.astype(BF)
-    at_row = jnp.arange(32, dtype=jnp.int32)[:, None]
-    nines = (features[None, :] % 9 == at_row % 9) & (at_row < 18)
-    gain_rows = jnp.where(nines, jnp.where(at_row < 9, g_gain_one, g_gain_two), 0.0).astype(BF)
-    loss_rows = jnp.where(
-        at_row == 18, loss_high, jnp.where(at_row == 19, loss_mid, jnp.where(at_row == 20, loss_low, 0))
-    ).astype(F32)
-    more_side = (dot(gain_rows, put_marks) + loss_rows * (j == 11)[None, :]).astype(BF)
-    lines = jnp.arange(32, dtype=jnp.int32)
-    line_at = jnp.where(lines < 18, lines, jnp.where(lines < 21, lines + 3 * core, -1))
-    more_grad = table(line_at, jnp.arange(512, dtype=jnp.int32))
-    sums = [
-        jnp.concatenate(
-            [
-                (dot_tl(sides[0], g_q[i]) + dot_tl(more_side, more_grad)).astype(BF),
-                dot_tl(sides[1], g_k[i]).astype(BF),
-                dot_tl(sides[2], g_v[i]).astype(BF),
-            ],
-            axis=1,
-        )
-        for i in (0, 1)
-    ]
-    chip_sums = jnp.concatenate([of_chip(sums[0], sums[1]), chip_out], axis=2)
-    parts = exchange(chip_sums, CHIPS)
-    slab, down_second, _ = after(chip_sums, slab, down_second)
+    grad_hidden = (g_after + norm_back(scale_one, n_one, gain_one_full, g_u_one)).astype(BF)
 
     narrow = dot_tr(slab.reshape(256, 896), wider).reshape(8, 32, 864)
     wide = jnp.concatenate([narrow[t] for t in range(8)], axis=1)
     ga = jnp.sum(slab[:, 22:31, :512].astype(F32), axis=0)
-    down_sum = sum(m.astype(F32) for m in down_second).astype(BF)
-    gw_down_own = lax.ppermute(down_sum, EVERY, [(b, a) for a, b in down_route()])[:54]
+    gw_down_own = lax.ppermute(
+        add(down_second).astype(BF), EVERY, [(b, a) for a, b in down_route()]
+    )[:54]
     ga_down_own = dot_tr(gw_down_own, b_down)
-    all_owned = jnp.sum(parts.astype(F32), axis=0)
-    owned, owned_out = all_owned[:, :768], all_owned[:, 768:]
-    left, right = both_halves(owned_out)
-    own_out = jnp.concatenate([left, right[:, 128:]], axis=1)
-    d = dot_tr(own_out[:8, :640].astype(BF), pick(is_first, *raw_out)[0][:, :640]) + dot_tr(
-        own_out[:8, 640:].astype(BF), pick(is_first, *raw_out)[1][:, 128:640]
-    )
-    ga_out_own = dot_tr(d.astype(BF), put_inner_out)
-    ga_out_own = jnp.concatenate(pick(is_first, ga_out_own[:, :128], ga_out_own[:, 128:]), axis=1)
-    loss_value = jnp.sum(owned[11, 18:24]) / (1152.0 * valid_count)
+
+    def over_columns(pairs):
+        return sum(jnp.sum(a.astype(F32) * b, axis=1) for a, b in pairs)
+
+    gain_two_own = over_columns(
+        ((wg, wide[:9]), (wu, wide[9:18]), (ag, ga[:, :256]), (au, ga[:, 256:]))
+    ) / (1.0 + gain_two.astype(F32))
+
+    owned = jnp.sum(parts.astype(F32), axis=0)
+    loss_value = jnp.sum(owned[11, :6]) / (1152.0 * valid_count)
     left, right = both_halves(owned)
-    gains = left[11]
-    left_b, right_b = left.astype(BF), right.astype(BF)
-    mine_b, other_b = pick(is_first, left_b, right_b)
-    ga_own = []
-    for first, last in ((0, 512), (512, 640), (640, 768)):
-        d = dot_tr(mine_b[:, first:last], raw[0][:, first:last]) + dot_tr(
-            other_b[:, first:last], raw[1][:, first:last]
-        )
-        g = dot_tr(d.astype(BF), put_inner)[:9]
-        ga_own.append(jnp.concatenate(pick(is_first, g[:, :128], g[:, 128:]), axis=1))
+    own_out = jnp.concatenate([left[:, 768:], right[:, 896:]], axis=1)
+    ga_out_own = dot_tr(own_out[:8].astype(BF), b_out)
+    left_b, right_b = left[:9].astype(BF), right[:9].astype(BF)
+    ga_own = [
+        dot_tr(left_b[:, first:last], b_left[:, first:last])
+        + dot_tr(right_b[:, first:last], b_right[:, first:last])
+        for first, last in ((0, 512), (512, 640), (640, 768))
+    ]
 
     def columns(first, last, rows):
         return jnp.concatenate([left[rows, first:last], right[rows, first:last]], axis=1)
 
     top_rows, low_rows = slice(0, 9), slice(9, 11)
+    gw_own = [columns(0, 512, top_rows), columns(512, 640, top_rows), columns(640, 768, top_rows)]
+    gain_one_own = over_columns(
+        list(zip((wq, wk, wv), gw_own)) + list(zip((aq, ak, av), ga_own))
+    ) / (1.0 + gain_one.astype(F32))
 
     return (
         result.astype(BF)[None],
         loss_value,
         grad_hidden[None],
-        gains[:9],
-        columns(0, 512, top_rows),
-        columns(512, 640, top_rows),
-        columns(640, 768, top_rows),
+        gain_one_own,
+        *gw_own,
         own_out[:8],
         ga_own[0],
         columns(0, 512, low_rows),
@@ -552,7 +562,7 @@
         columns(640, 768, low_rows),
         ga_out_own,
         own_out[8:10],
-        gains[9:18],
+        gain_two_own,
         wide[:9],
         wide[9:18],
         gw_down_own.astype(F32),

time: 756 us -> 696 us (0.921)
  waiting for transfers between devices: 212 us -> 176 us
  other arithmetic: 109 us -> 83.3 us
  matrix products: 184 us -> 166 us
  starting transfers between devices: 134 us -> 151 us
    ppermute x2, waiting for transfers between devices: 73.2 us -> 21.3 us  [other_half(): return lax.ppermute(x, 'xh', [(0, 1), (1, 0)])]
    ppermute x30 -> x36, waiting for transfers between devices: 70 us -> 99 us  [shift(): lax.ppermute(x, RING[axis], [(number[i], number[(i + k) % 4]) for i in ra...]
    ppermute x1, waiting for transfers between devices: 18.8 us -> 0.01 us  [on_device(): lax.ppermute(add(down_second).astype(BF), EVERY, [(b, a) for a, b in down...]
    dot_general x39 -> x38, matrix products: 75.5 us -> 58.2 us  [dot_tr(): lax.dot_general(a, b, (((1,), (1,)), ((), ())), preferred_element_type=F32)]
    all_to_all x6, starting transfers between devices: 42.5 us -> 57 us  [exchange(): return lax.all_to_all(x, axes, split_axis=0, concat_axis=0, tiled=True)]
    ppermute x7, waiting for transfers between devices: 0.02 us -> 12.2 us  [column_shift(): return lax.ppermute(x, ('y', 'c'), route)]
    dot_general x20 -> x19, matrix products: 51.6 us -> 40.2 us  [dot_tl(): lax.dot_general(a, b, (((0,), (0,)), ((), ())), preferred_element_type=F32)]
    dot_general x35 -> x37, matrix products: 56.9 us -> 67.8 us  [dot(): return jnp.dot(a, b, preferred_element_type=F32)]
  transfers between devices with their start and end apart: 73 -> 79, of which waited for: 19 -> 26; matrix products, arithmetic and copies ran while one was open for 33% -> 39% of each run, Pallas kernels for 0% -> 0%
where the time goes in v6:
time: 696 us; the launch traced here: 684 us
  waiting for transfers between devices  176 us (25%)
  matrix products  166 us (24%)
  starting transfers between devices  151 us (22%)
  local copies, waits for them, and re-layouts  99 us (14%)
  other arithmetic  83.3 us (12%)
  between operations  9.16 us (1%)
    ppermute x36, waiting for transfers between devices, shift(): lax.ppermute(x, RING[axis], [(number[i], number[(i + k) % 4]) for i in ra...  99 us
    dot_general x37, matrix products, dot(): return jnp.dot(a, b, preferred_element_type=F32)  67.8 us
    dot_general x38, matrix products, dot_tr(): lax.dot_general(a, b, (((1,), (1,)), ((), ())), preferred_element_type=F32)  58.2 us
    all_to_all x6, starting transfers between devices, exchange(): return lax.all_to_all(x, axes, split_axis=0, concat_axis=0, tiled=True)  57 us
    all_to_all x6, waiting for transfers between devices, exchange(): return lax.all_to_all(x, axes, split_axis=0, concat_axis=0, tiled=True)  43.5 us
    dot_general x19, matrix products, dot_tl(): lax.dot_general(a, b, (((0,), (0,)), ((), ())), preferred_element_type=F32)  40.2 us
    ppermute x36, starting transfers between devices, shift(): lax.ppermute(x, RING[axis], [(number[i], number[(i + k) % 4]) for i in ra...  38.5 us
    unnamed x384, local copies, waits for them, and re-layouts  34.6 us
  transfers between devices with their start and end apart: 79, of which 26 were waited for; matrix products, arithmetic and copies ran while one was open for 39% of the time, Pallas kernels for 0%

profile of v6, /device:TPU:1, one launch (start us, length us, event | category | flops | bytes accessed | tf_op | source)
XLA Modules:
  0.0 684.2 jit_solution(14960330296921246789)
XLA Ops:
  20.4 11.2 %all-to-all-start = ((bf16[64,24,1152]{2,1,0:T(8,128)(2,1)}), bf16[64,24,1152]{2,1,0:T(8,128)(2,1)S(1)}, u32[]{:S(2)}, u32[]{:S(2)}) async-start(bf16[64,24,1152]{2,1,0:T(8,128)(2,1)} %broadcast_in_dim.75), calls=%async_computation | async-start | bytes 7077888 | tf_op jit(solution)/shard_map/all_to_all | solution.py:35
  55.3 10.8 %collective-permute-done.2 = bf16[24,896]{1,0:T(8,128)(2,1)S(1)} collective-permute-done((bf16[24,896]{1,0:T(8,128)(2,1)}, bf16[24,896]{1,0:T(8,128)(2,1)S(1)}, u32[]{:S(2)}, u32[]{:S(2)}) %collective-permute-start.2) | collective-permute-done | bytes 43040 | tf_op jit(solution)/shard_map/ppermute | solution.py:223
  66.1 9.8 %collective-permute-start.7 = (bf16[24,896]{1,0:T(8,128)(2,1)}, bf16[24,896]{1,0:T(8,128)(2,1)S(1)}, u32[]{:S(2)}, u32[]{:S(2)}) collective-permute-start(bf16[24,896]{1,0:T(8,128)(2,1)} %get-tuple-element.337), channel_id=1, source_target_pairs={{0,7},{1,6},{2,1},{3,0},{4,3},{5,2},{6,5},{7,4},{8,15},{9,14},{10,... | collective-permute-start | bytes 129032 | tf_op jit(solution)/shard_map/ppermute | solution.py:223
  107.4 13.4 %all-to-all-start.1 = ((bf16[64,24,1024]{2,1,0:T(8,128)(2,1)}), bf16[64,24,1024]{2,1,0:T(8,128)(2,1)}, u32[]{:S(2)}, u32[]{:S(2)}) async-start(bf16[64,24,1024]{2,1,0:T(8,128)(2,1)} %broadcast_in_dim.78), calls=%async_computation.1 | async-start | bytes 6291456 | tf_op jit(solution)/shard_map/all_to_all | solution.py:35
  143.9 6.3 collective-permute-start.23
  150.9 14.7 %collective-permute-done.10 = bf16[160,512]{1,0:T(8,128)(2,1)} collective-permute-done((bf16[160,512]{1,0:T(8,128)(2,1)}, bf16[160,512]{1,0:T(8,128)(2,1)}, u32[]{:S(2)}, u32[]{:S(2)}) %collective-permute-start.10) | collective-permute-done | bytes 163872 | tf_op jit(solution)/shard_map/ppermute | solution.py:52
  175.0 12.8 %collective-permute-done.13 = bf16[640,512]{1,0:T(8,128)(2,1)S(1)} collective-permute-done((bf16[640,512]{1,0:T(8,128)(2,1)S(1)}, bf16[640,512]{1,0:T(8,128)(2,1)S(1)}, u32[]{:S(2)}, u32[]{:S(2)}) %collective-permute-start.13) | collective-permute-done | bytes 655392 | tf_op jit(solution)/shard_map/ppermute | solution.py:47
  201.6 8.0 %all-to-all-start.2 = ((bf16[16,176,896]{2,1,0:T(8,128)(2,1)}), bf16[16,176,896]{2,1,0:T(8,128)(2,1)}, u32[]{:S(2)}, u32[]{:S(2)}) async-start(bf16[16,176,896]{2,1,0:T(8,128)(2,1)} %broadcast_in_dim.79), calls=%async_computation.2 | async-start | bytes 10092544 | tf_op jit(solution)/shard_map/all_to_all | solution.py:35
  253.8 23.5 %all-to-all-done.2 = bf16[16,176,896]{2,1,0:T(8,128)(2,1)} async-done(((bf16[16,176,896]{2,1,0:T(8,128)(2,1)}), bf16[16,176,896]{2,1,0:T(8,128)(2,1)}, u32[]{:S(2)}, u32[]{:S(2)}) %all-to-all-start.2) | async-done | bytes 5046304 | tf_op jit(solution)/shard_map/all_to_all | solution.py:35
  277.3 4.6 fusion.591
  284.4 8.8 %all-to-all-start.3 = ((bf16[16,56,1408]{2,1,0:T(8,128)(2,1)}), bf16[16,56,1408]{2,1,0:T(8,128)(2,1)}, u32[]{:S(2)}, u32[]{:S(2)}) async-start(bf16[16,56,1408]{2,1,0:T(8,128)(2,1)} %broadcast_in_dim.82), calls=%async_computation.3 | async-start | bytes 5046272 | tf_op jit(solution)/shard_map/all_to_all | solution.py:35
  299.6 5.3 fusion.613
  307.2 8.4 %multiply_convert_fusion.1 = (bf16[1280,896]{1,0:T(8,128)(2,1)}, f32[1280,896]{1,0:T(8,128)}) fusion(f32[1280,896]{1,0:T(8,128)S(1)} %fusion.613, bf16[1280,1152]{1,0:T(8,128)(2,1)} %constant_dynamic-update-slice_fusion.28, bf16[1152,896]{1,0:T(8,128)(2,1)S(1)} %fusion.31), kind=kOutput, calls=%fused_computation.42 | convolution fusion | flops 2653880320 | bytes 16482304 | tf_op jit(solution)/shard_map/dot_general | solution.py:23
  315.5 9.2 %all-to-all-done.3 = bf16[16,56,1408]{2,1,0:T(8,128)(2,1)} async-done(((bf16[16,56,1408]{2,1,0:T(8,128)(2,1)}), bf16[16,56,1408]{2,1,0:T(8,128)(2,1)}, u32[]{:S(2)}, u32[]{:S(2)}) %all-to-all-start.3) | async-done | bytes 2523168 | tf_op jit(solution)/shard_map/all_to_all | solution.py:35
  343.9 7.4 %collective-permute-done.25 = bf16[160,1152]{1,0:T(8,128)(2,1)S(1)} collective-permute-done((bf16[160,1152]{1,0:T(8,128)(2,1)S(1)}, bf16[160,1152]{1,0:T(8,128)(2,1)S(1)}, u32[]{:S(2)}, u32[]{:S(2)}) %collective-permute-start.25) | collective-permute-done | bytes 368672 | tf_op jit(solution)/shard_map/ppermute | solution.py:52
  351.3 4.7 collective-permute-done.27
  370.7 10.9 %collective-permute-done.31 = bf16[160,1152]{1,0:T(8,128)(2,1)} collective-permute-done((bf16[160,1152]{1,0:T(8,128)(2,1)}, bf16[160,1152]{1,0:T(8,128)(2,1)}, u32[]{:S(2)}, u32[]{:S(2)}) %collective-permute-start.31) | collective-permute-done | bytes 368672 | tf_op jit(solution)/shard_map/ppermute | solution.py:52
  388.2 9.9 %fusion.10 = (bf16[1280,896]{1,0:T(8,128)(2,1)S(1)}, bf16[1280,896]{1,0:T(8,128)(2,1)S(1)}) fusion(f32[1280,896]{1,0:T(8,128)} %copy-done.173, f32[1280,896]{1,0:T(8,128)} %get-tuple-element.425, bf16[1280,1152]{1,0:T(8,128)(2,1)S(1)} %constant_dynamic-update-slice_fusion.36, bf16[896,1152]{1,0:T(8,128)(2,1)S(1)} %copy-done.163), kind=kOutput, calls=%fused_computation.34 | convolution fusion | flops 2672230400 | bytes 18776064 | tf_op jit(solution)/shard_map/dot_general | solution.py:31
  406.9 5.1 convolution_convert_fusion.1
  415.7 5.1 convolution_convert_fusion.2
  427.2 5.2 collective-permute-done.39
  432.5 6.5 collective-permute-done.41
  452.3 4.3 collective-permute-done.50
  462.1 10.7 %collective-permute-done.47 = bf16[4,88,896]{2,1,0:T(8,128)(2,1)} collective-permute-done((bf16[4,88,896]{2,1,0:T(8,128)(2,1)}, bf16[4,88,896]{2,1,0:T(8,128)(2,1)}, u32[]{:S(2)}, u32[]{:S(2)}) %collective-permute-start.47) | collective-permute-done | bytes 630816 | tf_op jit(solution)/shard_map/ppermute | solution.py:52
  472.8 5.1 multiply_reduce_fusion
  510.9 10.0 %collective-permute-done.61 = bf16[88,896]{1,0:T(8,128)(2,1)S(1)} collective-permute-done((bf16[88,896]{1,0:T(8,128)(2,1)S(1)}, bf16[88,896]{1,0:T(8,128)(2,1)S(1)}, u32[]{:S(2)}, u32[]{:S(2)}) %collective-permute-start.61) | collective-permute-done | bytes 157728 | tf_op jit(solution)/shard_map/ppermute | solution.py:52
  536.9 8.5 %collective-permute-done.53 = bf16[640,512]{1,0:T(8,128)(2,1)S(1)} collective-permute-done((bf16[640,512]{1,0:T(8,128)(2,1)S(1)}, bf16[640,512]{1,0:T(8,128)(2,1)S(1)}, u32[]{:S(2)}, u32[]{:S(2)}) %collective-permute-start.53) | collective-permute-done | bytes 655392 | tf_op jit(solution)/shard_map/ppermute | solution.py:47
  552.9 8.7 %collective-permute-done.68 = bf16[4,56,1152]{2,1,0:T(8,128)(2,1)S(1)} collective-permute-done((bf16[4,56,1152]{2,1,0:T(8,128)(2,1)S(1)}, bf16[4,56,1152]{2,1,0:T(8,128)(2,1)S(1)}, u32[]{:S(2)}, u32[]{:S(2)}) %collective-permute-start.68) | collective-permute-done | bytes 516128 | tf_op jit(solution)/shard_map/ppermute | solution.py:52
  563.3 6.4 all-to-all-start.5
  572.5 4.5 add_convert_fusion.2
  601.7 9.2 %all-to-all-start.4 = ((bf16[64,24,1408]{2,1,0:T(8,128)(2,1)}), bf16[64,24,1408]{2,1,0:T(8,128)(2,1)}, u32[]{:S(2)}, u32[]{:S(2)}) async-start(bf16[64,24,1408]{2,1,0:T(8,128)(2,1)} %pad_maximum_fusion), calls=%async_computation.4 | async-start | bytes 8650752 | tf_op jit(solution)/shard_map/all_to_all | solution.py:35
  656.6 10.8 %all-to-all-done.4 = bf16[64,24,1408]{2,1,0:T(8,128)(2,1)} async-done(((bf16[64,24,1408]{2,1,0:T(8,128)(2,1)}), bf16[64,24,1408]{2,1,0:T(8,128)(2,1)}, u32[]{:S(2)}, u32[]{:S(2)}) %all-to-all-start.4) | async-done | bytes 4325408 | tf_op jit(solution)/shard_map/all_to_all | solution.py:35
  (777 shorter events, 395.3 us)
Async XLA Ops:
  20.4 58.7 %all-to-all-start = ((bf16[64,24,1152]{2,1,0:T(8,128)(2,1)}), bf16[64,24,1152]{2,1,0:T(8,128)(2,1)S(1)}, u32[]{:S(2)}, u32[]{:S(2)}) async-start(bf16[64,24,1152]{2,1,0:T(8,128)(2,1)} %broadcast_in_dim.75), calls=%async_computation | async-start | bytes 7077888 | tf_op jit(solution)/shard_map/all_to_all | solution.py:35
  48.3 27.6 %collective-permute-start.3 = (bf16[24,896]{1,0:T(8,128)(2,1)}, bf16[24,896]{1,0:T(8,128)(2,1)S(1)}, u32[]{:S(2)}, u32[]{:S(2)}) collective-permute-start(bf16[24,896]{1,0:T(8,128)(2,1)} %get-tuple-element.341), channel_id=1, source_target_pairs={{0,3},{1,2},{2,5},{3,4},{4,7},{5,6},{6,1},{7,0},{8,11},{9,10},{10,... | collective-permute-start | bytes 129032 | tf_op jit(solution)/shard_map/ppermute | solution.py:223
  49.7 26.3 %collective-permute-start.4 = (bf16[24,896]{1,0:T(8,128)(2,1)}, bf16[24,896]{1,0:T(8,128)(2,1)S(1)}, u32[]{:S(2)}, u32[]{:S(2)}) collective-permute-start(bf16[24,896]{1,0:T(8,128)(2,1)} %get-tuple-element.340), channel_id=1, source_target_pairs={{0,4},{1,5},{2,6},{3,7},{4,0},{5,1},{6,2},{7,3},{8,12},{9,13},{10,... | collective-permute-start | bytes 129032 | tf_op jit(solution)/shard_map/ppermute | solution.py:223
  51.3 25.8 %collective-permute-start.5 = (bf16[24,896]{1,0:T(8,128)(2,1)}, bf16[24,896]{1,0:T(8,128)(2,1)S(1)}, u32[]{:S(2)}, u32[]{:S(2)}) collective-permute-start(bf16[24,896]{1,0:T(8,128)(2,1)} %get-tuple-element.339), channel_id=1, source_target_pairs={{0,5},{1,4},{2,7},{3,6},{4,1},{5,0},{6,3},{7,2},{8,13},{9,12},{10,... | collective-permute-start | bytes 129032 | tf_op jit(solution)/shard_map/ppermute | solution.py:223
  53.0 24.1 %collective-permute-start.6 = (bf16[24,896]{1,0:T(8,128)(2,1)}, bf16[24,896]{1,0:T(8,128)(2,1)S(1)}, u32[]{:S(2)}, u32[]{:S(2)}) collective-permute-start(bf16[24,896]{1,0:T(8,128)(2,1)} %get-tuple-element.338), channel_id=1, source_target_pairs={{0,6},{1,7},{2,0},{3,1},{4,2},{5,3},{6,4},{7,5},{8,14},{9,15},{10,... | collective-permute-start | bytes 129032 | tf_op jit(solution)/shard_map/ppermute | solution.py:223
  79.1 48.3 %collective-permute-start.9 = (bf16[64,24,1152]{2,1,0:T(8,128)(2,1)S(1)}, bf16[64,24,1152]{2,1,0:T(8,128)(2,1)}, u32[]{:S(2)}, u32[]{:S(2)}) collective-permute-start(bf16[64,24,1152]{2,1,0:T(8,128)(2,1)S(1)} %all-to-all-done), channel_id=1, source_target_pairs={{0,1},{1,0},{2,3},{3,2},{4,5},{5,4},{6,7},{7,6},{8,9},{9,8},{10,11... | collective-permute-start | bytes 10616840 | tf_op jit(solution)/shard_map/ppermute | solution.py:43
  107.4 90.7 %all-to-all-start.1 = ((bf16[64,24,1024]{2,1,0:T(8,128)(2,1)}), bf16[64,24,1024]{2,1,0:T(8,128)(2,1)}, u32[]{:S(2)}, u32[]{:S(2)}) async-start(bf16[64,24,1024]{2,1,0:T(8,128)(2,1)} %broadcast_in_dim.78), calls=%async_computation.1 | async-start | bytes 6291456 | tf_op jit(solution)/shard_map/all_to_all | solution.py:35
  135.9 29.7 %collective-permute-start.10 = (bf16[160,512]{1,0:T(8,128)(2,1)}, bf16[160,512]{1,0:T(8,128)(2,1)}, u32[]{:S(2)}, u32[]{:S(2)}) collective-permute-start(bf16[160,512]{1,0:T(8,128)(2,1)} %pad_maximum_fusion.10), channel_id=1, source_target_pairs={{0,2},{2,4},{4,6},{6,0},{1,3},{3,5},{5,7},{7,1},{8,10},{10,12},{12... | collective-permute-start | bytes 491528 | tf_op jit(solution)/shard_map/ppermute | solution.py:52
  137.1 31.9 %collective-permute-start.11 = (bf16[160,512]{1,0:T(8,128)(2,1)}, bf16[160,512]{1,0:T(8,128)(2,1)}, u32[]{:S(2)}, u32[]{:S(2)}) collective-permute-start(bf16[160,512]{1,0:T(8,128)(2,1)} %pad_maximum_fusion.10), channel_id=1, source_target_pairs={{0,4},{2,6},{4,0},{6,2},{1,5},{3,7},{5,1},{7,3},{8,12},{10,14},{12... | collective-permute-start | bytes 491528 | tf_op jit(solution)/shard_map/ppermute | solution.py:52
  139.5 29.5 %collective-permute-start.12 = (bf16[160,512]{1,0:T(8,128)(2,1)}, bf16[160,512]{1,0:T(8,128)(2,1)}, u32[]{:S(2)}, u32[]{:S(2)}) collective-permute-start(bf16[160,512]{1,0:T(8,128)(2,1)} %pad_maximum_fusion.10), channel_id=1, source_target_pairs={{0,6},{2,0},{4,2},{6,4},{1,7},{3,1},{5,3},{7,5},{8,14},{10,8},{12,... | collective-permute-start | bytes 491528 | tf_op jit(solution)/shard_map/ppermute | solution.py:52
  143.9 137.9 %collective-permute-start.23 = (bf16[56,1408]{1,0:T(8,128)(2,1)}, bf16[56,1408]{1,0:T(8,128)(2,1)}, u32[]{:S(2)}, u32[]{:S(2)}) collective-permute-start(bf16[56,1408]{1,0:T(8,128)(2,1)} %fusion.327), channel_id=1, source_target_pairs={{0,0},{1,8},{2,16},{3,24},{4,32},{5,40},{6,48},{7,56},{8,64},{9,72... | collective-permute-start | bytes 473096 | tf_op jit(solution)/shard_map/ppermute | solution.py:251
  189.1 23.7 %collective-permute-start.14 = (bf16[1280,512]{1,0:T(8,128)(2,1)}, bf16[1280,512]{1,0:T(8,128)(2,1)}, u32[]{:S(2)}, u32[]{:S(2)}) collective-permute-start(bf16[1280,512]{1,0:T(8,128)(2,1)} %pad_maximum_fusion.3), channel_id=1, source_target_pairs={{0,1},{1,0},{2,3},{3,2},{4,5},{5,4},{6,7},{7,6},{8,9},{9,8},{10,11... | collective-permute-start | bytes 3932168 | tf_op jit(solution)/shard_map/ppermute | solution.py:43
  201.6 75.7 %all-to-all-start.2 = ((bf16[16,176,896]{2,1,0:T(8,128)(2,1)}), bf16[16,176,896]{2,1,0:T(8,128)(2,1)}, u32[]{:S(2)}, u32[]{:S(2)}) async-start(bf16[16,176,896]{2,1,0:T(8,128)(2,1)} %broadcast_in_dim.79), calls=%async_computation.2 | async-start | bytes 10092544 | tf_op jit(solution)/shard_map/all_to_all | solution.py:35
  227.7 20.1 %collective-permute-start.17 = (bf16[160,1152]{1,0:T(8,128)(2,1)S(1)}, bf16[160,1152]{1,0:T(8,128)(2,1)S(1)}, u32[]{:S(2)}, u32[]{:S(2)}) collective-permute-start(bf16[160,1152]{1,0:T(8,128)(2,1)S(1)} %get-tuple-element.266), channel_id=1, source_target_pairs={{0,4},{2,6},{4,0},{6,2},{1,5},{3,7},{5,1},{7,3},{8,12},{10,14},{12... | collective-permute-start | bytes 1105928 | tf_op jit(solution)/shard_map/ppermute | solution.py:52
  230.3 20.4 %collective-permute-start.19 = (bf16[160,1152]{1,0:T(8,128)(2,1)S(1)}, bf16[160,1152]{1,0:T(8,128)(2,1)S(1)}, u32[]{:S(2)}, u32[]{:S(2)}) collective-permute-start(bf16[160,1152]{1,0:T(8,128)(2,1)S(1)} %get-tuple-element.266), channel_id=1, source_target_pairs={{0,1},{1,0},{2,3},{3,2},{4,5},{5,4},{6,7},{7,6},{8,9},{9,8},{10,11... | collective-permute-start | bytes 1105928 | tf_op jit(solution)/shard_map/ppermute | solution.py:43
  284.4 40.3 %all-to-all-start.3 = ((bf16[16,56,1408]{2,1,0:T(8,128)(2,1)}), bf16[16,56,1408]{2,1,0:T(8,128)(2,1)}, u32[]{:S(2)}, u32[]{:S(2)}) async-start(bf16[16,56,1408]{2,1,0:T(8,128)(2,1)} %broadcast_in_dim.82), calls=%async_computation.3 | async-start | bytes 5046272 | tf_op jit(solution)/shard_map/all_to_all | solution.py:35
  362.5 20.4 %collective-permute-start.32 = (bf16[160,1152]{1,0:T(8,128)(2,1)}, bf16[160,1152]{1,0:T(8,128)(2,1)}, u32[]{:S(2)}, u32[]{:S(2)}) collective-permute-start(bf16[160,1152]{1,0:T(8,128)(2,1)} %get-tuple-element.264), channel_id=1, source_target_pairs={{0,4},{2,6},{4,0},{6,2},{1,5},{3,7},{5,1},{7,3},{8,12},{10,14},{12... | collective-permute-start | bytes 1105928 | tf_op jit(solution)/shard_map/ppermute | solution.py:52
  363.7 20.3 %collective-permute-start.33 = (bf16[160,1152]{1,0:T(8,128)(2,1)}, bf16[160,1152]{1,0:T(8,128)(2,1)}, u32[]{:S(2)}, u32[]{:S(2)}) collective-permute-start(bf16[160,1152]{1,0:T(8,128)(2,1)} %get-tuple-element.264), channel_id=1, source_target_pairs={{0,6},{2,0},{4,2},{6,4},{1,7},{3,1},{5,3},{7,5},{8,14},{10,8},{12,... | collective-permute-start | bytes 1105928 | tf_op jit(solution)/shard_map/ppermute | solution.py:52
  365.2 21.8 %collective-permute-start.34 = (bf16[160,1152]{1,0:T(8,128)(2,1)}, bf16[160,1152]{1,0:T(8,128)(2,1)}, u32[]{:S(2)}, u32[]{:S(2)}) collective-permute-start(bf16[160,1152]{1,0:T(8,128)(2,1)} %get-tuple-element.264), channel_id=1, source_target_pairs={{0,1},{1,0},{2,3},{3,2},{4,5},{5,4},{6,7},{7,6},{8,9},{9,8},{10,11... | collective-permute-start | bytes 1105928 | tf_op jit(solution)/shard_map/ppermute | solution.py:43
  414.1 35.7 %collective-permute-start.48 = (bf16[4,88,896]{2,1,0:T(8,128)(2,1)S(1)}, bf16[4,88,896]{2,1,0:T(8,128)(2,1)S(1)}, u32[]{:S(2)}, u32[]{:S(2)}) collective-permute-start(bf16[4,88,896]{2,1,0:T(8,128)(2,1)S(1)} %get-tuple-element.289), channel_id=1, source_target_pairs={{0,24},{16,0},{8,16},{24,8},{1,25},{17,1},{9,17},{25,9},{2,26},{18... | collective-permute-start | bytes 1892360 | tf_op jit(solution)/shard_map/ppermute | solution.py:52
  425.3 27.0 %collective-permute-start.49 = (bf16[4,88,896]{2,1,0:T(8,128)(2,1)S(1)}, bf16[4,88,896]{2,1,0:T(8,128)(2,1)S(1)}, u32[]{:S(2)}, u32[]{:S(2)}) collective-permute-start(bf16[4,88,896]{2,1,0:T(8,128)(2,1)S(1)} %get-tuple-element.290), channel_id=1, source_target_pairs={{0,8},{16,24},{8,0},{24,16},{1,9},{17,25},{9,1},{25,17},{2,10},{18... | collective-permute-start | bytes 1892360 | tf_op jit(solution)/shard_map/ppermute | solution.py:52
  432.4 24.2 %collective-permute-start.50 = (bf16[4,88,896]{2,1,0:T(8,128)(2,1)S(1)}, bf16[4,88,896]{2,1,0:T(8,128)(2,1)S(1)}, u32[]{:S(2)}, u32[]{:S(2)}) collective-permute-start(bf16[4,88,896]{2,1,0:T(8,128)(2,1)S(1)} %get-tuple-element.287), channel_id=1, source_target_pairs={{0,16},{16,8},{8,24},{24,0},{1,17},{17,9},{9,25},{25,1},{2,18},{18... | collective-permute-start | bytes 1892360 | tf_op jit(solution)/shard_map/ppermute | solution.py:52
  439.0 23.1 %collective-permute-start.45 = (bf16[4,88,896]{2,1,0:T(8,128)(2,1)}, bf16[4,88,896]{2,1,0:T(8,128)(2,1)}, u32[]{:S(2)}, u32[]{:S(2)}) collective-permute-start(bf16[4,88,896]{2,1,0:T(8,128)(2,1)} %get-tuple-element.293), channel_id=1, source_target_pairs={{0,96},{32,0},{64,32},{96,64},{1,97},{33,1},{65,33},{97,65},{2,98}... | collective-permute-start | bytes 1892360 | tf_op jit(solution)/shard_map/ppermute | solution.py:52
  441.1 20.9 %collective-permute-start.46 = (bf16[4,88,896]{2,1,0:T(8,128)(2,1)}, bf16[4,88,896]{2,1,0:T(8,128)(2,1)}, u32[]{:S(2)}, u32[]{:S(2)}) collective-permute-start(bf16[4,88,896]{2,1,0:T(8,128)(2,1)} %get-tuple-element.294), channel_id=1, source_target_pairs={{0,64},{32,96},{64,0},{96,32},{1,65},{33,97},{65,1},{97,33},{2,66}... | collective-permute-start | bytes 1892360 | tf_op jit(solution)/shard_map/ppermute | solution.py:52
  449.7 23.0 %collective-permute-start.47 = (bf16[4,88,896]{2,1,0:T(8,128)(2,1)}, bf16[4,88,896]{2,1,0:T(8,128)(2,1)}, u32[]{:S(2)}, u32[]{:S(2)}) collective-permute-start(bf16[4,88,896]{2,1,0:T(8,128)(2,1)} %get-tuple-element.291), channel_id=1, source_target_pairs={{0,32},{32,64},{64,96},{96,0},{1,33},{33,65},{65,97},{97,1},{2,34}... | collective-permute-start | bytes 1892360 | tf_op jit(solution)/shard_map/ppermute | solution.py:52
  493.5 58.4 %collective-permute-start.66 = (bf16[4,56,1152]{2,1,0:T(8,128)(2,1)S(1)}, bf16[4,56,1152]{2,1,0:T(8,128)(2,1)}, u32[]{:S(2)}, u32[]{:S(2)}) collective-permute-start(bf16[4,56,1152]{2,1,0:T(8,128)(2,1)S(1)} %get-tuple-element.297), channel_id=1, source_target_pairs={{0,96},{32,0},{64,32},{96,64},{1,97},{33,1},{65,33},{97,65},{2,98}... | collective-permute-start | bytes 1548296 | tf_op jit(solution)/shard_map/ppermute | solution.py:52
  493.5 59.4 %collective-permute-start.67 = (bf16[4,56,1152]{2,1,0:T(8,128)(2,1)S(1)}, bf16[4,56,1152]{2,1,0:T(8,128)(2,1)}, u32[]{:S(2)}, u32[]{:S(2)}) collective-permute-start(bf16[4,56,1152]{2,1,0:T(8,128)(2,1)S(1)} %get-tuple-element.296), channel_id=1, source_target_pairs={{0,64},{32,96},{64,0},{96,32},{1,65},{33,97},{65,1},{97,33},{2,66}... | collective-permute-start | bytes 1548296 | tf_op jit(solution)/shard_map/ppermute | solution.py:52
  525.3 47.2 %collective-permute-start.52 = (bf16[1536,512]{1,0:T(8,128)(2,1)}, bf16[1536,512]{1,0:T(8,128)(2,1)}, u32[]{:S(2)}, u32[]{:S(2)}) collective-permute-start(bf16[1536,512]{1,0:T(8,128)(2,1)} %fusion.48), channel_id=1, source_target_pairs={{0,1},{1,0},{2,3},{3,2},{4,5},{5,4},{6,7},{7,6},{8,9},{9,8},{10,11... | collective-permute-start | bytes 4718600 | tf_op jit(solution)/shard_map/ppermute | solution.py:43
  532.6 44.4 %collective-permute-start.57 = (bf16[1536,640]{1,0:T(8,128)(2,1)}, bf16[1536,640]{1,0:T(8,128)(2,1)}, u32[]{:S(2)}, u32[]{:S(2)}) collective-permute-start(bf16[1536,640]{1,0:T(8,128)(2,1)} %add_convert_fusion.1), channel_id=1, source_target_pairs={{0,1},{1,0},{2,3},{3,2},{4,5},{5,4},{6,7},{7,6},{8,9},{9,8},{10,11... | collective-permute-start | bytes 5898248 | tf_op jit(solution)/shard_map/ppermute | solution.py:43
  563.3 38.4 %all-to-all-start.5 = ((bf16[8,32,896]{2,1,0:T(8,128)(2,1)}), bf16[8,32,896]{2,1,0:T(8,128)(2,1)}, u32[]{:S(2)}, u32[]{:S(2)}) async-start(bf16[8,32,896]{2,1,0:T(8,128)(2,1)} %bitcast.315), calls=%async_computation.5 | async-start | bytes 917504 | tf_op jit(solution)/shard_map/all_to_all | solution.py:35
  598.0 55.0 %collective-permute-start.72 = (bf16[56,1152]{1,0:T(8,128)(2,1)}, bf16[56,1152]{1,0:T(8,128)(2,1)}, u32[]{:S(2)}, u32[]{:S(2)}) collective-permute-start(bf16[56,1152]{1,0:T(8,128)(2,1)} %add_convert_fusion.9), channel_id=1, source_target_pairs={{0,0},{8,1},{16,2},{24,3},{32,4},{40,5},{48,6},{56,7},{64,8},{72,9... | collective-permute-start | bytes 387080 | tf_op jit(solution)/shard_map/ppermute | solution.py:517
  601.7 65.7 %all-to-all-start.4 = ((bf16[64,24,1408]{2,1,0:T(8,128)(2,1)}), bf16[64,24,1408]{2,1,0:T(8,128)(2,1)}, u32[]{:S(2)}, u32[]{:S(2)}) async-start(bf16[64,24,1408]{2,1,0:T(8,128)(2,1)} %pad_maximum_fusion), calls=%async_computation.4 | async-start | bytes 8650752 | tf_op jit(solution)/shard_map/all_to_all | solution.py:35
  (223 other events, 1831.4 us)

commit v7 on v6

--- a/solution.py
+++ b/solution.py
@@ -33,10 +33,6 @@
 
 def exchange(x, axes):
     return lax.all_to_all(x, axes, split_axis=0, concat_axis=0, tiled=True)
-
-
-def gather_chips(x):
-    return exchange(jnp.broadcast_to(x[None], (64,) + x.shape), CHIPS)
 
 
 def other_core(x):
@@ -195,9 +191,10 @@
     keep, send = pick(is_first, attention_half(0), attention_half(1))
     lower, upper = pick(is_first, keep, other_core(send))
     att_own = jnp.concatenate([lower, upper], axis=0)
-    raw_one = gather_chips(att_own)
+    att_wide = jnp.broadcast_to(att_own[None], (64, 24, 1152))
+    raw_one = exchange(att_wide, CHIPS)
     (layer_input, wg, wu, bg, bu, wd, ad, ag, au, wo, ao, bo, bd, segment, position, core, at_z, _) = after(
-        att_own,
+        att_wide,
         layer_input, wg, wu, bg, bu, wd, ad, ag, au, wo, ao, bo, bd, segment, position, core, at_z,
     )
     is_first = core == 0
@@ -251,7 +248,27 @@
     down_own = lax.ppermute(
         jnp.pad(jnp.concatenate([wd, ad], axis=1), ((0, 2), (0, 0))), EVERY, down_route()
     )
-    raw_one, _ = after(ff_own, raw_one)
+    seq = (at_xh * 4 + at_y) * 2 + core
+    tree_seg = segment[0]
+    tree_pos = position[0]
+    own_seg = lax.dynamic_slice_in_dim(tree_seg, seq * TOKENS, TOKENS)
+    own_pos = lax.dynamic_slice_in_dim(tree_pos, seq * TOKENS, TOKENS)
+    freq = ROPE_BASE ** (-(jnp.arange(128, dtype=F32) * 2.0 / WIDTH))
+    angles = own_pos.astype(F32)[:, None] * freq[None, :]
+    cos, sin = jnp.cos(angles), jnp.sin(angles)
+    back = jnp.arange(16, dtype=jnp.int32)
+    block_at = (((at_xh - back % 2) % 2) * 4 + (at_y - back % 8 // 2) % 4) * 2 + jnp.where(
+        back < 8, core, 1 - core
+    )
+    chosen = (block_at[:, None] == back[None, :]).astype(jnp.int32)[:, :, None]
+    key_seg = jnp.sum(chosen * tree_seg.reshape(1, 16, TOKENS), axis=1).reshape(1, 2560)
+    key_pos = jnp.sum(chosen * tree_pos.reshape(1, 16, TOKENS), axis=1).reshape(1, 2560)
+    q_seg, q_pos = own_seg[:, None], own_pos[:, None]
+    parent = (key_seg >= 1) & (key_seg <= 4) & (q_seg >= 5) & ((q_seg - 5) // 2 + 1 == key_seg)
+    allowed = ((key_seg == q_seg) | (key_seg == 0) | parent) & (key_pos <= q_pos)
+
+    scale_one = lax.rsqrt(jnp.mean(hidden * hidden, axis=-1, keepdims=True) + EPSILON)
+    raw_one, _ = after((ff_own, out_own, down_own, cos, sin, allowed, scale_one), raw_one)
     raw_two = other_core(raw_one)
     marks = raw_one.reshape(128, 12, 1152)[:, 9, 768:896]
     gain_one_full = marks[:, :9].reshape(1, 1152).astype(F32)
@@ -283,27 +300,9 @@
     put_inner_out = table(inner_ids, jnp.where((j >= 8) & (j < 10), 2 * dev + j - 8, -1))
     put_inner_down = table(halves, jnp.where(j >= 10, 2 * dev + j - 10, -1))
 
-    seq = (at_xh * 4 + at_y) * 2 + core
-    tree_seg = segment[0]
-    tree_pos = position[0]
-    own_seg = lax.dynamic_slice_in_dim(tree_seg, seq * TOKENS, TOKENS)
-    own_pos = lax.dynamic_slice_in_dim(tree_pos, seq * TOKENS, TOKENS)
-    freq = ROPE_BASE ** (-(jnp.arange(128, dtype=F32) * 2.0 / WIDTH))
-    angles = own_pos.astype(F32)[:, None] * freq[None, :]
-    cos, sin = jnp.cos(angles), jnp.sin(angles)
-    back = jnp.arange(16, dtype=jnp.int32)
-    block_at = (((at_xh - (back % 8) // 4) % 2) * 4 + (at_y - back % 4) % 4) * 2 + jnp.where(
-        back < 8, core, 1 - core
-    )
-    chosen = (block_at[:, None] == back[None, :]).astype(jnp.int32)[:, :, None]
-    key_seg = jnp.sum(chosen * tree_seg.reshape(1, 16, TOKENS), axis=1).reshape(1, 2560)
-    key_pos = jnp.sum(chosen * tree_pos.reshape(1, 16, TOKENS), axis=1).reshape(1, 2560)
-    q_seg, q_pos = own_seg[:, None], own_pos[:, None]
-    parent = (key_seg >= 1) & (key_seg <= 4) & (q_seg >= 5) & ((q_seg - 5) // 2 + 1 == key_seg)
-    allowed = ((key_seg == q_seg) | (key_seg == 0) | parent) & (key_pos <= q_pos)
     allowed = jnp.concatenate([allowed] * HEADS, axis=0)
-
-    scale_one, n_one, u_one = norm_parts(hidden, gain_one_full)
+    n_one = hidden * scale_one
+    u_one = (n_one * (1.0 + gain_one_full)).astype(BF)
     u_rows = dot(u_one, put_rows).astype(BF)
     inner = [dot(u_rows, raw[i][:, 768:]).astype(BF) for i in (0, 1)]
     sides = []
@@ -314,10 +313,10 @@
     vv = pick(is_first, *[dot(sides[2], raw[i][:, 640:768]) for i in (0, 1)])
     kv_own = jnp.concatenate([turn(jnp.concatenate(kk, axis=1), cos, sin), vv[0], vv[1]], axis=1).astype(BF)
 
-    kv_line = gather_line(kv_own, "y").reshape(640, 512)
-    kv_mine = jnp.concatenate([kv_line, other_half(kv_line)], axis=0)
+    pair = jnp.concatenate([kv_own, other_half(kv_own)], axis=0)
+    kv_parts = [pair] + list(after(ff_wide, *[shift(pair, "y", k) for k in (1, 2, 3)])[:3])
+    kv_mine = jnp.concatenate(kv_parts, axis=0)
     kv = jnp.concatenate([kv_mine, other_core(kv_mine)], axis=0)
-    kv, _ = after(ff_wide, kv)
     keys, values = kv[:, :256], kv[:, 256:]
     queries = [dot(sides[0], raw[i][:, :512]) for i in (0, 1)]
     q_rows = jnp.concatenate(
@@ -379,16 +378,10 @@
     gb_gate = dot_tl(a_gate, gw_gate).astype(BF)
     gate_grads = jnp.concatenate([gw_gate.reshape(16, 72, 896), gb_gate.reshape(16, 16, 896)], axis=1)
     gate_first = leave(gate_grads.reshape(4, 4, 88, 896), "z", 0, at_z, at_x)
-    gate_first, _ = after(g_u_two, gate_first)
-    gate_line = add(gate_first).astype(BF)
-    gate_second = leave(gate_line, "x", 0, at_z, at_x)
     gw_up = dot_tl(u_all, g_up).astype(BF)
     gb_up = dot_tl(a_up, gw_up).astype(BF)
     up_grads = jnp.concatenate([gw_up.reshape(16, 72, 896), gb_up.reshape(16, 16, 896)], axis=1)
     up_first = leave(up_grads.reshape(4, 4, 88, 896), "x", 1, at_z, at_x)
-    up_first, _ = after(g_u_two, up_first)
-    up_line = add(up_first).astype(BF)
-    up_second = leave(up_line, "z", 0, at_z, at_x)
     gw_down = dot_tl(act, g_all).astype(BF)
     gb_down = dot_tl(a_down, gw_down).astype(BF)
     down_first = leave(gw_down.reshape(4, 4, 56, 1152), "z", 0, at_z, at_x)
@@ -412,6 +405,10 @@
     probs = jnp.where(allowed, jnp.exp(scores_again - lse), 0.0)
     g_probs = dot_tr(g_rows, values)
     g_scores = (probs * (g_probs - jnp.sum(probs * g_probs, axis=-1, keepdims=True))).astype(BF)
+    gate_first, up_first, _ = after(g_scores, gate_first, up_first)
+    gate_line, up_line = add(gate_first).astype(BF), add(up_first).astype(BF)
+    gate_second = leave(gate_line, "x", 0, at_z, at_x)
+    up_second = leave(up_line, "z", 0, at_z, at_x)
     g_scores, probs, _ = after((gate_line, up_line), g_scores, probs)
     g_keys = dot_tl(g_scores, q_rows) * score_scale
     g_values = dot_tl(probs.astype(BF), g_rows)
@@ -419,11 +416,7 @@
     n_mine = 8 * TOKENS
     g_kv_sum = g_kv[:n_mine] + other_core(g_kv[n_mine:].astype(BF)).astype(F32)
     g_kv_b = g_kv_sum.astype(BF)
-    g_line = g_kv_sum[:640] + other_half(g_kv_b[640:]).astype(F32)
-    g_kv_own = g_line[:TOKENS]
-    g_line = g_line.astype(BF)
-    for k in (1, 2, 3):
-        g_kv_own = g_kv_own + shift(g_line[TOKENS * k : TOKENS * (k + 1)], "y", 4 - k).astype(F32)
+    g_parts = [shift(g_kv_b[320 * k : 320 * (k + 1)], "y", 4 - k) for k in (1, 2, 3)]
     g_scores, side_out, gate_second, up_second, down_first, gb_down, _ = after(
         g_kv_b, g_scores, side_out, gate_second, up_second, down_first, gb_down
     )
@@ -465,11 +458,6 @@
         mine, away = pick(is_first, owned[:12], owned[12:])
         return pick(is_first, mine, other_core(away.astype(BF)).astype(F32))
 
-    left, right = pick(is_first, gb_down[:, :640], gb_down[:, 512:])
-    chip_out = of_chip(
-        dot_tl(side_out, g_half[0]) + dot_tl(put_inner_down, left),
-        dot_tl(side_out, g_half[1]) + dot_tl(put_inner_down, right),
-    )
     loss_high, loss_rest = split_in_two(loss_here)
     loss_mid, loss_low = split_in_two(loss_rest)
     lines = jnp.arange(16, dtype=jnp.int32)
@@ -483,7 +471,16 @@
     chip_q = of_chip(
         *[(dot_tl(sides[0], g_q[i]) + dot_tl(more_side, more_grad)).astype(BF) for i in (0, 1)]
     )
-    g_kv_own, _ = after((chip_q, chip_out, leaving), g_kv_own)
+    g_parts = after(chip_q, *g_parts)[:3]
+    g_pair = add([g_kv_sum[:320]] + list(g_parts))
+    away = other_half(g_pair[160:].astype(BF))
+    side_out, _ = after(g_pair, side_out)
+    left, right = pick(is_first, gb_down[:, :640], gb_down[:, 512:])
+    chip_out = of_chip(
+        dot_tl(side_out, g_half[0]) + dot_tl(put_inner_down, left),
+        dot_tl(side_out, g_half[1]) + dot_tl(put_inner_down, right),
+    )
+    g_kv_own = g_pair[:160] + after((leaving, chip_out), away)[0].astype(F32)
     g_k = turn_back(g_kv_own[:, :256], cos, sin).astype(BF)
     g_v = g_kv_own[:, 256:].astype(BF)
     g_k = pick(is_first, g_k[:, :128], g_k[:, 128:])

time: 696 us -> 649 us (0.932)
  the two profiles are of different devices: /device:TPU:1 before, /device:TPU:13 now
where the time goes in v7:
time: 649 us; the launch traced here: 638 us
  matrix products  159 us (24%)
  starting transfers between devices  153 us (24%)
  waiting for transfers between devices  148 us (23%)
  local copies, waits for them, and re-layouts  89.2 us (14%)
  other arithmetic  79.9 us (12%)
  between operations  9.23 us (1%)
    ppermute x36, waiting for transfers between devices, shift(): lax.ppermute(x, RING[axis], [(number[i], number[(i + k) % 4]) for i in ra...  77.4 us
    dot_general x37, matrix products, dot(): return jnp.dot(a, b, preferred_element_type=F32)  65.6 us
    dot_general x38, matrix products, dot_tr(): lax.dot_general(a, b, (((1,), (1,)), ((), ())), preferred_element_type=F32)  59.6 us
    all_to_all x6, starting transfers between devices, exchange(): return lax.all_to_all(x, axes, split_axis=0, concat_axis=0, tiled=True)  54.6 us
    ppermute x36, starting transfers between devices, shift(): lax.ppermute(x, RING[axis], [(number[i], number[(i + k) % 4]) for i in ra...  50.3 us
    all_to_all x6, waiting for transfers between devices, exchange(): return lax.all_to_all(x, axes, split_axis=0, concat_axis=0, tiled=True)  34.9 us
    dot_general x19, matrix products, dot_tl(): lax.dot_general(a, b, (((0,), (0,)), ((), ())), preferred_element_type=F32)  33.8 us
    ppermute x26, starting transfers between devices, other_core(): return lax.ppermute(x, 'c', [(0, 1), (1, 0)])  27.6 us
  transfers between devices with their start and end apart: 79, of which 25 were waited for; matrix products, arithmetic and copies ran while one was open for 37% of the time, Pallas kernels for 0%

profile of v7, /device:TPU:13, one launch (start us, length us, event | category | flops | bytes accessed | tf_op | source)
XLA Modules:
  0.0 638.5 jit_solution(18182027391103221143)
XLA Ops:
  14.6 10.9 %all-to-all-start = ((bf16[64,24,1152]{2,1,0:T(8,128)(2,1)}), bf16[64,24,1152]{2,1,0:T(8,128)(2,1)S(1)}, u32[]{:S(2)}, u32[]{:S(2)}) async-start(bf16[64,24,1152]{2,1,0:T(8,128)(2,1)} %broadcast_in_dim.71), calls=%async_computation | async-start | bytes 7077888 | tf_op jit(solution)/shard_map/all_to_all | solution.py:35
  45.6 5.3 collective-permute-start.9
  70.5 3.8 collective-permute-start.3
  74.3 5.6 collective-permute-done.3
  94.3 10.9 %all-to-all-start.1 = ((bf16[64,24,1024]{2,1,0:T(8,128)(2,1)}), bf16[64,24,1024]{2,1,0:T(8,128)(2,1)}, u32[]{:S(2)}, u32[]{:S(2)}) async-start(bf16[64,24,1024]{2,1,0:T(8,128)(2,1)} %broadcast_in_dim.78), calls=%async_computation.1 | async-start | bytes 6291456 | tf_op jit(solution)/shard_map/all_to_all | solution.py:35
  123.7 19.0 %collective-permute-done.11 = bf16[160,512]{1,0:T(8,128)(2,1)S(1)} collective-permute-done((bf16[160,512]{1,0:T(8,128)(2,1)S(1)}, bf16[160,512]{1,0:T(8,128)(2,1)S(1)}, u32[]{:S(2)}, u32[]{:S(2)}) %collective-permute-start.11) | collective-permute-done | bytes 163872 | tf_op jit(solution)/shard_map/ppermute | solution.py:43
  153.0 5.1 collective-permute-done.13
  164.4 7.2 %all-to-all-start.2 = ((bf16[16,176,896]{2,1,0:T(8,128)(2,1)}), bf16[16,176,896]{2,1,0:T(8,128)(2,1)}, u32[]{:S(2)}, u32[]{:S(2)}) async-start(bf16[16,176,896]{2,1,0:T(8,128)(2,1)} %broadcast_in_dim.79), calls=%async_computation.2 | async-start | bytes 10092544 | tf_op jit(solution)/shard_map/all_to_all | solution.py:35
  202.7 5.8 collective-permute-done.18
  215.8 24.9 %all-to-all-done.2 = bf16[16,176,896]{2,1,0:T(8,128)(2,1)} async-done(((bf16[16,176,896]{2,1,0:T(8,128)(2,1)}), bf16[16,176,896]{2,1,0:T(8,128)(2,1)}, u32[]{:S(2)}, u32[]{:S(2)}) %all-to-all-start.2) | async-done | bytes 5046304 | tf_op jit(solution)/shard_map/all_to_all | solution.py:35
  240.7 4.5 fusion.592
  247.7 7.6 %all-to-all-start.3 = ((bf16[16,56,1408]{2,1,0:T(8,128)(2,1)}), bf16[16,56,1408]{2,1,0:T(8,128)(2,1)}, u32[]{:S(2)}, u32[]{:S(2)}) async-start(bf16[16,56,1408]{2,1,0:T(8,128)(2,1)} %broadcast_in_dim.82), calls=%async_computation.3 | async-start | bytes 5046272 | tf_op jit(solution)/shard_map/all_to_all | solution.py:35
  260.6 6.1 fusion.614
  268.8 8.3 %multiply_convert_fusion.1 = (bf16[1280,896]{1,0:T(8,128)(2,1)}, f32[1280,896]{1,0:T(8,128)}) fusion(f32[1280,896]{1,0:T(8,128)S(1)} %fusion.614, bf16[1280,1152]{1,0:T(8,128)(2,1)} %constant_dynamic-update-slice_fusion.39, bf16[1152,896]{1,0:T(8,128)(2,1)S(1)} %fusion.31), kind=kOutput, calls=%fused_computation.42 | convolution fusion | flops 2653880320 | bytes 16482304 | tf_op jit(solution)/shard_map/dot_general | solution.py:23
  277.2 10.0 %all-to-all-done.3 = bf16[16,56,1408]{2,1,0:T(8,128)(2,1)} async-done(((bf16[16,56,1408]{2,1,0:T(8,128)(2,1)}), bf16[16,56,1408]{2,1,0:T(8,128)(2,1)}, u32[]{:S(2)}, u32[]{:S(2)}) %all-to-all-start.3) | async-done | bytes 2523168 | tf_op jit(solution)/shard_map/all_to_all | solution.py:35
  304.9 3.8 collective-permute-start.25
  313.5 4.1 collective-permute-done.25
  317.6 6.8 %collective-permute-done.29 = bf16[160,1152]{1,0:T(8,128)(2,1)} collective-permute-done((bf16[160,1152]{1,0:T(8,128)(2,1)}, bf16[160,1152]{1,0:T(8,128)(2,1)}, u32[]{:S(2)}, u32[]{:S(2)}) %collective-permute-start.29) | collective-permute-done | bytes 368672 | tf_op jit(solution)/shard_map/ppermute | solution.py:48
  340.0 8.1 %collective-permute-done.32 = bf16[160,1152]{1,0:T(8,128)(2,1)S(1)} collective-permute-done((bf16[160,1152]{1,0:T(8,128)(2,1)S(1)}, bf16[160,1152]{1,0:T(8,128)(2,1)S(1)}, u32[]{:S(2)}, u32[]{:S(2)}) %collective-permute-start.32) | collective-permute-done | bytes 368672 | tf_op jit(solution)/shard_map/ppermute | solution.py:48
  351.6 9.4 %fusion.10 = (bf16[1280,896]{1,0:T(8,128)(2,1)S(1)}, bf16[1280,896]{1,0:T(8,128)(2,1)S(1)}) fusion(f32[1280,896]{1,0:T(8,128)S(1)} %bitcast.319, f32[1280,896]{1,0:T(8,128)} %get-tuple-element.448, bf16[1280,1152]{1,0:T(8,128)(2,1)S(1)} %constant_dynamic-update-slice_fusion.47, bf16[896,1152]{1,0:T(8,128)(2,1)S(1)} %copy-done.148), kind=kOutput, calls=%fused_computation.34 | convolution fusion | flops 2672230400 | bytes 18776064 | tf_op jit(solution)/shard_map/dot_general | solution.py:31
  364.6 3.7 convolution_add_fusion
  368.3 5.1 convolution_convert_fusion.1
  377.4 5.1 convolution_convert_fusion.2
  395.1 7.1 %collective-permute-done.43 = bf16[160,1152]{1,0:T(8,128)(2,1)S(1)} collective-permute-done((bf16[160,1152]{1,0:T(8,128)(2,1)S(1)}, bf16[160,1152]{1,0:T(8,128)(2,1)S(1)}, u32[]{:S(2)}, u32[]{:S(2)}) %collective-permute-start.43) | collective-permute-done | bytes 368672 | tf_op jit(solution)/shard_map/ppermute | solution.py:48
  414.6 4.6 multiply_reduce_fusion
  421.3 14.3 %collective-permute-done.46 = bf16[4,88,896]{2,1,0:T(8,128)(2,1)} collective-permute-done((bf16[4,88,896]{2,1,0:T(8,128)(2,1)}, bf16[4,88,896]{2,1,0:T(8,128)(2,1)}, u32[]{:S(2)}, u32[]{:S(2)}) %collective-permute-start.46) | collective-permute-done | bytes 630816 | tf_op jit(solution)/shard_map/ppermute | solution.py:48
  495.4 6.2 collective-permute-done.62
  515.5 9.2 %all-to-all-start.5 = ((bf16[8,32,896]{2,1,0:T(8,128)(2,1)}), bf16[8,32,896]{2,1,0:T(8,128)(2,1)}, u32[]{:S(2)}, u32[]{:S(2)}) async-start(bf16[8,32,896]{2,1,0:T(8,128)(2,1)} %bitcast.306), calls=%async_computation.5 | async-start | bytes 917504 | tf_op jit(solution)/shard_map/all_to_all | solution.py:35
  533.0 4.1 add_convert_fusion
  547.9 3.7 pad_maximum_fusion
  551.6 8.7 %all-to-all-start.4 = ((bf16[64,24,1408]{2,1,0:T(8,128)(2,1)}), bf16[64,24,1408]{2,1,0:T(8,128)(2,1)}, u32[]{:S(2)}, u32[]{:S(2)}) async-start(bf16[64,24,1408]{2,1,0:T(8,128)(2,1)} %pad_maximum_fusion), calls=%async_computation.4 | async-start | bytes 8650752 | tf_op jit(solution)/shard_map/all_to_all | solution.py:35
  611.6 5.1 collective-permute-done.72
  (754 shorter events, 385.2 us)
Async XLA Ops:
  14.6 71.5 %all-to-all-start = ((bf16[64,24,1152]{2,1,0:T(8,128)(2,1)}), bf16[64,24,1152]{2,1,0:T(8,128)(2,1)S(1)}, u32[]{:S(2)}, u32[]{:S(2)}) async-start(bf16[64,24,1152]{2,1,0:T(8,128)(2,1)} %broadcast_in_dim.71), calls=%async_computation | async-start | bytes 7077888 | tf_op jit(solution)/shard_map/all_to_all | solution.py:35
  43.4 22.0 %collective-permute-start.8 = (bf16[12,1024]{1,0:T(8,128)(2,1)}, bf16[12,1024]{1,0:T(8,128)(2,1)}, u32[]{:S(2)}, u32[]{:S(2)}) collective-permute-start(bf16[12,1024]{1,0:T(8,128)(2,1)} %broadcast_select_fusion.23), channel_id=1, source_target_pairs={{0,1},{1,0},{2,3},{3,2},{4,5},{5,4},{6,7},{7,6},{8,9},{9,8},{10,11... | collective-permute-start | bytes 73736 | tf_op jit(solution)/shard_map/ppermute | solution.py:39
  45.6 40.5 %collective-permute-start.9 = (bf16[56,1408]{1,0:T(8,128)(2,1)}, bf16[56,1408]{1,0:T(8,128)(2,1)}, u32[]{:S(2)}, u32[]{:S(2)}) collective-permute-start(bf16[56,1408]{1,0:T(8,128)(2,1)} %fusion.328), channel_id=1, source_target_pairs={{0,0},{1,8},{2,16},{3,24},{4,32},{5,40},{6,48},{7,56},{8,64},{9,72... | collective-permute-start | bytes 473096 | tf_op jit(solution)/shard_map/ppermute | solution.py:248
  62.1 22.2 %collective-permute-start.7 = (bf16[24,896]{1,0:T(8,128)(2,1)S(1)}, bf16[24,896]{1,0:T(8,128)(2,1)S(1)}, u32[]{:S(2)}, u32[]{:S(2)}) collective-permute-start(bf16[24,896]{1,0:T(8,128)(2,1)S(1)} %get-tuple-element.349), channel_id=1, source_target_pairs={{0,7},{1,6},{2,1},{3,0},{4,3},{5,2},{6,5},{7,4},{8,15},{9,14},{10,... | collective-permute-start | bytes 129032 | tf_op jit(solution)/shard_map/ppermute | solution.py:220
  62.1 22.2 %collective-permute-start.6 = (bf16[24,896]{1,0:T(8,128)(2,1)S(1)}, bf16[24,896]{1,0:T(8,128)(2,1)S(1)}, u32[]{:S(2)}, u32[]{:S(2)}) collective-permute-start(bf16[24,896]{1,0:T(8,128)(2,1)S(1)} %get-tuple-element.350), channel_id=1, source_target_pairs={{0,6},{1,7},{2,0},{3,1},{4,2},{5,3},{6,4},{7,5},{8,14},{9,15},{10,... | collective-permute-start | bytes 129032 | tf_op jit(solution)/shard_map/ppermute | solution.py:220
  64.3 20.1 %collective-permute-start.5 = (bf16[24,896]{1,0:T(8,128)(2,1)S(1)}, bf16[24,896]{1,0:T(8,128)(2,1)S(1)}, u32[]{:S(2)}, u32[]{:S(2)}) collective-permute-start(bf16[24,896]{1,0:T(8,128)(2,1)S(1)} %get-tuple-element.351), channel_id=1, source_target_pairs={{0,5},{1,4},{2,7},{3,6},{4,1},{5,0},{6,3},{7,2},{8,13},{9,12},{10,... | collective-permute-start | bytes 129032 | tf_op jit(solution)/shard_map/ppermute | solution.py:220
  86.1 29.1 %collective-permute-start.10 = (bf16[64,24,1152]{2,1,0:T(8,128)(2,1)S(1)}, bf16[64,24,1152]{2,1,0:T(8,128)(2,1)}, u32[]{:S(2)}, u32[]{:S(2)}) collective-permute-start(bf16[64,24,1152]{2,1,0:T(8,128)(2,1)S(1)} %all-to-all-done), channel_id=1, source_target_pairs={{0,1},{1,0},{2,3},{3,2},{4,5},{5,4},{6,7},{7,6},{8,9},{9,8},{10,11... | collective-permute-start | bytes 10616840 | tf_op jit(solution)/shard_map/ppermute | solution.py:39
  94.3 52.1 %all-to-all-start.1 = ((bf16[64,24,1024]{2,1,0:T(8,128)(2,1)}), bf16[64,24,1024]{2,1,0:T(8,128)(2,1)}, u32[]{:S(2)}, u32[]{:S(2)}) async-start(bf16[64,24,1024]{2,1,0:T(8,128)(2,1)} %broadcast_in_dim.78), calls=%async_computation.1 | async-start | bytes 6291456 | tf_op jit(solution)/shard_map/all_to_all | solution.py:35
  123.4 19.2 %collective-permute-start.11 = (bf16[160,512]{1,0:T(8,128)(2,1)S(1)}, bf16[160,512]{1,0:T(8,128)(2,1)S(1)}, u32[]{:S(2)}, u32[]{:S(2)}) collective-permute-start(bf16[160,512]{1,0:T(8,128)(2,1)S(1)} %get-tuple-element.388), channel_id=1, source_target_pairs={{0,8},{8,0},{1,9},{9,1},{2,10},{10,2},{3,11},{11,3},{4,12},{12,4},... | collective-permute-start | bytes 491528 | tf_op jit(solution)/shard_map/ppermute | solution.py:43
  164.4 76.3 %all-to-all-start.2 = ((bf16[16,176,896]{2,1,0:T(8,128)(2,1)}), bf16[16,176,896]{2,1,0:T(8,128)(2,1)}, u32[]{:S(2)}, u32[]{:S(2)}) async-start(bf16[16,176,896]{2,1,0:T(8,128)(2,1)} %broadcast_in_dim.79), calls=%async_computation.2 | async-start | bytes 10092544 | tf_op jit(solution)/shard_map/all_to_all | solution.py:35
  188.0 24.6 %collective-permute-start.20 = (bf16[160,1152]{1,0:T(8,128)(2,1)S(1)}, bf16[160,1152]{1,0:T(8,128)(2,1)S(1)}, u32[]{:S(2)}, u32[]{:S(2)}) collective-permute-start(bf16[160,1152]{1,0:T(8,128)(2,1)S(1)} %get-tuple-element.278), channel_id=1, source_target_pairs={{0,1},{1,0},{2,3},{3,2},{4,5},{5,4},{6,7},{7,6},{8,9},{9,8},{10,11... | collective-permute-start | bytes 1105928 | tf_op jit(solution)/shard_map/ppermute | solution.py:39
  190.4 18.1 %collective-permute-start.18 = (bf16[160,1152]{1,0:T(8,128)(2,1)S(1)}, bf16[160,1152]{1,0:T(8,128)(2,1)S(1)}, u32[]{:S(2)}, u32[]{:S(2)}) collective-permute-start(bf16[160,1152]{1,0:T(8,128)(2,1)S(1)} %get-tuple-element.278), channel_id=1, source_target_pairs={{0,4},{2,6},{4,0},{6,2},{1,5},{3,7},{5,1},{7,3},{8,12},{10,14},{12... | collective-permute-start | bytes 1105928 | tf_op jit(solution)/shard_map/ppermute | solution.py:48
  191.9 17.4 %collective-permute-start.17 = (bf16[160,1152]{1,0:T(8,128)(2,1)S(1)}, bf16[160,1152]{1,0:T(8,128)(2,1)S(1)}, u32[]{:S(2)}, u32[]{:S(2)}) collective-permute-start(bf16[160,1152]{1,0:T(8,128)(2,1)S(1)} %get-tuple-element.278), channel_id=1, source_target_pairs={{0,2},{2,4},{4,6},{6,0},{1,3},{3,5},{5,7},{7,1},{8,10},{10,12},{12... | collective-permute-start | bytes 1105928 | tf_op jit(solution)/shard_map/ppermute | solution.py:48
  247.7 39.4 %all-to-all-start.3 = ((bf16[16,56,1408]{2,1,0:T(8,128)(2,1)}), bf16[16,56,1408]{2,1,0:T(8,128)(2,1)}, u32[]{:S(2)}, u32[]{:S(2)}) async-start(bf16[16,56,1408]{2,1,0:T(8,128)(2,1)} %broadcast_in_dim.82), calls=%async_computation.3 | async-start | bytes 5046272 | tf_op jit(solution)/shard_map/all_to_all | solution.py:35
  308.8 17.3 %collective-permute-start.27 = (bf16[160,1152]{1,0:T(8,128)(2,1)}, bf16[160,1152]{1,0:T(8,128)(2,1)}, u32[]{:S(2)}, u32[]{:S(2)}) collective-permute-start(bf16[160,1152]{1,0:T(8,128)(2,1)} %get-tuple-element.286), channel_id=1, source_target_pairs={{0,6},{2,0},{4,2},{6,4},{1,7},{3,1},{5,3},{7,5},{8,14},{10,8},{12,... | collective-permute-start | bytes 1105928 | tf_op jit(solution)/shard_map/ppermute | solution.py:48
  330.2 17.9 %collective-permute-start.32 = (bf16[160,1152]{1,0:T(8,128)(2,1)S(1)}, bf16[160,1152]{1,0:T(8,128)(2,1)S(1)}, u32[]{:S(2)}, u32[]{:S(2)}) collective-permute-start(bf16[160,1152]{1,0:T(8,128)(2,1)S(1)} %get-tuple-element.276), channel_id=1, source_target_pairs={{0,4},{2,6},{4,0},{6,2},{1,5},{3,7},{5,1},{7,3},{8,12},{10,14},{12... | collective-permute-start | bytes 1105928 | tf_op jit(solution)/shard_map/ppermute | solution.py:48
  331.8 17.4 %collective-permute-start.31 = (bf16[160,1152]{1,0:T(8,128)(2,1)S(1)}, bf16[160,1152]{1,0:T(8,128)(2,1)S(1)}, u32[]{:S(2)}, u32[]{:S(2)}) collective-permute-start(bf16[160,1152]{1,0:T(8,128)(2,1)S(1)} %get-tuple-element.276), channel_id=1, source_target_pairs={{0,2},{2,4},{4,6},{6,0},{1,3},{3,5},{5,7},{7,1},{8,10},{10,12},{12... | collective-permute-start | bytes 1105928 | tf_op jit(solution)/shard_map/ppermute | solution.py:48
  375.7 43.6 %collective-permute-start.50 = (bf16[4,88,896]{2,1,0:T(8,128)(2,1)}, bf16[4,88,896]{2,1,0:T(8,128)(2,1)}, u32[]{:S(2)}, u32[]{:S(2)}) collective-permute-start(bf16[4,88,896]{2,1,0:T(8,128)(2,1)} %get-tuple-element.299), channel_id=1, source_target_pairs={{0,16},{16,8},{8,24},{24,0},{1,17},{17,9},{9,25},{25,1},{2,18},{18... | collective-permute-start | bytes 1892360 | tf_op jit(solution)/shard_map/ppermute | solution.py:48
  385.7 16.5 %collective-permute-start.43 = (bf16[160,1152]{1,0:T(8,128)(2,1)S(1)}, bf16[160,1152]{1,0:T(8,128)(2,1)S(1)}, u32[]{:S(2)}, u32[]{:S(2)}) collective-permute-start(bf16[160,1152]{1,0:T(8,128)(2,1)S(1)} %get-tuple-element.282), channel_id=1, source_target_pairs={{0,2},{2,4},{4,6},{6,0},{1,3},{3,5},{5,7},{7,1},{8,10},{10,12},{12... | collective-permute-start | bytes 1105928 | tf_op jit(solution)/shard_map/ppermute | solution.py:48
  389.6 31.6 %collective-permute-start.48 = (bf16[4,88,896]{2,1,0:T(8,128)(2,1)}, bf16[4,88,896]{2,1,0:T(8,128)(2,1)}, u32[]{:S(2)}, u32[]{:S(2)}) collective-permute-start(bf16[4,88,896]{2,1,0:T(8,128)(2,1)} %get-tuple-element.301), channel_id=1, source_target_pairs={{0,24},{16,0},{8,16},{24,8},{1,25},{17,1},{9,17},{25,9},{2,26},{18... | collective-permute-start | bytes 1892360 | tf_op jit(solution)/shard_map/ppermute | solution.py:48
  394.2 27.0 %collective-permute-start.49 = (bf16[4,88,896]{2,1,0:T(8,128)(2,1)}, bf16[4,88,896]{2,1,0:T(8,128)(2,1)}, u32[]{:S(2)}, u32[]{:S(2)}) collective-permute-start(bf16[4,88,896]{2,1,0:T(8,128)(2,1)} %get-tuple-element.302), channel_id=1, source_target_pairs={{0,8},{16,24},{8,0},{24,16},{1,9},{17,25},{9,1},{25,17},{2,10},{18... | collective-permute-start | bytes 1892360 | tf_op jit(solution)/shard_map/ppermute | solution.py:48
  402.2 19.1 %collective-permute-start.47 = (bf16[4,88,896]{2,1,0:T(8,128)(2,1)}, bf16[4,88,896]{2,1,0:T(8,128)(2,1)}, u32[]{:S(2)}, u32[]{:S(2)}) collective-permute-start(bf16[4,88,896]{2,1,0:T(8,128)(2,1)} %get-tuple-element.303), channel_id=1, source_target_pairs={{0,32},{32,64},{64,96},{96,0},{1,33},{33,65},{65,97},{97,1},{2,34}... | collective-permute-start | bytes 1892360 | tf_op jit(solution)/shard_map/ppermute | solution.py:48
  402.9 18.3 %collective-permute-start.45 = (bf16[4,88,896]{2,1,0:T(8,128)(2,1)}, bf16[4,88,896]{2,1,0:T(8,128)(2,1)}, u32[]{:S(2)}, u32[]{:S(2)}) collective-permute-start(bf16[4,88,896]{2,1,0:T(8,128)(2,1)} %get-tuple-element.305), channel_id=1, source_target_pairs={{0,96},{32,0},{64,32},{96,64},{1,97},{33,1},{65,33},{97,65},{2,98}... | collective-permute-start | bytes 1892360 | tf_op jit(solution)/shard_map/ppermute | solution.py:48
  419.2 16.3 %collective-permute-start.46 = (bf16[4,88,896]{2,1,0:T(8,128)(2,1)}, bf16[4,88,896]{2,1,0:T(8,128)(2,1)}, u32[]{:S(2)}, u32[]{:S(2)}) collective-permute-start(bf16[4,88,896]{2,1,0:T(8,128)(2,1)} %get-tuple-element.306), channel_id=1, source_target_pairs={{0,64},{32,96},{64,0},{96,32},{1,65},{33,97},{65,1},{97,33},{2,66}... | collective-permute-start | bytes 1892360 | tf_op jit(solution)/shard_map/ppermute | solution.py:48
  469.8 43.5 %collective-permute-start.68 = (bf16[4,56,1152]{2,1,0:T(8,128)(2,1)S(1)}, bf16[4,56,1152]{2,1,0:T(8,128)(2,1)S(1)}, u32[]{:S(2)}, u32[]{:S(2)}) collective-permute-start(bf16[4,56,1152]{2,1,0:T(8,128)(2,1)S(1)} %get-tuple-element.307), channel_id=1, source_target_pairs={{0,32},{32,64},{64,96},{96,0},{1,33},{33,65},{65,97},{97,1},{2,34}... | collective-permute-start | bytes 1548296 | tf_op jit(solution)/shard_map/ppermute | solution.py:48
  469.8 43.5 %collective-permute-start.67 = (bf16[4,56,1152]{2,1,0:T(8,128)(2,1)S(1)}, bf16[4,56,1152]{2,1,0:T(8,128)(2,1)S(1)}, u32[]{:S(2)}, u32[]{:S(2)}) collective-permute-start(bf16[4,56,1152]{2,1,0:T(8,128)(2,1)S(1)} %get-tuple-element.308), channel_id=1, source_target_pairs={{0,64},{32,96},{64,0},{96,32},{1,65},{33,97},{65,1},{97,33},{2,66}... | collective-permute-start | bytes 1548296 | tf_op jit(solution)/shard_map/ppermute | solution.py:48
  473.5 17.7 %collective-permute-start.53 = (bf16[320,512]{1,0:T(8,128)(2,1)S(1)}, bf16[320,512]{1,0:T(8,128)(2,1)S(1)}, u32[]{:S(2)}, u32[]{:S(2)}) collective-permute-start(bf16[320,512]{1,0:T(8,128)(2,1)S(1)} %get-tuple-element.311), channel_id=1, source_target_pairs={{0,6},{2,0},{4,2},{6,4},{1,7},{3,1},{5,3},{7,5},{8,14},{10,8},{12,... | collective-permute-start | bytes 983048 | tf_op jit(solution)/shard_map/ppermute | solution.py:48
  483.4 18.2 %collective-permute-start.62 = (bf16[88,896]{1,0:T(8,128)(2,1)S(1)}, bf16[88,896]{1,0:T(8,128)(2,1)S(1)}, u32[]{:S(2)}, u32[]{:S(2)}) collective-permute-start(bf16[88,896]{1,0:T(8,128)(2,1)S(1)} %get-tuple-element.341), channel_id=1, source_target_pairs={{0,32},{32,64},{64,96},{96,0},{1,33},{33,65},{65,97},{97,1},{2,34}... | collective-permute-start | bytes 473096 | tf_op jit(solution)/shard_map/ppermute | solution.py:48
  509.5 23.4 %collective-permute-start.63 = (bf16[1536,640]{1,0:T(8,128)(2,1)}, bf16[1536,640]{1,0:T(8,128)(2,1)}, u32[]{:S(2)}, u32[]{:S(2)}) collective-permute-start(bf16[1536,640]{1,0:T(8,128)(2,1)} %add_convert_fusion.1), channel_id=1, source_target_pairs={{0,1},{1,0},{2,3},{3,2},{4,5},{5,4},{6,7},{7,6},{8,9},{9,8},{10,11... | collective-permute-start | bytes 5898248 | tf_op jit(solution)/shard_map/ppermute | solution.py:39
  515.5 36.1 %all-to-all-start.5 = ((bf16[8,32,896]{2,1,0:T(8,128)(2,1)}), bf16[8,32,896]{2,1,0:T(8,128)(2,1)}, u32[]{:S(2)}, u32[]{:S(2)}) async-start(bf16[8,32,896]{2,1,0:T(8,128)(2,1)} %bitcast.306), calls=%async_computation.5 | async-start | bytes 917504 | tf_op jit(solution)/shard_map/all_to_all | solution.py:35
  551.6 68.7 %all-to-all-start.4 = ((bf16[64,24,1408]{2,1,0:T(8,128)(2,1)}), bf16[64,24,1408]{2,1,0:T(8,128)(2,1)}, u32[]{:S(2)}, u32[]{:S(2)}) async-start(bf16[64,24,1408]{2,1,0:T(8,128)(2,1)} %pad_maximum_fusion), calls=%async_computation.4 | async-start | bytes 8650752 | tf_op jit(solution)/shard_map/all_to_all | solution.py:35
  563.8 53.0 %collective-permute-start.72 = (bf16[56,1152]{1,0:T(8,128)(2,1)}, bf16[56,1152]{1,0:T(8,128)(2,1)}, u32[]{:S(2)}, u32[]{:S(2)}) collective-permute-start(bf16[56,1152]{1,0:T(8,128)(2,1)} %add_convert_fusion.9), channel_id=1, source_target_pairs={{0,0},{8,1},{16,2},{24,3},{32,4},{40,5},{48,6},{56,7},{64,8},{72,9... | collective-permute-start | bytes 387080 | tf_op jit(solution)/shard_map/ppermute | solution.py:514
  (210 other events, 2106.2 us)

commit v8 on v7

--- a/solution.py
+++ b/solution.py
@@ -66,19 +66,26 @@
     pairs = []
     for o in range(16):
         for t in range(8):
-            pairs.append((8 * o + t, 8 * (8 * (o % 2) + t) + o // 2))
+            block = 8 * (o % 2) + t
+            pairs.append((8 * o + t, 8 * (block % 4 * 4 + block // 4) + o // 2))
     return pairs
 
 
-def gather_line(x, axis):
-    return jnp.stack([x] + [shift(x, axis, k) for k in (1, 2, 3)])
+def ring_place(axis, k, at_z, at_x):
+    return (at_z - k) % 4 if axis == "z" else (at_x - k) % 4 % 2 * 2 + (at_x - k) % 4 // 2
+
+
+def placed(parts, axis, at_z, at_x):
+    stack = jnp.zeros((4,) + parts[0].shape, parts[0].dtype)
+    for k, part in enumerate(parts):
+        stack = lax.dynamic_update_index_in_dim(stack, part, ring_place(axis, k, at_z, at_x), 0)
+    return stack
 
 
 def leave(x, axis, dim, at_z, at_x):
     parts = []
     for k in range(4):
-        place = (at_z - k) % 4 if axis == "z" else (at_x - k) % 4 % 2 * 2 + (at_x - k) % 4 // 2
-        block = lax.dynamic_index_in_dim(x, place, dim, keepdims=False)
+        block = lax.dynamic_index_in_dim(x, ring_place(axis, k, at_z, at_x), dim, keepdims=False)
         parts.append(shift(block, axis, 4 - k) if k else block)
     return parts
 
@@ -224,6 +231,72 @@
     wider = jnp.arange(896, dtype=jnp.int32)
     wider = table(jnp.arange(864, dtype=jnp.int32), jnp.where(wider % 56 < 54, wider // 56 * 54 + wider % 56, -1))
     rows22 = dot(rows22, wider).astype(BF).reshape(8, 24, 896)
+    down_own = lax.ppermute(
+        jnp.pad(jnp.concatenate([wd, ad], axis=1), ((0, 2), (0, 0))), EVERY, down_route()
+    )
+    seq = (at_xh * 4 + at_y) * 2 + core
+    tree_seg = segment[0]
+    tree_pos = position[0]
+    own_seg = lax.dynamic_slice_in_dim(tree_seg, seq * TOKENS, TOKENS)
+    own_pos = lax.dynamic_slice_in_dim(tree_pos, seq * TOKENS, TOKENS)
+    freq = ROPE_BASE ** (-(jnp.arange(128, dtype=F32) * 2.0 / WIDTH))
+    angles = own_pos.astype(F32)[:, None] * freq[None, :]
+    cos, sin = jnp.cos(angles), jnp.sin(angles)
+    back = jnp.arange(16, dtype=jnp.int32)
+    block_at = (((at_xh - back % 2) % 2) * 4 + (at_y - back % 8 // 2) % 4) * 2 + jnp.where(
+        back < 8, core, 1 - core
+    )
+    chosen = (block_at[:, None] == back[None, :]).astype(jnp.int32)[:, :, None]
+    key_seg = jnp.sum(chosen * tree_seg.reshape(1, 16, TOKENS), axis=1).reshape(1, 2560)
+    key_pos = jnp.sum(chosen * tree_pos.reshape(1, 16, TOKENS), axis=1).reshape(1, 2560)
+    q_seg, q_pos = own_seg[:, None], own_pos[:, None]
+    parent = (key_seg >= 1) & (key_seg <= 4) & (q_seg >= 5) & ((q_seg - 5) // 2 + 1 == key_seg)
+    allowed = ((key_seg == q_seg) | (key_seg == 0) | parent) & (key_pos <= q_pos)
+
+    scale_one = lax.rsqrt(jnp.mean(hidden * hidden, axis=-1, keepdims=True) + EPSILON)
+    raw_one, _ = after((rows22, out_own, down_own, cos, sin, allowed, scale_one), raw_one)
+    raw_two = other_core(raw_one)
+    marks = raw_one.reshape(128, 12, 1152)[:, 9, 768:896]
+    gain_one_full = marks[:, :9].reshape(1, 1152).astype(F32)
+    gain_two_full = marks[:, 9:18].reshape(1, 1152).astype(F32)
+    valid_count = jnp.sum(marks[:, 18].astype(F32))
+    out_own, _ = after(raw_one, out_own)
+    out_wide = jnp.broadcast_to(out_own[None], (64, 24, 1024))
+    out_one = exchange(out_wide, CHIPS)
+    out_two = other_core(out_one)
+    raw_out = [out_one.reshape(1536, 1024), out_two.reshape(1536, 1024)]
+    raw_one, raw_two, _ = after(out_wide, raw_one, raw_two)
+    raw = [raw_one.reshape(1536, 1152), raw_two.reshape(1536, 1152)]
+    ids = jnp.arange(1536, dtype=jnp.int32)
+    dev, j = 2 * (ids // 24) + (ids % 24) // 12, ids % 12
+    halves = jnp.arange(256, dtype=jnp.int32)
+    inner_ids = jnp.where(halves < 128, 128 * core + halves, 128 * (1 - core) + halves - 128)
+    heads_at = jnp.arange(1024, dtype=jnp.int32)
+    head_ids = jnp.where(heads_at < 512, 512 * core + heads_at, 512 * (1 - core) + heads_at - 512)
+    features = jnp.arange(1152, dtype=jnp.int32)
+    put_rows = table(features, jnp.where(j < 9, 9 * dev + j, -1))
+    put_inner = table(inner_ids, jnp.where((j >= 9) & (j < 11), 2 * dev + j - 9, -1))
+    take_b = table(halves, jnp.where((j >= 9) & (j < 11), 2 * dev + j - 9, -1))
+    take_b_out = table(halves, jnp.where((j >= 8) & (j < 10), 2 * dev + j - 8, -1))
+    put_mix = table(head_ids, jnp.where(j < 8, 8 * dev + j, -1))
+    put_inner_out = table(inner_ids, jnp.where((j >= 8) & (j < 10), 2 * dev + j - 8, -1))
+    put_inner_down = table(halves, jnp.where(j >= 10, 2 * dev + j - 10, -1))
+
+    allowed = jnp.concatenate([allowed] * HEADS, axis=0)
+    n_one = hidden * scale_one
+    u_one = (n_one * (1.0 + gain_one_full)).astype(BF)
+    u_rows = dot(u_one, put_rows).astype(BF)
+    inner = [dot(u_rows, raw[i][:, 768:]).astype(BF) for i in (0, 1)]
+    sides = []
+    for i in range(3):
+        part = jnp.concatenate([inner[0][:, 128 * i : 128 * i + 128], inner[1][:, 128 * i : 128 * i + 128]], axis=1)
+        sides.append(u_rows + dot(part, put_inner).astype(BF))
+    kk = pick(is_first, *[dot(sides[1], raw[i][:, 512:640]) for i in (0, 1)])
+    vv = pick(is_first, *[dot(sides[2], raw[i][:, 640:768]) for i in (0, 1)])
+    kv_own = jnp.concatenate([turn(jnp.concatenate(kk, axis=1), cos, sin), vv[0], vv[1]], axis=1).astype(BF)
+
+    pair = jnp.concatenate([kv_own, other_half(kv_own)], axis=0)
+    rows22, down_own, _ = after(kv_own, rows22, down_own)
     slab = []
     for k in range(8):
         piece = lax.dynamic_index_in_dim(rows22, column_of(k), 0, keepdims=False)
@@ -245,75 +318,11 @@
     in_slab = jnp.arange(192, dtype=jnp.int32)
     in_slab = jnp.repeat(sources, 24) * 24 + in_slab % 24
     ff_own = dot(table(at_row, in_slab), slab).astype(BF)
-    down_own = lax.ppermute(
-        jnp.pad(jnp.concatenate([wd, ad], axis=1), ((0, 2), (0, 0))), EVERY, down_route()
-    )
-    seq = (at_xh * 4 + at_y) * 2 + core
-    tree_seg = segment[0]
-    tree_pos = position[0]
-    own_seg = lax.dynamic_slice_in_dim(tree_seg, seq * TOKENS, TOKENS)
-    own_pos = lax.dynamic_slice_in_dim(tree_pos, seq * TOKENS, TOKENS)
-    freq = ROPE_BASE ** (-(jnp.arange(128, dtype=F32) * 2.0 / WIDTH))
-    angles = own_pos.astype(F32)[:, None] * freq[None, :]
-    cos, sin = jnp.cos(angles), jnp.sin(angles)
-    back = jnp.arange(16, dtype=jnp.int32)
-    block_at = (((at_xh - back % 2) % 2) * 4 + (at_y - back % 8 // 2) % 4) * 2 + jnp.where(
-        back < 8, core, 1 - core
-    )
-    chosen = (block_at[:, None] == back[None, :]).astype(jnp.int32)[:, :, None]
-    key_seg = jnp.sum(chosen * tree_seg.reshape(1, 16, TOKENS), axis=1).reshape(1, 2560)
-    key_pos = jnp.sum(chosen * tree_pos.reshape(1, 16, TOKENS), axis=1).reshape(1, 2560)
-    q_seg, q_pos = own_seg[:, None], own_pos[:, None]
-    parent = (key_seg >= 1) & (key_seg <= 4) & (q_seg >= 5) & ((q_seg - 5) // 2 + 1 == key_seg)
-    allowed = ((key_seg == q_seg) | (key_seg == 0) | parent) & (key_pos <= q_pos)
-
-    scale_one = lax.rsqrt(jnp.mean(hidden * hidden, axis=-1, keepdims=True) + EPSILON)
-    raw_one, _ = after((ff_own, out_own, down_own, cos, sin, allowed, scale_one), raw_one)
-    raw_two = other_core(raw_one)
-    marks = raw_one.reshape(128, 12, 1152)[:, 9, 768:896]
-    gain_one_full = marks[:, :9].reshape(1, 1152).astype(F32)
-    gain_two_full = marks[:, 9:18].reshape(1, 1152).astype(F32)
-    valid_count = jnp.sum(marks[:, 18].astype(F32))
-    out_own, _ = after(raw_one, out_own)
-    out_wide = jnp.broadcast_to(out_own[None], (64, 24, 1024))
-    out_one = exchange(out_wide, CHIPS)
-    out_two = other_core(out_one)
-    raw_out = [out_one.reshape(1536, 1024), out_two.reshape(1536, 1024)]
-    raw_one, raw_two, _ = after(out_wide, raw_one, raw_two)
-    raw = [raw_one.reshape(1536, 1152), raw_two.reshape(1536, 1152)]
-    ff_own, _ = after(out_one, ff_own)
+    down_line = placed([down_own] + [shift(down_own, "z", k) for k in (1, 2, 3)], "z", at_z, at_x)
+    ff_own, _ = after((out_one, down_line), ff_own)
     ff_wide = jnp.broadcast_to(ff_own[None], (16, 176, 896))
     ff_all = exchange(ff_wide, PLANE)
-
-    ids = jnp.arange(1536, dtype=jnp.int32)
-    dev, j = 2 * (ids // 24) + (ids % 24) // 12, ids % 12
-    halves = jnp.arange(256, dtype=jnp.int32)
-    inner_ids = jnp.where(halves < 128, 128 * core + halves, 128 * (1 - core) + halves - 128)
-    heads_at = jnp.arange(1024, dtype=jnp.int32)
-    head_ids = jnp.where(heads_at < 512, 512 * core + heads_at, 512 * (1 - core) + heads_at - 512)
-    features = jnp.arange(1152, dtype=jnp.int32)
-    put_rows = table(features, jnp.where(j < 9, 9 * dev + j, -1))
-    put_inner = table(inner_ids, jnp.where((j >= 9) & (j < 11), 2 * dev + j - 9, -1))
-    take_b = table(halves, jnp.where((j >= 9) & (j < 11), 2 * dev + j - 9, -1))
-    take_b_out = table(halves, jnp.where((j >= 8) & (j < 10), 2 * dev + j - 8, -1))
-    put_mix = table(head_ids, jnp.where(j < 8, 8 * dev + j, -1))
-    put_inner_out = table(inner_ids, jnp.where((j >= 8) & (j < 10), 2 * dev + j - 8, -1))
-    put_inner_down = table(halves, jnp.where(j >= 10, 2 * dev + j - 10, -1))
-
-    allowed = jnp.concatenate([allowed] * HEADS, axis=0)
-    n_one = hidden * scale_one
-    u_one = (n_one * (1.0 + gain_one_full)).astype(BF)
-    u_rows = dot(u_one, put_rows).astype(BF)
-    inner = [dot(u_rows, raw[i][:, 768:]).astype(BF) for i in (0, 1)]
-    sides = []
-    for i in range(3):
-        part = jnp.concatenate([inner[0][:, 128 * i : 128 * i + 128], inner[1][:, 128 * i : 128 * i + 128]], axis=1)
-        sides.append(u_rows + dot(part, put_inner).astype(BF))
-    kk = pick(is_first, *[dot(sides[1], raw[i][:, 512:640]) for i in (0, 1)])
-    vv = pick(is_first, *[dot(sides[2], raw[i][:, 640:768]) for i in (0, 1)])
-    kv_own = jnp.concatenate([turn(jnp.concatenate(kk, axis=1), cos, sin), vv[0], vv[1]], axis=1).astype(BF)
-
-    pair = jnp.concatenate([kv_own, other_half(kv_own)], axis=0)
+    down_parts = [down_line] + [shift(down_line, "x", k) for k in (1, 2, 3)]
     kv_parts = [pair] + list(after(ff_wide, *[shift(pair, "y", k) for k in (1, 2, 3)])[:3])
     kv_mine = jnp.concatenate(kv_parts, axis=0)
     kv = jnp.concatenate([kv_mine, other_core(kv_mine)], axis=0)
@@ -339,20 +348,21 @@
     scale_two, n_two, u_two = norm_parts(after_att, gain_two_full)
     u_all = gather_tokens(u_two)
 
-    raw_late, out_late, ff_all, _ = after(u_two, raw, raw_out, ff_all)
-    down_own, _ = after(ff_all, down_own)
-    down_raw = exchange(jnp.broadcast_to(down_own[None], (16, 56, 1408)), PLANE).reshape(896, 1408)
+    raw_late, out_late, _ = after(u_two, raw, raw_out)
     b_left, b_right = pick(is_first, *[dot(take_b, raw_late[i][:, :768]).astype(BF) for i in (0, 1)])
     left, right = pick(is_first, *[dot(take_b_out, out_late[i][:, :640]).astype(BF) for i in (0, 1)])
     b_out = jnp.concatenate([left, right[:, 128:]], axis=1)
     left, right = pick(is_first, *[dot(put_inner_down, out_late[i][:, :640]).astype(BF) for i in (0, 1)])
     b_down = jnp.concatenate([left, right[:, 128:]], axis=1)
     a_gate, a_up = pick(is_first, *[dot(put_rows, out_late[i][:, 768:]).astype(BF) for i in (0, 1)])
+    ff_all, _ = after((b_left, b_right, b_out, b_down, a_gate, a_up), ff_all)
     b_gate = ff_all[:, 144:160].reshape(256, 896)
     b_up = ff_all[:, 160:].reshape(256, 896)
-    w_gate = (ff_all[:, :72].reshape(1152, 896).astype(F32) + dot(a_gate, b_gate)).astype(BF)
-    w_up = (ff_all[:, 72:144].reshape(1152, 896).astype(F32) + dot(a_up, b_up)).astype(BF)
-
+    w_gate = (ff_all[:, :72].astype(F32) + dot(a_gate, b_gate).reshape(16, 72, 896)).astype(BF)
+    w_up = (ff_all[:, 72:144].astype(F32) + dot(a_up, b_up).reshape(16, 72, 896)).astype(BF)
+    w_gate, w_up = w_gate.reshape(1152, 896), w_up.reshape(1152, 896)
+    down_parts, _ = after(w_up, down_parts)
+    down_raw = placed(down_parts, "x", at_z, at_x).reshape(896, 1408)
     a_down = down_raw[:, 1152:]
     w_down = (down_raw[:, :1152].astype(F32) + dot(a_down, b_down)).astype(BF)
 
@@ -384,7 +394,6 @@
     up_first = leave(up_grads.reshape(4, 4, 88, 896), "x", 1, at_z, at_x)
     gw_down = dot_tl(act, g_all).astype(BF)
     gb_down = dot_tl(a_down, gw_down).astype(BF)
-    down_first = leave(gw_down.reshape(4, 4, 56, 1152), "z", 0, at_z, at_x)
 
     norm_two_back = norm_back(scale_two, n_two, gain_two_full, g_u_two)
     g_after = grad_result + norm_two_back
@@ -405,21 +414,23 @@
     probs = jnp.where(allowed, jnp.exp(scores_again - lse), 0.0)
     g_probs = dot_tr(g_rows, values)
     g_scores = (probs * (g_probs - jnp.sum(probs * g_probs, axis=-1, keepdims=True))).astype(BF)
-    gate_first, up_first, _ = after(g_scores, gate_first, up_first)
-    gate_line, up_line = add(gate_first).astype(BF), add(up_first).astype(BF)
-    gate_second = leave(gate_line, "x", 0, at_z, at_x)
-    up_second = leave(up_line, "z", 0, at_z, at_x)
-    g_scores, probs, _ = after((gate_line, up_line), g_scores, probs)
     g_keys = dot_tl(g_scores, q_rows) * score_scale
     g_values = dot_tl(probs.astype(BF), g_rows)
     g_kv = jnp.concatenate([g_keys, g_values], axis=1)
     n_mine = 8 * TOKENS
-    g_kv_sum = g_kv[:n_mine] + other_core(g_kv[n_mine:].astype(BF)).astype(F32)
+    gate_first, up_first, _ = after(g_kv, gate_first, up_first)
+    gate_line, up_line = add(gate_first).astype(BF), add(up_first).astype(BF)
+    gate_second = leave(gate_line, "x", 0, at_z, at_x)
+    up_second = leave(up_line, "z", 0, at_z, at_x)
+    g_away, _ = after((gate_line, up_line), g_kv[n_mine:].astype(BF))
+    g_kv_sum = g_kv[:n_mine] + other_core(g_away).astype(F32)
     g_kv_b = g_kv_sum.astype(BF)
     g_parts = [shift(g_kv_b[320 * k : 320 * (k + 1)], "y", 4 - k) for k in (1, 2, 3)]
-    g_scores, side_out, gate_second, up_second, down_first, gb_down, _ = after(
-        g_kv_b, g_scores, side_out, gate_second, up_second, down_first, gb_down
-    )
+    g_scores, gb_down, _ = after(g_kv_b, g_scores, gb_down)
+    g_pair = add([g_kv_sum[:320]] + list(g_parts))
+    away = other_half(g_pair[160:].astype(BF))
+    gate_second, up_second, gw_down, _ = after(g_pair, gate_second, up_second, gw_down)
+    down_first = leave(gw_down.reshape(4, 4, 56, 1152), "z", 1, at_z, at_x)
     g_q_rows = dot(g_scores, keys) * score_scale
     g_q = [
         jnp.concatenate(
@@ -471,16 +482,13 @@
     chip_q = of_chip(
         *[(dot_tl(sides[0], g_q[i]) + dot_tl(more_side, more_grad)).astype(BF) for i in (0, 1)]
     )
-    g_parts = after(chip_q, *g_parts)[:3]
-    g_pair = add([g_kv_sum[:320]] + list(g_parts))
-    away = other_half(g_pair[160:].astype(BF))
     side_out, _ = after(g_pair, side_out)
     left, right = pick(is_first, gb_down[:, :640], gb_down[:, 512:])
     chip_out = of_chip(
         dot_tl(side_out, g_half[0]) + dot_tl(put_inner_down, left),
         dot_tl(side_out, g_half[1]) + dot_tl(put_inner_down, right),
     )
-    g_kv_own = g_pair[:160] + after((leaving, chip_out), away)[0].astype(F32)
+    g_kv_own = g_pair[:160] + after(chip_q, away)[0].astype(F32)
     g_k = turn_back(g_kv_own[:, :256], cos, sin).astype(BF)
     g_v = g_kv_own[:, 256:].astype(BF)
     g_k = pick(is_first, g_k[:, :128], g_k[:, 128:])
@@ -491,6 +499,7 @@
             for i in (0, 1)
         ]
     )
+    chip_kv, _ = after(slab, chip_kv)
     chip_sums = jnp.concatenate([chip_q, chip_kv, chip_out], axis=2)
     parts = exchange(chip_sums, CHIPS)
     down_first, _ = after(g_kv_own, down_first)

time: 649 us -> 665 us (1.025)
  the two profiles are of different devices: /device:TPU:13 before, /device:TPU:1 now
where the time goes in v8:
time: 665 us; the launch traced here: 655 us
  matrix products  176 us (26%)
  starting transfers between devices  158 us (24%)
  waiting for transfers between devices  132 us (20%)
  local copies, waits for them, and re-layouts  96.2 us (14%)
  other arithmetic  82.3 us (12%)
  between operations  9.43 us (1%)
    ppermute x42, waiting for transfers between devices, shift(): lax.ppermute(x, RING[axis], [(number[i], number[(i + k) % 4]) for i in ra...  82.6 us
    dot_general x37, matrix products, dot(): return jnp.dot(a, b, preferred_element_type=F32)  77.6 us
    dot_general x38, matrix products, dot_tr(): lax.dot_general(a, b, (((1,), (1,)), ((), ())), preferred_element_type=F32)  64.6 us
    all_to_all x5, starting transfers between devices, exchange(): return lax.all_to_all(x, axes, split_axis=0, concat_axis=0, tiled=True)  57.4 us
    ppermute x42, starting transfers between devices, shift(): lax.ppermute(x, RING[axis], [(number[i], number[(i + k) % 4]) for i in ra...  48.5 us
    dot_general x19, matrix products, dot_tl(): lax.dot_general(a, b, (((0,), (0,)), ((), ())), preferred_element_type=F32)  34.1 us
    ppermute x26, starting transfers between devices, other_core(): return lax.ppermute(x, 'c', [(0, 1), (1, 0)])  32.5 us
    ppermute x7, waiting for transfers between devices, column_shift(): return lax.ppermute(x, ('y', 'c'), route)  26.5 us
  transfers between devices with their start and end apart: 84, of which 24 were waited for; matrix products, arithmetic and copies ran while one was open for 43% of the time, Pallas kernels for 0%

profile of v8, /device:TPU:1, one launch (start us, length us, event | category | flops | bytes accessed | tf_op | source)
XLA Modules:
  0.0 655.0 jit_solution(3072263374784477312)
XLA Ops:
  14.5 11.3 %all-to-all-start = ((bf16[64,24,1152]{2,1,0:T(8,128)(2,1)}), bf16[64,24,1152]{2,1,0:T(8,128)(2,1)S(1)}, u32[]{:S(2)}, u32[]{:S(2)}) async-start(bf16[64,24,1152]{2,1,0:T(8,128)(2,1)} %broadcast_in_dim.163), calls=%async_computation | async-start | bytes 7077888 | tf_op jit(solution)/shard_map/all_to_all | solution.py:35
  57.5 14.5 %collective-permute-done.2 = bf16[56,1408]{1,0:T(8,128)(2,1)} collective-permute-done((bf16[56,1408]{1,0:T(8,128)(2,1)}, bf16[56,1408]{1,0:T(8,128)(2,1)}, u32[]{:S(2)}, u32[]{:S(2)}) %collective-permute-start.2) | collective-permute-done | bytes 157728 | tf_op jit(solution)/shard_map/ppermute | solution.py:234
  84.9 19.4 %all-to-all-start.1 = ((bf16[64,24,1024]{2,1,0:T(8,128)(2,1)}), bf16[64,24,1024]{2,1,0:T(8,128)(2,1)}, u32[]{:S(2)}, u32[]{:S(2)}) async-start(bf16[64,24,1024]{2,1,0:T(8,128)(2,1)} %broadcast_in_dim.166), calls=%async_computation.1 | async-start | bytes 6291456 | tf_op jit(solution)/shard_map/all_to_all | solution.py:35
  133.2 8.1 %collective-permute-done.7 = bf16[24,896]{1,0:T(8,128)(2,1)S(1)} collective-permute-done((bf16[24,896]{1,0:T(8,128)(2,1)S(1)}, bf16[24,896]{1,0:T(8,128)(2,1)S(1)}, u32[]{:S(2)}, u32[]{:S(2)}) %collective-permute-start.7) | collective-permute-done | bytes 43040 | tf_op jit(solution)/shard_map/ppermute | solution.py:227
  141.3 5.0 collective-permute-done.8
  146.4 4.7 collective-permute-done.9
  151.8 4.7 collective-permute-done.10
  179.8 4.4 collective-permute-done.16
  199.7 12.5 %all-to-all-start.2 = ((bf16[16,176,896]{2,1,0:T(8,128)(2,1)}), bf16[16,176,896]{2,1,0:T(8,128)(2,1)}, u32[]{:S(2)}, u32[]{:S(2)}) async-start(bf16[16,176,896]{2,1,0:T(8,128)(2,1)} %broadcast_in_dim.173), calls=%async_computation.2 | async-start | bytes 10092544 | tf_op jit(solution)/shard_map/all_to_all | solution.py:35
  262.8 3.7 collective-permute-start.24
  271.1 6.7 %all-to-all-done.2 = bf16[16,176,896]{2,1,0:T(8,128)(2,1)} async-done(((bf16[16,176,896]{2,1,0:T(8,128)(2,1)}), bf16[16,176,896]{2,1,0:T(8,128)(2,1)}, u32[]{:S(2)}, u32[]{:S(2)}) %all-to-all-start.2) | async-done | bytes 5046304 | tf_op jit(solution)/shard_map/all_to_all | solution.py:35
  281.9 6.1 fusion.606
  288.0 3.9 add_convert_fusion
  291.9 8.9 %multiply_convert_fusion.1 = (bf16[1280,896]{1,0:T(8,128)(2,1)S(1)}, f32[1280,896]{1,0:T(8,128)}) fusion(f32[1280,896]{1,0:T(8,128)S(1)} %fusion.606, bf16[1280,1152]{1,0:T(8,128)(2,1)} %constant_dynamic-update-slice_fusion.39, bf16[1152,896]{1,0:T(8,128)(2,1)S(1)} %bitcast.325), kind=kOutput, calls=%fused_computation.45 | convolution fusion | flops 2653880320 | bytes 16482304 | tf_op jit(solution)/shard_map/dot_general | solution.py:23
  300.8 9.4 %collective-permute-done.28 = bf16[4,56,1408]{2,1,0:T(8,128)(2,1)} collective-permute-done((bf16[4,56,1408]{2,1,0:T(8,128)(2,1)}, bf16[4,56,1408]{2,1,0:T(8,128)(2,1)}, u32[]{:S(2)}, u32[]{:S(2)}) %collective-permute-start.28) | collective-permute-done | bytes 630816 | tf_op jit(solution)/shard_map/ppermute | solution.py:48
  316.0 3.9 fusion.607
  336.7 12.4 %collective-permute-done.35 = bf16[160,1152]{1,0:T(8,128)(2,1)S(1)} collective-permute-done((bf16[160,1152]{1,0:T(8,128)(2,1)S(1)}, bf16[160,1152]{1,0:T(8,128)(2,1)S(1)}, u32[]{:S(2)}, u32[]{:S(2)}) %collective-permute-start.35) | collective-permute-done | bytes 368672 | tf_op jit(solution)/shard_map/ppermute | solution.py:48
  366.1 4.9 collective-permute-done.38
  379.2 11.0 %fusion.10 = (bf16[1280,896]{1,0:T(8,128)(2,1)S(1)}, bf16[1280,896]{1,0:T(8,128)(2,1)S(1)}) fusion(f32[1280,896]{1,0:T(8,128)} %copy-done.178, f32[1280,896]{1,0:T(8,128)} %get-tuple-element.442, bf16[1280,1152]{1,0:T(8,128)(2,1)} %constant_dynamic-update-slice_fusion.47, bf16[896,1152]{1,0:T(8,128)(2,1)S(1)} %copy-done.169), kind=kOutput, calls=%fused_computation.37 | convolution fusion | flops 2672230400 | bytes 18776064 | tf_op jit(solution)/shard_map/dot_general | solution.py:31
  399.1 5.1 convolution_convert_fusion.2
  406.6 5.1 convolution_convert_fusion.1
  425.5 5.8 collective-permute-done.45
  442.9 4.7 multiply_reduce_fusion
  448.1 5.8 multiply_convert_fusion
  460.0 11.1 %collective-permute-done.56 = bf16[4,88,896]{2,1,0:T(8,128)(2,1)S(1)} collective-permute-done((bf16[4,88,896]{2,1,0:T(8,128)(2,1)S(1)}, bf16[4,88,896]{2,1,0:T(8,128)(2,1)S(1)}, u32[]{:S(2)}, u32[]{:S(2)}) %collective-permute-start.56) | collective-permute-done | bytes 630816 | tf_op jit(solution)/shard_map/ppermute | solution.py:48
  474.8 6.5 collective-permute-start.57
  501.7 6.7 %collective-permute-done.60 = bf16[320,512]{1,0:T(8,128)(2,1)S(1)} collective-permute-done((bf16[320,512]{1,0:T(8,128)(2,1)S(1)}, bf16[320,512]{1,0:T(8,128)(2,1)S(1)}, u32[]{:S(2)}, u32[]{:S(2)}) %collective-permute-start.60) | collective-permute-done | bytes 327712 | tf_op jit(solution)/shard_map/ppermute | solution.py:48
  521.8 5.0 all-to-all-start.3
  540.4 13.8 %collective-permute-done.72 = bf16[4,56,1152]{2,1,0:T(8,128)(2,1)S(1)} collective-permute-done((bf16[4,56,1152]{2,1,0:T(8,128)(2,1)S(1)}, bf16[4,56,1152]{2,1,0:T(8,128)(2,1)S(1)}, u32[]{:S(2)}, u32[]{:S(2)}) %collective-permute-start.72) | collective-permute-done | bytes 516128 | tf_op jit(solution)/shard_map/ppermute | solution.py:48
  554.2 4.2 collective-permute-done.74
  570.9 9.2 %all-to-all-start.4 = ((bf16[64,24,1408]{2,1,0:T(8,128)(2,1)}), bf16[64,24,1408]{2,1,0:T(8,128)(2,1)}, u32[]{:S(2)}, u32[]{:S(2)}) async-start(bf16[64,24,1408]{2,1,0:T(8,128)(2,1)} %pad_maximum_fusion.1), calls=%async_computation.4 | async-start | bytes 8650752 | tf_op jit(solution)/shard_map/all_to_all | solution.py:35
  616.3 5.0 collective-permute-start.78
  (812 shorter events, 401.9 us)
Async XLA Ops:
  14.5 57.5 %all-to-all-start = ((bf16[64,24,1152]{2,1,0:T(8,128)(2,1)}), bf16[64,24,1152]{2,1,0:T(8,128)(2,1)S(1)}, u32[]{:S(2)}, u32[]{:S(2)}) async-start(bf16[64,24,1152]{2,1,0:T(8,128)(2,1)} %broadcast_in_dim.163), calls=%async_computation | async-start | bytes 7077888 | tf_op jit(solution)/shard_map/all_to_all | solution.py:35
  34.0 21.9 %collective-permute-start.1 = (bf16[12,1024]{1,0:T(8,128)(2,1)}, bf16[12,1024]{1,0:T(8,128)(2,1)}, u32[]{:S(2)}, u32[]{:S(2)}) collective-permute-start(bf16[12,1024]{1,0:T(8,128)(2,1)} %broadcast_select_fusion.19), channel_id=1, source_target_pairs={{0,1},{1,0},{2,3},{3,2},{4,5},{5,4},{6,7},{7,6},{8,9},{9,8},{10,11... | collective-permute-start | bytes 73736 | tf_op jit(solution)/shard_map/ppermute | solution.py:39
  36.3 35.7 %collective-permute-start.2 = (bf16[56,1408]{1,0:T(8,128)(2,1)}, bf16[56,1408]{1,0:T(8,128)(2,1)}, u32[]{:S(2)}, u32[]{:S(2)}) collective-permute-start(bf16[56,1408]{1,0:T(8,128)(2,1)} %fusion.322), channel_id=1, source_target_pairs={{0,0},{1,32},{2,64},{3,96},{4,8},{5,40},{6,72},{7,104},{8,16},{9,4... | collective-permute-start | bytes 473096 | tf_op jit(solution)/shard_map/ppermute | solution.py:234
  72.0 39.4 %collective-permute-start.3 = (bf16[64,24,1152]{2,1,0:T(8,128)(2,1)S(1)}, bf16[64,24,1152]{2,1,0:T(8,128)(2,1)}, u32[]{:S(2)}, u32[]{:S(2)}) collective-permute-start(bf16[64,24,1152]{2,1,0:T(8,128)(2,1)S(1)} %all-to-all-done), channel_id=1, source_target_pairs={{0,1},{1,0},{2,3},{3,2},{4,5},{5,4},{6,7},{7,6},{8,9},{9,8},{10,11... | collective-permute-start | bytes 10616840 | tf_op jit(solution)/shard_map/ppermute | solution.py:39
  84.9 86.5 %all-to-all-start.1 = ((bf16[64,24,1024]{2,1,0:T(8,128)(2,1)}), bf16[64,24,1024]{2,1,0:T(8,128)(2,1)}, u32[]{:S(2)}, u32[]{:S(2)}) async-start(bf16[64,24,1024]{2,1,0:T(8,128)(2,1)} %broadcast_in_dim.166), calls=%async_computation.1 | async-start | bytes 6291456 | tf_op jit(solution)/shard_map/all_to_all | solution.py:35
  120.0 45.5 %collective-permute-start.4 = (bf16[160,512]{1,0:T(8,128)(2,1)S(1)}, bf16[160,512]{1,0:T(8,128)(2,1)S(1)}, u32[]{:S(2)}, u32[]{:S(2)}) collective-permute-start(bf16[160,512]{1,0:T(8,128)(2,1)S(1)} %get-tuple-element.382), channel_id=1, source_target_pairs={{0,8},{8,0},{1,9},{9,1},{2,10},{10,2},{3,11},{11,3},{4,12},{12,4},... | collective-permute-start | bytes 491528 | tf_op jit(solution)/shard_map/ppermute | solution.py:43
  122.7 41.5 %collective-permute-start.13 = (bf16[56,1408]{1,0:T(8,128)(2,1)}, bf16[56,1408]{1,0:T(8,128)(2,1)S(1)}, u32[]{:S(2)}, u32[]{:S(2)}) collective-permute-start(bf16[56,1408]{1,0:T(8,128)(2,1)} %collective-permute-done.2), channel_id=1, source_target_pairs={{0,32},{32,64},{64,96},{96,0},{1,33},{33,65},{65,97},{97,1},{2,34}... | collective-permute-start | bytes 473096 | tf_op jit(solution)/shard_map/ppermute | solution.py:48
  123.9 41.0 %collective-permute-start.14 = (bf16[56,1408]{1,0:T(8,128)(2,1)}, bf16[56,1408]{1,0:T(8,128)(2,1)S(1)}, u32[]{:S(2)}, u32[]{:S(2)}) collective-permute-start(bf16[56,1408]{1,0:T(8,128)(2,1)} %collective-permute-done.2), channel_id=1, source_target_pairs={{0,64},{32,96},{64,0},{96,32},{1,65},{33,97},{65,1},{97,33},{2,66}... | collective-permute-start | bytes 473096 | tf_op jit(solution)/shard_map/ppermute | solution.py:48
  126.5 44.3 %collective-permute-start.15 = (bf16[56,1408]{1,0:T(8,128)(2,1)}, bf16[56,1408]{1,0:T(8,128)(2,1)S(1)}, u32[]{:S(2)}, u32[]{:S(2)}) collective-permute-start(bf16[56,1408]{1,0:T(8,128)(2,1)} %collective-permute-done.2), channel_id=1, source_target_pairs={{0,96},{32,0},{64,32},{96,64},{1,97},{33,1},{65,33},{97,65},{2,98}... | collective-permute-start | bytes 473096 | tf_op jit(solution)/shard_map/ppermute | solution.py:48
  190.3 27.0 %collective-permute-start.18 = (bf16[1280,512]{1,0:T(8,128)(2,1)}, bf16[1280,512]{1,0:T(8,128)(2,1)}, u32[]{:S(2)}, u32[]{:S(2)}) collective-permute-start(bf16[1280,512]{1,0:T(8,128)(2,1)} %get-tuple-element.366), channel_id=1, source_target_pairs={{0,1},{1,0},{2,3},{3,2},{4,5},{5,4},{6,7},{7,6},{8,9},{9,8},{10,11... | collective-permute-start | bytes 3932168 | tf_op jit(solution)/shard_map/ppermute | solution.py:39
  196.1 34.7 %collective-permute-start.19 = (bf16[64,24,1024]{2,1,0:T(8,128)(2,1)}, bf16[64,24,1024]{2,1,0:T(8,128)(2,1)}, u32[]{:S(2)}, u32[]{:S(2)}) collective-permute-start(bf16[64,24,1024]{2,1,0:T(8,128)(2,1)} %all-to-all-done.1), channel_id=1, source_target_pairs={{0,1},{1,0},{2,3},{3,2},{4,5},{5,4},{6,7},{7,6},{8,9},{9,8},{10,11... | collective-permute-start | bytes 9437192 | tf_op jit(solution)/shard_map/ppermute | solution.py:39
  199.7 78.2 %all-to-all-start.2 = ((bf16[16,176,896]{2,1,0:T(8,128)(2,1)}), bf16[16,176,896]{2,1,0:T(8,128)(2,1)}, u32[]{:S(2)}, u32[]{:S(2)}) async-start(bf16[16,176,896]{2,1,0:T(8,128)(2,1)} %broadcast_in_dim.173), calls=%async_computation.2 | async-start | bytes 10092544 | tf_op jit(solution)/shard_map/all_to_all | solution.py:35
  212.3 88.5 %collective-permute-start.27 = (bf16[4,56,1408]{2,1,0:T(8,128)(2,1)}, bf16[4,56,1408]{2,1,0:T(8,128)(2,1)}, u32[]{:S(2)}, u32[]{:S(2)}) collective-permute-start(bf16[4,56,1408]{2,1,0:T(8,128)(2,1)} %bitcast_dynamic-update-slice_fusion.4), channel_id=1, source_target_pairs={{0,16},{16,8},{8,24},{24,0},{1,17},{17,9},{9,25},{25,1},{2,18},{18... | collective-permute-start | bytes 1892360 | tf_op jit(solution)/shard_map/ppermute | solution.py:48
  213.7 96.6 %collective-permute-start.28 = (bf16[4,56,1408]{2,1,0:T(8,128)(2,1)}, bf16[4,56,1408]{2,1,0:T(8,128)(2,1)}, u32[]{:S(2)}, u32[]{:S(2)}) collective-permute-start(bf16[4,56,1408]{2,1,0:T(8,128)(2,1)} %bitcast_dynamic-update-slice_fusion.4), channel_id=1, source_target_pairs={{0,8},{16,24},{8,0},{24,16},{1,9},{17,25},{9,1},{25,17},{2,10},{18... | collective-permute-start | bytes 1892360 | tf_op jit(solution)/shard_map/ppermute | solution.py:48
  216.1 94.2 %collective-permute-start.29 = (bf16[4,56,1408]{2,1,0:T(8,128)(2,1)}, bf16[4,56,1408]{2,1,0:T(8,128)(2,1)}, u32[]{:S(2)}, u32[]{:S(2)}) collective-permute-start(bf16[4,56,1408]{2,1,0:T(8,128)(2,1)} %bitcast_dynamic-update-slice_fusion.4), channel_id=1, source_target_pairs={{0,24},{16,0},{8,16},{24,8},{1,25},{17,1},{9,17},{25,9},{2,26},{18... | collective-permute-start | bytes 1892360 | tf_op jit(solution)/shard_map/ppermute | solution.py:48
  406.6 50.6 %collective-permute-start.51 = (bf16[4,88,896]{2,1,0:T(8,128)(2,1)}, bf16[4,88,896]{2,1,0:T(8,128)(2,1)}, u32[]{:S(2)}, u32[]{:S(2)}) collective-permute-start(bf16[4,88,896]{2,1,0:T(8,128)(2,1)} %get-tuple-element.297), channel_id=1, source_target_pairs={{0,96},{32,0},{64,32},{96,64},{1,97},{33,1},{65,33},{97,65},{2,98}... | collective-permute-start | bytes 1892360 | tf_op jit(solution)/shard_map/ppermute | solution.py:48
  417.3 42.6 %collective-permute-start.52 = (bf16[4,88,896]{2,1,0:T(8,128)(2,1)}, bf16[4,88,896]{2,1,0:T(8,128)(2,1)}, u32[]{:S(2)}, u32[]{:S(2)}) collective-permute-start(bf16[4,88,896]{2,1,0:T(8,128)(2,1)} %get-tuple-element.298), channel_id=1, source_target_pairs={{0,64},{32,96},{64,0},{96,32},{1,65},{33,97},{65,1},{97,33},{2,66}... | collective-permute-start | bytes 1892360 | tf_op jit(solution)/shard_map/ppermute | solution.py:48
  423.1 36.8 %collective-permute-start.53 = (bf16[4,88,896]{2,1,0:T(8,128)(2,1)}, bf16[4,88,896]{2,1,0:T(8,128)(2,1)}, u32[]{:S(2)}, u32[]{:S(2)}) collective-permute-start(bf16[4,88,896]{2,1,0:T(8,128)(2,1)} %get-tuple-element.295), channel_id=1, source_target_pairs={{0,32},{32,64},{64,96},{96,0},{1,33},{33,65},{65,97},{97,1},{2,34}... | collective-permute-start | bytes 1892360 | tf_op jit(solution)/shard_map/ppermute | solution.py:48
  424.3 35.8 %collective-permute-start.54 = (bf16[4,88,896]{2,1,0:T(8,128)(2,1)}, bf16[4,88,896]{2,1,0:T(8,128)(2,1)}, u32[]{:S(2)}, u32[]{:S(2)}) collective-permute-start(bf16[4,88,896]{2,1,0:T(8,128)(2,1)} %get-tuple-element.293), channel_id=1, source_target_pairs={{0,24},{16,0},{8,16},{24,8},{1,25},{17,1},{9,17},{25,9},{2,26},{18... | collective-permute-start | bytes 1892360 | tf_op jit(solution)/shard_map/ppermute | solution.py:48
  431.3 28.7 %collective-permute-start.55 = (bf16[4,88,896]{2,1,0:T(8,128)(2,1)}, bf16[4,88,896]{2,1,0:T(8,128)(2,1)}, u32[]{:S(2)}, u32[]{:S(2)}) collective-permute-start(bf16[4,88,896]{2,1,0:T(8,128)(2,1)} %get-tuple-element.294), channel_id=1, source_target_pairs={{0,8},{16,24},{8,0},{24,16},{1,9},{17,25},{9,1},{25,17},{2,10},{18... | collective-permute-start | bytes 1892360 | tf_op jit(solution)/shard_map/ppermute | solution.py:48
  487.5 23.1 %collective-permute-start.67 = (bf16[88,896]{1,0:T(8,128)(2,1)S(1)}, bf16[88,896]{1,0:T(8,128)(2,1)S(1)}, u32[]{:S(2)}, u32[]{:S(2)}) collective-permute-start(bf16[88,896]{1,0:T(8,128)(2,1)S(1)} %get-tuple-element.337), channel_id=1, source_target_pairs={{0,96},{32,0},{64,32},{96,64},{1,97},{33,1},{65,33},{97,65},{2,98}... | collective-permute-start | bytes 473096 | tf_op jit(solution)/shard_map/ppermute | solution.py:48
  487.8 26.9 %collective-permute-start.68 = (bf16[88,896]{1,0:T(8,128)(2,1)S(1)}, bf16[88,896]{1,0:T(8,128)(2,1)S(1)}, u32[]{:S(2)}, u32[]{:S(2)}) collective-permute-start(bf16[88,896]{1,0:T(8,128)(2,1)S(1)} %get-tuple-element.336), channel_id=1, source_target_pairs={{0,64},{32,96},{64,0},{96,32},{1,65},{33,97},{65,1},{97,33},{2,66}... | collective-permute-start | bytes 473096 | tf_op jit(solution)/shard_map/ppermute | solution.py:48
  516.9 44.7 %collective-permute-start.70 = (bf16[1536,640]{1,0:T(8,128)(2,1)}, bf16[1536,640]{1,0:T(8,128)(2,1)}, u32[]{:S(2)}, u32[]{:S(2)}) collective-permute-start(bf16[1536,640]{1,0:T(8,128)(2,1)} %add_convert_fusion.3), channel_id=1, source_target_pairs={{0,1},{1,0},{2,3},{3,2},{4,5},{5,4},{6,7},{7,6},{8,9},{9,8},{10,11... | collective-permute-start | bytes 5898248 | tf_op jit(solution)/shard_map/ppermute | solution.py:39
  521.8 45.9 %all-to-all-start.3 = ((bf16[8,32,896]{2,1,0:T(8,128)(2,1)}), bf16[8,32,896]{2,1,0:T(8,128)(2,1)}, u32[]{:S(2)}, u32[]{:S(2)}) async-start(bf16[8,32,896]{2,1,0:T(8,128)(2,1)} %bitcast.331), calls=%async_computation.3 | async-start | bytes 917504 | tf_op jit(solution)/shard_map/all_to_all | solution.py:35
  528.6 25.6 %collective-permute-start.72 = (bf16[4,56,1152]{2,1,0:T(8,128)(2,1)S(1)}, bf16[4,56,1152]{2,1,0:T(8,128)(2,1)S(1)}, u32[]{:S(2)}, u32[]{:S(2)}) collective-permute-start(bf16[4,56,1152]{2,1,0:T(8,128)(2,1)S(1)} %get-tuple-element.301), channel_id=1, source_target_pairs={{0,96},{32,0},{64,32},{96,64},{1,97},{33,1},{65,33},{97,65},{2,98}... | collective-permute-start | bytes 1548296 | tf_op jit(solution)/shard_map/ppermute | solution.py:48
  532.2 22.1 %collective-permute-start.73 = (bf16[4,56,1152]{2,1,0:T(8,128)(2,1)S(1)}, bf16[4,56,1152]{2,1,0:T(8,128)(2,1)S(1)}, u32[]{:S(2)}, u32[]{:S(2)}) collective-permute-start(bf16[4,56,1152]{2,1,0:T(8,128)(2,1)S(1)} %get-tuple-element.300), channel_id=1, source_target_pairs={{0,64},{32,96},{64,0},{96,32},{1,65},{33,97},{65,1},{97,33},{2,66}... | collective-permute-start | bytes 1548296 | tf_op jit(solution)/shard_map/ppermute | solution.py:48
  533.1 25.4 %collective-permute-start.74 = (bf16[4,56,1152]{2,1,0:T(8,128)(2,1)S(1)}, bf16[4,56,1152]{2,1,0:T(8,128)(2,1)S(1)}, u32[]{:S(2)}, u32[]{:S(2)}) collective-permute-start(bf16[4,56,1152]{2,1,0:T(8,128)(2,1)S(1)} %get-tuple-element.299), channel_id=1, source_target_pairs={{0,32},{32,64},{64,96},{96,0},{1,33},{33,65},{65,97},{97,1},{2,34}... | collective-permute-start | bytes 1548296 | tf_op jit(solution)/shard_map/ppermute | solution.py:48
  539.6 24.7 %collective-permute-start.63 = (bf16[1536,256]{0,1:T(8,128)(2,1)S(1)}, bf16[1536,256]{0,1:T(8,128)(2,1)S(1)}, u32[]{:S(2)}, u32[]{:S(2)}) collective-permute-start(bf16[1536,256]{0,1:T(8,128)(2,1)S(1)} %pad_maximum_fusion.2), channel_id=1, source_target_pairs={{0,1},{1,0},{2,3},{3,2},{4,5},{5,4},{6,7},{7,6},{8,9},{9,8},{10,11... | collective-permute-start | bytes 2359304 | tf_op jit(solution)/shard_map/ppermute | solution.py:39
  559.8 54.7 %collective-permute-start.75 = (bf16[56,1152]{1,0:T(8,128)(2,1)}, bf16[56,1152]{1,0:T(8,128)(2,1)}, u32[]{:S(2)}, u32[]{:S(2)}) collective-permute-start(bf16[56,1152]{1,0:T(8,128)(2,1)} %get-tuple-element.341), channel_id=1, source_target_pairs={{0,24},{16,0},{8,16},{24,8},{1,25},{17,1},{9,17},{25,9},{2,26},{18... | collective-permute-start | bytes 387080 | tf_op jit(solution)/shard_map/ppermute | solution.py:48
  560.5 54.1 %collective-permute-start.76 = (bf16[56,1152]{1,0:T(8,128)(2,1)}, bf16[56,1152]{1,0:T(8,128)(2,1)}, u32[]{:S(2)}, u32[]{:S(2)}) collective-permute-start(bf16[56,1152]{1,0:T(8,128)(2,1)} %get-tuple-element.340), channel_id=1, source_target_pairs={{0,8},{16,24},{8,0},{24,16},{1,9},{17,25},{9,1},{25,17},{2,10},{18... | collective-permute-start | bytes 387080 | tf_op jit(solution)/shard_map/ppermute | solution.py:48
  560.8 53.8 %collective-permute-start.77 = (bf16[56,1152]{1,0:T(8,128)(2,1)}, bf16[56,1152]{1,0:T(8,128)(2,1)}, u32[]{:S(2)}, u32[]{:S(2)}) collective-permute-start(bf16[56,1152]{1,0:T(8,128)(2,1)} %get-tuple-element.339), channel_id=1, source_target_pairs={{0,16},{16,8},{8,24},{24,0},{1,17},{17,9},{9,25},{25,1},{2,18},{18... | collective-permute-start | bytes 387080 | tf_op jit(solution)/shard_map/ppermute | solution.py:48
  570.9 68.8 %all-to-all-start.4 = ((bf16[64,24,1408]{2,1,0:T(8,128)(2,1)}), bf16[64,24,1408]{2,1,0:T(8,128)(2,1)}, u32[]{:S(2)}, u32[]{:S(2)}) async-start(bf16[64,24,1408]{2,1,0:T(8,128)(2,1)} %pad_maximum_fusion.1), calls=%async_computation.4 | async-start | bytes 8650752 | tf_op jit(solution)/shard_map/all_to_all | solution.py:35
  (235 other events, 2462.3 us)

commit v9 on v8

--- a/solution.py
+++ b/solution.py
@@ -216,21 +216,36 @@
     lower, upper = pick(is_first, keep, other_core(send))
     out_own = jnp.concatenate([lower, upper], axis=0)
 
-    def column_of(k):
-        return 2 * ((at_y + k // 2) % 4) + (core + k) % 2
-
-    def column_shift(x, k):
-        route = []
-        for y in range(4):
-            for c in range(2):
-                route.append((2 * y + c, 2 * ((y + k // 2) % 4) + (c + k) % 2))
-        return lax.ppermute(x, ("y", "c"), route)
-
     rows22 = jnp.pad(jnp.concatenate([wg, wu, bg, bu], axis=0), ((0, 2), (0, 0)))
     rows22 = jnp.concatenate([rows22[:, 864 * t : 864 * (t + 1)] for t in range(8)], axis=0)
     wider = jnp.arange(896, dtype=jnp.int32)
     wider = table(jnp.arange(864, dtype=jnp.int32), jnp.where(wider % 56 < 54, wider // 56 * 54 + wider % 56, -1))
     rows22 = dot(rows22, wider).astype(BF).reshape(8, 24, 896)
+    columns_of = rows22.reshape(4, 2, 24, 896)
+    mine = lax.dynamic_index_in_dim(columns_of, core, 1, keepdims=False)
+    theirs = lax.dynamic_index_in_dim(columns_of, 1 - core, 1, keepdims=False)
+    columns_of = jnp.stack([mine, other_core(theirs)], axis=1).reshape(4, 48, 896)
+    slab = []
+    for k in range(4):
+        piece = lax.dynamic_index_in_dim(columns_of, (at_y + k) % 4, 0, keepdims=False)
+        slab.append(shift(piece, "y", k) if k else piece)
+    slab = jnp.concatenate(slab, axis=0)
+    back = jnp.arange(8, dtype=jnp.int32)
+    sources = 2 * ((at_y - back // 2) % 4) + (core - back) % 2
+    row = jnp.arange(176, dtype=jnp.int32)
+    low = row - 144
+    at_row = jnp.where(
+        row < 72,
+        row // 9 * 24 + row % 9,
+        jnp.where(
+            row < 144,
+            (row - 72) // 9 * 24 + 9 + (row - 72) % 9,
+            low % 16 // 2 * 24 + 18 + low // 16 * 2 + low % 2,
+        ),
+    )
+    in_slab = jnp.arange(192, dtype=jnp.int32)
+    in_slab = jnp.repeat(sources, 24) * 24 + in_slab % 24
+    ff_own = dot(table(at_row, in_slab), slab).astype(BF)
     down_own = lax.ppermute(
         jnp.pad(jnp.concatenate([wd, ad], axis=1), ((0, 2), (0, 0))), EVERY, down_route()
     )
@@ -254,7 +269,7 @@
     allowed = ((key_seg == q_seg) | (key_seg == 0) | parent) & (key_pos <= q_pos)
 
     scale_one = lax.rsqrt(jnp.mean(hidden * hidden, axis=-1, keepdims=True) + EPSILON)
-    raw_one, _ = after((rows22, out_own, down_own, cos, sin, allowed, scale_one), raw_one)
+    raw_one, _ = after((ff_own, out_own, down_own, cos, sin, allowed, scale_one), raw_one)
     raw_two = other_core(raw_one)
     marks = raw_one.reshape(128, 12, 1152)[:, 9, 768:896]
     gain_one_full = marks[:, :9].reshape(1, 1152).astype(F32)
@@ -296,28 +311,7 @@
     kv_own = jnp.concatenate([turn(jnp.concatenate(kk, axis=1), cos, sin), vv[0], vv[1]], axis=1).astype(BF)
 
     pair = jnp.concatenate([kv_own, other_half(kv_own)], axis=0)
-    rows22, down_own, _ = after(kv_own, rows22, down_own)
-    slab = []
-    for k in range(8):
-        piece = lax.dynamic_index_in_dim(rows22, column_of(k), 0, keepdims=False)
-        slab.append(column_shift(piece, k) if k else piece)
-    slab = jnp.concatenate(slab, axis=0)
-    back = jnp.arange(8, dtype=jnp.int32)
-    sources = 2 * ((at_y - back // 2) % 4) + (core - back) % 2
-    row = jnp.arange(176, dtype=jnp.int32)
-    low = row - 144
-    at_row = jnp.where(
-        row < 72,
-        row // 9 * 24 + row % 9,
-        jnp.where(
-            row < 144,
-            (row - 72) // 9 * 24 + 9 + (row - 72) % 9,
-            low % 16 // 2 * 24 + 18 + low // 16 * 2 + low % 2,
-        ),
-    )
-    in_slab = jnp.arange(192, dtype=jnp.int32)
-    in_slab = jnp.repeat(sources, 24) * 24 + in_slab % 24
-    ff_own = dot(table(at_row, in_slab), slab).astype(BF)
+    down_own, _ = after(kv_own, down_own)
     down_line = placed([down_own] + [shift(down_own, "z", k) for k in (1, 2, 3)], "z", at_z, at_x)
     ff_own, _ = after((out_one, down_line), ff_own)
     ff_wide = jnp.broadcast_to(ff_own[None], (16, 176, 896))
@@ -409,6 +403,10 @@
         + dot_tr(gi_out[:, 128:], raw_out[1][:, 640:768])
     )
     g_mix = dot_tr(d_out.astype(BF), put_mix).astype(BF)
+    gate_first, _ = after(g_mix, gate_first)
+    gate_line = add(gate_first).astype(BF)
+    g_mix, _ = after(gate_line, g_mix)
+    gate_second = leave(gate_line, "x", 0, at_z, at_x)
     g_rows = jnp.concatenate([g_mix[:, WIDTH * h : WIDTH * (h + 1)] for h in range(HEADS)], axis=0)
     scores_again = jnp.where(allowed, dot_tr(q_rows, keys) * score_scale, MASKED_SCORE)
     probs = jnp.where(allowed, jnp.exp(scores_again - lse), 0.0)
@@ -418,11 +416,10 @@
     g_values = dot_tl(probs.astype(BF), g_rows)
     g_kv = jnp.concatenate([g_keys, g_values], axis=1)
     n_mine = 8 * TOKENS
-    gate_first, up_first, _ = after(g_kv, gate_first, up_first)
-    gate_line, up_line = add(gate_first).astype(BF), add(up_first).astype(BF)
-    gate_second = leave(gate_line, "x", 0, at_z, at_x)
+    up_first, g_kv = lax.optimization_barrier((up_first, g_kv))
+    up_line = add(up_first).astype(BF)
     up_second = leave(up_line, "z", 0, at_z, at_x)
-    g_away, _ = after((gate_line, up_line), g_kv[n_mine:].astype(BF))
+    g_away, _ = after(up_line, g_kv[n_mine:].astype(BF))
     g_kv_sum = g_kv[:n_mine] + other_core(g_away).astype(F32)
     g_kv_b = g_kv_sum.astype(BF)
     g_parts = [shift(g_kv_b[320 * k : 320 * (k + 1)], "y", 4 - k) for k in (1, 2, 3)]
@@ -502,9 +499,9 @@
     chip_kv, _ = after(slab, chip_kv)
     chip_sums = jnp.concatenate([chip_q, chip_kv, chip_out], axis=2)
     parts = exchange(chip_sums, CHIPS)
-    down_first, _ = after(g_kv_own, down_first)
+    down_first, _ = after(chip_sums, down_first)
     down_second = leave(add(down_first).astype(BF), "x", 0, at_z, at_x)
-    slab, down_second, g_q, g_k, g_v, _ = after(chip_sums, slab, down_second, g_q, g_k, g_v)
+    slab, g_q, g_k, g_v, _ = after(chip_sums, slab, g_q, g_k, g_v)
 
     d_one = None
     for i, (g, first, last) in enumerate(((g_q, 0, 512), (g_k, 512, 640), (g_v, 640, 768))):

time: 665 us -> 645 us (0.970)
  the two profiles are of different devices: /device:TPU:1 before, /device:TPU:17 now
where the time goes in v9:
time: 645 us; the launch traced here: 634 us
  matrix products  174 us (27%)
  starting transfers between devices  163 us (25%)
  waiting for transfers between devices  108 us (17%)
  local copies, waits for them, and re-layouts  98.3 us (15%)
  other arithmetic  81.8 us (13%)
  between operations  8.96 us (1%)
    ppermute x45, waiting for transfers between devices, shift(): lax.ppermute(x, RING[axis], [(number[i], number[(i + k) % 4]) for i in ra...  92.8 us
    dot_general x37, matrix products, dot(): return jnp.dot(a, b, preferred_element_type=F32)  77.4 us
    ppermute x45, starting transfers between devices, shift(): lax.ppermute(x, RING[axis], [(number[i], number[(i + k) % 4]) for i in ra...  72 us
    dot_general x38, matrix products, dot_tr(): lax.dot_general(a, b, (((1,), (1,)), ((), ())), preferred_element_type=F32)  60 us
    all_to_all x5, starting transfers between devices, exchange(): return lax.all_to_all(x, axes, split_axis=0, concat_axis=0, tiled=True)  50.3 us
    dot_general x19, matrix products, dot_tl(): lax.dot_general(a, b, (((0,), (0,)), ((), ())), preferred_element_type=F32)  36.5 us
    unnamed x344, local copies, waits for them, and re-layouts  32.2 us
    ppermute x27, starting transfers between devices, other_core(): return lax.ppermute(x, 'c', [(0, 1), (1, 0)])  26.1 us
  transfers between devices with their start and end apart: 81, of which 23 were waited for; matrix products, arithmetic and copies ran while one was open for 45% of the time, Pallas kernels for 0%

profile of v9, /device:TPU:17, one launch (start us, length us, event | category | flops | bytes accessed | tf_op | source)
XLA Modules:
  0.0 633.7 jit_solution(2788017102817259846)
XLA Ops:
  13.8 10.7 %all-to-all-start = ((bf16[64,24,1152]{2,1,0:T(8,128)(2,1)}), bf16[64,24,1152]{2,1,0:T(8,128)(2,1)S(1)}, u32[]{:S(2)}, u32[]{:S(2)}) async-start(bf16[64,24,1152]{2,1,0:T(8,128)(2,1)} %broadcast_in_dim.163), calls=%async_computation | async-start | bytes 7077888 | tf_op jit(solution)/shard_map/all_to_all | solution.py:35
  43.5 5.9 collective-permute-start.6
  67.6 4.1 collective-permute-start.3
  88.6 15.0 %all-to-all-start.1 = ((bf16[64,24,1024]{2,1,0:T(8,128)(2,1)}), bf16[64,24,1024]{2,1,0:T(8,128)(2,1)}, u32[]{:S(2)}, u32[]{:S(2)}) async-start(bf16[64,24,1024]{2,1,0:T(8,128)(2,1)} %broadcast_in_dim.167), calls=%async_computation.1 | async-start | bytes 6291456 | tf_op jit(solution)/shard_map/all_to_all | solution.py:35
  129.4 14.8 %collective-permute-done.10 = bf16[56,1408]{1,0:T(8,128)(2,1)S(1)} collective-permute-done((bf16[56,1408]{1,0:T(8,128)(2,1)}, bf16[56,1408]{1,0:T(8,128)(2,1)S(1)}, u32[]{:S(2)}, u32[]{:S(2)}) %collective-permute-start.10) | collective-permute-done | bytes 157728 | tf_op jit(solution)/shard_map/ppermute | solution.py:48
  162.8 4.3 collective-permute-done.13
  182.5 7.3 %all-to-all-start.2 = ((bf16[16,176,896]{2,1,0:T(8,128)(2,1)}), bf16[16,176,896]{2,1,0:T(8,128)(2,1)}, u32[]{:S(2)}, u32[]{:S(2)}) async-start(bf16[16,176,896]{2,1,0:T(8,128)(2,1)} %broadcast_in_dim.173), calls=%async_computation.2 | async-start | bytes 10092544 | tf_op jit(solution)/shard_map/all_to_all | solution.py:35
  248.7 6.8 %all-to-all-done.2 = bf16[16,176,896]{2,1,0:T(8,128)(2,1)} async-done(((bf16[16,176,896]{2,1,0:T(8,128)(2,1)}), bf16[16,176,896]{2,1,0:T(8,128)(2,1)}, u32[]{:S(2)}, u32[]{:S(2)}) %all-to-all-start.2) | async-done | bytes 5046304 | tf_op jit(solution)/shard_map/all_to_all | solution.py:35
  259.4 6.1 fusion.612
  265.6 3.9 add_convert_fusion
  269.5 8.8 %multiply_convert_fusion.1 = (bf16[1280,896]{1,0:T(8,128)(2,1)S(1)}, f32[1280,896]{1,0:T(8,128)}) fusion(f32[1280,896]{1,0:T(8,128)S(1)} %fusion.612, bf16[1280,1152]{1,0:T(8,128)(2,1)} %constant_dynamic-update-slice_fusion.31, bf16[1152,896]{1,0:T(8,128)(2,1)S(1)} %bitcast.321), kind=kOutput, calls=%fused_computation.41 | convolution fusion | flops 2653880320 | bytes 16482304 | tf_op jit(solution)/shard_map/dot_general | solution.py:23
  278.3 9.5 %collective-permute-done.25 = bf16[4,56,1408]{2,1,0:T(8,128)(2,1)} collective-permute-done((bf16[4,56,1408]{2,1,0:T(8,128)(2,1)}, bf16[4,56,1408]{2,1,0:T(8,128)(2,1)}, u32[]{:S(2)}, u32[]{:S(2)}) %collective-permute-start.25) | collective-permute-done | bytes 630816 | tf_op jit(solution)/shard_map/ppermute | solution.py:48
  294.2 3.7 fusion.613
  319.0 7.3 %collective-permute-done.28 = bf16[160,1152]{1,0:T(8,128)(2,1)S(1)} collective-permute-done((bf16[160,1152]{1,0:T(8,128)(2,1)S(1)}, bf16[160,1152]{1,0:T(8,128)(2,1)S(1)}, u32[]{:S(2)}, u32[]{:S(2)}) %collective-permute-start.28) | collective-permute-done | bytes 368672 | tf_op jit(solution)/shard_map/ppermute | solution.py:48
  343.6 4.3 collective-permute-done.35
  357.9 11.0 %fusion.10 = (bf16[1280,896]{1,0:T(8,128)(2,1)S(1)}, bf16[1280,896]{1,0:T(8,128)(2,1)S(1)}) fusion(f32[1280,896]{1,0:T(8,128)} %copy-done.153, f32[1280,896]{1,0:T(8,128)} %get-tuple-element.434, bf16[1280,1152]{1,0:T(8,128)(2,1)} %constant_dynamic-update-slice_fusion.39, bf16[896,1152]{1,0:T(8,128)(2,1)S(1)} %copy-done.144), kind=kOutput, calls=%fused_computation.33 | convolution fusion | flops 2672230400 | bytes 18776064 | tf_op jit(solution)/shard_map/dot_general | solution.py:31
  377.8 5.1 convolution_convert_fusion.1
  387.3 5.1 convolution_convert_fusion.2
  394.2 4.2 collective-permute-start.42
  406.7 5.3 collective-permute-done.42
  421.6 3.7 fusion.127
  426.6 9.5 %collective-permute-done.50 = bf16[4,88,896]{2,1,0:T(8,128)(2,1)} collective-permute-done((bf16[4,88,896]{2,1,0:T(8,128)(2,1)}, bf16[4,88,896]{2,1,0:T(8,128)(2,1)}, u32[]{:S(2)}, u32[]{:S(2)}) %collective-permute-start.50) | collective-permute-done | bytes 630816 | tf_op jit(solution)/shard_map/ppermute | solution.py:48
  438.1 4.3 fusion.36
  446.1 5.8 multiply_convert_fusion
  481.7 5.8 collective-permute-done.57
  487.5 3.7 collective-permute-start.61
  503.4 8.2 %all-to-all-start.3 = ((bf16[8,32,896]{2,1,0:T(8,128)(2,1)}), bf16[8,32,896]{2,1,0:T(8,128)(2,1)}, u32[]{:S(2)}, u32[]{:S(2)}) async-start(bf16[8,32,896]{2,1,0:T(8,128)(2,1)} %bitcast.328), calls=%async_computation.3 | async-start | bytes 917504 | tf_op jit(solution)/shard_map/all_to_all | solution.py:35
  535.2 9.0 %all-to-all-start.4 = ((bf16[64,24,1408]{2,1,0:T(8,128)(2,1)}), bf16[64,24,1408]{2,1,0:T(8,128)(2,1)}, u32[]{:S(2)}, u32[]{:S(2)}) async-start(bf16[64,24,1408]{2,1,0:T(8,128)(2,1)} %pad_maximum_fusion.1), calls=%async_computation.4 | async-start | bytes 8650752 | tf_op jit(solution)/shard_map/all_to_all | solution.py:35
  587.9 9.7 %collective-permute-done.74 = bf16[56,1152]{1,0:T(8,128)(2,1)} collective-permute-done((bf16[56,1152]{1,0:T(8,128)(2,1)}, bf16[56,1152]{1,0:T(8,128)(2,1)}, u32[]{:S(2)}, u32[]{:S(2)}) %collective-permute-start.74) | collective-permute-done | bytes 129056 | tf_op jit(solution)/shard_map/ppermute | solution.py:48
  597.6 4.9 collective-permute-done.73
  603.6 3.8 collective-permute-start.75
  607.9 8.0 %collective-permute-done.75 = bf16[56,1152]{1,0:T(8,128)(2,1)S(1)} collective-permute-done((bf16[56,1152]{1,0:T(8,128)(2,1)S(1)}, bf16[56,1152]{1,0:T(8,128)(2,1)S(1)}, u32[]{:S(2)}, u32[]{:S(2)}) %collective-permute-start.75) | collective-permute-done | bytes 129056 | tf_op jit(solution)/shard_map/ppermute | solution.py:520
  (751 shorter events, 405.1 us)
Async XLA Ops:
  13.8 64.1 %all-to-all-start = ((bf16[64,24,1152]{2,1,0:T(8,128)(2,1)}), bf16[64,24,1152]{2,1,0:T(8,128)(2,1)S(1)}, u32[]{:S(2)}, u32[]{:S(2)}) async-start(bf16[64,24,1152]{2,1,0:T(8,128)(2,1)} %broadcast_in_dim.163), calls=%async_computation | async-start | bytes 7077888 | tf_op jit(solution)/shard_map/all_to_all | solution.py:35
  36.0 30.4 %collective-permute-start.1 = (bf16[4,24,896]{2,1,0:T(8,128)(2,1)}, bf16[4,24,896]{2,1,0:T(8,128)(2,1)}, u32[]{:S(2)}, u32[]{:S(2)}) collective-permute-start(bf16[4,24,896]{2,1,0:T(8,128)(2,1)} %get-tuple-element.341), channel_id=1, source_target_pairs={{0,1},{1,0},{2,3},{3,2},{4,5},{5,4},{6,7},{7,6},{8,9},{9,8},{10,11... | collective-permute-start | bytes 516104 | tf_op jit(solution)/shard_map/ppermute | solution.py:39
  41.9 22.9 %collective-permute-start.5 = (bf16[12,1024]{1,0:T(8,128)(2,1)}, bf16[12,1024]{1,0:T(8,128)(2,1)}, u32[]{:S(2)}, u32[]{:S(2)}) collective-permute-start(bf16[12,1024]{1,0:T(8,128)(2,1)} %broadcast_select_fusion.19), channel_id=1, source_target_pairs={{0,1},{1,0},{2,3},{3,2},{4,5},{5,4},{6,7},{7,6},{8,9},{9,8},{10,11... | collective-permute-start | bytes 73736 | tf_op jit(solution)/shard_map/ppermute | solution.py:39
  43.5 34.4 %collective-permute-start.6 = (bf16[56,1408]{1,0:T(8,128)(2,1)}, bf16[56,1408]{1,0:T(8,128)(2,1)}, u32[]{:S(2)}, u32[]{:S(2)}) collective-permute-start(bf16[56,1408]{1,0:T(8,128)(2,1)} %fusion.328), channel_id=1, source_target_pairs={{0,0},{1,32},{2,64},{3,96},{4,8},{5,40},{6,72},{7,104},{8,16},{9,4... | collective-permute-start | bytes 473096 | tf_op jit(solution)/shard_map/ppermute | solution.py:249
  77.9 32.8 %collective-permute-start.7 = (bf16[64,24,1152]{2,1,0:T(8,128)(2,1)S(1)}, bf16[64,24,1152]{2,1,0:T(8,128)(2,1)}, u32[]{:S(2)}, u32[]{:S(2)}) collective-permute-start(bf16[64,24,1152]{2,1,0:T(8,128)(2,1)S(1)} %all-to-all-done), channel_id=1, source_target_pairs={{0,1},{1,0},{2,3},{3,2},{4,5},{5,4},{6,7},{7,6},{8,9},{9,8},{10,11... | collective-permute-start | bytes 10616840 | tf_op jit(solution)/shard_map/ppermute | solution.py:39
  88.6 66.9 %all-to-all-start.1 = ((bf16[64,24,1024]{2,1,0:T(8,128)(2,1)}), bf16[64,24,1024]{2,1,0:T(8,128)(2,1)}, u32[]{:S(2)}, u32[]{:S(2)}) async-start(bf16[64,24,1024]{2,1,0:T(8,128)(2,1)} %broadcast_in_dim.167), calls=%async_computation.1 | async-start | bytes 6291456 | tf_op jit(solution)/shard_map/all_to_all | solution.py:35
  119.3 29.6 %collective-permute-start.8 = (bf16[160,512]{1,0:T(8,128)(2,1)S(1)}, bf16[160,512]{1,0:T(8,128)(2,1)S(1)}, u32[]{:S(2)}, u32[]{:S(2)}) collective-permute-start(bf16[160,512]{1,0:T(8,128)(2,1)S(1)} %get-tuple-element.374), channel_id=1, source_target_pairs={{0,8},{8,0},{1,9},{9,1},{2,10},{10,2},{3,11},{11,3},{4,12},{12,4},... | collective-permute-start | bytes 491528 | tf_op jit(solution)/shard_map/ppermute | solution.py:43
  122.0 22.2 %collective-permute-start.10 = (bf16[56,1408]{1,0:T(8,128)(2,1)}, bf16[56,1408]{1,0:T(8,128)(2,1)S(1)}, u32[]{:S(2)}, u32[]{:S(2)}) collective-permute-start(bf16[56,1408]{1,0:T(8,128)(2,1)} %collective-permute-done.6), channel_id=1, source_target_pairs={{0,32},{32,64},{64,96},{96,0},{1,33},{33,65},{65,97},{97,1},{2,34}... | collective-permute-start | bytes 473096 | tf_op jit(solution)/shard_map/ppermute | solution.py:48
  123.2 25.0 %collective-permute-start.11 = (bf16[56,1408]{1,0:T(8,128)(2,1)}, bf16[56,1408]{1,0:T(8,128)(2,1)S(1)}, u32[]{:S(2)}, u32[]{:S(2)}) collective-permute-start(bf16[56,1408]{1,0:T(8,128)(2,1)} %collective-permute-done.6), channel_id=1, source_target_pairs={{0,64},{32,96},{64,0},{96,32},{1,65},{33,97},{65,1},{97,33},{2,66}... | collective-permute-start | bytes 473096 | tf_op jit(solution)/shard_map/ppermute | solution.py:48
  125.8 28.9 %collective-permute-start.12 = (bf16[56,1408]{1,0:T(8,128)(2,1)}, bf16[56,1408]{1,0:T(8,128)(2,1)S(1)}, u32[]{:S(2)}, u32[]{:S(2)}) collective-permute-start(bf16[56,1408]{1,0:T(8,128)(2,1)} %collective-permute-done.6), channel_id=1, source_target_pairs={{0,96},{32,0},{64,32},{96,64},{1,97},{33,1},{65,33},{97,65},{2,98}... | collective-permute-start | bytes 473096 | tf_op jit(solution)/shard_map/ppermute | solution.py:48
  179.3 29.4 %collective-permute-start.16 = (bf16[64,24,1024]{2,1,0:T(8,128)(2,1)}, bf16[64,24,1024]{2,1,0:T(8,128)(2,1)}, u32[]{:S(2)}, u32[]{:S(2)}) collective-permute-start(bf16[64,24,1024]{2,1,0:T(8,128)(2,1)} %all-to-all-done.1), channel_id=1, source_target_pairs={{0,1},{1,0},{2,3},{3,2},{4,5},{5,4},{6,7},{7,6},{8,9},{9,8},{10,11... | collective-permute-start | bytes 9437192 | tf_op jit(solution)/shard_map/ppermute | solution.py:39
  182.5 73.0 %all-to-all-start.2 = ((bf16[16,176,896]{2,1,0:T(8,128)(2,1)}), bf16[16,176,896]{2,1,0:T(8,128)(2,1)}, u32[]{:S(2)}, u32[]{:S(2)}) async-start(bf16[16,176,896]{2,1,0:T(8,128)(2,1)} %broadcast_in_dim.173), calls=%async_computation.2 | async-start | bytes 10092544 | tf_op jit(solution)/shard_map/all_to_all | solution.py:35
  189.9 88.5 %collective-permute-start.24 = (bf16[4,56,1408]{2,1,0:T(8,128)(2,1)}, bf16[4,56,1408]{2,1,0:T(8,128)(2,1)}, u32[]{:S(2)}, u32[]{:S(2)}) collective-permute-start(bf16[4,56,1408]{2,1,0:T(8,128)(2,1)} %bitcast_dynamic-update-slice_fusion.4), channel_id=1, source_target_pairs={{0,16},{16,8},{8,24},{24,0},{1,17},{17,9},{9,25},{25,1},{2,18},{18... | collective-permute-start | bytes 1892360 | tf_op jit(solution)/shard_map/ppermute | solution.py:48
  191.3 96.6 %collective-permute-start.25 = (bf16[4,56,1408]{2,1,0:T(8,128)(2,1)}, bf16[4,56,1408]{2,1,0:T(8,128)(2,1)}, u32[]{:S(2)}, u32[]{:S(2)}) collective-permute-start(bf16[4,56,1408]{2,1,0:T(8,128)(2,1)} %bitcast_dynamic-update-slice_fusion.4), channel_id=1, source_target_pairs={{0,8},{16,24},{8,0},{24,16},{1,9},{17,25},{9,1},{25,17},{2,10},{18... | collective-permute-start | bytes 1892360 | tf_op jit(solution)/shard_map/ppermute | solution.py:48
  193.6 94.2 %collective-permute-start.26 = (bf16[4,56,1408]{2,1,0:T(8,128)(2,1)}, bf16[4,56,1408]{2,1,0:T(8,128)(2,1)}, u32[]{:S(2)}, u32[]{:S(2)}) collective-permute-start(bf16[4,56,1408]{2,1,0:T(8,128)(2,1)} %bitcast_dynamic-update-slice_fusion.4), channel_id=1, source_target_pairs={{0,24},{16,0},{8,16},{24,8},{1,25},{17,1},{9,17},{25,9},{2,26},{18... | collective-permute-start | bytes 1892360 | tf_op jit(solution)/shard_map/ppermute | solution.py:48
  376.4 24.4 %collective-permute-start.47 = (bf16[160,1152]{1,0:T(8,128)(2,1)S(1)}, bf16[160,1152]{1,0:T(8,128)(2,1)S(1)}, u32[]{:S(2)}, u32[]{:S(2)}) collective-permute-start(bf16[160,1152]{1,0:T(8,128)(2,1)S(1)} %get-tuple-element.278), channel_id=1, source_target_pairs={{0,1},{1,0},{2,3},{3,2},{4,5},{5,4},{6,7},{7,6},{8,9},{9,8},{10,11... | collective-permute-start | bytes 1105928 | tf_op jit(solution)/shard_map/ppermute | solution.py:39
  385.1 68.9 %collective-permute-start.51 = (bf16[4,88,896]{2,1,0:T(8,128)(2,1)}, bf16[4,88,896]{2,1,0:T(8,128)(2,1)}, u32[]{:S(2)}, u32[]{:S(2)}) collective-permute-start(bf16[4,88,896]{2,1,0:T(8,128)(2,1)} %get-tuple-element.291), channel_id=1, source_target_pairs={{0,24},{16,0},{8,16},{24,8},{1,25},{17,1},{9,17},{25,9},{2,26},{18... | collective-permute-start | bytes 1892360 | tf_op jit(solution)/shard_map/ppermute | solution.py:48
  400.8 53.2 %collective-permute-start.52 = (bf16[4,88,896]{2,1,0:T(8,128)(2,1)}, bf16[4,88,896]{2,1,0:T(8,128)(2,1)}, u32[]{:S(2)}, u32[]{:S(2)}) collective-permute-start(bf16[4,88,896]{2,1,0:T(8,128)(2,1)} %get-tuple-element.292), channel_id=1, source_target_pairs={{0,8},{16,24},{8,0},{24,16},{1,9},{17,25},{9,1},{25,17},{2,10},{18... | collective-permute-start | bytes 1892360 | tf_op jit(solution)/shard_map/ppermute | solution.py:48
  404.6 22.0 %collective-permute-start.49 = (bf16[4,88,896]{2,1,0:T(8,128)(2,1)}, bf16[4,88,896]{2,1,0:T(8,128)(2,1)}, u32[]{:S(2)}, u32[]{:S(2)}) collective-permute-start(bf16[4,88,896]{2,1,0:T(8,128)(2,1)} %get-tuple-element.288), channel_id=1, source_target_pairs={{0,64},{32,96},{64,0},{96,32},{1,65},{33,97},{65,1},{97,33},{2,66}... | collective-permute-start | bytes 1892360 | tf_op jit(solution)/shard_map/ppermute | solution.py:48
  412.0 24.0 %collective-permute-start.50 = (bf16[4,88,896]{2,1,0:T(8,128)(2,1)}, bf16[4,88,896]{2,1,0:T(8,128)(2,1)}, u32[]{:S(2)}, u32[]{:S(2)}) collective-permute-start(bf16[4,88,896]{2,1,0:T(8,128)(2,1)} %get-tuple-element.285), channel_id=1, source_target_pairs={{0,32},{32,64},{64,96},{96,0},{1,33},{33,65},{65,97},{97,1},{2,34}... | collective-permute-start | bytes 1892360 | tf_op jit(solution)/shard_map/ppermute | solution.py:48
  425.3 28.7 %collective-permute-start.53 = (bf16[4,88,896]{2,1,0:T(8,128)(2,1)}, bf16[4,88,896]{2,1,0:T(8,128)(2,1)S(1)}, u32[]{:S(2)}, u32[]{:S(2)}) collective-permute-start(bf16[4,88,896]{2,1,0:T(8,128)(2,1)} %get-tuple-element.289), channel_id=1, source_target_pairs={{0,16},{16,8},{8,24},{24,0},{1,17},{17,9},{9,25},{25,1},{2,18},{18... | collective-permute-start | bytes 1892360 | tf_op jit(solution)/shard_map/ppermute | solution.py:48
  463.3 30.3 %collective-permute-start.64 = (bf16[88,896]{1,0:T(8,128)(2,1)S(1)}, bf16[88,896]{1,0:T(8,128)(2,1)S(1)}, u32[]{:S(2)}, u32[]{:S(2)}) collective-permute-start(bf16[88,896]{1,0:T(8,128)(2,1)S(1)} %get-tuple-element.331), channel_id=1, source_target_pairs={{0,96},{32,0},{64,32},{96,64},{1,97},{33,1},{65,33},{97,65},{2,98}... | collective-permute-start | bytes 473096 | tf_op jit(solution)/shard_map/ppermute | solution.py:48
  463.7 33.0 %collective-permute-start.65 = (bf16[88,896]{1,0:T(8,128)(2,1)S(1)}, bf16[88,896]{1,0:T(8,128)(2,1)S(1)}, u32[]{:S(2)}, u32[]{:S(2)}) collective-permute-start(bf16[88,896]{1,0:T(8,128)(2,1)S(1)} %get-tuple-element.330), channel_id=1, source_target_pairs={{0,64},{32,96},{64,0},{96,32},{1,65},{33,97},{65,1},{97,33},{2,66}... | collective-permute-start | bytes 473096 | tf_op jit(solution)/shard_map/ppermute | solution.py:48
  498.6 27.3 %collective-permute-start.67 = (bf16[1536,640]{1,0:T(8,128)(2,1)}, bf16[1536,640]{1,0:T(8,128)(2,1)}, u32[]{:S(2)}, u32[]{:S(2)}) collective-permute-start(bf16[1536,640]{1,0:T(8,128)(2,1)} %add_convert_fusion.3), channel_id=1, source_target_pairs={{0,1},{1,0},{2,3},{3,2},{4,5},{5,4},{6,7},{7,6},{8,9},{9,8},{10,11... | collective-permute-start | bytes 5898248 | tf_op jit(solution)/shard_map/ppermute | solution.py:39
  498.8 23.0 %collective-permute-start.59 = (bf16[160,512]{1,0:T(8,128)(2,1)}, bf16[160,512]{1,0:T(8,128)(2,1)}, u32[]{:S(2)}, u32[]{:S(2)}) collective-permute-start(bf16[160,512]{1,0:T(8,128)(2,1)} %slice.1370), channel_id=1, source_target_pairs={{0,8},{8,0},{1,9},{9,1},{2,10},{10,2},{3,11},{11,3},{4,12},{12,4},... | collective-permute-start | bytes 491528 | tf_op jit(solution)/shard_map/ppermute | solution.py:43
  503.4 28.6 %all-to-all-start.3 = ((bf16[8,32,896]{2,1,0:T(8,128)(2,1)}), bf16[8,32,896]{2,1,0:T(8,128)(2,1)}, u32[]{:S(2)}, u32[]{:S(2)}) async-start(bf16[8,32,896]{2,1,0:T(8,128)(2,1)} %bitcast.328), calls=%async_computation.3 | async-start | bytes 917504 | tf_op jit(solution)/shard_map/all_to_all | solution.py:35
  514.6 50.7 %collective-permute-start.69 = (bf16[4,56,1152]{2,1,0:T(8,128)(2,1)}, bf16[4,56,1152]{2,1,0:T(8,128)(2,1)}, u32[]{:S(2)}, u32[]{:S(2)}) collective-permute-start(bf16[4,56,1152]{2,1,0:T(8,128)(2,1)} %get-tuple-element.295), channel_id=1, source_target_pairs={{0,96},{32,0},{64,32},{96,64},{1,97},{33,1},{65,33},{97,65},{2,98}... | collective-permute-start | bytes 1548296 | tf_op jit(solution)/shard_map/ppermute | solution.py:48
  517.0 48.2 %collective-permute-start.70 = (bf16[4,56,1152]{2,1,0:T(8,128)(2,1)}, bf16[4,56,1152]{2,1,0:T(8,128)(2,1)}, u32[]{:S(2)}, u32[]{:S(2)}) collective-permute-start(bf16[4,56,1152]{2,1,0:T(8,128)(2,1)} %get-tuple-element.294), channel_id=1, source_target_pairs={{0,64},{32,96},{64,0},{96,32},{1,65},{33,97},{65,1},{97,33},{2,66}... | collective-permute-start | bytes 1548296 | tf_op jit(solution)/shard_map/ppermute | solution.py:48
  518.2 47.1 %collective-permute-start.71 = (bf16[4,56,1152]{2,1,0:T(8,128)(2,1)}, bf16[4,56,1152]{2,1,0:T(8,128)(2,1)}, u32[]{:S(2)}, u32[]{:S(2)}) collective-permute-start(bf16[4,56,1152]{2,1,0:T(8,128)(2,1)} %get-tuple-element.293), channel_id=1, source_target_pairs={{0,32},{32,64},{64,96},{96,0},{1,33},{33,65},{65,97},{97,1},{2,34}... | collective-permute-start | bytes 1548296 | tf_op jit(solution)/shard_map/ppermute | solution.py:48
  535.2 82.5 %all-to-all-start.4 = ((bf16[64,24,1408]{2,1,0:T(8,128)(2,1)}), bf16[64,24,1408]{2,1,0:T(8,128)(2,1)}, u32[]{:S(2)}, u32[]{:S(2)}) async-start(bf16[64,24,1408]{2,1,0:T(8,128)(2,1)} %pad_maximum_fusion.1), calls=%async_computation.4 | async-start | bytes 8650752 | tf_op jit(solution)/shard_map/all_to_all | solution.py:35
  578.1 24.4 %collective-permute-start.73 = (bf16[56,1152]{1,0:T(8,128)(2,1)}, bf16[56,1152]{1,0:T(8,128)(2,1)}, u32[]{:S(2)}, u32[]{:S(2)}) collective-permute-start(bf16[56,1152]{1,0:T(8,128)(2,1)} %get-tuple-element.335), channel_id=1, source_target_pairs={{0,8},{16,24},{8,0},{24,16},{1,9},{17,25},{9,1},{25,17},{2,10},{18... | collective-permute-start | bytes 387080 | tf_op jit(solution)/shard_map/ppermute | solution.py:48
  580.5 22.0 %collective-permute-start.72 = (bf16[56,1152]{1,0:T(8,128)(2,1)}, bf16[56,1152]{1,0:T(8,128)(2,1)}, u32[]{:S(2)}, u32[]{:S(2)}) collective-permute-start(bf16[56,1152]{1,0:T(8,128)(2,1)} %get-tuple-element.333), channel_id=1, source_target_pairs={{0,24},{16,0},{8,16},{24,8},{1,25},{17,1},{9,17},{25,9},{2,26},{18... | collective-permute-start | bytes 387080 | tf_op jit(solution)/shard_map/ppermute | solution.py:48
  (207 other events, 2117.3 us)

commit v10 on v9

--- a/solution.py
+++ b/solution.py
@@ -277,6 +277,8 @@
     valid_count = jnp.sum(marks[:, 18].astype(F32))
     out_own, _ = after(raw_one, out_own)
     out_wide = jnp.broadcast_to(out_own[None], (64, 24, 1024))
+    down_z = [shift(down_own, "z", k) for k in (1, 2, 3)]
+    out_wide, down_z = lax.optimization_barrier((out_wide, down_z))
     out_one = exchange(out_wide, CHIPS)
     out_two = other_core(out_one)
     raw_out = [out_one.reshape(1536, 1024), out_two.reshape(1536, 1024)]
@@ -311,8 +313,7 @@
     kv_own = jnp.concatenate([turn(jnp.concatenate(kk, axis=1), cos, sin), vv[0], vv[1]], axis=1).astype(BF)
 
     pair = jnp.concatenate([kv_own, other_half(kv_own)], axis=0)
-    down_own, _ = after(kv_own, down_own)
-    down_line = placed([down_own] + [shift(down_own, "z", k) for k in (1, 2, 3)], "z", at_z, at_x)
+    down_line = placed([down_own] + down_z, "z", at_z, at_x)
     ff_own, _ = after((out_one, down_line), ff_own)
     ff_wide = jnp.broadcast_to(ff_own[None], (16, 176, 896))
     ff_all = exchange(ff_wide, PLANE)
@@ -422,12 +423,13 @@
     g_away, _ = after(up_line, g_kv[n_mine:].astype(BF))
     g_kv_sum = g_kv[:n_mine] + other_core(g_away).astype(F32)
     g_kv_b = g_kv_sum.astype(BF)
+    g_kv_b, gw_down = lax.optimization_barrier((g_kv_b, gw_down))
+    down_first = leave(gw_down.reshape(4, 4, 56, 1152), "z", 1, at_z, at_x)
     g_parts = [shift(g_kv_b[320 * k : 320 * (k + 1)], "y", 4 - k) for k in (1, 2, 3)]
     g_scores, gb_down, _ = after(g_kv_b, g_scores, gb_down)
     g_pair = add([g_kv_sum[:320]] + list(g_parts))
     away = other_half(g_pair[160:].astype(BF))
-    gate_second, up_second, gw_down, _ = after(g_pair, gate_second, up_second, gw_down)
-    down_first = leave(gw_down.reshape(4, 4, 56, 1152), "z", 1, at_z, at_x)
+    gate_second, up_second, _ = after(g_pair, gate_second, up_second)
     g_q_rows = dot(g_scores, keys) * score_scale
     g_q = [
         jnp.concatenate(
@@ -486,6 +488,8 @@
         dot_tl(side_out, g_half[1]) + dot_tl(put_inner_down, right),
     )
     g_kv_own = g_pair[:160] + after(chip_q, away)[0].astype(F32)
+    g_kv_own, down_first = lax.optimization_barrier((g_kv_own, down_first))
+    down_second = leave(add(down_first).astype(BF), "x", 0, at_z, at_x)
     g_k = turn_back(g_kv_own[:, :256], cos, sin).astype(BF)
     g_v = g_kv_own[:, 256:].astype(BF)
     g_k = pick(is_first, g_k[:, :128], g_k[:, 128:])
@@ -496,12 +500,10 @@
             for i in (0, 1)
         ]
     )
-    chip_kv, _ = after(slab, chip_kv)
     chip_sums = jnp.concatenate([chip_q, chip_kv, chip_out], axis=2)
+    chip_sums, slab, g_q, g_k, g_v = lax.optimization_barrier((chip_sums, slab, g_q, g_k, g_v))
     parts = exchange(chip_sums, CHIPS)
-    down_first, _ = after(chip_sums, down_first)
-    down_second = leave(add(down_first).astype(BF), "x", 0, at_z, at_x)
-    slab, g_q, g_k, g_v, _ = after(chip_sums, slab, g_q, g_k, g_v)
+    g_q, down_second = lax.optimization_barrier((g_q, down_second))
 
     d_one = None
     for i, (g, first, last) in enumerate(((g_q, 0, 512), (g_k, 512, 640), (g_v, 640, 768))):

time: 645 us -> 652 us (1.011)
  the two profiles are of different devices: /device:TPU:17 before, /device:TPU:63 now
where the time goes in v10:
time: 652 us; the launch traced here: 640 us
  matrix products  173 us (27%)
  starting transfers between devices  160 us (25%)
  waiting for transfers between devices  111 us (17%)
  local copies, waits for them, and re-layouts  106 us (16%)
  other arithmetic  81 us (12%)
  between operations  9.07 us (1%)
    ppermute x45, starting transfers between devices, shift(): lax.ppermute(x, RING[axis], [(number[i], number[(i + k) % 4]) for i in ra...  72.3 us
    dot_general x37, matrix products, dot(): return jnp.dot(a, b, preferred_element_type=F32)  70.8 us
    dot_general x38, matrix products, dot_tr(): lax.dot_general(a, b, (((1,), (1,)), ((), ())), preferred_element_type=F32)  64.3 us
    ppermute x45, waiting for transfers between devices, shift(): lax.ppermute(x, RING[axis], [(number[i], number[(i + k) % 4]) for i in ra...  57.7 us
    all_to_all x5, starting transfers between devices, exchange(): return lax.all_to_all(x, axes, split_axis=0, concat_axis=0, tiled=True)  48.2 us
    dot_general x19, matrix products, dot_tl(): lax.dot_general(a, b, (((0,), (0,)), ((), ())), preferred_element_type=F32)  37.5 us
    unnamed x372, local copies, waits for them, and re-layouts  32.6 us
    ppermute x27, starting transfers between devices, other_core(): return lax.ppermute(x, 'c', [(0, 1), (1, 0)])  28.8 us
  transfers between devices with their start and end apart: 81, of which 21 were waited for; matrix products, arithmetic and copies ran while one was open for 45% of the time, Pallas kernels for 0%

profile of v10, /device:TPU:63, one launch (start us, length us, event | category | flops | bytes accessed | tf_op | source)
XLA Modules:
  0.0 639.9 jit_solution(13318581906966000090)
XLA Ops:
  13.7 10.2 %all-to-all-start = ((bf16[64,24,1152]{2,1,0:T(8,128)(2,1)}), bf16[64,24,1152]{2,1,0:T(8,128)(2,1)S(1)}, u32[]{:S(2)}, u32[]{:S(2)}) async-start(bf16[64,24,1152]{2,1,0:T(8,128)(2,1)} %broadcast_in_dim.163), calls=%async_computation | async-start | bytes 7077888 | tf_op jit(solution)/shard_map/all_to_all | solution.py:35
  42.9 4.8 collective-permute-start.6
  69.8 4.2 collective-permute-done.4
  82.1 5.3 collective-permute-start.8
  98.6 12.7 %all-to-all-start.1 = ((bf16[64,24,1024]{2,1,0:T(8,128)(2,1)}), bf16[64,24,1024]{2,1,0:T(8,128)(2,1)}, u32[]{:S(2)}, u32[]{:S(2)}) async-start(bf16[64,24,1024]{2,1,0:T(8,128)(2,1)} %broadcast_in_dim.167), calls=%async_computation.1 | async-start | bytes 6291456 | tf_op jit(solution)/shard_map/all_to_all | solution.py:35
  131.5 17.5 %collective-permute-done.11 = bf16[160,512]{1,0:T(8,128)(2,1)S(1)} collective-permute-done((bf16[160,512]{1,0:T(8,128)(2,1)S(1)}, bf16[160,512]{1,0:T(8,128)(2,1)S(1)}, u32[]{:S(2)}, u32[]{:S(2)}) %collective-permute-start.11) | collective-permute-done | bytes 163872 | tf_op jit(solution)/shard_map/ppermute | solution.py:43
  161.5 7.4 %collective-permute-done.14 = bf16[320,512]{1,0:T(8,128)(2,1)} collective-permute-done((bf16[320,512]{1,0:T(8,128)(2,1)}, bf16[320,512]{1,0:T(8,128)(2,1)}, u32[]{:S(2)}, u32[]{:S(2)}) %collective-permute-start.14) | collective-permute-done | bytes 327712 | tf_op jit(solution)/shard_map/ppermute | solution.py:48
  182.0 7.7 %all-to-all-start.2 = ((bf16[16,176,896]{2,1,0:T(8,128)(2,1)}), bf16[16,176,896]{2,1,0:T(8,128)(2,1)}, u32[]{:S(2)}, u32[]{:S(2)}) async-start(bf16[16,176,896]{2,1,0:T(8,128)(2,1)} %broadcast_in_dim.173), calls=%async_computation.2 | async-start | bytes 10092544 | tf_op jit(solution)/shard_map/all_to_all | solution.py:35
  213.0 4.0 collective-permute-start.18
  228.7 4.4 collective-permute-start.19
  235.6 4.7 collective-permute-done.19
  246.4 26.7 %all-to-all-done.2 = bf16[16,176,896]{2,1,0:T(8,128)(2,1)} async-done(((bf16[16,176,896]{2,1,0:T(8,128)(2,1)}), bf16[16,176,896]{2,1,0:T(8,128)(2,1)}, u32[]{:S(2)}, u32[]{:S(2)}) %all-to-all-start.2) | async-done | bytes 5046304 | tf_op jit(solution)/shard_map/all_to_all | solution.py:35
  277.1 6.1 fusion.608
  283.2 3.9 add_convert_fusion
  287.2 8.9 %multiply_convert_fusion.1 = (bf16[1280,896]{1,0:T(8,128)(2,1)S(1)}, f32[1280,896]{1,0:T(8,128)}) fusion(f32[1280,896]{1,0:T(8,128)S(1)} %fusion.608, bf16[1280,1152]{1,0:T(8,128)(2,1)} %constant_dynamic-update-slice_fusion.31, bf16[1152,896]{1,0:T(8,128)(2,1)S(1)} %bitcast.320), kind=kOutput, calls=%fused_computation.41 | convolution fusion | flops 2653880320 | bytes 16482304 | tf_op jit(solution)/shard_map/dot_general | solution.py:23
  321.4 5.1 collective-permute-done.32
  327.4 8.4 %collective-permute-done.28 = bf16[160,1152]{1,0:T(8,128)(2,1)S(1)} collective-permute-done((bf16[160,1152]{1,0:T(8,128)(2,1)S(1)}, bf16[160,1152]{1,0:T(8,128)(2,1)S(1)}, u32[]{:S(2)}, u32[]{:S(2)}) %collective-permute-start.28) | collective-permute-done | bytes 368672 | tf_op jit(solution)/shard_map/ppermute | solution.py:48
  366.6 11.0 %fusion.10 = (bf16[1280,896]{1,0:T(8,128)(2,1)S(1)}, bf16[1280,896]{1,0:T(8,128)(2,1)S(1)}) fusion(f32[1280,896]{1,0:T(8,128)} %copy-done.167, f32[1280,896]{1,0:T(8,128)} %get-tuple-element.455, bf16[1280,1152]{1,0:T(8,128)(2,1)} %constant_dynamic-update-slice_fusion.39, bf16[896,1152]{1,0:T(8,128)(2,1)S(1)} %copy-done.158), kind=kOutput, calls=%fused_computation.33 | convolution fusion | flops 2672230400 | bytes 18776064 | tf_op jit(solution)/shard_map/dot_general | solution.py:31
  386.4 5.1 convolution_convert_fusion.1
  394.0 5.1 convolution_convert_fusion.2
  405.2 5.3 collective-permute-start.52
  430.8 7.8 %collective-permute-start.53 = (bf16[4,88,896]{2,1,0:T(8,128)(2,1)}, bf16[4,88,896]{2,1,0:T(8,128)(2,1)S(1)}, u32[]{:S(2)}, u32[]{:S(2)}) collective-permute-start(bf16[4,88,896]{2,1,0:T(8,128)(2,1)} %get-tuple-element.309), channel_id=1, source_target_pairs={{0,16},{16,8},{8,24},{24,0},{1,17},{17,9},{9,25},{25,1},{2,18},{18... | collective-permute-start | bytes 1892360 | tf_op jit(solution)/shard_map/ppermute | solution.py:48
  440.8 4.3 fusion.36
  448.8 5.8 multiply_convert_fusion
  458.7 5.3 collective-permute-start.54
  469.9 4.3 collective-permute-start.68
  488.6 7.7 %collective-permute-done.56 = bf16[320,512]{1,0:T(8,128)(2,1)S(1)} collective-permute-done((bf16[320,512]{1,0:T(8,128)(2,1)S(1)}, bf16[320,512]{1,0:T(8,128)(2,1)S(1)}, u32[]{:S(2)}, u32[]{:S(2)}) %collective-permute-start.56) | collective-permute-done | bytes 327712 | tf_op jit(solution)/shard_map/ppermute | solution.py:48
  496.2 5.7 collective-permute-start.66
  514.0 7.3 %all-to-all-start.3 = ((bf16[8,32,896]{2,1,0:T(8,128)(2,1)}), bf16[8,32,896]{2,1,0:T(8,128)(2,1)}, u32[]{:S(2)}, u32[]{:S(2)}) async-start(bf16[8,32,896]{2,1,0:T(8,128)(2,1)} %bitcast.334), calls=%async_computation.3 | async-start | bytes 917504 | tf_op jit(solution)/shard_map/all_to_all | solution.py:35
  552.5 10.4 %all-to-all-start.4 = ((bf16[64,24,1408]{2,1,0:T(8,128)(2,1)}), bf16[64,24,1408]{2,1,0:T(8,128)(2,1)}, u32[]{:S(2)}, u32[]{:S(2)}) async-start(bf16[64,24,1408]{2,1,0:T(8,128)(2,1)} %pad_maximum_fusion.1), calls=%async_computation.4 | async-start | bytes 8650752 | tf_op jit(solution)/shard_map/all_to_all | solution.py:35
  598.4 4.3 collective-permute-start.75
  615.9 5.4 collective-permute-done.75
  (780 shorter events, 394.2 us)
Async XLA Ops:
  13.7 63.8 %all-to-all-start = ((bf16[64,24,1152]{2,1,0:T(8,128)(2,1)}), bf16[64,24,1152]{2,1,0:T(8,128)(2,1)S(1)}, u32[]{:S(2)}, u32[]{:S(2)}) async-start(bf16[64,24,1152]{2,1,0:T(8,128)(2,1)} %broadcast_in_dim.163), calls=%async_computation | async-start | bytes 7077888 | tf_op jit(solution)/shard_map/all_to_all | solution.py:35
  35.4 29.3 %collective-permute-start.1 = (bf16[4,24,896]{2,1,0:T(8,128)(2,1)}, bf16[4,24,896]{2,1,0:T(8,128)(2,1)}, u32[]{:S(2)}, u32[]{:S(2)}) collective-permute-start(bf16[4,24,896]{2,1,0:T(8,128)(2,1)} %get-tuple-element.362), channel_id=1, source_target_pairs={{0,1},{1,0},{2,3},{3,2},{4,5},{5,4},{6,7},{7,6},{8,9},{9,8},{10,11... | collective-permute-start | bytes 516104 | tf_op jit(solution)/shard_map/ppermute | solution.py:39
  41.3 21.8 %collective-permute-start.5 = (bf16[12,1024]{1,0:T(8,128)(2,1)}, bf16[12,1024]{1,0:T(8,128)(2,1)}, u32[]{:S(2)}, u32[]{:S(2)}) collective-permute-start(bf16[12,1024]{1,0:T(8,128)(2,1)} %broadcast_select_fusion.19), channel_id=1, source_target_pairs={{0,1},{1,0},{2,3},{3,2},{4,5},{5,4},{6,7},{7,6},{8,9},{9,8},{10,11... | collective-permute-start | bytes 73736 | tf_op jit(solution)/shard_map/ppermute | solution.py:39
  42.9 34.7 %collective-permute-start.6 = (bf16[56,1408]{1,0:T(8,128)(2,1)}, bf16[56,1408]{1,0:T(8,128)(2,1)}, u32[]{:S(2)}, u32[]{:S(2)}) collective-permute-start(bf16[56,1408]{1,0:T(8,128)(2,1)} %fusion.325), channel_id=1, source_target_pairs={{0,0},{1,32},{2,64},{3,96},{4,8},{5,40},{6,72},{7,104},{8,16},{9,4... | collective-permute-start | bytes 473096 | tf_op jit(solution)/shard_map/ppermute | solution.py:249
  77.6 42.4 %collective-permute-start.10 = (bf16[64,24,1152]{2,1,0:T(8,128)(2,1)S(1)}, bf16[64,24,1152]{2,1,0:T(8,128)(2,1)}, u32[]{:S(2)}, u32[]{:S(2)}) collective-permute-start(bf16[64,24,1152]{2,1,0:T(8,128)(2,1)S(1)} %all-to-all-done), channel_id=1, source_target_pairs={{0,1},{1,0},{2,3},{3,2},{4,5},{5,4},{6,7},{7,6},{8,9},{9,8},{10,11... | collective-permute-start | bytes 10616840 | tf_op jit(solution)/shard_map/ppermute | solution.py:39
  98.6 55.8 %all-to-all-start.1 = ((bf16[64,24,1024]{2,1,0:T(8,128)(2,1)}), bf16[64,24,1024]{2,1,0:T(8,128)(2,1)}, u32[]{:S(2)}, u32[]{:S(2)}) async-start(bf16[64,24,1024]{2,1,0:T(8,128)(2,1)} %broadcast_in_dim.167), calls=%async_computation.1 | async-start | bytes 6291456 | tf_op jit(solution)/shard_map/all_to_all | solution.py:35
  128.8 20.2 %collective-permute-start.11 = (bf16[160,512]{1,0:T(8,128)(2,1)S(1)}, bf16[160,512]{1,0:T(8,128)(2,1)S(1)}, u32[]{:S(2)}, u32[]{:S(2)}) collective-permute-start(bf16[160,512]{1,0:T(8,128)(2,1)S(1)} %get-tuple-element.395), channel_id=1, source_target_pairs={{0,8},{8,0},{1,9},{9,1},{2,10},{10,2},{3,11},{11,3},{4,12},{12,4},... | collective-permute-start | bytes 491528 | tf_op jit(solution)/shard_map/ppermute | solution.py:43
  178.2 117.9 %collective-permute-start.24 = (bf16[4,56,1408]{2,1,0:T(8,128)(2,1)}, bf16[4,56,1408]{2,1,0:T(8,128)(2,1)}, u32[]{:S(2)}, u32[]{:S(2)}) collective-permute-start(bf16[4,56,1408]{2,1,0:T(8,128)(2,1)} %bitcast_dynamic-update-slice_fusion.4), channel_id=1, source_target_pairs={{0,16},{16,8},{8,24},{24,0},{1,17},{17,9},{9,25},{25,1},{2,18},{18... | collective-permute-start | bytes 1892360 | tf_op jit(solution)/shard_map/ppermute | solution.py:48
  179.9 116.1 %collective-permute-start.25 = (bf16[4,56,1408]{2,1,0:T(8,128)(2,1)}, bf16[4,56,1408]{2,1,0:T(8,128)(2,1)}, u32[]{:S(2)}, u32[]{:S(2)}) collective-permute-start(bf16[4,56,1408]{2,1,0:T(8,128)(2,1)} %bitcast_dynamic-update-slice_fusion.4), channel_id=1, source_target_pairs={{0,8},{16,24},{8,0},{24,16},{1,9},{17,25},{9,1},{25,17},{2,10},{18... | collective-permute-start | bytes 1892360 | tf_op jit(solution)/shard_map/ppermute | solution.py:48
  180.1 116.0 %collective-permute-start.26 = (bf16[4,56,1408]{2,1,0:T(8,128)(2,1)}, bf16[4,56,1408]{2,1,0:T(8,128)(2,1)}, u32[]{:S(2)}, u32[]{:S(2)}) collective-permute-start(bf16[4,56,1408]{2,1,0:T(8,128)(2,1)} %bitcast_dynamic-update-slice_fusion.4), channel_id=1, source_target_pairs={{0,24},{16,0},{8,16},{24,8},{1,25},{17,1},{9,17},{25,9},{2,26},{18... | collective-permute-start | bytes 1892360 | tf_op jit(solution)/shard_map/ppermute | solution.py:48
  182.0 91.1 %all-to-all-start.2 = ((bf16[16,176,896]{2,1,0:T(8,128)(2,1)}), bf16[16,176,896]{2,1,0:T(8,128)(2,1)}, u32[]{:S(2)}, u32[]{:S(2)}) async-start(bf16[16,176,896]{2,1,0:T(8,128)(2,1)} %broadcast_in_dim.173), calls=%async_computation.2 | async-start | bytes 10092544 | tf_op jit(solution)/shard_map/all_to_all | solution.py:35
  213.0 20.8 %collective-permute-start.18 = (bf16[160,1152]{1,0:T(8,128)(2,1)S(1)}, bf16[160,1152]{1,0:T(8,128)(2,1)S(1)}, u32[]{:S(2)}, u32[]{:S(2)}) collective-permute-start(bf16[160,1152]{1,0:T(8,128)(2,1)S(1)} %get-tuple-element.286), channel_id=1, source_target_pairs={{0,4},{2,6},{4,0},{6,2},{1,5},{3,7},{5,1},{7,3},{8,12},{10,14},{12... | collective-permute-start | bytes 1105928 | tf_op jit(solution)/shard_map/ppermute | solution.py:48
  393.7 63.0 %collective-permute-start.51 = (bf16[4,88,896]{2,1,0:T(8,128)(2,1)}, bf16[4,88,896]{2,1,0:T(8,128)(2,1)}, u32[]{:S(2)}, u32[]{:S(2)}) collective-permute-start(bf16[4,88,896]{2,1,0:T(8,128)(2,1)} %get-tuple-element.311), channel_id=1, source_target_pairs={{0,24},{16,0},{8,16},{24,8},{1,25},{17,1},{9,17},{25,9},{2,26},{18... | collective-permute-start | bytes 1892360 | tf_op jit(solution)/shard_map/ppermute | solution.py:48
  405.2 51.5 %collective-permute-start.52 = (bf16[4,88,896]{2,1,0:T(8,128)(2,1)}, bf16[4,88,896]{2,1,0:T(8,128)(2,1)}, u32[]{:S(2)}, u32[]{:S(2)}) collective-permute-start(bf16[4,88,896]{2,1,0:T(8,128)(2,1)} %get-tuple-element.312), channel_id=1, source_target_pairs={{0,8},{16,24},{8,0},{24,16},{1,9},{17,25},{9,1},{25,17},{2,10},{18... | collective-permute-start | bytes 1892360 | tf_op jit(solution)/shard_map/ppermute | solution.py:48
  410.6 20.2 %collective-permute-start.48 = (bf16[4,88,896]{2,1,0:T(8,128)(2,1)}, bf16[4,88,896]{2,1,0:T(8,128)(2,1)}, u32[]{:S(2)}, u32[]{:S(2)}) collective-permute-start(bf16[4,88,896]{2,1,0:T(8,128)(2,1)} %get-tuple-element.307), channel_id=1, source_target_pairs={{0,96},{32,0},{64,32},{96,64},{1,97},{33,1},{65,33},{97,65},{2,98}... | collective-permute-start | bytes 1892360 | tf_op jit(solution)/shard_map/ppermute | solution.py:48
  413.1 25.5 %collective-permute-start.49 = (bf16[4,88,896]{2,1,0:T(8,128)(2,1)}, bf16[4,88,896]{2,1,0:T(8,128)(2,1)}, u32[]{:S(2)}, u32[]{:S(2)}) collective-permute-start(bf16[4,88,896]{2,1,0:T(8,128)(2,1)} %get-tuple-element.308), channel_id=1, source_target_pairs={{0,64},{32,96},{64,0},{96,32},{1,65},{33,97},{65,1},{97,33},{2,66}... | collective-permute-start | bytes 1892360 | tf_op jit(solution)/shard_map/ppermute | solution.py:48
  430.8 25.9 %collective-permute-start.53 = (bf16[4,88,896]{2,1,0:T(8,128)(2,1)}, bf16[4,88,896]{2,1,0:T(8,128)(2,1)S(1)}, u32[]{:S(2)}, u32[]{:S(2)}) collective-permute-start(bf16[4,88,896]{2,1,0:T(8,128)(2,1)} %get-tuple-element.309), channel_id=1, source_target_pairs={{0,16},{16,8},{8,24},{24,0},{1,17},{17,9},{9,25},{25,1},{2,18},{18... | collective-permute-start | bytes 1892360 | tf_op jit(solution)/shard_map/ppermute | solution.py:48
  469.9 33.1 %collective-permute-start.68 = (bf16[88,896]{1,0:T(8,128)(2,1)S(1)}, bf16[88,896]{1,0:T(8,128)(2,1)S(1)}, u32[]{:S(2)}, u32[]{:S(2)}) collective-permute-start(bf16[88,896]{1,0:T(8,128)(2,1)S(1)} %get-tuple-element.351), channel_id=1, source_target_pairs={{0,96},{32,0},{64,32},{96,64},{1,97},{33,1},{65,33},{97,65},{2,98}... | collective-permute-start | bytes 473096 | tf_op jit(solution)/shard_map/ppermute | solution.py:48
  474.2 28.9 %collective-permute-start.69 = (bf16[88,896]{1,0:T(8,128)(2,1)S(1)}, bf16[88,896]{1,0:T(8,128)(2,1)S(1)}, u32[]{:S(2)}, u32[]{:S(2)}) collective-permute-start(bf16[88,896]{1,0:T(8,128)(2,1)S(1)} %get-tuple-element.350), channel_id=1, source_target_pairs={{0,64},{32,96},{64,0},{96,32},{1,65},{33,97},{65,1},{97,33},{2,66}... | collective-permute-start | bytes 473096 | tf_op jit(solution)/shard_map/ppermute | solution.py:48
  486.6 20.6 %collective-permute-start.70 = (bf16[88,896]{1,0:T(8,128)(2,1)S(1)}, bf16[88,896]{1,0:T(8,128)(2,1)S(1)}, u32[]{:S(2)}, u32[]{:S(2)}) collective-permute-start(bf16[88,896]{1,0:T(8,128)(2,1)S(1)} %get-tuple-element.349), channel_id=1, source_target_pairs={{0,32},{32,64},{64,96},{96,0},{1,33},{33,65},{65,97},{97,1},{2,34}... | collective-permute-start | bytes 473096 | tf_op jit(solution)/shard_map/ppermute | solution.py:48
  488.6 20.7 %collective-permute-start.65 = (bf16[88,896]{1,0:T(8,128)(2,1)S(1)}, bf16[88,896]{1,0:T(8,128)(2,1)S(1)}, u32[]{:S(2)}, u32[]{:S(2)}) collective-permute-start(bf16[88,896]{1,0:T(8,128)(2,1)S(1)} %get-tuple-element.347), channel_id=1, source_target_pairs={{0,24},{16,0},{8,16},{24,8},{1,25},{17,1},{9,17},{25,9},{2,26},{18... | collective-permute-start | bytes 473096 | tf_op jit(solution)/shard_map/ppermute | solution.py:48
  503.1 20.1 %collective-permute-start.55 = (bf16[1536,512]{1,0:T(8,128)(2,1)}, bf16[1536,512]{1,0:T(8,128)(2,1)}, u32[]{:S(2)}, u32[]{:S(2)}) collective-permute-start(bf16[1536,512]{1,0:T(8,128)(2,1)} %fusion.46), channel_id=1, source_target_pairs={{0,1},{1,0},{2,3},{3,2},{4,5},{5,4},{6,7},{7,6},{8,9},{9,8},{10,11... | collective-permute-start | bytes 4718600 | tf_op jit(solution)/shard_map/ppermute | solution.py:39
  507.2 23.1 %collective-permute-start.60 = (bf16[4,56,1152]{2,1,0:T(8,128)(2,1)}, bf16[4,56,1152]{2,1,0:T(8,128)(2,1)}, u32[]{:S(2)}, u32[]{:S(2)}) collective-permute-start(bf16[4,56,1152]{2,1,0:T(8,128)(2,1)} %get-tuple-element.315), channel_id=1, source_target_pairs={{0,96},{32,0},{64,32},{96,64},{1,97},{33,1},{65,33},{97,65},{2,98}... | collective-permute-start | bytes 1548296 | tf_op jit(solution)/shard_map/ppermute | solution.py:48
  509.2 23.3 %collective-permute-start.61 = (bf16[4,56,1152]{2,1,0:T(8,128)(2,1)}, bf16[4,56,1152]{2,1,0:T(8,128)(2,1)}, u32[]{:S(2)}, u32[]{:S(2)}) collective-permute-start(bf16[4,56,1152]{2,1,0:T(8,128)(2,1)} %get-tuple-element.314), channel_id=1, source_target_pairs={{0,64},{32,96},{64,0},{96,32},{1,65},{33,97},{65,1},{97,33},{2,66}... | collective-permute-start | bytes 1548296 | tf_op jit(solution)/shard_map/ppermute | solution.py:48
  509.2 24.2 %collective-permute-start.62 = (bf16[4,56,1152]{2,1,0:T(8,128)(2,1)}, bf16[4,56,1152]{2,1,0:T(8,128)(2,1)}, u32[]{:S(2)}, u32[]{:S(2)}) collective-permute-start(bf16[4,56,1152]{2,1,0:T(8,128)(2,1)} %get-tuple-element.313), channel_id=1, source_target_pairs={{0,32},{32,64},{64,96},{96,0},{1,33},{33,65},{65,97},{97,1},{2,34}... | collective-permute-start | bytes 1548296 | tf_op jit(solution)/shard_map/ppermute | solution.py:48
  511.2 32.0 %collective-permute-start.64 = (bf16[1536,640]{1,0:T(8,128)(2,1)}, bf16[1536,640]{1,0:T(8,128)(2,1)}, u32[]{:S(2)}, u32[]{:S(2)}) collective-permute-start(bf16[1536,640]{1,0:T(8,128)(2,1)} %add_convert_fusion.3), channel_id=1, source_target_pairs={{0,1},{1,0},{2,3},{3,2},{4,5},{5,4},{6,7},{7,6},{8,9},{9,8},{10,11... | collective-permute-start | bytes 5898248 | tf_op jit(solution)/shard_map/ppermute | solution.py:39
  514.0 38.5 %all-to-all-start.3 = ((bf16[8,32,896]{2,1,0:T(8,128)(2,1)}), bf16[8,32,896]{2,1,0:T(8,128)(2,1)}, u32[]{:S(2)}, u32[]{:S(2)}) async-start(bf16[8,32,896]{2,1,0:T(8,128)(2,1)} %bitcast.334), calls=%async_computation.3 | async-start | bytes 917504 | tf_op jit(solution)/shard_map/all_to_all | solution.py:35
  538.9 34.3 %collective-permute-start.71 = (bf16[56,1152]{1,0:T(8,128)(2,1)}, bf16[56,1152]{1,0:T(8,128)(2,1)}, u32[]{:S(2)}, u32[]{:S(2)}) collective-permute-start(bf16[56,1152]{1,0:T(8,128)(2,1)} %get-tuple-element.355), channel_id=1, source_target_pairs={{0,24},{16,0},{8,16},{24,8},{1,25},{17,1},{9,17},{25,9},{2,26},{18... | collective-permute-start | bytes 387080 | tf_op jit(solution)/shard_map/ppermute | solution.py:48
  540.5 32.7 %collective-permute-start.72 = (bf16[56,1152]{1,0:T(8,128)(2,1)}, bf16[56,1152]{1,0:T(8,128)(2,1)}, u32[]{:S(2)}, u32[]{:S(2)}) collective-permute-start(bf16[56,1152]{1,0:T(8,128)(2,1)} %get-tuple-element.354), channel_id=1, source_target_pairs={{0,8},{16,24},{8,0},{24,16},{1,9},{17,25},{9,1},{25,17},{2,10},{18... | collective-permute-start | bytes 387080 | tf_op jit(solution)/shard_map/ppermute | solution.py:48
  540.5 32.7 %collective-permute-start.73 = (bf16[56,1152]{1,0:T(8,128)(2,1)}, bf16[56,1152]{1,0:T(8,128)(2,1)}, u32[]{:S(2)}, u32[]{:S(2)}) collective-permute-start(bf16[56,1152]{1,0:T(8,128)(2,1)} %get-tuple-element.353), channel_id=1, source_target_pairs={{0,16},{16,8},{8,24},{24,0},{1,17},{17,9},{9,25},{25,1},{2,18},{18... | collective-permute-start | bytes 387080 | tf_op jit(solution)/shard_map/ppermute | solution.py:48
  552.5 72.4 %all-to-all-start.4 = ((bf16[64,24,1408]{2,1,0:T(8,128)(2,1)}), bf16[64,24,1408]{2,1,0:T(8,128)(2,1)}, u32[]{:S(2)}, u32[]{:S(2)}) async-start(bf16[64,24,1408]{2,1,0:T(8,128)(2,1)} %pad_maximum_fusion.1), calls=%async_computation.4 | async-start | bytes 8650752 | tf_op jit(solution)/shard_map/all_to_all | solution.py:35
  598.4 22.8 %collective-permute-start.75 = (bf16[56,1152]{1,0:T(8,128)(2,1)}, bf16[56,1152]{1,0:T(8,128)(2,1)}, u32[]{:S(2)}, u32[]{:S(2)}) collective-permute-start(bf16[56,1152]{1,0:T(8,128)(2,1)} %add_convert_fusion.11), channel_id=1, source_target_pairs={{0,0},{32,1},{64,2},{96,3},{8,4},{40,5},{72,6},{104,7},{16,8},{48,... | collective-permute-start | bytes 387080 | tf_op jit(solution)/shard_map/ppermute | solution.py:522
  (221 other events, 2244.8 us)

commit v11 on v10

--- a/solution.py
+++ b/solution.py
@@ -317,10 +317,11 @@
     ff_own, _ = after((out_one, down_line), ff_own)
     ff_wide = jnp.broadcast_to(ff_own[None], (16, 176, 896))
     ff_all = exchange(ff_wide, PLANE)
-    down_parts = [down_line] + [shift(down_line, "x", k) for k in (1, 2, 3)]
     kv_parts = [pair] + list(after(ff_wide, *[shift(pair, "y", k) for k in (1, 2, 3)])[:3])
     kv_mine = jnp.concatenate(kv_parts, axis=0)
     kv = jnp.concatenate([kv_mine, other_core(kv_mine)], axis=0)
+    kv, down_line = lax.optimization_barrier((kv, down_line))
+    down_parts = [down_line] + [shift(down_line, "x", k) for k in (1, 2, 3)]
     keys, values = kv[:, :256], kv[:, 256:]
     queries = [dot(sides[0], raw[i][:, :512]) for i in (0, 1)]
     q_rows = jnp.concatenate(

time: 652 us -> 638 us (0.979)
  waiting for transfers between devices: 111 us -> 102 us
    all_to_all x5, waiting for transfers between devices: 26.8 us -> 7.51 us  [exchange(): return lax.all_to_all(x, axes, split_axis=0, concat_axis=0, tiled=True)]
    ppermute x45, waiting for transfers between devices: 57.7 us -> 67.3 us  [shift(): lax.ppermute(x, RING[axis], [(number[i], number[(i + k) % 4]) for i in ra...]
  transfers between devices with their start and end apart: 81 -> 81, of which waited for: 21 -> 21; matrix products, arithmetic and copies ran while one was open for 45% -> 46% of each run, Pallas kernels for 0% -> 0%
where the time goes in v11:
time: 638 us; the launch traced here: 626 us
  matrix products  173 us (27%)
  starting transfers between devices  156 us (24%)
  local copies, waits for them, and re-layouts  106 us (17%)
  waiting for transfers between devices  102 us (16%)
  other arithmetic  81.1 us (13%)
  between operations  9.15 us (1%)
    ppermute x45, starting transfers between devices, shift(): lax.ppermute(x, RING[axis], [(number[i], number[(i + k) % 4]) for i in ra...  71.7 us
    dot_general x37, matrix products, dot(): return jnp.dot(a, b, preferred_element_type=F32)  70.8 us
    ppermute x45, waiting for transfers between devices, shift(): lax.ppermute(x, RING[axis], [(number[i], number[(i + k) % 4]) for i in ra...  67.3 us
    dot_general x38, matrix products, dot_tr(): lax.dot_general(a, b, (((1,), (1,)), ((), ())), preferred_element_type=F32)  64.3 us
    all_to_all x5, starting transfers between devices, exchange(): return lax.all_to_all(x, axes, split_axis=0, concat_axis=0, tiled=True)  47.3 us
    dot_general x19, matrix products, dot_tl(): lax.dot_general(a, b, (((0,), (0,)), ((), ())), preferred_element_type=F32)  37.5 us
    unnamed x372, local copies, waits for them, and re-layouts  32.6 us
    ppermute x27, starting transfers between devices, other_core(): return lax.ppermute(x, 'c', [(0, 1), (1, 0)])  26.5 us
  transfers between devices with their start and end apart: 81, of which 21 were waited for; matrix products, arithmetic and copies ran while one was open for 46% of the time, Pallas kernels for 0%

profile of v11, /device:TPU:63, one launch (start us, length us, event | category | flops | bytes accessed | tf_op | source)
XLA Modules:
  0.0 626.5 jit_solution(9646282647223294002)
XLA Ops:
  13.7 10.2 %all-to-all-start = ((bf16[64,24,1152]{2,1,0:T(8,128)(2,1)}), bf16[64,24,1152]{2,1,0:T(8,128)(2,1)S(1)}, u32[]{:S(2)}, u32[]{:S(2)}) async-start(bf16[64,24,1152]{2,1,0:T(8,128)(2,1)} %broadcast_in_dim.163), calls=%async_computation | async-start | bytes 7077888 | tf_op jit(solution)/shard_map/all_to_all | solution.py:35
  42.9 4.8 collective-permute-start.6
  69.8 4.2 collective-permute-done.4
  82.1 5.3 collective-permute-start.8
  98.6 12.7 %all-to-all-start.1 = ((bf16[64,24,1024]{2,1,0:T(8,128)(2,1)}), bf16[64,24,1024]{2,1,0:T(8,128)(2,1)}, u32[]{:S(2)}, u32[]{:S(2)}) async-start(bf16[64,24,1024]{2,1,0:T(8,128)(2,1)} %broadcast_in_dim.167), calls=%async_computation.1 | async-start | bytes 6291456 | tf_op jit(solution)/shard_map/all_to_all | solution.py:35
  131.5 17.5 %collective-permute-done.11 = bf16[160,512]{1,0:T(8,128)(2,1)S(1)} collective-permute-done((bf16[160,512]{1,0:T(8,128)(2,1)S(1)}, bf16[160,512]{1,0:T(8,128)(2,1)S(1)}, u32[]{:S(2)}, u32[]{:S(2)}) %collective-permute-start.11) | collective-permute-done | bytes 163872 | tf_op jit(solution)/shard_map/ppermute | solution.py:43
  161.5 7.4 %collective-permute-done.14 = bf16[320,512]{1,0:T(8,128)(2,1)} collective-permute-done((bf16[320,512]{1,0:T(8,128)(2,1)}, bf16[320,512]{1,0:T(8,128)(2,1)}, u32[]{:S(2)}, u32[]{:S(2)}) %collective-permute-start.14) | collective-permute-done | bytes 327712 | tf_op jit(solution)/shard_map/ppermute | solution.py:48
  179.2 6.6 %all-to-all-start.2 = ((bf16[16,176,896]{2,1,0:T(8,128)(2,1)}), bf16[16,176,896]{2,1,0:T(8,128)(2,1)}, u32[]{:S(2)}, u32[]{:S(2)}) async-start(bf16[16,176,896]{2,1,0:T(8,128)(2,1)} %broadcast_in_dim.173), calls=%async_computation.2 | async-start | bytes 10092544 | tf_op jit(solution)/shard_map/all_to_all | solution.py:35
  210.6 4.0 collective-permute-start.18
  226.2 3.7 collective-permute-start.19
  243.2 7.5 %all-to-all-done.2 = bf16[16,176,896]{2,1,0:T(8,128)(2,1)} async-done(((bf16[16,176,896]{2,1,0:T(8,128)(2,1)}), bf16[16,176,896]{2,1,0:T(8,128)(2,1)}, u32[]{:S(2)}, u32[]{:S(2)}) %all-to-all-start.2) | async-done | bytes 5046304 | tf_op jit(solution)/shard_map/all_to_all | solution.py:35
  254.7 6.1 fusion.608
  260.8 3.9 add_convert_fusion
  264.7 8.9 %multiply_convert_fusion.1 = (bf16[1280,896]{1,0:T(8,128)(2,1)S(1)}, f32[1280,896]{1,0:T(8,128)}) fusion(f32[1280,896]{1,0:T(8,128)S(1)} %fusion.608, bf16[1280,1152]{1,0:T(8,128)(2,1)} %constant_dynamic-update-slice_fusion.31, bf16[1152,896]{1,0:T(8,128)(2,1)S(1)} %bitcast.320), kind=kOutput, calls=%fused_computation.41 | convolution fusion | flops 2653880320 | bytes 16482304 | tf_op jit(solution)/shard_map/dot_general | solution.py:23
  280.4 3.7 fusion.609
  299.8 5.2 collective-permute-done.32
  305.2 9.1 %collective-permute-done.28 = bf16[160,1152]{1,0:T(8,128)(2,1)S(1)} collective-permute-done((bf16[160,1152]{1,0:T(8,128)(2,1)S(1)}, bf16[160,1152]{1,0:T(8,128)(2,1)S(1)}, u32[]{:S(2)}, u32[]{:S(2)}) %collective-permute-start.28) | collective-permute-done | bytes 368672 | tf_op jit(solution)/shard_map/ppermute | solution.py:48
  334.9 3.7 collective-permute-done.36
  345.2 11.0 %fusion.10 = (bf16[1280,896]{1,0:T(8,128)(2,1)S(1)}, bf16[1280,896]{1,0:T(8,128)(2,1)S(1)}) fusion(f32[1280,896]{1,0:T(8,128)} %copy-done.167, f32[1280,896]{1,0:T(8,128)} %get-tuple-element.459, bf16[1280,1152]{1,0:T(8,128)(2,1)} %constant_dynamic-update-slice_fusion.39, bf16[896,1152]{1,0:T(8,128)(2,1)S(1)} %copy-done.158), kind=kOutput, calls=%fused_computation.33 | convolution fusion | flops 2672230400 | bytes 18776064 | tf_op jit(solution)/shard_map/dot_general | solution.py:31
  365.0 5.1 convolution_convert_fusion.1
  374.3 5.1 convolution_convert_fusion.2
  385.3 5.6 collective-permute-start.52
  390.8 6.0 collective-permute-start.48
  398.9 9.5 %collective-permute-start.50 = (bf16[4,88,896]{2,1,0:T(8,128)(2,1)}, bf16[4,88,896]{2,1,0:T(8,128)(2,1)}, u32[]{:S(2)}, u32[]{:S(2)}) collective-permute-start(bf16[4,88,896]{2,1,0:T(8,128)(2,1)} %get-tuple-element.309), channel_id=1, source_target_pairs={{0,32},{32,64},{64,96},{96,0},{1,33},{33,65},{65,97},{97,1},{2,34}... | collective-permute-start | bytes 1892360 | tf_op jit(solution)/shard_map/ppermute | solution.py:48
  420.7 15.2 %collective-permute-done.50 = bf16[4,88,896]{2,1,0:T(8,128)(2,1)} collective-permute-done((bf16[4,88,896]{2,1,0:T(8,128)(2,1)}, bf16[4,88,896]{2,1,0:T(8,128)(2,1)}, u32[]{:S(2)}, u32[]{:S(2)}) %collective-permute-start.50) | collective-permute-done | bytes 630816 | tf_op jit(solution)/shard_map/ppermute | solution.py:48
  437.9 4.3 fusion.36
  445.9 5.8 multiply_convert_fusion
  477.6 7.9 %collective-permute-done.56 = bf16[320,512]{1,0:T(8,128)(2,1)S(1)} collective-permute-done((bf16[320,512]{1,0:T(8,128)(2,1)S(1)}, bf16[320,512]{1,0:T(8,128)(2,1)S(1)}, u32[]{:S(2)}, u32[]{:S(2)}) %collective-permute-start.56) | collective-permute-done | bytes 327712 | tf_op jit(solution)/shard_map/ppermute | solution.py:48
  500.7 7.3 %all-to-all-start.3 = ((bf16[8,32,896]{2,1,0:T(8,128)(2,1)}), bf16[8,32,896]{2,1,0:T(8,128)(2,1)}, u32[]{:S(2)}, u32[]{:S(2)}) async-start(bf16[8,32,896]{2,1,0:T(8,128)(2,1)} %bitcast.334), calls=%async_computation.3 | async-start | bytes 917504 | tf_op jit(solution)/shard_map/all_to_all | solution.py:35
  538.8 10.6 %all-to-all-start.4 = ((bf16[64,24,1408]{2,1,0:T(8,128)(2,1)}), bf16[64,24,1408]{2,1,0:T(8,128)(2,1)}, u32[]{:S(2)}, u32[]{:S(2)}) async-start(bf16[64,24,1408]{2,1,0:T(8,128)(2,1)} %pad_maximum_fusion.1), calls=%async_computation.4 | async-start | bytes 8650752 | tf_op jit(solution)/shard_map/all_to_all | solution.py:35
  585.0 4.3 collective-permute-start.75
  602.5 5.4 collective-permute-done.75
  (780 shorter events, 389.8 us)
Async XLA Ops:
  13.7 63.8 %all-to-all-start = ((bf16[64,24,1152]{2,1,0:T(8,128)(2,1)}), bf16[64,24,1152]{2,1,0:T(8,128)(2,1)S(1)}, u32[]{:S(2)}, u32[]{:S(2)}) async-start(bf16[64,24,1152]{2,1,0:T(8,128)(2,1)} %broadcast_in_dim.163), calls=%async_computation | async-start | bytes 7077888 | tf_op jit(solution)/shard_map/all_to_all | solution.py:35
  35.4 29.3 %collective-permute-start.1 = (bf16[4,24,896]{2,1,0:T(8,128)(2,1)}, bf16[4,24,896]{2,1,0:T(8,128)(2,1)}, u32[]{:S(2)}, u32[]{:S(2)}) collective-permute-start(bf16[4,24,896]{2,1,0:T(8,128)(2,1)} %get-tuple-element.366), channel_id=1, source_target_pairs={{0,1},{1,0},{2,3},{3,2},{4,5},{5,4},{6,7},{7,6},{8,9},{9,8},{10,11... | collective-permute-start | bytes 516104 | tf_op jit(solution)/shard_map/ppermute | solution.py:39
  41.3 21.8 %collective-permute-start.5 = (bf16[12,1024]{1,0:T(8,128)(2,1)}, bf16[12,1024]{1,0:T(8,128)(2,1)}, u32[]{:S(2)}, u32[]{:S(2)}) collective-permute-start(bf16[12,1024]{1,0:T(8,128)(2,1)} %broadcast_select_fusion.19), channel_id=1, source_target_pairs={{0,1},{1,0},{2,3},{3,2},{4,5},{5,4},{6,7},{7,6},{8,9},{9,8},{10,11... | collective-permute-start | bytes 73736 | tf_op jit(solution)/shard_map/ppermute | solution.py:39
  42.9 34.7 %collective-permute-start.6 = (bf16[56,1408]{1,0:T(8,128)(2,1)}, bf16[56,1408]{1,0:T(8,128)(2,1)}, u32[]{:S(2)}, u32[]{:S(2)}) collective-permute-start(bf16[56,1408]{1,0:T(8,128)(2,1)} %fusion.325), channel_id=1, source_target_pairs={{0,0},{1,32},{2,64},{3,96},{4,8},{5,40},{6,72},{7,104},{8,16},{9,4... | collective-permute-start | bytes 473096 | tf_op jit(solution)/shard_map/ppermute | solution.py:249
  77.6 42.4 %collective-permute-start.10 = (bf16[64,24,1152]{2,1,0:T(8,128)(2,1)S(1)}, bf16[64,24,1152]{2,1,0:T(8,128)(2,1)}, u32[]{:S(2)}, u32[]{:S(2)}) collective-permute-start(bf16[64,24,1152]{2,1,0:T(8,128)(2,1)S(1)} %all-to-all-done), channel_id=1, source_target_pairs={{0,1},{1,0},{2,3},{3,2},{4,5},{5,4},{6,7},{7,6},{8,9},{9,8},{10,11... | collective-permute-start | bytes 10616840 | tf_op jit(solution)/shard_map/ppermute | solution.py:39
  98.6 55.8 %all-to-all-start.1 = ((bf16[64,24,1024]{2,1,0:T(8,128)(2,1)}), bf16[64,24,1024]{2,1,0:T(8,128)(2,1)}, u32[]{:S(2)}, u32[]{:S(2)}) async-start(bf16[64,24,1024]{2,1,0:T(8,128)(2,1)} %broadcast_in_dim.167), calls=%async_computation.1 | async-start | bytes 6291456 | tf_op jit(solution)/shard_map/all_to_all | solution.py:35
  128.8 20.2 %collective-permute-start.11 = (bf16[160,512]{1,0:T(8,128)(2,1)S(1)}, bf16[160,512]{1,0:T(8,128)(2,1)S(1)}, u32[]{:S(2)}, u32[]{:S(2)}) collective-permute-start(bf16[160,512]{1,0:T(8,128)(2,1)S(1)} %get-tuple-element.399), channel_id=1, source_target_pairs={{0,8},{8,0},{1,9},{9,1},{2,10},{10,2},{3,11},{11,3},{4,12},{12,4},... | collective-permute-start | bytes 491528 | tf_op jit(solution)/shard_map/ppermute | solution.py:43
  179.2 71.5 %all-to-all-start.2 = ((bf16[16,176,896]{2,1,0:T(8,128)(2,1)}), bf16[16,176,896]{2,1,0:T(8,128)(2,1)}, u32[]{:S(2)}, u32[]{:S(2)}) async-start(bf16[16,176,896]{2,1,0:T(8,128)(2,1)} %broadcast_in_dim.173), calls=%async_computation.2 | async-start | bytes 10092544 | tf_op jit(solution)/shard_map/all_to_all | solution.py:35
  191.5 82.1 %collective-permute-start.24 = (bf16[4,56,1408]{2,1,0:T(8,128)(2,1)}, bf16[4,56,1408]{2,1,0:T(8,128)(2,1)}, u32[]{:S(2)}, u32[]{:S(2)}) collective-permute-start(bf16[4,56,1408]{2,1,0:T(8,128)(2,1)} %bitcast_dynamic-update-slice_fusion.4), channel_id=1, source_target_pairs={{0,16},{16,8},{8,24},{24,0},{1,17},{17,9},{9,25},{25,1},{2,18},{18... | collective-permute-start | bytes 1892360 | tf_op jit(solution)/shard_map/ppermute | solution.py:48
  191.8 81.9 %collective-permute-start.25 = (bf16[4,56,1408]{2,1,0:T(8,128)(2,1)}, bf16[4,56,1408]{2,1,0:T(8,128)(2,1)}, u32[]{:S(2)}, u32[]{:S(2)}) collective-permute-start(bf16[4,56,1408]{2,1,0:T(8,128)(2,1)} %bitcast_dynamic-update-slice_fusion.4), channel_id=1, source_target_pairs={{0,8},{16,24},{8,0},{24,16},{1,9},{17,25},{9,1},{25,17},{2,10},{18... | collective-permute-start | bytes 1892360 | tf_op jit(solution)/shard_map/ppermute | solution.py:48
  193.8 79.8 %collective-permute-start.26 = (bf16[4,56,1408]{2,1,0:T(8,128)(2,1)}, bf16[4,56,1408]{2,1,0:T(8,128)(2,1)}, u32[]{:S(2)}, u32[]{:S(2)}) collective-permute-start(bf16[4,56,1408]{2,1,0:T(8,128)(2,1)} %bitcast_dynamic-update-slice_fusion.4), channel_id=1, source_target_pairs={{0,24},{16,0},{8,16},{24,8},{1,25},{17,1},{9,17},{25,9},{2,26},{18... | collective-permute-start | bytes 1892360 | tf_op jit(solution)/shard_map/ppermute | solution.py:48
  210.6 20.1 %collective-permute-start.18 = (bf16[160,1152]{1,0:T(8,128)(2,1)S(1)}, bf16[160,1152]{1,0:T(8,128)(2,1)S(1)}, u32[]{:S(2)}, u32[]{:S(2)}) collective-permute-start(bf16[160,1152]{1,0:T(8,128)(2,1)S(1)} %get-tuple-element.290), channel_id=1, source_target_pairs={{0,4},{2,6},{4,0},{6,2},{1,5},{3,7},{5,1},{7,3},{8,12},{10,14},{12... | collective-permute-start | bytes 1105928 | tf_op jit(solution)/shard_map/ppermute | solution.py:48
  363.7 21.6 %collective-permute-start.47 = (bf16[160,1152]{1,0:T(8,128)(2,1)S(1)}, bf16[160,1152]{1,0:T(8,128)(2,1)S(1)}, u32[]{:S(2)}, u32[]{:S(2)}) collective-permute-start(bf16[160,1152]{1,0:T(8,128)(2,1)S(1)} %get-tuple-element.302), channel_id=1, source_target_pairs={{0,1},{1,0},{2,3},{3,2},{4,5},{5,4},{6,7},{7,6},{8,9},{9,8},{10,11... | collective-permute-start | bytes 1105928 | tf_op jit(solution)/shard_map/ppermute | solution.py:39
  372.3 81.5 %collective-permute-start.51 = (bf16[4,88,896]{2,1,0:T(8,128)(2,1)}, bf16[4,88,896]{2,1,0:T(8,128)(2,1)}, u32[]{:S(2)}, u32[]{:S(2)}) collective-permute-start(bf16[4,88,896]{2,1,0:T(8,128)(2,1)} %get-tuple-element.315), channel_id=1, source_target_pairs={{0,24},{16,0},{8,16},{24,8},{1,25},{17,1},{9,17},{25,9},{2,26},{18... | collective-permute-start | bytes 1892360 | tf_op jit(solution)/shard_map/ppermute | solution.py:48
  385.3 68.5 %collective-permute-start.52 = (bf16[4,88,896]{2,1,0:T(8,128)(2,1)}, bf16[4,88,896]{2,1,0:T(8,128)(2,1)}, u32[]{:S(2)}, u32[]{:S(2)}) collective-permute-start(bf16[4,88,896]{2,1,0:T(8,128)(2,1)} %get-tuple-element.316), channel_id=1, source_target_pairs={{0,8},{16,24},{8,0},{24,16},{1,9},{17,25},{9,1},{25,17},{2,10},{18... | collective-permute-start | bytes 1892360 | tf_op jit(solution)/shard_map/ppermute | solution.py:48
  390.8 29.3 %collective-permute-start.48 = (bf16[4,88,896]{2,1,0:T(8,128)(2,1)}, bf16[4,88,896]{2,1,0:T(8,128)(2,1)}, u32[]{:S(2)}, u32[]{:S(2)}) collective-permute-start(bf16[4,88,896]{2,1,0:T(8,128)(2,1)} %get-tuple-element.311), channel_id=1, source_target_pairs={{0,96},{32,0},{64,32},{96,64},{1,97},{33,1},{65,33},{97,65},{2,98}... | collective-permute-start | bytes 1892360 | tf_op jit(solution)/shard_map/ppermute | solution.py:48
  396.9 23.8 %collective-permute-start.49 = (bf16[4,88,896]{2,1,0:T(8,128)(2,1)}, bf16[4,88,896]{2,1,0:T(8,128)(2,1)}, u32[]{:S(2)}, u32[]{:S(2)}) collective-permute-start(bf16[4,88,896]{2,1,0:T(8,128)(2,1)} %get-tuple-element.312), channel_id=1, source_target_pairs={{0,64},{32,96},{64,0},{96,32},{1,65},{33,97},{65,1},{97,33},{2,66}... | collective-permute-start | bytes 1892360 | tf_op jit(solution)/shard_map/ppermute | solution.py:48
  398.9 36.9 %collective-permute-start.50 = (bf16[4,88,896]{2,1,0:T(8,128)(2,1)}, bf16[4,88,896]{2,1,0:T(8,128)(2,1)}, u32[]{:S(2)}, u32[]{:S(2)}) collective-permute-start(bf16[4,88,896]{2,1,0:T(8,128)(2,1)} %get-tuple-element.309), channel_id=1, source_target_pairs={{0,32},{32,64},{64,96},{96,0},{1,33},{33,65},{65,97},{97,1},{2,34}... | collective-permute-start | bytes 1892360 | tf_op jit(solution)/shard_map/ppermute | solution.py:48
  420.2 33.7 %collective-permute-start.53 = (bf16[4,88,896]{2,1,0:T(8,128)(2,1)}, bf16[4,88,896]{2,1,0:T(8,128)(2,1)S(1)}, u32[]{:S(2)}, u32[]{:S(2)}) collective-permute-start(bf16[4,88,896]{2,1,0:T(8,128)(2,1)} %get-tuple-element.313), channel_id=1, source_target_pairs={{0,16},{16,8},{8,24},{24,0},{1,17},{17,9},{9,25},{25,1},{2,18},{18... | collective-permute-start | bytes 1892360 | tf_op jit(solution)/shard_map/ppermute | solution.py:48
  464.6 24.2 %collective-permute-start.68 = (bf16[88,896]{1,0:T(8,128)(2,1)S(1)}, bf16[88,896]{1,0:T(8,128)(2,1)S(1)}, u32[]{:S(2)}, u32[]{:S(2)}) collective-permute-start(bf16[88,896]{1,0:T(8,128)(2,1)S(1)} %get-tuple-element.355), channel_id=1, source_target_pairs={{0,96},{32,0},{64,32},{96,64},{1,97},{33,1},{65,33},{97,65},{2,98}... | collective-permute-start | bytes 473096 | tf_op jit(solution)/shard_map/ppermute | solution.py:48
  465.5 23.4 %collective-permute-start.69 = (bf16[88,896]{1,0:T(8,128)(2,1)S(1)}, bf16[88,896]{1,0:T(8,128)(2,1)S(1)}, u32[]{:S(2)}, u32[]{:S(2)}) collective-permute-start(bf16[88,896]{1,0:T(8,128)(2,1)S(1)} %get-tuple-element.354), channel_id=1, source_target_pairs={{0,64},{32,96},{64,0},{96,32},{1,65},{33,97},{65,1},{97,33},{2,66}... | collective-permute-start | bytes 473096 | tf_op jit(solution)/shard_map/ppermute | solution.py:48
  488.9 21.1 %collective-permute-start.55 = (bf16[1536,512]{1,0:T(8,128)(2,1)}, bf16[1536,512]{1,0:T(8,128)(2,1)}, u32[]{:S(2)}, u32[]{:S(2)}) collective-permute-start(bf16[1536,512]{1,0:T(8,128)(2,1)} %fusion.46), channel_id=1, source_target_pairs={{0,1},{1,0},{2,3},{3,2},{4,5},{5,4},{6,7},{7,6},{8,9},{9,8},{10,11... | collective-permute-start | bytes 4718600 | tf_op jit(solution)/shard_map/ppermute | solution.py:39
  492.9 24.2 %collective-permute-start.60 = (bf16[4,56,1152]{2,1,0:T(8,128)(2,1)}, bf16[4,56,1152]{2,1,0:T(8,128)(2,1)}, u32[]{:S(2)}, u32[]{:S(2)}) collective-permute-start(bf16[4,56,1152]{2,1,0:T(8,128)(2,1)} %get-tuple-element.319), channel_id=1, source_target_pairs={{0,96},{32,0},{64,32},{96,64},{1,97},{33,1},{65,33},{97,65},{2,98}... | collective-permute-start | bytes 1548296 | tf_op jit(solution)/shard_map/ppermute | solution.py:48
  493.6 25.6 %collective-permute-start.61 = (bf16[4,56,1152]{2,1,0:T(8,128)(2,1)}, bf16[4,56,1152]{2,1,0:T(8,128)(2,1)}, u32[]{:S(2)}, u32[]{:S(2)}) collective-permute-start(bf16[4,56,1152]{2,1,0:T(8,128)(2,1)} %get-tuple-element.318), channel_id=1, source_target_pairs={{0,64},{32,96},{64,0},{96,32},{1,65},{33,97},{65,1},{97,33},{2,66}... | collective-permute-start | bytes 1548296 | tf_op jit(solution)/shard_map/ppermute | solution.py:48
  496.0 24.1 %collective-permute-start.62 = (bf16[4,56,1152]{2,1,0:T(8,128)(2,1)}, bf16[4,56,1152]{2,1,0:T(8,128)(2,1)}, u32[]{:S(2)}, u32[]{:S(2)}) collective-permute-start(bf16[4,56,1152]{2,1,0:T(8,128)(2,1)} %get-tuple-element.317), channel_id=1, source_target_pairs={{0,32},{32,64},{64,96},{96,0},{1,33},{33,65},{65,97},{97,1},{2,34}... | collective-permute-start | bytes 1548296 | tf_op jit(solution)/shard_map/ppermute | solution.py:48
  498.0 31.6 %collective-permute-start.64 = (bf16[1536,640]{1,0:T(8,128)(2,1)}, bf16[1536,640]{1,0:T(8,128)(2,1)}, u32[]{:S(2)}, u32[]{:S(2)}) collective-permute-start(bf16[1536,640]{1,0:T(8,128)(2,1)} %add_convert_fusion.3), channel_id=1, source_target_pairs={{0,1},{1,0},{2,3},{3,2},{4,5},{5,4},{6,7},{7,6},{8,9},{9,8},{10,11... | collective-permute-start | bytes 5898248 | tf_op jit(solution)/shard_map/ppermute | solution.py:39
  500.7 38.1 %all-to-all-start.3 = ((bf16[8,32,896]{2,1,0:T(8,128)(2,1)}), bf16[8,32,896]{2,1,0:T(8,128)(2,1)}, u32[]{:S(2)}, u32[]{:S(2)}) async-start(bf16[8,32,896]{2,1,0:T(8,128)(2,1)} %bitcast.334), calls=%async_computation.3 | async-start | bytes 917504 | tf_op jit(solution)/shard_map/all_to_all | solution.py:35
  525.2 34.5 %collective-permute-start.71 = (bf16[56,1152]{1,0:T(8,128)(2,1)}, bf16[56,1152]{1,0:T(8,128)(2,1)}, u32[]{:S(2)}, u32[]{:S(2)}) collective-permute-start(bf16[56,1152]{1,0:T(8,128)(2,1)} %get-tuple-element.359), channel_id=1, source_target_pairs={{0,24},{16,0},{8,16},{24,8},{1,25},{17,1},{9,17},{25,9},{2,26},{18... | collective-permute-start | bytes 387080 | tf_op jit(solution)/shard_map/ppermute | solution.py:48
  526.9 32.9 %collective-permute-start.72 = (bf16[56,1152]{1,0:T(8,128)(2,1)}, bf16[56,1152]{1,0:T(8,128)(2,1)}, u32[]{:S(2)}, u32[]{:S(2)}) collective-permute-start(bf16[56,1152]{1,0:T(8,128)(2,1)} %get-tuple-element.358), channel_id=1, source_target_pairs={{0,8},{16,24},{8,0},{24,16},{1,9},{17,25},{9,1},{25,17},{2,10},{18... | collective-permute-start | bytes 387080 | tf_op jit(solution)/shard_map/ppermute | solution.py:48
  527.0 32.7 %collective-permute-start.73 = (bf16[56,1152]{1,0:T(8,128)(2,1)}, bf16[56,1152]{1,0:T(8,128)(2,1)}, u32[]{:S(2)}, u32[]{:S(2)}) collective-permute-start(bf16[56,1152]{1,0:T(8,128)(2,1)} %get-tuple-element.357), channel_id=1, source_target_pairs={{0,16},{16,8},{8,24},{24,0},{1,17},{17,9},{9,25},{25,1},{2,18},{18... | collective-permute-start | bytes 387080 | tf_op jit(solution)/shard_map/ppermute | solution.py:48
  538.8 72.6 %all-to-all-start.4 = ((bf16[64,24,1408]{2,1,0:T(8,128)(2,1)}), bf16[64,24,1408]{2,1,0:T(8,128)(2,1)}, u32[]{:S(2)}, u32[]{:S(2)}) async-start(bf16[64,24,1408]{2,1,0:T(8,128)(2,1)} %pad_maximum_fusion.1), calls=%async_computation.4 | async-start | bytes 8650752 | tf_op jit(solution)/shard_map/all_to_all | solution.py:35
  585.0 22.8 %collective-permute-start.75 = (bf16[56,1152]{1,0:T(8,128)(2,1)}, bf16[56,1152]{1,0:T(8,128)(2,1)}, u32[]{:S(2)}, u32[]{:S(2)}) collective-permute-start(bf16[56,1152]{1,0:T(8,128)(2,1)} %add_convert_fusion.11), channel_id=1, source_target_pairs={{0,0},{32,1},{64,2},{96,3},{8,4},{40,5},{72,6},{104,7},{16,8},{48,... | collective-permute-start | bytes 387080 | tf_op jit(solution)/shard_map/ppermute | solution.py:523
  (221 other events, 2219.3 us)

commit v12 on v11

--- a/solution.py
+++ b/solution.py
@@ -517,8 +517,8 @@
     g_u_one = select_back(d_one, put_rows)
     grad_hidden = (g_after + norm_back(scale_one, n_one, gain_one_full, g_u_one)).astype(BF)
 
-    narrow = dot_tr(slab.reshape(256, 896), wider).reshape(8, 32, 864)
-    wide = jnp.concatenate([narrow[t] for t in range(8)], axis=1)
+    narrow = dot_tr(slab.reshape(256, 896), wider).astype(BF).reshape(8, 32, 864)
+    wide = jnp.concatenate([narrow[t, :22] for t in range(8)], axis=1)
     ga = jnp.sum(slab[:, 22:31, :512].astype(F32), axis=0)
     gw_down_own = lax.ppermute(
         add(down_second).astype(BF), EVERY, [(b, a) for a, b in down_route()]
@@ -526,7 +526,7 @@
     ga_down_own = dot_tr(gw_down_own, b_down)
 
     def over_columns(pairs):
-        return sum(jnp.sum(a.astype(F32) * b, axis=1) for a, b in pairs)
+        return sum(jnp.sum(a.astype(F32) * b.astype(F32), axis=1) for a, b in pairs)
 
     gain_two_own = over_columns(
         ((wg, wide[:9]), (wu, wide[9:18]), (ag, ga[:, :256]), (au, ga[:, 256:]))
@@ -569,13 +569,13 @@
         ga_out_own,
         own_out[8:10],
         gain_two_own,
-        wide[:9],
-        wide[9:18],
+        wide[:9].astype(F32),
+        wide[9:18].astype(F32),
         gw_down_own.astype(F32),
         ga[:, :256],
-        wide[18:20],
+        wide[18:20].astype(F32),
         ga[:, 256:],
-        wide[20:22],
+        wide[20:22].astype(F32),
         ga_down_own,
         own_out[10:],
     )

time: 638 us -> 637 us (level)
  the two profiles are of different devices: /device:TPU:63 before, /device:TPU:37 now
where the time goes in v12:
time: 637 us; the launch traced here: 625 us
  matrix products  172 us (27%)
  starting transfers between devices  168 us (26%)
  waiting for transfers between devices  105 us (16%)
  local copies, waits for them, and re-layouts  89.9 us (14%)
  other arithmetic  81.3 us (13%)
  between operations  9.07 us (1%)
    ppermute x45, starting transfers between devices, shift(): lax.ppermute(x, RING[axis], [(number[i], number[(i + k) % 4]) for i in ra...  85.1 us
    dot_general x37, matrix products, dot(): return jnp.dot(a, b, preferred_element_type=F32)  70.9 us
    dot_general x38, matrix products, dot_tr(): lax.dot_general(a, b, (((1,), (1,)), ((), ())), preferred_element_type=F32)  64.1 us
    ppermute x45, waiting for transfers between devices, shift(): lax.ppermute(x, RING[axis], [(number[i], number[(i + k) % 4]) for i in ra...  54.2 us
    all_to_all x5, starting transfers between devices, exchange(): return lax.all_to_all(x, axes, split_axis=0, concat_axis=0, tiled=True)  39.4 us
    dot_general x19, matrix products, dot_tl(): lax.dot_general(a, b, (((0,), (0,)), ((), ())), preferred_element_type=F32)  37.4 us
    ppermute x27, starting transfers between devices, other_core(): return lax.ppermute(x, 'c', [(0, 1), (1, 0)])  33.7 us
    unnamed x380, local copies, waits for them, and re-layouts  32.6 us
  transfers between devices with their start and end apart: 81, of which 26 were waited for; matrix products, arithmetic and copies ran while one was open for 44% of the time, Pallas kernels for 0%

profile of v12, /device:TPU:37, one launch (start us, length us, event | category | flops | bytes accessed | tf_op | source)
XLA Modules:
  0.0 625.3 jit_solution(7255211130356600351)
XLA Ops:
  13.8 10.5 %all-to-all-start = ((bf16[64,24,1152]{2,1,0:T(8,128)(2,1)}), bf16[64,24,1152]{2,1,0:T(8,128)(2,1)S(1)}, u32[]{:S(2)}, u32[]{:S(2)}) async-start(bf16[64,24,1152]{2,1,0:T(8,128)(2,1)} %broadcast_in_dim.163), calls=%async_computation | async-start | bytes 7077888 | tf_op jit(solution)/shard_map/all_to_all | solution.py:35
  64.9 4.8 collective-permute-start.4
  85.2 6.4 %collective-permute-start.8 = (bf16[56,1408]{1,0:T(8,128)(2,1)}, bf16[56,1408]{1,0:T(8,128)(2,1)}, u32[]{:S(2)}, u32[]{:S(2)}) collective-permute-start(bf16[56,1408]{1,0:T(8,128)(2,1)} %collective-permute-done.6), channel_id=1, source_target_pairs={{0,64},{32,96},{64,0},{96,32},{1,65},{33,97},{65,1},{97,33},{2,66}... | collective-permute-start | bytes 473096 | tf_op jit(solution)/shard_map/ppermute | solution.py:48
  102.7 8.9 %all-to-all-start.1 = ((bf16[64,24,1024]{2,1,0:T(8,128)(2,1)}), bf16[64,24,1024]{2,1,0:T(8,128)(2,1)}, u32[]{:S(2)}, u32[]{:S(2)}) async-start(bf16[64,24,1024]{2,1,0:T(8,128)(2,1)} %broadcast_in_dim.167), calls=%async_computation.1 | async-start | bytes 6291456 | tf_op jit(solution)/shard_map/all_to_all | solution.py:35
  130.9 17.5 %collective-permute-done.11 = bf16[160,512]{1,0:T(8,128)(2,1)S(1)} collective-permute-done((bf16[160,512]{1,0:T(8,128)(2,1)S(1)}, bf16[160,512]{1,0:T(8,128)(2,1)S(1)}, u32[]{:S(2)}, u32[]{:S(2)}) %collective-permute-start.11) | collective-permute-done | bytes 163872 | tf_op jit(solution)/shard_map/ppermute | solution.py:43
  162.3 4.6 collective-permute-done.13
  179.4 7.2 %all-to-all-start.2 = ((bf16[16,176,896]{2,1,0:T(8,128)(2,1)}), bf16[16,176,896]{2,1,0:T(8,128)(2,1)}, u32[]{:S(2)}, u32[]{:S(2)}) async-start(bf16[16,176,896]{2,1,0:T(8,128)(2,1)} %broadcast_in_dim.173), calls=%async_computation.2 | async-start | bytes 10092544 | tf_op jit(solution)/shard_map/all_to_all | solution.py:35
  242.6 10.5 %all-to-all-done.2 = bf16[16,176,896]{2,1,0:T(8,128)(2,1)} async-done(((bf16[16,176,896]{2,1,0:T(8,128)(2,1)}), bf16[16,176,896]{2,1,0:T(8,128)(2,1)}, u32[]{:S(2)}, u32[]{:S(2)}) %all-to-all-start.2) | async-done | bytes 5046304 | tf_op jit(solution)/shard_map/all_to_all | solution.py:35
  257.1 6.1 fusion.607
  263.2 3.9 add_convert_fusion
  267.1 8.9 %multiply_convert_fusion.1 = (bf16[1280,896]{1,0:T(8,128)(2,1)S(1)}, f32[1280,896]{1,0:T(8,128)}) fusion(f32[1280,896]{1,0:T(8,128)S(1)} %fusion.607, bf16[1280,1152]{1,0:T(8,128)(2,1)} %constant_dynamic-update-slice_fusion.31, bf16[1152,896]{1,0:T(8,128)(2,1)S(1)} %bitcast.337), kind=kOutput, calls=%fused_computation.41 | convolution fusion | flops 2653880320 | bytes 16482304 | tf_op jit(solution)/shard_map/dot_general | solution.py:23
  308.4 8.5 %collective-permute-done.28 = bf16[160,1152]{1,0:T(8,128)(2,1)S(1)} collective-permute-done((bf16[160,1152]{1,0:T(8,128)(2,1)S(1)}, bf16[160,1152]{1,0:T(8,128)(2,1)S(1)}, u32[]{:S(2)}, u32[]{:S(2)}) %collective-permute-start.28) | collective-permute-done | bytes 368672 | tf_op jit(solution)/shard_map/ppermute | solution.py:48
  334.3 4.1 collective-permute-done.35
  348.5 11.0 %fusion.10 = (bf16[1280,896]{1,0:T(8,128)(2,1)S(1)}, bf16[1280,896]{1,0:T(8,128)(2,1)S(1)}) fusion(f32[1280,896]{1,0:T(8,128)} %copy-done.171, f32[1280,896]{1,0:T(8,128)} %get-tuple-element.407, bf16[1280,1152]{1,0:T(8,128)(2,1)} %constant_dynamic-update-slice_fusion.39, bf16[896,1152]{1,0:T(8,128)(2,1)S(1)} %copy-done.162), kind=kOutput, calls=%fused_computation.33 | convolution fusion | flops 2672230400 | bytes 18776064 | tf_op jit(solution)/shard_map/dot_general | solution.py:31
  368.4 5.1 convolution_convert_fusion.1
  375.8 5.1 convolution_convert_fusion.2
  386.3 5.0 collective-permute-start.52
  392.5 9.6 %collective-permute-start.48 = (bf16[4,88,896]{2,1,0:T(8,128)(2,1)}, bf16[4,88,896]{2,1,0:T(8,128)(2,1)}, u32[]{:S(2)}, u32[]{:S(2)}) collective-permute-start(bf16[4,88,896]{2,1,0:T(8,128)(2,1)} %get-tuple-element.259), channel_id=1, source_target_pairs={{0,96},{32,0},{64,32},{96,64},{1,97},{33,1},{65,33},{97,65},{2,98}... | collective-permute-start | bytes 1892360 | tf_op jit(solution)/shard_map/ppermute | solution.py:48
  402.1 4.2 collective-permute-start.50
  420.6 5.2 collective-permute-done.50
  427.8 4.3 fusion.36
  435.8 5.8 multiply_convert_fusion
  445.7 6.8 %collective-permute-start.54 = (bf16[1280,512]{1,0:T(8,128)(2,1)S(1)}, bf16[1280,512]{1,0:T(8,128)(2,1)S(1)}, u32[]{:S(2)}, u32[]{:S(2)}) collective-permute-start(bf16[1280,512]{1,0:T(8,128)(2,1)S(1)} %slice.1366), channel_id=1, source_target_pairs={{0,1},{1,0},{2,3},{3,2},{4,5},{5,4},{6,7},{7,6},{8,9},{9,8},{10,11... | collective-permute-start | bytes 3932168 | tf_op jit(solution)/shard_map/ppermute | solution.py:39
  461.9 7.0 %collective-permute-start.57 = (bf16[320,512]{1,0:T(8,128)(2,1)S(1)}, bf16[320,512]{1,0:T(8,128)(2,1)S(1)}, u32[]{:S(2)}, u32[]{:S(2)}) collective-permute-start(bf16[320,512]{1,0:T(8,128)(2,1)S(1)} %get-tuple-element.271), channel_id=1, source_target_pairs={{0,4},{2,6},{4,0},{6,2},{1,5},{3,7},{5,1},{7,3},{8,12},{10,14},{12... | collective-permute-start | bytes 983048 | tf_op jit(solution)/shard_map/ppermute | solution.py:48
  476.8 6.2 collective-permute-done.57
  483.1 4.1 collective-permute-start.65
  502.8 4.1 all-to-all-start.3
  516.5 4.8 collective-permute-done.61
  541.0 8.8 %all-to-all-start.4 = ((bf16[64,24,1408]{2,1,0:T(8,128)(2,1)}), bf16[64,24,1408]{2,1,0:T(8,128)(2,1)}, u32[]{:S(2)}, u32[]{:S(2)}) async-start(bf16[64,24,1408]{2,1,0:T(8,128)(2,1)} %pad_maximum_fusion.1), calls=%async_computation.4 | async-start | bytes 8650752 | tf_op jit(solution)/shard_map/all_to_all | solution.py:35
  572.8 4.6 collective-permute-start.75
  589.5 10.7 %collective-permute-done.75 = bf16[56,1152]{1,0:T(8,128)(2,1)S(1)} collective-permute-done((bf16[56,1152]{1,0:T(8,128)(2,1)}, bf16[56,1152]{1,0:T(8,128)(2,1)S(1)}, u32[]{:S(2)}, u32[]{:S(2)}) %collective-permute-start.75) | collective-permute-done | bytes 129056 | tf_op jit(solution)/shard_map/ppermute | solution.py:523
  601.9 7.6 %all-to-all-done.4 = bf16[64,24,1408]{2,1,0:T(8,128)(2,1)} async-done(((bf16[64,24,1408]{2,1,0:T(8,128)(2,1)}), bf16[64,24,1408]{2,1,0:T(8,128)(2,1)}, u32[]{:S(2)}, u32[]{:S(2)}) %all-to-all-start.4) | async-done | bytes 4325408 | tf_op jit(solution)/shard_map/all_to_all | solution.py:35
  (781 shorter events, 394.4 us)
Async XLA Ops:
  13.8 65.8 %all-to-all-start = ((bf16[64,24,1152]{2,1,0:T(8,128)(2,1)}), bf16[64,24,1152]{2,1,0:T(8,128)(2,1)S(1)}, u32[]{:S(2)}, u32[]{:S(2)}) async-start(bf16[64,24,1152]{2,1,0:T(8,128)(2,1)} %broadcast_in_dim.163), calls=%async_computation | async-start | bytes 7077888 | tf_op jit(solution)/shard_map/all_to_all | solution.py:35
  35.7 28.0 %collective-permute-start.1 = (bf16[4,24,896]{2,1,0:T(8,128)(2,1)}, bf16[4,24,896]{2,1,0:T(8,128)(2,1)}, u32[]{:S(2)}, u32[]{:S(2)}) collective-permute-start(bf16[4,24,896]{2,1,0:T(8,128)(2,1)} %get-tuple-element.310), channel_id=1, source_target_pairs={{0,1},{1,0},{2,3},{3,2},{4,5},{5,4},{6,7},{7,6},{8,9},{9,8},{10,11... | collective-permute-start | bytes 516104 | tf_op jit(solution)/shard_map/ppermute | solution.py:39
  41.6 20.5 %collective-permute-start.5 = (bf16[12,1024]{1,0:T(8,128)(2,1)}, bf16[12,1024]{1,0:T(8,128)(2,1)}, u32[]{:S(2)}, u32[]{:S(2)}) collective-permute-start(bf16[12,1024]{1,0:T(8,128)(2,1)} %broadcast_select_fusion.19), channel_id=1, source_target_pairs={{0,1},{1,0},{2,3},{3,2},{4,5},{5,4},{6,7},{7,6},{8,9},{9,8},{10,11... | collective-permute-start | bytes 73736 | tf_op jit(solution)/shard_map/ppermute | solution.py:39
  43.2 35.5 %collective-permute-start.6 = (bf16[56,1408]{1,0:T(8,128)(2,1)}, bf16[56,1408]{1,0:T(8,128)(2,1)}, u32[]{:S(2)}, u32[]{:S(2)}) collective-permute-start(bf16[56,1408]{1,0:T(8,128)(2,1)} %fusion.326), channel_id=1, source_target_pairs={{0,0},{1,32},{2,64},{3,96},{4,8},{5,40},{6,72},{7,104},{8,16},{9,4... | collective-permute-start | bytes 473096 | tf_op jit(solution)/shard_map/ppermute | solution.py:249
  79.6 40.7 %collective-permute-start.10 = (bf16[64,24,1152]{2,1,0:T(8,128)(2,1)S(1)}, bf16[64,24,1152]{2,1,0:T(8,128)(2,1)}, u32[]{:S(2)}, u32[]{:S(2)}) collective-permute-start(bf16[64,24,1152]{2,1,0:T(8,128)(2,1)S(1)} %all-to-all-done), channel_id=1, source_target_pairs={{0,1},{1,0},{2,3},{3,2},{4,5},{5,4},{6,7},{7,6},{8,9},{9,8},{10,11... | collective-permute-start | bytes 10616840 | tf_op jit(solution)/shard_map/ppermute | solution.py:39
  102.7 53.6 %all-to-all-start.1 = ((bf16[64,24,1024]{2,1,0:T(8,128)(2,1)}), bf16[64,24,1024]{2,1,0:T(8,128)(2,1)}, u32[]{:S(2)}, u32[]{:S(2)}) async-start(bf16[64,24,1024]{2,1,0:T(8,128)(2,1)} %broadcast_in_dim.167), calls=%async_computation.1 | async-start | bytes 6291456 | tf_op jit(solution)/shard_map/all_to_all | solution.py:35
  129.1 19.4 %collective-permute-start.11 = (bf16[160,512]{1,0:T(8,128)(2,1)S(1)}, bf16[160,512]{1,0:T(8,128)(2,1)S(1)}, u32[]{:S(2)}, u32[]{:S(2)}) collective-permute-start(bf16[160,512]{1,0:T(8,128)(2,1)S(1)} %get-tuple-element.347), channel_id=1, source_target_pairs={{0,8},{8,0},{1,9},{9,1},{2,10},{10,2},{3,11},{11,3},{4,12},{12,4},... | collective-permute-start | bytes 491528 | tf_op jit(solution)/shard_map/ppermute | solution.py:43
  179.4 73.7 %all-to-all-start.2 = ((bf16[16,176,896]{2,1,0:T(8,128)(2,1)}), bf16[16,176,896]{2,1,0:T(8,128)(2,1)}, u32[]{:S(2)}, u32[]{:S(2)}) async-start(bf16[16,176,896]{2,1,0:T(8,128)(2,1)} %broadcast_in_dim.173), calls=%async_computation.2 | async-start | bytes 10092544 | tf_op jit(solution)/shard_map/all_to_all | solution.py:35
  186.6 19.2 %collective-permute-start.16 = (bf16[64,24,1024]{2,1,0:T(8,128)(2,1)}, bf16[64,24,1024]{2,1,0:T(8,128)(2,1)S(1)}, u32[]{:S(2)}, u32[]{:S(2)}) collective-permute-start(bf16[64,24,1024]{2,1,0:T(8,128)(2,1)} %all-to-all-done.1), channel_id=1, source_target_pairs={{0,1},{1,0},{2,3},{3,2},{4,5},{5,4},{6,7},{7,6},{8,9},{9,8},{10,11... | collective-permute-start | bytes 9437192 | tf_op jit(solution)/shard_map/ppermute | solution.py:39
  192.2 84.2 %collective-permute-start.24 = (bf16[4,56,1408]{2,1,0:T(8,128)(2,1)}, bf16[4,56,1408]{2,1,0:T(8,128)(2,1)}, u32[]{:S(2)}, u32[]{:S(2)}) collective-permute-start(bf16[4,56,1408]{2,1,0:T(8,128)(2,1)} %bitcast_dynamic-update-slice_fusion.4), channel_id=1, source_target_pairs={{0,16},{16,8},{8,24},{24,0},{1,17},{17,9},{9,25},{25,1},{2,18},{18... | collective-permute-start | bytes 1892360 | tf_op jit(solution)/shard_map/ppermute | solution.py:48
  193.1 83.3 %collective-permute-start.25 = (bf16[4,56,1408]{2,1,0:T(8,128)(2,1)}, bf16[4,56,1408]{2,1,0:T(8,128)(2,1)}, u32[]{:S(2)}, u32[]{:S(2)}) collective-permute-start(bf16[4,56,1408]{2,1,0:T(8,128)(2,1)} %bitcast_dynamic-update-slice_fusion.4), channel_id=1, source_target_pairs={{0,8},{16,24},{8,0},{24,16},{1,9},{17,25},{9,1},{25,17},{2,10},{18... | collective-permute-start | bytes 1892360 | tf_op jit(solution)/shard_map/ppermute | solution.py:48
  193.7 82.7 %collective-permute-start.26 = (bf16[4,56,1408]{2,1,0:T(8,128)(2,1)}, bf16[4,56,1408]{2,1,0:T(8,128)(2,1)}, u32[]{:S(2)}, u32[]{:S(2)}) collective-permute-start(bf16[4,56,1408]{2,1,0:T(8,128)(2,1)} %bitcast_dynamic-update-slice_fusion.4), channel_id=1, source_target_pairs={{0,24},{16,0},{8,16},{24,8},{1,25},{17,1},{9,17},{25,9},{2,26},{18... | collective-permute-start | bytes 1892360 | tf_op jit(solution)/shard_map/ppermute | solution.py:48
  367.1 19.2 %collective-permute-start.47 = (bf16[160,1152]{1,0:T(8,128)(2,1)S(1)}, bf16[160,1152]{1,0:T(8,128)(2,1)S(1)}, u32[]{:S(2)}, u32[]{:S(2)}) collective-permute-start(bf16[160,1152]{1,0:T(8,128)(2,1)S(1)} %get-tuple-element.250), channel_id=1, source_target_pairs={{0,1},{1,0},{2,3},{3,2},{4,5},{5,4},{6,7},{7,6},{8,9},{9,8},{10,11... | collective-permute-start | bytes 1105928 | tf_op jit(solution)/shard_map/ppermute | solution.py:39
  375.8 68.0 %collective-permute-start.51 = (bf16[4,88,896]{2,1,0:T(8,128)(2,1)}, bf16[4,88,896]{2,1,0:T(8,128)(2,1)}, u32[]{:S(2)}, u32[]{:S(2)}) collective-permute-start(bf16[4,88,896]{2,1,0:T(8,128)(2,1)} %get-tuple-element.263), channel_id=1, source_target_pairs={{0,24},{16,0},{8,16},{24,8},{1,25},{17,1},{9,17},{25,9},{2,26},{18... | collective-permute-start | bytes 1892360 | tf_op jit(solution)/shard_map/ppermute | solution.py:48
  381.3 20.8 %collective-permute-start.44 = (bf16[160,1152]{1,0:T(8,128)(2,1)S(1)}, bf16[160,1152]{1,0:T(8,128)(2,1)S(1)}, u32[]{:S(2)}, u32[]{:S(2)}) collective-permute-start(bf16[160,1152]{1,0:T(8,128)(2,1)S(1)} %get-tuple-element.243), channel_id=1, source_target_pairs={{0,6},{2,0},{4,2},{6,4},{1,7},{3,1},{5,3},{7,5},{8,14},{10,8},{12,... | collective-permute-start | bytes 1105928 | tf_op jit(solution)/shard_map/ppermute | solution.py:48
  386.3 57.4 %collective-permute-start.52 = (bf16[4,88,896]{2,1,0:T(8,128)(2,1)}, bf16[4,88,896]{2,1,0:T(8,128)(2,1)}, u32[]{:S(2)}, u32[]{:S(2)}) collective-permute-start(bf16[4,88,896]{2,1,0:T(8,128)(2,1)} %get-tuple-element.264), channel_id=1, source_target_pairs={{0,8},{16,24},{8,0},{24,16},{1,9},{17,25},{9,1},{25,17},{2,10},{18... | collective-permute-start | bytes 1892360 | tf_op jit(solution)/shard_map/ppermute | solution.py:48
  392.5 25.5 %collective-permute-start.48 = (bf16[4,88,896]{2,1,0:T(8,128)(2,1)}, bf16[4,88,896]{2,1,0:T(8,128)(2,1)}, u32[]{:S(2)}, u32[]{:S(2)}) collective-permute-start(bf16[4,88,896]{2,1,0:T(8,128)(2,1)} %get-tuple-element.259), channel_id=1, source_target_pairs={{0,96},{32,0},{64,32},{96,64},{1,97},{33,1},{65,33},{97,65},{2,98}... | collective-permute-start | bytes 1892360 | tf_op jit(solution)/shard_map/ppermute | solution.py:48
  402.1 23.7 %collective-permute-start.50 = (bf16[4,88,896]{2,1,0:T(8,128)(2,1)}, bf16[4,88,896]{2,1,0:T(8,128)(2,1)}, u32[]{:S(2)}, u32[]{:S(2)}) collective-permute-start(bf16[4,88,896]{2,1,0:T(8,128)(2,1)} %get-tuple-element.257), channel_id=1, source_target_pairs={{0,32},{32,64},{64,96},{96,0},{1,33},{33,65},{65,97},{97,1},{2,34}... | collective-permute-start | bytes 1892360 | tf_op jit(solution)/shard_map/ppermute | solution.py:48
  418.0 25.7 %collective-permute-start.53 = (bf16[4,88,896]{2,1,0:T(8,128)(2,1)}, bf16[4,88,896]{2,1,0:T(8,128)(2,1)S(1)}, u32[]{:S(2)}, u32[]{:S(2)}) collective-permute-start(bf16[4,88,896]{2,1,0:T(8,128)(2,1)} %get-tuple-element.261), channel_id=1, source_target_pairs={{0,16},{16,8},{8,24},{24,0},{1,17},{17,9},{9,25},{25,1},{2,18},{18... | collective-permute-start | bytes 1892360 | tf_op jit(solution)/shard_map/ppermute | solution.py:48
  458.4 30.8 %collective-permute-start.68 = (bf16[88,896]{1,0:T(8,128)(2,1)S(1)}, bf16[88,896]{1,0:T(8,128)(2,1)S(1)}, u32[]{:S(2)}, u32[]{:S(2)}) collective-permute-start(bf16[88,896]{1,0:T(8,128)(2,1)S(1)} %get-tuple-element.291), channel_id=1, source_target_pairs={{0,96},{32,0},{64,32},{96,64},{1,97},{33,1},{65,33},{97,65},{2,98}... | collective-permute-start | bytes 473096 | tf_op jit(solution)/shard_map/ppermute | solution.py:48
  461.1 29.0 %collective-permute-start.69 = (bf16[88,896]{1,0:T(8,128)(2,1)S(1)}, bf16[88,896]{1,0:T(8,128)(2,1)S(1)}, u32[]{:S(2)}, u32[]{:S(2)}) collective-permute-start(bf16[88,896]{1,0:T(8,128)(2,1)S(1)} %get-tuple-element.290), channel_id=1, source_target_pairs={{0,64},{32,96},{64,0},{96,32},{1,65},{33,97},{65,1},{97,33},{2,66}... | collective-permute-start | bytes 473096 | tf_op jit(solution)/shard_map/ppermute | solution.py:48
  461.9 21.2 %collective-permute-start.57 = (bf16[320,512]{1,0:T(8,128)(2,1)S(1)}, bf16[320,512]{1,0:T(8,128)(2,1)S(1)}, u32[]{:S(2)}, u32[]{:S(2)}) collective-permute-start(bf16[320,512]{1,0:T(8,128)(2,1)S(1)} %get-tuple-element.271), channel_id=1, source_target_pairs={{0,4},{2,6},{4,0},{6,2},{1,5},{3,7},{5,1},{7,3},{8,12},{10,14},{12... | collective-permute-start | bytes 983048 | tf_op jit(solution)/shard_map/ppermute | solution.py:48
  495.0 21.5 %collective-permute-start.60 = (bf16[4,56,1152]{2,1,0:T(8,128)(2,1)}, bf16[4,56,1152]{2,1,0:T(8,128)(2,1)}, u32[]{:S(2)}, u32[]{:S(2)}) collective-permute-start(bf16[4,56,1152]{2,1,0:T(8,128)(2,1)} %get-tuple-element.267), channel_id=1, source_target_pairs={{0,96},{32,0},{64,32},{96,64},{1,97},{33,1},{65,33},{97,65},{2,98}... | collective-permute-start | bytes 1548296 | tf_op jit(solution)/shard_map/ppermute | solution.py:48
  496.0 25.3 %collective-permute-start.61 = (bf16[4,56,1152]{2,1,0:T(8,128)(2,1)}, bf16[4,56,1152]{2,1,0:T(8,128)(2,1)}, u32[]{:S(2)}, u32[]{:S(2)}) collective-permute-start(bf16[4,56,1152]{2,1,0:T(8,128)(2,1)} %get-tuple-element.266), channel_id=1, source_target_pairs={{0,64},{32,96},{64,0},{96,32},{1,65},{33,97},{65,1},{97,33},{2,66}... | collective-permute-start | bytes 1548296 | tf_op jit(solution)/shard_map/ppermute | solution.py:48
  498.0 24.1 %collective-permute-start.62 = (bf16[4,56,1152]{2,1,0:T(8,128)(2,1)}, bf16[4,56,1152]{2,1,0:T(8,128)(2,1)}, u32[]{:S(2)}, u32[]{:S(2)}) collective-permute-start(bf16[4,56,1152]{2,1,0:T(8,128)(2,1)} %get-tuple-element.265), channel_id=1, source_target_pairs={{0,32},{32,64},{64,96},{96,0},{1,33},{33,65},{65,97},{97,1},{2,34}... | collective-permute-start | bytes 1548296 | tf_op jit(solution)/shard_map/ppermute | solution.py:48
  500.0 31.7 %collective-permute-start.64 = (bf16[1536,640]{1,0:T(8,128)(2,1)}, bf16[1536,640]{1,0:T(8,128)(2,1)}, u32[]{:S(2)}, u32[]{:S(2)}) collective-permute-start(bf16[1536,640]{1,0:T(8,128)(2,1)} %add_convert_fusion.3), channel_id=1, source_target_pairs={{0,1},{1,0},{2,3},{3,2},{4,5},{5,4},{6,7},{7,6},{8,9},{9,8},{10,11... | collective-permute-start | bytes 5898248 | tf_op jit(solution)/shard_map/ppermute | solution.py:39
  502.8 38.2 %all-to-all-start.3 = ((bf16[8,32,896]{2,1,0:T(8,128)(2,1)}), bf16[8,32,896]{2,1,0:T(8,128)(2,1)}, u32[]{:S(2)}, u32[]{:S(2)}) async-start(bf16[8,32,896]{2,1,0:T(8,128)(2,1)} %bitcast.352), calls=%async_computation.3 | async-start | bytes 917504 | tf_op jit(solution)/shard_map/all_to_all | solution.py:35
  527.3 32.8 %collective-permute-start.71 = (bf16[56,1152]{1,0:T(8,128)(2,1)}, bf16[56,1152]{1,0:T(8,128)(2,1)}, u32[]{:S(2)}, u32[]{:S(2)}) collective-permute-start(bf16[56,1152]{1,0:T(8,128)(2,1)} %get-tuple-element.295), channel_id=1, source_target_pairs={{0,24},{16,0},{8,16},{24,8},{1,25},{17,1},{9,17},{25,9},{2,26},{18... | collective-permute-start | bytes 387080 | tf_op jit(solution)/shard_map/ppermute | solution.py:48
  528.0 32.1 %collective-permute-start.72 = (bf16[56,1152]{1,0:T(8,128)(2,1)}, bf16[56,1152]{1,0:T(8,128)(2,1)}, u32[]{:S(2)}, u32[]{:S(2)}) collective-permute-start(bf16[56,1152]{1,0:T(8,128)(2,1)} %get-tuple-element.294), channel_id=1, source_target_pairs={{0,8},{16,24},{8,0},{24,16},{1,9},{17,25},{9,1},{25,17},{2,10},{18... | collective-permute-start | bytes 387080 | tf_op jit(solution)/shard_map/ppermute | solution.py:48
  531.4 28.7 %collective-permute-start.73 = (bf16[56,1152]{1,0:T(8,128)(2,1)}, bf16[56,1152]{1,0:T(8,128)(2,1)}, u32[]{:S(2)}, u32[]{:S(2)}) collective-permute-start(bf16[56,1152]{1,0:T(8,128)(2,1)} %get-tuple-element.293), channel_id=1, source_target_pairs={{0,16},{16,8},{8,24},{24,0},{1,17},{17,9},{9,25},{25,1},{2,18},{18... | collective-permute-start | bytes 387080 | tf_op jit(solution)/shard_map/ppermute | solution.py:48
  541.0 68.5 %all-to-all-start.4 = ((bf16[64,24,1408]{2,1,0:T(8,128)(2,1)}), bf16[64,24,1408]{2,1,0:T(8,128)(2,1)}, u32[]{:S(2)}, u32[]{:S(2)}) async-start(bf16[64,24,1408]{2,1,0:T(8,128)(2,1)} %pad_maximum_fusion.1), calls=%async_computation.4 | async-start | bytes 8650752 | tf_op jit(solution)/shard_map/all_to_all | solution.py:35
  572.8 27.4 %collective-permute-start.75 = (bf16[56,1152]{1,0:T(8,128)(2,1)}, bf16[56,1152]{1,0:T(8,128)(2,1)S(1)}, u32[]{:S(2)}, u32[]{:S(2)}) collective-permute-start(bf16[56,1152]{1,0:T(8,128)(2,1)} %add_convert_fusion.11), channel_id=1, source_target_pairs={{0,0},{32,1},{64,2},{96,3},{8,4},{40,5},{72,6},{104,7},{16,8},{48,... | collective-permute-start | bytes 387080 | tf_op jit(solution)/shard_map/ppermute | solution.py:523
  (225 other events, 2354.8 us)
